TPU v7x, 32 devices: a whole 2x2x4 slice. The times are simulated.
32 devices in a mesh: slab: 4 (over y, x), chan: 8 (over z, core).
Axes of the slice: x: 2, y: 2, z: 4, core: 2. Of those that a mesh axis runs over, the one named last changes fastest.
Arguments:
- x_in: bfloat16 [256, 8, 8, 128], P('chan', 'slab'), may hold values from -6 to 6
- weight: bfloat16 [256, 27, 256], P('chan'), may hold values from -0.109375 to 0.109375
- bias_vec: bfloat16 [256], P('chan'), may hold values from -3 to 3
- grad_out: bfloat16 [256, 8, 8, 128], P('chan', 'slab'), may hold values from -6 to 6
Outputs:
- activation: bfloat16 [256, 8, 8, 128], P('chan', 'slab')
- input_grad: bfloat16 [256, 8, 8, 128], P('chan', 'slab')
- weight_grad: float32 [256, 27, 256], P('chan')
- bias_grad: float32 [256], P('chan')
All inputs are finite; a program needn't handle non-finite values.
Results may differ from a plain program's by a relative error of at most 0.008.
Values may be sent and summed in bfloat16 or wider, within the bound.
No kernel may reach another device: no remote copies, remote signals or barrier semaphores. Data moves between devices by JAX's collectives and lax.ppermute only.
A program may use at most 64 MiB of HBM per device.

v0:
```python
import math

import jax
import jax.numpy as jnp
from jax import lax
from jax.sharding import PartitionSpec as P


def with_halo(block, sides, width):
    for axis, dim in sides:
        count = lax.axis_size(axis)
        forward = [(i, i + 1) for i in range(count - 1)]
        forward.append((count - 1, 0))
        backward = [(target, source) for source, target in forward]
        low = lax.ppermute(
            lax.slice_in_dim(block, block.shape[dim] - width, None, axis=dim), axis, forward
        )
        high = lax.ppermute(lax.slice_in_dim(block, 0, width, axis=dim), axis, backward)
        block = jnp.concatenate([low, block, high], axis=dim)
    return block


def tap_list():
    return [(9 * i + 3 * j + l, i, j, l) for i in range(3) for j in range(3) for l in range(3)]


def on_device(x_in, weight, bias_vec, grad_out):
    out_local, n_taps, in_total = weight.shape
    n_planes, n_rows, n_depth = (x_in.shape[1], x_in.shape[2], x_in.shape[3])
    rimmed = with_halo(x_in, (("slab", 1),), 1)
    padded = lax.all_gather(rimmed, "chan", axis=0, tiled=True)
    own_planes = padded[:, 1 : n_planes + 1]
    pre_act = (
        jnp.zeros((out_local, n_planes, n_rows, n_depth), jnp.float32)
        + bias_vec.astype(jnp.float32)[:, None, None, None]
    )
    for i in range(3):
        w_plane = jnp.transpose(weight[:, 9 * i : 9 * i + 9], (1, 0, 2)).reshape(
            9 * out_local, in_total
        )
        plane_part = jnp.dot(
            w_plane,
            padded[:, i : i + n_planes].reshape(in_total, -1),
            preferred_element_type=jnp.float32,
        )
        plane_part = plane_part.reshape(9, out_local, n_planes, n_rows, n_depth)
        for j in range(3):
            for l in range(3):
                pre_act = pre_act + jnp.roll(plane_part[3 * j + l], (1 - j, 1 - l), axis=(2, 3))
    sigmoid_v = jax.nn.sigmoid(pre_act)
    activation = (pre_act * sigmoid_v).astype(jnp.bfloat16)
    slope = sigmoid_v * (1.0 + pre_act * (1.0 - sigmoid_v))
    grad_pre = (grad_out.astype(jnp.float32) * slope).astype(jnp.bfloat16)
    padded_grad = with_halo(grad_pre, (("slab", 1),), 1)
    shifted = jnp.stack(
        [
            jnp.roll(padded_grad[:, 2 - i : 2 - i + n_planes], (j - 1, l - 1), axis=(2, 3))
            for k, i, j, l in tap_list()
        ],
        0,
    )
    shifted = shifted.reshape(n_taps * out_local, -1)
    grad_scale = 1.0 / math.sqrt(lax.axis_size("slab") * n_planes * n_rows * n_depth)
    filter_local = lax.dot_general(
        shifted,
        own_planes.reshape(in_total, -1),
        (((1,), (1,)), ((), ())),
        preferred_element_type=jnp.float32,
    )
    filter_part = (
        jnp.transpose(filter_local.reshape(n_taps, out_local, in_total), (1, 0, 2)) * grad_scale
    )
    bias_part = grad_scale * jnp.sum(grad_pre.astype(jnp.float32), axis=(1, 2, 3))
    bias_row = jnp.concatenate(
        [bias_part[:, None, None], jnp.zeros((out_local, 1, in_total - 1), jnp.float32)], 2
    )
    summed_filters = lax.psum(jnp.concatenate([filter_part, bias_row], 1), "slab")
    weight_grad = summed_filters[:, :n_taps]
    bias_grad = summed_filters[:, n_taps, 0]
    flat_w = jnp.transpose(weight, (1, 0, 2)).reshape(n_taps * out_local, in_total)
    product = lax.dot_general(
        flat_w, shifted, (((0,), (0,)), ((), ())), preferred_element_type=jnp.float32
    )
    grad_in = lax.psum_scatter(
        product.reshape(
            in_total // lax.axis_size("chan") * lax.axis_size("chan"), n_planes, n_rows, n_depth
        ),
        "chan",
        scatter_dimension=0,
        tiled=True,
    )
    return (activation, grad_in.astype(jnp.bfloat16), weight_grad, bias_grad)


def solution(mesh):
    placed = (
        P("chan", "slab", None, None),
        P("chan", None, None),
        P("chan"),
        P("chan", "slab", None, None),
    )
    return jax.shard_map(
        on_device,
        mesh=mesh,
        in_specs=placed,
        out_specs=(
            P("chan", "slab", None, None),
            P("chan", "slab", None, None),
            P("chan", None, None),
            P("chan"),
        ),
        check_vma=False,
    )
```

profile of v0, /device:TPU:0, one launch (start us, length us, event | category | flops | bytes accessed | tf_op | source)
XLA Modules:
  0.0 185.1 jit_solution(13694304946928512164)
XLA Ops:
  8.2 3.9 %collective-permute-start.1 = (bf16[32,1,8,128]{3,0,2,1:T(8,128)(2,1)S(1)}, bf16[32,1,8,128]{3,0,2,1:T(8,128)(2,1)S(1)}, u32[]{:S(2)}, u32[]{:S(2)}) collective-permute-start(bf16[32,1,8,128]{3,0,2,1:T(8,128)(2,1)S(1)} %get-tuple-element.105), channel_id=1, source_target_pairs={{8,0},{16,8},{24,16},{0,24},{9,1},{17,9},{25,17},{1,25},{10,2},{18... | collective-permute-start | bytes 196616 | tf_op jit(solution)/shard_map/ppermute | solution.py:18
  12.1 2.0 %collective-permute-done.1 = bf16[32,1,8,128]{3,0,2,1:T(8,128)(2,1)S(1)} collective-permute-done((bf16[32,1,8,128]{3,0,2,1:T(8,128)(2,1)S(1)}, bf16[32,1,8,128]{3,0,2,1:T(8,128)(2,1)S(1)}, u32[]{:S(2)}, u32[]{:S(2)}) %collective-permute-start.1) | collective-permute-done | bytes 65568 | tf_op jit(solution)/shard_map/ppermute | solution.py:18
  14.2 3.1 %collective-permute-done = bf16[32,1,8,128]{3,0,2,1:T(8,128)(2,1)S(1)} collective-permute-done((bf16[32,1,8,128]{3,0,2,1:T(8,128)(2,1)S(1)}, bf16[32,1,8,128]{3,0,2,1:T(8,128)(2,1)S(1)}, u32[]{:S(2)}, u32[]{:S(2)}) %collective-permute-start) | collective-permute-done | bytes 65568 | tf_op jit(solution)/shard_map/ppermute | solution.py:15
  18.1 1.2 convert_element_type.18
  19.3 1.7 fusion.95
  21.0 25.7 %all-gather.2.cloned.1.call-done = bf16[256,4,8,128]{3,0,2,1:T(8,128)(2,1)} async-done(((bf16[32,4,8,128]{3,0,2,1:T(8,128)(2,1)}), bf16[256,4,8,128]{3,0,2,1:T(8,128)(2,1)}) %all-gather.2.cloned.1.call-update) | async-done | bytes 2097168 | tf_op jit(solution)/shard_map/all_gather | solution.py:31
  46.7 3.1 %fusion.94 = (bf16[256,2,8,128]{3,0,2,1:T(8,128)(2,1)S(1)}, bf16[256,2,8,128]{3,0,2,1:T(8,128)(2,1)}, bf16[256,2,8,128]{3,0,2,1:T(8,128)(2,1)S(1)}) fusion(bf16[256,4,8,128]{3,0,2,1:T(8,128)(2,1)} %all-gather.2.cloned.1.call-done), kind=kLoop, calls=%fused_computation.234 | loop fusion | bytes 6291456 | tf_op jit(solution)/shard_map/slice | solution.py:43
  49.8 1.5 copy.105
  51.3 1.4 convolution_bitcast_fusion
  52.7 1.1 slice_bitcast_fusion.8
  73.2 2.6 %convert_reduce_fusion = (f32[32]{0:T(128)S(1)}, bf16[32,2,8,128]{3,0,2,1:T(8,128)(2,1)S(1)}, f32[32,2,8,128]{3,0,2,1:T(8,128)}) fusion(bf16[32,2,8,128]{3,2,1,0:T(8,128)(2,1)S(1)} %copy-done.16, f32[32,2,8,1]{3,0,2,1:T(8,128)S(1)} %bitcast.308, f32[32,2,8,127]{3,0,2,1:T(8,128)S(1)} %slice.880, f32[32,2,1,128]{3,0,2,1:T(8,128)S(1)} %copy.176, ...), kind=kLoop, calls=%fused_computation.116 | loop fusion | flops 4128736 | bytes 7602432 | tf_op jit(solution)/shard_map/reduce_sum | solution.py:73
  75.9 1.5 collective-permute-start.3
  77.4 1.5 collective-permute-start.2
  78.9 2.5 %collective-permute-done.3 = bf16[32,1,8,128]{3,0,2,1:T(8,128)(2,1)S(1)} collective-permute-done((bf16[32,1,8,128]{3,0,2,1:T(8,128)(2,1)S(1)}, bf16[32,1,8,128]{3,0,2,1:T(8,128)(2,1)S(1)}, u32[]{:S(2)}, u32[]{:S(2)}) %collective-permute-start.3) | collective-permute-done | bytes 65568 | tf_op jit(solution)/shard_map/ppermute | solution.py:15
  86.5 1.1 fusion.1
  89.3 3.6 %copy.124 = bf16[27,32,2,8,128]{4,3,2,1,0:T(8,128)(2,1)S(1)} copy(bf16[27,32,2,8,128]{4,1,3,2,0:T(8,128)(2,1)} %copy-done.1) | data formatting | bytes 7077888 | tf_op jit(solution)/shard_map/stack | solution.py:55
  93.0 3.5 %reshape.112 = bf16[864,2048]{1,0:T(8,128)(2,1)} reshape(bf16[27,32,2,8,128]{4,3,2,1,0:T(8,128)(2,1)S(1)} %copy.124) | data formatting | bytes 7077888 | tf_op jit(solution)/shard_map/reshape | solution.py:62
  96.5 3.4 %fusion.102 = f32[2048,256]{1,0:T(8,128)S(1)} fusion(bf16[864,2048]{1,0:T(8,128)(2,1)} %reshape.112, bf16[864,256]{1,0:T(8,128)(2,1)} %bitcast.363), kind=kOutput, calls=%fused_computation.242 | convolution fusion | flops 905969664 | bytes 6078464 | tf_op jit(solution)/shard_map/dot_general | solution.py:81
  99.9 2.0 %copy.125 = f32[256,2,8,128]{3,2,1,0:T(8,128)} copy(f32[256,2,8,128]{0,3,2,1:T(8,128)S(1)} %bitcast.314) | data formatting | bytes 4194304 | tf_op jit(solution)/shard_map/reshape | solution.py:85
  102.7 36.0 %all-reduce.3.cloned.1.call-done = f32[32,28,256]{2,0,1:T(8,128)} async-done(((f32[32,28,256]{2,0,1:T(8,128)}), f32[32,28,256]{2,0,1:T(8,128)}) %all-reduce.3.cloned.1.call-update) | async-done | bytes 917520 | tf_op jit(solution)/shard_map/psum | solution.py:77
  138.7 2.2 %slice.964 = f32[32,27,256]{2,0,1:T(8,128)} slice(f32[32,28,256]{2,0,1:T(8,128)} %all-reduce.3.cloned.1.call-done), slice={[0:32], [0:27], [0:256]} | slice | bytes 1769472 | tf_op jit(solution)/shard_map/slice | solution.py:78
  140.9 1.3 slice_reduce_fusion
  142.2 34.7 %reduce-scatter.2.cloned.1.call-done = f32[32,2,8,128]{3,2,1,0:T(8,128)} async-done(((f32[256,2,8,128]{3,2,1,0:T(8,128)}), f32[32,2,8,128]{3,2,1,0:T(8,128)}) %reduce-scatter.2.cloned.1.call-update) | async-done | bytes 262160 | tf_op jit(solution)/shard_map/reduce_scatter | solution.py:84
  177.0 1.6 convert_element_type.22
  (229 shorter events, 27.6 us)
Async XLA Ops:
  7.2 39.5 %all-gather.2.cloned.1.call-start = ((), (), s32[]{:S(2)}) async-start(), calls=%async_computation.1 | async-start | bytes 2359296 | tf_op jit(solution)/shard_map/all_gather | solution.py:31
  8.2 6.0 %collective-permute-start.1 = (bf16[32,1,8,128]{3,0,2,1:T(8,128)(2,1)S(1)}, bf16[32,1,8,128]{3,0,2,1:T(8,128)(2,1)S(1)}, u32[]{:S(2)}, u32[]{:S(2)}) collective-permute-start(bf16[32,1,8,128]{3,0,2,1:T(8,128)(2,1)S(1)} %get-tuple-element.105), channel_id=1, source_target_pairs={{8,0},{16,8},{24,16},{0,24},{9,1},{17,9},{25,17},{1,25},{10,2},{18... | collective-permute-start | bytes 196616 | tf_op jit(solution)/shard_map/ppermute | solution.py:18
  12.1 5.2 %collective-permute-start = (bf16[32,1,8,128]{3,0,2,1:T(8,128)(2,1)S(1)}, bf16[32,1,8,128]{3,0,2,1:T(8,128)(2,1)S(1)}, u32[]{:S(2)}, u32[]{:S(2)}) collective-permute-start(bf16[32,1,8,128]{3,0,2,1:T(8,128)(2,1)S(1)} %get-tuple-element.104), channel_id=1, source_target_pairs={{0,8},{8,16},{16,24},{24,0},{1,9},{9,17},{17,25},{25,1},{2,10},{10... | collective-permute-start | bytes 196616 | tf_op jit(solution)/shard_map/ppermute | solution.py:15
  18.0 120.7 %all-reduce.3.cloned.1.call-start = ((), (), s32[]{:S(2)}) async-start(), calls=%async_computation.3 | async-start | bytes 1835008 | tf_op jit(solution)/shard_map/psum | solution.py:77
  65.6 1.3 copy-start.9
  65.7 1.6 copy-start.8
  65.8 1.6 copy-start.7
  66.4 1.4 copy-start.6
  66.8 1.4 copy-start.5
  67.0 1.4 copy-start.3
  67.3 1.4 copy-start.11
  67.4 1.4 copy-start.17
  67.5 1.5 copy-start.18
  67.5 1.5 copy-start.10
  67.6 1.4 copy-start.12
  67.7 1.4 copy-start.19
  67.9 1.5 copy-start.4
  71.9 1.3 copy-start.16
  75.9 5.5 %collective-permute-start.3 = (bf16[32,1,8,128]{3,0,2,1:T(8,128)(2,1)S(1)}, bf16[32,1,8,128]{3,0,2,1:T(8,128)(2,1)S(1)}, u32[]{:S(2)}, u32[]{:S(2)}) collective-permute-start(bf16[32,1,8,128]{3,0,2,1:T(8,128)(2,1)S(1)} %get-tuple-element.86), channel_id=1, source_target_pairs={{0,8},{8,16},{16,24},{24,0},{1,9},{9,17},{17,25},{25,1},{2,10},{10... | collective-permute-start | bytes 196616 | tf_op jit(solution)/shard_map/ppermute | solution.py:15
  77.4 5.1 %collective-permute-start.2 = (bf16[32,1,8,128]{3,0,2,1:T(8,128)(2,1)S(1)}, bf16[32,1,8,128]{3,0,2,1:T(8,128)(2,1)S(1)}, u32[]{:S(2)}, u32[]{:S(2)}) collective-permute-start(bf16[32,1,8,128]{3,0,2,1:T(8,128)(2,1)S(1)} %get-tuple-element.87), channel_id=1, source_target_pairs={{8,0},{16,8},{24,16},{0,24},{9,1},{17,9},{25,17},{1,25},{10,2},{18... | collective-permute-start | bytes 196616 | tf_op jit(solution)/shard_map/ppermute | solution.py:18
  84.5 2.0 %copy-start = (bf16[256,4,8,128]{3,0,2,1:T(8,128)(2,1)S(1)}, bf16[256,4,8,128]{3,0,2,1:T(8,128)(2,1)}, u32[]{:S(2)}) copy-start(bf16[256,4,8,128]{3,0,2,1:T(8,128)(2,1)} %all-gather.2.cloned.1.call-done) | copy-start | bytes 6291460
  86.5 1.7 copy-start.1
  89.3 87.7 %reduce-scatter.2.cloned.1.call-start = ((), (), s32[]{:S(2)}) async-start(), calls=%async_computation.2 | async-start | bytes 2359296 | tf_op jit(solution)/shard_map/reduce_scatter | solution.py:84
  99.9 2.0 %copy-start.2 = (f32[32,2,8,128]{3,0,2,1:T(8,128)S(1)}, f32[32,2,8,128]{3,0,2,1:T(8,128)}, u32[]{:S(2)}) copy-start(f32[32,2,8,128]{3,0,2,1:T(8,128)} %get-tuple-element.14) | copy-start | bytes 786436
  (7 other events, 7.9 us)
Sparse Core Ops, SparseCore 0:
  18.2 28.4 all-gather.1
  89.4 49.2 all-reduce.2
  141.1 35.7 reduce-scatter.1
where the time goes:
time: 186 us; the launch traced here: 185 us
  waiting for transfers between devices  105 us (56%)
  local copies, waits for them, and re-layouts  40.1 us (22%)
  between operations  15.2 us (8%)
  other arithmetic  10.7 us (6%)
  starting transfers between devices  7.05 us (4%)
  matrix products  6.93 us (4%)
    psum x1, waiting for transfers between devices, on_device(): lax.psum(jnp.concatenate([filter_part, bias_row], 1), 'slab')  36 us
    reduce_scatter x1, waiting for transfers between devices, on_device(): lax.psum_scatter(product.reshape(in_total // lax.axis_size('chan') * lax....  34.7 us
    all_gather x1, waiting for transfers between devices, on_device(): padded = lax.all_gather(rimmed, 'chan', axis=0, tiled=True)  25.7 us
    slice x45, local copies, waits for them, and re-layouts, on_device(): jnp.roll(plane_part[3 * j + l], (1 - j, 1 - l), axis=(2, 3))  10.9 us
    unnamed x119, local copies, waits for them, and re-layouts  8.39 us
    slice x4, local copies, waits for them, and re-layouts, on_device(): padded[:, i:i + n_planes].reshape(in_total, -1)  5.62 us
    ppermute x2, waiting for transfers between devices, with_halo(): lax.ppermute(lax.slice_in_dim(block, block.shape[dim] - width, None, axis...  5.57 us
    ppermute x2, starting transfers between devices, with_halo(): lax.ppermute(lax.slice_in_dim(block, 0, width, axis=dim), axis, backward)  5.41 us
  transfers between devices with their start and end apart: 7, of which 7 were waited for; matrix products, arithmetic and copies ran while one was open for 11% of the time, Pallas kernels for 0%

commit v1 on v0

--- a/solution.py
+++ b/solution.py
@@ -1,9 +1,16 @@
+import functools
 import math
 
 import jax
 import jax.numpy as jnp
 from jax import lax
+from jax.experimental import pallas as pl
+from jax.experimental.pallas import tpu as pltpu
 from jax.sharding import PartitionSpec as P
+
+LANES = 128
+VMEM = pl.BlockSpec(memory_space=pltpu.VMEM)
+SMEM = pl.BlockSpec(memory_space=pltpu.SMEM)
 
 
 def with_halo(block, sides, width):
@@ -24,7 +31,7 @@
     return [(9 * i + 3 * j + l, i, j, l) for i in range(3) for j in range(3) for l in range(3)]
 
 
-def on_device(x_in, weight, bias_vec, grad_out):
+def plain(x_in, weight, bias_vec, grad_out):
     out_local, n_taps, in_total = weight.shape
     n_planes, n_rows, n_depth = (x_in.shape[1], x_in.shape[2], x_in.shape[3])
     rimmed = with_halo(x_in, (("slab", 1),), 1)
@@ -92,6 +99,283 @@
     return (activation, grad_in.astype(jnp.bfloat16), weight_grad, bias_grad)
 
 
+def call(body, out_shape, operands, specs=None, scratch=(), flops=0, name=None):
+    read = sum(math.prod(a.shape) * a.dtype.itemsize for a in operands)
+    written = sum(math.prod(a.shape) * a.dtype.itemsize for a in out_shape)
+    return pl.pallas_call(
+        body,
+        out_shape=out_shape,
+        in_specs=specs or [VMEM] * len(operands),
+        out_specs=[VMEM] * len(out_shape),
+        scratch_shapes=list(scratch),
+        compiler_params=pltpu.CompilerParams(vmem_limit_bytes=24 * 2**20),
+        cost_estimate=pl.CostEstimate(
+            flops=flops, bytes_accessed=read + written, transcendentals=0
+        ),
+        name=name,
+    )(*operands)
+
+
+def shape_of(shape, dtype):
+    return jax.ShapeDtypeStruct(shape, dtype)
+
+
+def forward_body(n, rows, o, count, me_ref, w_ref, *refs):
+    blocks = refs[:count]
+    own_ref, low_ref, high_ref, x_ref, acc = refs[count:]
+    me = me_ref[0]
+    for r in range(count // 2):
+        for side in range(2):
+            mine = me if side == 0 else me + 1 - 2 * lax.rem(me, 2)
+            source = lax.rem(mine - 2 * r + count, count)
+            place = pl.ds(pl.multiple_of(source * o, o), o)
+            for k in range(n * rows):
+                x_ref[place, k * LANES : (k + 1) * LANES] = blocks[2 * r + side][k]
+    w = w_ref[...].reshape(27 * o, w_ref.shape[2])
+    seen = set()
+    for p in range(n):
+        for t in range(0, rows, 2):
+            at = (p * rows + t) * LANES
+            part = jnp.dot(
+                w, x_ref[:, at : at + 2 * LANES], preferred_element_type=jnp.float32
+            )
+            for k, i, j, l in tap_list():
+                for h in range(2):
+                    slot = (l, p + 2 - i, (t + h + 1 - j) % rows)
+                    value = part[k * o : (k + 1) * o, h * LANES : (h + 1) * LANES]
+                    if slot in seen:
+                        acc[slot] += value
+                    else:
+                        acc[slot] = value
+                        seen.add(slot)
+    for q in range(n + 2):
+        for y in range(rows):
+            total = (
+                pltpu.roll(acc[0, q, y], 1, 1)
+                + acc[1, q, y]
+                + pltpu.roll(acc[2, q, y], LANES - 1, 1)
+            )
+            if q == 0:
+                low_ref[y] = total.astype(low_ref.dtype)
+            elif q == n + 1:
+                high_ref[y] = total.astype(high_ref.dtype)
+            else:
+                own_ref[(q - 1) * rows + y] = total
+
+
+def activation_body(n, rows, own_ref, below_ref, above_ref, bias_ref, go_ref, act_ref, gp_ref):
+    for p in range(n):
+        for y in range(rows):
+            k = p * rows + y
+            pre = own_ref[k] + bias_ref[...]
+            if p == 0:
+                pre = pre + below_ref[y].astype(jnp.float32)
+            if p == n - 1:
+                pre = pre + above_ref[y].astype(jnp.float32)
+            s = jax.nn.sigmoid(pre)
+            act_ref[k] = (pre * s).astype(act_ref.dtype)
+            slope = s * (1.0 + pre * (1.0 - s))
+            gp_ref[k] = (go_ref[k].astype(jnp.float32) * slope).astype(gp_ref.dtype)
+
+
+def input_grad_body(
+    n, rows, o, count, me_ref, gp_ref, below_ref, above_ref, wt_ref, mine_ref, other_ref, s_ref, w_ref
+):
+    me = me_ref[0]
+    core = lax.rem(me, 2)
+    for side in range(2):
+        for r in range(count // 2):
+            owner = lax.rem(me - core + 2 * r, count) + (core if side == 0 else 1 - core)
+            rel = (side * (count // 2) + r) * o
+            w_ref[rel : rel + o] = wt_ref[pl.ds(pl.multiple_of(owner * o, o), o)]
+    for q in range(n + 2):
+        for y in range(rows):
+            if q == 0:
+                value = below_ref[y]
+            elif q == n + 1:
+                value = above_ref[y]
+            else:
+                value = gp_ref[(q - 1) * rows + y]
+            wide = value.astype(jnp.float32)
+            turned = [
+                pltpu.roll(wide, LANES - 1, 1).astype(value.dtype),
+                value,
+                pltpu.roll(wide, 1, 1).astype(value.dtype),
+            ]
+            for k, i, j, l in tap_list():
+                p = q - 2 + i
+                if 0 <= p < n:
+                    at = (p * rows + (y + j - 1) % rows) * LANES
+                    s_ref[k * o : (k + 1) * o, at : at + LANES] = turned[l]
+    w = w_ref[...]
+    half = count // 2 * o
+    for t in range(0, n * rows, 2):
+        part = jnp.dot(
+            w, s_ref[:, t * LANES : (t + 2) * LANES], preferred_element_type=jnp.float32
+        ).astype(mine_ref.dtype)
+        for h in range(2):
+            for r in range(count // 2):
+                cut = part[r * o : (r + 1) * o, h * LANES : (h + 1) * LANES]
+                mine_ref[r, t + h] = cut
+                cut = part[half + r * o : half + (r + 1) * o, h * LANES : (h + 1) * LANES]
+                other_ref[r, t + h] = cut
+
+
+def filter_grad_body(scale, taps, s_ref, x_ref, gp_ref, first_ref, second_ref):
+    o = gp_ref.shape[1]
+    full = lax.dot_general(
+        s_ref[...], x_ref[...], (((1,), (1,)), ((), ())), preferred_element_type=jnp.float32
+    )
+    full = (full * scale).astype(first_ref.dtype)
+    first_ref[...] = full[: taps * o]
+    second_ref[: (27 - taps) * o] = full[taps * o :]
+    total = jnp.sum(gp_ref[...].astype(jnp.float32), axis=0)
+    total = jnp.sum(total, axis=1, keepdims=True) * scale
+    second_ref[(27 - taps) * o :] = jnp.broadcast_to(
+        total, (o, second_ref.shape[1])
+    ).astype(second_ref.dtype)
+
+
+def pair_body(a_ref, b_ref, out_ref):
+    out_ref[...] = (a_ref[...].astype(jnp.float32) + b_ref[...].astype(jnp.float32)).astype(
+        out_ref.dtype
+    )
+
+
+def split_sum_body(a_ref, b_ref, *outs):
+    for r, out in enumerate(outs):
+        total = a_ref[r].astype(jnp.float32) + b_ref[r].astype(jnp.float32)
+        out[...] = total.astype(out.dtype)
+
+
+def sum_body(*refs):
+    total = refs[0][...].astype(jnp.float32)
+    for ref in refs[1:-1]:
+        total = total + ref[...].astype(jnp.float32)
+    refs[-1][...] = total.astype(refs[-1].dtype)
+
+
+def last_body(taps, a_ref, b_ref, c_ref, d_ref, out_ref, bias_ref):
+    o = out_ref.shape[1]
+    f32 = jnp.float32
+    for k in range(27):
+        left, right, at = (a_ref, b_ref, k) if k < taps else (c_ref, d_ref, k - taps)
+        cut = slice(at * o, (at + 1) * o)
+        out_ref[k] = left[cut].astype(f32) + right[cut].astype(f32)
+    cut = slice((27 - taps) * o, (28 - taps) * o)
+    bias_ref[...] = (c_ref[cut].astype(f32) + d_ref[cut].astype(f32))[:, :LANES]
+
+
+def rotate(value, axis, step):
+    count = lax.axis_size(axis)
+    return lax.ppermute(value, axis, [(i, (i + step) % count) for i in range(count)])
+
+
+def swap(value, axis, bit):
+    return lax.ppermute(value, axis, [(i, i ^ bit) for i in range(lax.axis_size(axis))])
+
+
+def on_device(x_in, weight, bias_vec, grad_out):
+    count = lax.axis_size("chan")
+    o, _, c_all = weight.shape
+    _, n, rows, depth = x_in.shape
+    f32, bf16 = jnp.float32, jnp.bfloat16
+    cells = n * rows
+    scale = 1.0 / math.sqrt(lax.axis_size("slab") * cells * depth)
+    me = lax.axis_index("chan").astype(jnp.int32).reshape(1)
+
+    def by_row(a):
+        return jnp.transpose(a, (1, 2, 0, 3)).reshape(cells, o, depth)
+
+    def by_channel(a):
+        return jnp.transpose(a.reshape(n, rows, o, depth), (2, 0, 1, 3))
+
+    x_own = by_row(x_in)
+    blocks = [x_own, swap(x_own, "chan", 1)]
+    for r in range(1, count // 2):
+        far = rotate(x_own, "chan", 2 * r)
+        blocks += [far, swap(far, "chan", 1)]
+    w_taps = jnp.transpose(weight, (1, 0, 2))
+    w_back = jnp.transpose(w_taps.reshape(27 * o, c_all))
+    go = by_row(grad_out)
+    bias = jnp.broadcast_to(bias_vec.astype(f32)[:, None], (o, depth))
+
+    own, low, high, x_all = call(
+        functools.partial(forward_body, n, rows, o, count),
+        [
+            shape_of((cells, o, depth), f32),
+            shape_of((rows, o, depth), bf16),
+            shape_of((rows, o, depth), bf16),
+            shape_of((c_all, cells * depth), bf16),
+        ],
+        [me, w_taps, *blocks],
+        [SMEM] + [VMEM] * (1 + count),
+        [pltpu.VMEM((3, n + 2, rows, o, depth), f32)],
+        flops=2 * 27 * o * c_all * cells * depth,
+        name="forward",
+    )
+    above = rotate(low, "slab", -1)
+    below = rotate(high, "slab", 1)
+    act, gp = call(
+        functools.partial(activation_body, n, rows),
+        [shape_of((cells, o, depth), bf16)] * 2,
+        [own, below, above, bias, go],
+        name="activation",
+    )
+    gp_above = rotate(gp[:rows], "slab", -1)
+    gp_below = rotate(gp[cells - rows :], "slab", 1)
+    half = (count // 2, cells, o, depth)
+    mine, other, stacked = call(
+        functools.partial(input_grad_body, n, rows, o, count),
+        [
+            shape_of(half, bf16),
+            shape_of(half, bf16),
+            shape_of((27 * o, cells * depth), bf16),
+        ],
+        [me, gp, gp_below, gp_above, w_back],
+        [SMEM] + [VMEM] * 4,
+        [pltpu.VMEM((c_all, 27 * o), bf16)],
+        flops=2 * 27 * o * c_all * cells * depth,
+        name="input_grad",
+    )
+    other = swap(other, "chan", 1)
+    taps = 14
+    first, second = call(
+        functools.partial(filter_grad_body, scale, taps),
+        [shape_of((taps * o, c_all), bf16), shape_of(((28 - taps) * o, c_all), bf16)],
+        [stacked, x_all, gp],
+        flops=2 * 27 * o * c_all * cells * depth,
+        name="filter_grad",
+    )
+    first_far = swap(first, "slab", 1)
+    second_far = swap(second, "slab", 2)
+    sums = call(
+        split_sum_body,
+        [shape_of((cells, o, depth), f32)]
+        + [shape_of((cells, o, depth), bf16)] * (count // 2 - 1),
+        [mine, other],
+        name="pair_sum",
+    )
+    far = [rotate(sums[r], "chan", 2 * r) for r in range(1, count // 2)]
+    (first,) = call(pair_body, [shape_of(first.shape, bf16)], [first, first_far], name="first")
+    (second,) = call(pair_body, [shape_of(second.shape, bf16)], [second, second_far], name="second")
+    first_far = swap(first, "slab", 2)
+    second_far = swap(second, "slab", 1)
+    (grad_in,) = call(sum_body, [shape_of((cells, o, depth), bf16)], [sums[0], *far], name="sum")
+    weight_grad, bias_grad = call(
+        functools.partial(last_body, taps),
+        [shape_of((27, o, c_all), f32), shape_of((o, LANES), f32)],
+        [first, first_far, second, second_far],
+        name="last",
+    )
+    return (
+        by_channel(act),
+        by_channel(grad_in),
+        jnp.transpose(weight_grad, (1, 0, 2)),
+        bias_grad[:, 0],
+    )
+
+
 def solution(mesh):
     placed = (
         P("chan", "slab", None, None),
@@ -99,8 +383,18 @@
         P("chan"),
         P("chan", "slab", None, None),
     )
+
+    def body(x_in, weight, bias_vec, grad_out):
+        tiled = (
+            weight.shape[0] % 32 == 0
+            and x_in.shape[3] == LANES
+            and lax.axis_size("slab") == 4
+            and lax.axis_size("chan") % 2 == 0
+        )
+        return (on_device if tiled else plain)(x_in, weight, bias_vec, grad_out)
+
     return jax.shard_map(
-        on_device,
+        body,
         mesh=mesh,
         in_specs=placed,
         out_specs=(

time: 186 us -> 61.8 us (0.33)
  waiting for transfers between devices: 105 us -> 30.3 us
  local copies, waits for them, and re-layouts: 40.1 us -> 4.4 us
  between operations: 15.2 us -> 0.74 us
  starting transfers between devices: 7.05 us -> 20.7 us
  other arithmetic: 10.7 us -> 0 us
  matrix products: 6.93 us -> 0 us
  Pallas kernels: 0 us -> 5.46 us
    psum x1 -> x0, waiting for transfers between devices: 36 us -> none  [on_device(): lax.psum(jnp.concatenate([filter_part, bias_row], 1), 'slab')]
    reduce_scatter x1 -> x0, waiting for transfers between devices: 34.7 us -> none  [on_device(): lax.psum_scatter(product.reshape(in_total // lax.axis_size('chan') * lax....]
    all_gather x1 -> x0, waiting for transfers between devices: 25.7 us -> none  [on_device(): padded = lax.all_gather(rimmed, 'chan', axis=0, tiled=True)]
    ppermute x4 -> x19, waiting for transfers between devices: 8.68 us -> 30.3 us  [the longest x10 22.5 us: rotate(): lax.ppermute(value, axis, [(i, (i + step) % count) for i in range(count)])]
    slice x56 -> x2, local copies, waits for them, and re-layouts: 22 us -> 0.64 us  [the longest x1 0.62 us: on_device(): bias_grad[:, 0]]
    ppermute x4 -> x19, starting transfers between devices: 6.93 us -> 20.7 us  [the longest x10 16.6 us: rotate(): lax.ppermute(value, axis, [(i, (i + step) % count) for i in range(count)])]
    unnamed x119 -> x8, local copies, waits for them, and re-layouts: 8.39 us -> 1.03 us
    dot_general x5 -> x0, matrix products: 6.93 us -> none  [the longest x1 3.4 us: on_device(): lax.dot_general(flat_w, shifted, (((0,), (0,)), ((), ())), preferred_elem...]
  transfers between devices with their start and end apart: 7 -> 19, of which waited for: 7 -> 12; matrix products, arithmetic and copies ran while one was open for 11% -> 3% of each run, Pallas kernels for 0% -> 4%
where the time goes in v1:
time: 61.8 us; the launch traced here: 61.7 us
  waiting for transfers between devices  30.3 us (49%)
  starting transfers between devices  20.7 us (33%)
  Pallas kernels  5.46 us (9%)
  local copies, waits for them, and re-layouts  4.4 us (7%)
  between operations  0.74 us (1%)
    ppermute x10, waiting for transfers between devices, rotate(): lax.ppermute(value, axis, [(i, (i + step) % count) for i in range(count)])  22.5 us
    ppermute x10, starting transfers between devices, rotate(): lax.ppermute(value, axis, [(i, (i + step) % count) for i in range(count)])  16.6 us
    ppermute x9, waiting for transfers between devices, swap(): lax.ppermute(value, axis, [(i, i ^ bit) for i in range(lax.axis_size(axis...  7.86 us
    pallas_call x9, Pallas kernels, call(): pl.pallas_call(body, out_shape=out_shape, in_specs=specs or [VMEM] * len(...  5.46 us
    ppermute x9, starting transfers between devices, swap(): lax.ppermute(value, axis, [(i, i ^ bit) for i in range(lax.axis_size(axis...  4.18 us
    reshape x2, local copies, waits for them, and re-layouts, by_channel(): return jnp.transpose(a.reshape(n, rows, o, depth), (2, 0, 1, 3))  1.42 us
  transfers between devices with their start and end apart: 19, of which 12 were waited for; matrix products, arithmetic and copies ran while one was open for 3% of the time, Pallas kernels for 4%

profile of v1, /device:TPU:0, one launch (start us, length us, event | category | flops | bytes accessed | tf_op | source)
XLA Modules:
  0.0 61.7 jit_solution(9220967877672510469)
XLA Ops:
  0.7 1.0 %copy.13 = bf16[2,8,32,128]{3,2,1,0:T(8,128)(2,1)S(1)} copy(bf16[2,8,32,128]{3,1,0,2:T(8,128)(2,1)} %bitcast.29) | data formatting | bytes 262144 | tf_op jit(solution)/shard_map/transpose | solution.py:288
  1.6 5.1 %collective-permute-start.5 = (bf16[16,32,128]{2,1,0:T(8,128)(2,1)S(1)}, bf16[16,32,128]{2,1,0:T(8,128)(2,1)S(1)}, u32[]{:S(2)}, u32[]{:S(2)}) collective-permute-start(bf16[16,32,128]{2,1,0:T(8,128)(2,1)S(1)} %bitcast.24), channel_id=1, source_target_pairs={{0,6},{1,7},{2,0},{3,1},{4,2},{5,3},{6,4},{7,5},{8,14},{9,15},{10,... | collective-permute-start | bytes 393224 | tf_op jit(solution)/shard_map/ppermute | solution.py:271
  6.7 1.0 %collective-permute-start.1 = (bf16[16,32,128]{2,1,0:T(8,128)(2,1)S(1)}, bf16[16,32,128]{2,1,0:T(8,128)(2,1)S(1)}, u32[]{:S(2)}, u32[]{:S(2)}) collective-permute-start(bf16[16,32,128]{2,1,0:T(8,128)(2,1)S(1)} %bitcast.26), channel_id=1, source_target_pairs={{0,2},{1,3},{2,4},{3,5},{4,6},{5,7},{6,0},{7,1},{8,10},{9,11},{10,... | collective-permute-start | bytes 393224 | tf_op jit(solution)/shard_map/ppermute | solution.py:271
  7.7 2.9 %collective-permute-done.5.refs_6_ = bf16[16,32,128]{2,1,0:T(8,128)(2,1)S(1)} collective-permute-done((bf16[16,32,128]{2,1,0:T(8,128)(2,1)S(1)}, bf16[16,32,128]{2,1,0:T(8,128)(2,1)S(1)}, u32[]{:S(2)}, u32[]{:S(2)}) %collective-permute-start.5) | collective-permute-done | bytes 131104 | tf_op jit(solution)/shard_map/ppermute | solution.py:271
  10.6 7.3 %collective-permute-done.3.refs_4_ = bf16[16,32,128]{2,1,0:T(8,128)(2,1)S(1)} collective-permute-done((bf16[16,32,128]{2,1,0:T(8,128)(2,1)S(1)}, bf16[16,32,128]{2,1,0:T(8,128)(2,1)S(1)}, u32[]{:S(2)}, u32[]{:S(2)}) %collective-permute-start.3) | collective-permute-done | bytes 131104 | tf_op jit(solution)/shard_map/ppermute | solution.py:271
  18.5 0.8 %collective-permute-done.4.refs_5_ = bf16[16,32,128]{2,1,0:T(8,128)(2,1)S(1)} collective-permute-done((bf16[16,32,128]{2,1,0:T(8,128)(2,1)S(1)}, bf16[16,32,128]{2,1,0:T(8,128)(2,1)S(1)}, u32[]{:S(2)}, u32[]{:S(2)}) %collective-permute-start.4) | collective-permute-done | bytes 131104 | tf_op jit(solution)/shard_map/ppermute | solution.py:275
  19.5 1.0 %copy-done = bf16[32,27,256]{2,0,1:T(8,128)(2,1)S(1)} copy-done((bf16[32,27,256]{2,0,1:T(8,128)(2,1)S(1)}, bf16[32,27,256]{2,0,1:T(8,128)(2,1)}, u32[]{:S(2)}) %copy-start) | copy-done | bytes 442392
  20.5 1.4 %forward.1 = (f32[16,32,128]{2,1,0:T(8,128)S(1)}, bf16[8,32,128]{2,1,0:T(8,128)(2,1)S(1)}, bf16[8,32,128]{2,1,0:T(8,128)(2,1)S(1)}, bf16[256,2048]{1,0:T(8,128)(2,1)S(1)}) custom-call(s32[1]{0:T(128)} %bitcast.me_ref, bf16[27,32,256]{2,1,0:T(8,128)(2,1)S(1)} %bitcast.21, bf16[16,32,128]{2,1,0:T(8,128)(2,1)S(1)} %bitcast.28, ...), custom_call_target="tpu_custom_call" | custom-call | flops 905969664 | bytes 2932740 | tf_op jit(solution)/shard_map/forward/pallas_call | solution.py:105
  21.9 1.5 %collective-permute-start.7 = (bf16[8,32,128]{2,1,0:T(8,128)(2,1)S(1)}, bf16[8,32,128]{2,1,0:T(8,128)(2,1)S(1)}, u32[]{:S(2)}, u32[]{:S(2)}) collective-permute-start(bf16[8,32,128]{2,1,0:T(8,128)(2,1)S(1)} %get-tuple-element.22), channel_id=1, source_target_pairs={{0,8},{8,16},{16,24},{24,0},{1,9},{9,17},{17,25},{25,1},{2,10},{10... | collective-permute-start | bytes 196616 | tf_op jit(solution)/shard_map/ppermute | solution.py:271
  23.4 1.4 %collective-permute-start.8 = (bf16[8,32,128]{2,1,0:T(8,128)(2,1)S(1)}, bf16[8,32,128]{2,1,0:T(8,128)(2,1)S(1)}, u32[]{:S(2)}, u32[]{:S(2)}) collective-permute-start(bf16[8,32,128]{2,1,0:T(8,128)(2,1)S(1)} %get-tuple-element.23), channel_id=1, source_target_pairs={{0,24},{8,0},{16,8},{24,16},{1,25},{9,1},{17,9},{25,17},{2,26},{10... | collective-permute-start | bytes 196616 | tf_op jit(solution)/shard_map/ppermute | solution.py:271
  24.9 2.4 %collective-permute-done.7.below_ref = bf16[8,32,128]{2,1,0:T(8,128)(2,1)S(1)} collective-permute-done((bf16[8,32,128]{2,1,0:T(8,128)(2,1)S(1)}, bf16[8,32,128]{2,1,0:T(8,128)(2,1)S(1)}, u32[]{:S(2)}, u32[]{:S(2)}) %collective-permute-start.7) | collective-permute-done | bytes 65568 | tf_op jit(solution)/shard_map/ppermute | solution.py:271
  27.3 1.3 %collective-permute-done.8.above_ref = bf16[8,32,128]{2,1,0:T(8,128)(2,1)S(1)} collective-permute-done((bf16[8,32,128]{2,1,0:T(8,128)(2,1)S(1)}, bf16[8,32,128]{2,1,0:T(8,128)(2,1)S(1)}, u32[]{:S(2)}, u32[]{:S(2)}) %collective-permute-start.8) | collective-permute-done | bytes 65568 | tf_op jit(solution)/shard_map/ppermute | solution.py:271
  28.8 1.5 %collective-permute-start.10 = (bf16[8,32,128]{2,1,0:T(8,128)(2,1)S(1)}, bf16[8,32,128]{2,1,0:T(8,128)(2,1)S(1)}, u32[]{:S(2)}, u32[]{:S(2)}) collective-permute-start(bf16[8,32,128]{2,1,0:T(8,128)(2,1)S(1)} %get-tuple-element.38), channel_id=1, source_target_pairs={{0,24},{8,0},{16,8},{24,16},{1,25},{9,1},{17,9},{25,17},{2,26},{10... | collective-permute-start | bytes 196616 | tf_op jit(solution)/shard_map/ppermute | solution.py:271
  31.2 2.2 %collective-permute-done.10.above_ref = bf16[8,32,128]{2,1,0:T(8,128)(2,1)S(1)} collective-permute-done((bf16[8,32,128]{2,1,0:T(8,128)(2,1)S(1)}, bf16[8,32,128]{2,1,0:T(8,128)(2,1)S(1)}, u32[]{:S(2)}, u32[]{:S(2)}) %collective-permute-start.10) | collective-permute-done | bytes 65568 | tf_op jit(solution)/shard_map/ppermute | solution.py:271
  33.3 2.2 %collective-permute-done.9.below_ref = bf16[8,32,128]{2,1,0:T(8,128)(2,1)S(1)} collective-permute-done((bf16[8,32,128]{2,1,0:T(8,128)(2,1)S(1)}, bf16[8,32,128]{2,1,0:T(8,128)(2,1)S(1)}, u32[]{:S(2)}, u32[]{:S(2)}) %collective-permute-start.9) | collective-permute-done | bytes 65568 | tf_op jit(solution)/shard_map/ppermute | solution.py:271
  35.5 1.6 %input_grad.1 = (bf16[4,16,32,128]{3,2,1,0:T(8,128)(2,1)S(1)}, bf16[4,16,32,128]{3,2,1,0:T(8,128)(2,1)S(1)}, bf16[864,2048]{1,0:T(8,128)(2,1)S(1)}) custom-call(s32[1]{0:T(128)} %bitcast.me_ref, bf16[16,32,128]{2,1,0:T(8,128)(2,1)S(1)} %get-tuple-element.25.gp_ref, bf16[8,32,128]{2,1,0:T(8,128)(2,1)S(1)} %collective-permute-done.9.below_ref, ...), custom_call_target="tpu_custom_call" | custom-call | flops 905969664 | bytes 5292036 | tf_op jit(solution)/shard_map/input_grad/pallas_call | solution.py:105
  37.1 1.1 %filter_grad.1 = (bf16[448,256]{1,0:T(8,128)(2,1)S(1)}, bf16[448,256]{1,0:T(8,128)(2,1)S(1)}) custom-call(bf16[864,2048]{1,0:T(8,128)(2,1)S(1)} %get-tuple-element.32.s_ref, bf16[256,2048]{1,0:T(8,128)(2,1)S(1)} %get-tuple-element.33.x_ref, bf16[16,32,128]{2,1,0:T(8,128)(2,1)S(1)} %get-tuple-element.25.gp_ref), custom_call_target="tpu_custom_call" | custom-call | flops 905969664 | bytes 5177344 | tf_op jit(solution)/shard_map/filter_grad/pallas_call | solution.py:105
  38.4 1.5 %collective-permute-start.17 = (bf16[448,256]{1,0:T(8,128)(2,1)S(1)}, bf16[448,256]{1,0:T(8,128)(2,1)S(1)}, u32[]{:S(2)}, u32[]{:S(2)}) collective-permute-start(bf16[448,256]{1,0:T(8,128)(2,1)S(1)} %get-tuple-element.35.a_ref), channel_id=1, source_target_pairs={{0,16},{8,24},{16,0},{24,8},{1,17},{9,25},{17,1},{25,9},{2,18},{10... | collective-permute-start | bytes 688136 | tf_op jit(solution)/shard_map/ppermute | solution.py:275
  39.9 6.4 %collective-permute-done.15.b_ref = bf16[448,256]{1,0:T(8,128)(2,1)S(1)} collective-permute-done((bf16[448,256]{1,0:T(8,128)(2,1)S(1)}, bf16[448,256]{1,0:T(8,128)(2,1)S(1)}, u32[]{:S(2)}, u32[]{:S(2)}) %collective-permute-start.15) | collective-permute-done | bytes 229408 | tf_op jit(solution)/shard_map/ppermute | solution.py:275
  46.4 1.6 %collective-permute-start.16 = (bf16[448,256]{1,0:T(8,128)(2,1)S(1)}, bf16[448,256]{1,0:T(8,128)(2,1)S(1)}, u32[]{:S(2)}, u32[]{:S(2)}) collective-permute-start(bf16[448,256]{1,0:T(8,128)(2,1)S(1)} %first.1.a_ref), channel_id=1, source_target_pairs={{0,16},{8,24},{16,0},{24,8},{1,17},{9,25},{17,1},{25,9},{2,18},{10... | collective-permute-start | bytes 688136 | tf_op jit(solution)/shard_map/ppermute | solution.py:275
  49.1 2.0 %collective-permute-start.13 = (bf16[16,32,128]{2,1,0:T(8,128)(2,1)S(1)}, bf16[16,32,128]{2,1,0:T(8,128)(2,1)S(1)}, u32[]{:S(2)}, u32[]{:S(2)}) collective-permute-start(bf16[16,32,128]{2,1,0:T(8,128)(2,1)S(1)} %get-tuple-element.30), channel_id=1, source_target_pairs={{0,4},{1,5},{2,6},{3,7},{4,0},{5,1},{6,2},{7,3},{8,12},{9,13},{10,... | collective-permute-start | bytes 393224 | tf_op jit(solution)/shard_map/ppermute | solution.py:271
  51.0 2.8 %collective-permute-start.14 = (bf16[16,32,128]{2,1,0:T(8,128)(2,1)S(1)}, bf16[16,32,128]{2,1,0:T(8,128)(2,1)S(1)}, u32[]{:S(2)}, u32[]{:S(2)}) collective-permute-start(bf16[16,32,128]{2,1,0:T(8,128)(2,1)S(1)} %get-tuple-element.31), channel_id=1, source_target_pairs={{0,6},{1,7},{2,0},{3,1},{4,2},{5,3},{6,4},{7,5},{8,14},{9,15},{10,... | collective-permute-start | bytes 393224 | tf_op jit(solution)/shard_map/ppermute | solution.py:271
  55.0 1.0 %last.1 = (f32[27,32,256]{2,1,0:T(8,128)}, f32[32,128]{1,0:T(8,128)S(1)}) custom-call(bf16[448,256]{1,0:T(8,128)(2,1)S(1)} %first.1.a_ref, bf16[448,256]{1,0:T(8,128)(2,1)S(1)} %collective-permute-done.16.b_ref, bf16[448,256]{1,0:T(8,128)(2,1)S(1)} %second.1.c_ref, bf16[448,256]{1,0:T(8,128)(2,1)S(1)} %collective-permute-done.18.d_ref), custom_call_target="tpu_custom_call" | custom-call | bytes 1818624 | tf_op jit(solution)/shard_map/last/pallas_call | solution.py:105
  56.8 4.1 %collective-permute-done.13.refs_2_ = bf16[16,32,128]{2,1,0:T(8,128)(2,1)S(1)} collective-permute-done((bf16[16,32,128]{2,1,0:T(8,128)(2,1)S(1)}, bf16[16,32,128]{2,1,0:T(8,128)(2,1)S(1)}, u32[]{:S(2)}, u32[]{:S(2)}) %collective-permute-start.13) | collective-permute-done | bytes 131104 | tf_op jit(solution)/shard_map/ppermute | solution.py:271
  (39 shorter events, 5.9 us)
Async XLA Ops:
  0.6 24.2 %copy-start.2 = (bf16[32,2,8,128]{3,2,1,0:T(8,128)(2,1)S(1)}, bf16[32,2,8,128]{3,2,1,0:T(8,128)(2,1)}, u32[]{:S(2)}) copy-start(bf16[32,2,8,128]{3,2,1,0:T(8,128)(2,1)} %param.7) | copy-start | bytes 393220
  0.6 28.0 %copy-start.3 = (bf16[32]{0:T(256)(128)(2,1)S(1)}, bf16[32]{0:T(256)(128)(2,1)}, u32[]{:S(2)}) copy-start(bf16[32]{0:T(256)(128)(2,1)} %param.6) | copy-start | bytes 196
  1.6 9.0 %collective-permute-start.5 = (bf16[16,32,128]{2,1,0:T(8,128)(2,1)S(1)}, bf16[16,32,128]{2,1,0:T(8,128)(2,1)S(1)}, u32[]{:S(2)}, u32[]{:S(2)}) collective-permute-start(bf16[16,32,128]{2,1,0:T(8,128)(2,1)S(1)} %bitcast.24), channel_id=1, source_target_pairs={{0,6},{1,7},{2,0},{3,1},{4,2},{5,3},{6,4},{7,5},{8,14},{9,15},{10,... | collective-permute-start | bytes 393224 | tf_op jit(solution)/shard_map/ppermute | solution.py:271
  6.7 11.2 %collective-permute-start.3 = (bf16[16,32,128]{2,1,0:T(8,128)(2,1)S(1)}, bf16[16,32,128]{2,1,0:T(8,128)(2,1)S(1)}, u32[]{:S(2)}, u32[]{:S(2)}) collective-permute-start(bf16[16,32,128]{2,1,0:T(8,128)(2,1)S(1)} %bitcast.25), channel_id=1, source_target_pairs={{0,4},{1,5},{2,6},{3,7},{4,0},{5,1},{6,2},{7,3},{8,12},{9,13},{10,... | collective-permute-start | bytes 393224 | tf_op jit(solution)/shard_map/ppermute | solution.py:271
  6.7 11.2 %collective-permute-start.1 = (bf16[16,32,128]{2,1,0:T(8,128)(2,1)S(1)}, bf16[16,32,128]{2,1,0:T(8,128)(2,1)S(1)}, u32[]{:S(2)}, u32[]{:S(2)}) collective-permute-start(bf16[16,32,128]{2,1,0:T(8,128)(2,1)S(1)} %bitcast.26), channel_id=1, source_target_pairs={{0,2},{1,3},{2,4},{3,5},{4,6},{5,7},{6,0},{7,1},{8,10},{9,11},{10,... | collective-permute-start | bytes 393224 | tf_op jit(solution)/shard_map/ppermute | solution.py:271
  7.7 10.7 %collective-permute-start = (bf16[16,32,128]{2,1,0:T(8,128)(2,1)S(1)}, bf16[16,32,128]{2,1,0:T(8,128)(2,1)S(1)}, u32[]{:S(2)}, u32[]{:S(2)}) collective-permute-start(bf16[16,32,128]{2,1,0:T(8,128)(2,1)S(1)} %bitcast.27), channel_id=1, source_target_pairs={{0,1},{1,0},{2,3},{3,2},{4,5},{5,4},{6,7},{7,6},{8,9},{9,8},{10,11... | collective-permute-start | bytes 393224 | tf_op jit(solution)/shard_map/ppermute | solution.py:275
  10.6 7.8 %collective-permute-start.6 = (bf16[16,32,128]{2,1,0:T(8,128)(2,1)S(1)}, bf16[16,32,128]{2,1,0:T(8,128)(2,1)S(1)}, u32[]{:S(2)}, u32[]{:S(2)}) collective-permute-start(bf16[16,32,128]{2,1,0:T(8,128)(2,1)S(1)} %collective-permute-done.5.refs_6_), channel_id=1, source_target_pairs={{0,1},{1,0},{2,3},{3,2},{4,5},{5,4},{6,7},{7,6},{8,9},{9,8},{10,11... | collective-permute-start | bytes 393224 | tf_op jit(solution)/shard_map/ppermute | solution.py:275
  17.9 1.3 %collective-permute-start.4 = (bf16[16,32,128]{2,1,0:T(8,128)(2,1)S(1)}, bf16[16,32,128]{2,1,0:T(8,128)(2,1)S(1)}, u32[]{:S(2)}, u32[]{:S(2)}) collective-permute-start(bf16[16,32,128]{2,1,0:T(8,128)(2,1)S(1)} %collective-permute-done.3.refs_4_), channel_id=1, source_target_pairs={{0,1},{1,0},{2,3},{3,2},{4,5},{5,4},{6,7},{7,6},{8,9},{9,8},{10,11... | collective-permute-start | bytes 393224 | tf_op jit(solution)/shard_map/ppermute | solution.py:275
  17.9 1.5 %collective-permute-start.2 = (bf16[16,32,128]{2,1,0:T(8,128)(2,1)S(1)}, bf16[16,32,128]{2,1,0:T(8,128)(2,1)S(1)}, u32[]{:S(2)}, u32[]{:S(2)}) collective-permute-start(bf16[16,32,128]{2,1,0:T(8,128)(2,1)S(1)} %collective-permute-done.1.refs_2_), channel_id=1, source_target_pairs={{0,1},{1,0},{2,3},{3,2},{4,5},{5,4},{6,7},{7,6},{8,9},{9,8},{10,11... | collective-permute-start | bytes 393224 | tf_op jit(solution)/shard_map/ppermute | solution.py:275
  19.5 1.0 %copy-start = (bf16[32,27,256]{2,0,1:T(8,128)(2,1)S(1)}, bf16[32,27,256]{2,0,1:T(8,128)(2,1)}, u32[]{:S(2)}) copy-start(bf16[32,27,256]{2,0,1:T(8,128)(2,1)} %param.5) | copy-start | bytes 1327108
  20.5 10.4 %copy-start.1 = (bf16[32,27,256]{2,0,1:T(8,128)(2,1)S(1)}, bf16[32,27,256]{2,0,1:T(8,128)(2,1)}, u32[]{:S(2)}) copy-start(bf16[32,27,256]{2,0,1:T(8,128)(2,1)} %param.5) | copy-start | bytes 1327108
  21.9 5.5 %collective-permute-start.7 = (bf16[8,32,128]{2,1,0:T(8,128)(2,1)S(1)}, bf16[8,32,128]{2,1,0:T(8,128)(2,1)S(1)}, u32[]{:S(2)}, u32[]{:S(2)}) collective-permute-start(bf16[8,32,128]{2,1,0:T(8,128)(2,1)S(1)} %get-tuple-element.22), channel_id=1, source_target_pairs={{0,8},{8,16},{16,24},{24,0},{1,9},{9,17},{17,25},{25,1},{2,10},{10... | collective-permute-start | bytes 196616 | tf_op jit(solution)/shard_map/ppermute | solution.py:271
  23.4 5.2 %collective-permute-start.8 = (bf16[8,32,128]{2,1,0:T(8,128)(2,1)S(1)}, bf16[8,32,128]{2,1,0:T(8,128)(2,1)S(1)}, u32[]{:S(2)}, u32[]{:S(2)}) collective-permute-start(bf16[8,32,128]{2,1,0:T(8,128)(2,1)S(1)} %get-tuple-element.23), channel_id=1, source_target_pairs={{0,24},{8,0},{16,8},{24,16},{1,25},{9,1},{17,9},{25,17},{2,26},{10... | collective-permute-start | bytes 196616 | tf_op jit(solution)/shard_map/ppermute | solution.py:271
  28.8 4.5 %collective-permute-start.10 = (bf16[8,32,128]{2,1,0:T(8,128)(2,1)S(1)}, bf16[8,32,128]{2,1,0:T(8,128)(2,1)S(1)}, u32[]{:S(2)}, u32[]{:S(2)}) collective-permute-start(bf16[8,32,128]{2,1,0:T(8,128)(2,1)S(1)} %get-tuple-element.38), channel_id=1, source_target_pairs={{0,24},{8,0},{16,8},{24,16},{1,25},{9,1},{17,9},{25,17},{2,26},{10... | collective-permute-start | bytes 196616 | tf_op jit(solution)/shard_map/ppermute | solution.py:271
  30.3 5.2 %collective-permute-start.9 = (bf16[8,32,128]{2,1,0:T(8,128)(2,1)S(1)}, bf16[8,32,128]{2,1,0:T(8,128)(2,1)S(1)}, u32[]{:S(2)}, u32[]{:S(2)}) collective-permute-start(bf16[8,32,128]{2,1,0:T(8,128)(2,1)S(1)} %get-tuple-element.39), channel_id=1, source_target_pairs={{0,8},{8,16},{16,24},{24,0},{1,9},{9,17},{17,25},{25,1},{2,10},{10... | collective-permute-start | bytes 196616 | tf_op jit(solution)/shard_map/ppermute | solution.py:271
  37.1 11.3 %collective-permute-start.11 = (bf16[4,16,32,128]{3,2,1,0:T(8,128)(2,1)S(1)}, bf16[4,16,32,128]{3,2,1,0:T(8,128)(2,1)S(1)}, u32[]{:S(2)}, u32[]{:S(2)}) collective-permute-start(bf16[4,16,32,128]{3,2,1,0:T(8,128)(2,1)S(1)} %get-tuple-element.27), channel_id=1, source_target_pairs={{0,1},{1,0},{2,3},{3,2},{4,5},{5,4},{6,7},{7,6},{8,9},{9,8},{10,11... | collective-permute-start | bytes 1572872 | tf_op jit(solution)/shard_map/ppermute | solution.py:275
  38.3 8.1 %collective-permute-start.15 = (bf16[448,256]{1,0:T(8,128)(2,1)S(1)}, bf16[448,256]{1,0:T(8,128)(2,1)S(1)}, u32[]{:S(2)}, u32[]{:S(2)}) collective-permute-start(bf16[448,256]{1,0:T(8,128)(2,1)S(1)} %get-tuple-element.34.a_ref), channel_id=1, source_target_pairs={{0,8},{8,0},{16,24},{24,16},{1,9},{9,1},{17,25},{25,17},{2,10},{10... | collective-permute-start | bytes 688136 | tf_op jit(solution)/shard_map/ppermute | solution.py:275
  38.4 9.6 %collective-permute-start.17 = (bf16[448,256]{1,0:T(8,128)(2,1)S(1)}, bf16[448,256]{1,0:T(8,128)(2,1)S(1)}, u32[]{:S(2)}, u32[]{:S(2)}) collective-permute-start(bf16[448,256]{1,0:T(8,128)(2,1)S(1)} %get-tuple-element.35.a_ref), channel_id=1, source_target_pairs={{0,16},{8,24},{16,0},{24,8},{1,17},{9,25},{17,1},{25,9},{2,18},{10... | collective-permute-start | bytes 688136 | tf_op jit(solution)/shard_map/ppermute | solution.py:275
  46.4 8.2 %collective-permute-start.16 = (bf16[448,256]{1,0:T(8,128)(2,1)S(1)}, bf16[448,256]{1,0:T(8,128)(2,1)S(1)}, u32[]{:S(2)}, u32[]{:S(2)}) collective-permute-start(bf16[448,256]{1,0:T(8,128)(2,1)S(1)} %first.1.a_ref), channel_id=1, source_target_pairs={{0,16},{8,24},{16,0},{24,8},{1,17},{9,25},{17,1},{25,9},{2,18},{10... | collective-permute-start | bytes 688136 | tf_op jit(solution)/shard_map/ppermute | solution.py:275
  48.0 7.0 %collective-permute-start.18 = (bf16[448,256]{1,0:T(8,128)(2,1)S(1)}, bf16[448,256]{1,0:T(8,128)(2,1)S(1)}, u32[]{:S(2)}, u32[]{:S(2)}) collective-permute-start(bf16[448,256]{1,0:T(8,128)(2,1)S(1)} %second.1.c_ref), channel_id=1, source_target_pairs={{0,8},{8,0},{16,24},{24,16},{1,9},{9,1},{17,25},{25,17},{2,10},{10... | collective-permute-start | bytes 688136 | tf_op jit(solution)/shard_map/ppermute | solution.py:275
  48.5 8.3 %collective-permute-start.12 = (bf16[16,32,128]{2,1,0:T(8,128)(2,1)S(1)}, bf16[16,32,128]{2,1,0:T(8,128)(2,1)S(1)}, u32[]{:S(2)}, u32[]{:S(2)}) collective-permute-start(bf16[16,32,128]{2,1,0:T(8,128)(2,1)S(1)} %get-tuple-element.29), channel_id=1, source_target_pairs={{0,2},{1,3},{2,4},{3,5},{4,6},{5,7},{6,0},{7,1},{8,10},{9,11},{10,... | collective-permute-start | bytes 393224 | tf_op jit(solution)/shard_map/ppermute | solution.py:271
  49.1 11.8 %collective-permute-start.13 = (bf16[16,32,128]{2,1,0:T(8,128)(2,1)S(1)}, bf16[16,32,128]{2,1,0:T(8,128)(2,1)S(1)}, u32[]{:S(2)}, u32[]{:S(2)}) collective-permute-start(bf16[16,32,128]{2,1,0:T(8,128)(2,1)S(1)} %get-tuple-element.30), channel_id=1, source_target_pairs={{0,4},{1,5},{2,6},{3,7},{4,0},{5,1},{6,2},{7,3},{8,12},{9,13},{10,... | collective-permute-start | bytes 393224 | tf_op jit(solution)/shard_map/ppermute | solution.py:271
  51.0 9.9 %collective-permute-start.14 = (bf16[16,32,128]{2,1,0:T(8,128)(2,1)S(1)}, bf16[16,32,128]{2,1,0:T(8,128)(2,1)S(1)}, u32[]{:S(2)}, u32[]{:S(2)}) collective-permute-start(bf16[16,32,128]{2,1,0:T(8,128)(2,1)S(1)} %get-tuple-element.31), channel_id=1, source_target_pairs={{0,6},{1,7},{2,0},{3,1},{4,2},{5,3},{6,4},{7,5},{8,14},{9,15},{10,... | collective-permute-start | bytes 393224 | tf_op jit(solution)/shard_map/ppermute | solution.py:271

commit v2 on v1

--- a/solution.py
+++ b/solution.py
@@ -120,18 +120,21 @@
     return jax.ShapeDtypeStruct(shape, dtype)
 
 
-def forward_body(n, rows, o, count, me_ref, w_ref, *refs):
-    blocks = refs[:count]
-    own_ref, low_ref, high_ref, x_ref, acc = refs[count:]
-    me = me_ref[0]
-    for r in range(count // 2):
-        for side in range(2):
-            mine = me if side == 0 else me + 1 - 2 * lax.rem(me, 2)
-            source = lax.rem(mine - 2 * r + count, count)
-            place = pl.ds(pl.multiple_of(source * o, o), o)
-            for k in range(n * rows):
-                x_ref[place, k * LANES : (k + 1) * LANES] = blocks[2 * r + side][k]
-    w = w_ref[...].reshape(27 * o, w_ref.shape[2])
+def prepare_body(w_ref, bias_ref, flat_ref, back_ref, wide_ref):
+    flat = w_ref[...].reshape(flat_ref.shape)
+    flat_ref[...] = flat
+    back_ref[...] = jnp.transpose(flat)
+    wide_ref[...] = jnp.broadcast_to(bias_ref[...].astype(jnp.float32), wide_ref.shape)
+
+
+def forward_body(n, rows, o, owner_ref, w_ref, *refs):
+    blocks = refs[:8]
+    own_ref, low_ref, high_ref, x_ref, acc = refs[10:]
+    for b in range(8):
+        place = pl.ds(pl.multiple_of(owner_ref[b] * o, o), o)
+        for k in range(n * rows):
+            x_ref[place, k * LANES : (k + 1) * LANES] = blocks[b][k]
+    w = w_ref[...]
     seen = set()
     for p in range(n):
         for t in range(0, rows, 2):
@@ -161,85 +164,105 @@
                 high_ref[y] = total.astype(high_ref.dtype)
             else:
                 own_ref[(q - 1) * rows + y] = total
-
-
-def activation_body(n, rows, own_ref, below_ref, above_ref, bias_ref, go_ref, act_ref, gp_ref):
-    for p in range(n):
-        for y in range(rows):
-            k = p * rows + y
-            pre = own_ref[k] + bias_ref[...]
-            if p == 0:
-                pre = pre + below_ref[y].astype(jnp.float32)
-            if p == n - 1:
-                pre = pre + above_ref[y].astype(jnp.float32)
-            s = jax.nn.sigmoid(pre)
-            act_ref[k] = (pre * s).astype(act_ref.dtype)
-            slope = s * (1.0 + pre * (1.0 - s))
-            gp_ref[k] = (go_ref[k].astype(jnp.float32) * slope).astype(gp_ref.dtype)
-
-
-def input_grad_body(
-    n, rows, o, count, me_ref, gp_ref, below_ref, above_ref, wt_ref, mine_ref, other_ref, s_ref, w_ref
+            if q == 1:
+                low_ref[rows + y] = total.astype(low_ref.dtype)
+            if q == n:
+                high_ref[rows + y] = total.astype(high_ref.dtype)
+
+
+def gradient_body(
+    n,
+    rows,
+    o,
+    scale,
+    owner_ref,
+    own_ref,
+    low_ref,
+    high_ref,
+    below_ref,
+    above_ref,
+    bias_ref,
+    go_ref,
+    go_below_ref,
+    go_above_ref,
+    back_ref,
+    act_ref,
+    total_ref,
+    s_ref,
+    w_ref,
+    other_ref,
 ):
-    me = me_ref[0]
-    core = lax.rem(me, 2)
-    for side in range(2):
-        for r in range(count // 2):
-            owner = lax.rem(me - core + 2 * r, count) + (core if side == 0 else 1 - core)
-            rel = (side * (count // 2) + r) * o
-            w_ref[rel : rel + o] = wt_ref[pl.ds(pl.multiple_of(owner * o, o), o)]
+    f32, bf16 = jnp.float32, jnp.bfloat16
+    for b in range(8):
+        place = pl.ds(pl.multiple_of(owner_ref[b] * o, o), o)
+        w_ref[b * o : (b + 1) * o] = back_ref[place]
+    total = jnp.zeros((o, LANES), f32)
     for q in range(n + 2):
         for y in range(rows):
             if q == 0:
-                value = below_ref[y]
+                pre = below_ref[rows + y].astype(f32) + low_ref[y].astype(f32)
+                go = go_below_ref[y]
             elif q == n + 1:
-                value = above_ref[y]
+                pre = above_ref[rows + y].astype(f32) + high_ref[y].astype(f32)
+                go = go_above_ref[y]
             else:
-                value = gp_ref[(q - 1) * rows + y]
-            wide = value.astype(jnp.float32)
+                pre = own_ref[(q - 1) * rows + y]
+                go = go_ref[(q - 1) * rows + y]
+                if q == 1:
+                    pre = pre + below_ref[y].astype(f32)
+                if q == n:
+                    pre = pre + above_ref[y].astype(f32)
+            pre = pre + bias_ref[...]
+            s = jax.nn.sigmoid(pre)
+            slope = s * (1.0 + pre * (1.0 - s))
+            value = (go.astype(f32) * slope).astype(bf16)
+            wide = value.astype(f32)
+            if 1 <= q <= n:
+                act_ref[(q - 1) * rows + y] = (pre * s).astype(bf16)
+                total = total + wide
             turned = [
-                pltpu.roll(wide, LANES - 1, 1).astype(value.dtype),
+                pltpu.roll(wide, LANES - 1, 1).astype(bf16),
                 value,
-                pltpu.roll(wide, 1, 1).astype(value.dtype),
+                pltpu.roll(wide, 1, 1).astype(bf16),
             ]
             for k, i, j, l in tap_list():
                 p = q - 2 + i
                 if 0 <= p < n:
                     at = (p * rows + (y + j - 1) % rows) * LANES
                     s_ref[k * o : (k + 1) * o, at : at + LANES] = turned[l]
-    w = w_ref[...]
-    half = count // 2 * o
-    for t in range(0, n * rows, 2):
+    total_ref[...] = jnp.broadcast_to(
+        jnp.sum(total, axis=1, keepdims=True) * scale, total_ref.shape
+    )
+    input_grad(n * rows, o, w_ref[4 * o :], s_ref, other_ref)
+
+
+def input_grad(cells, o, w, s_ref, out_ref):
+    for t in range(0, cells, 2):
         part = jnp.dot(
             w, s_ref[:, t * LANES : (t + 2) * LANES], preferred_element_type=jnp.float32
-        ).astype(mine_ref.dtype)
+        ).astype(out_ref.dtype)
         for h in range(2):
-            for r in range(count // 2):
+            for r in range(4):
                 cut = part[r * o : (r + 1) * o, h * LANES : (h + 1) * LANES]
-                mine_ref[r, t + h] = cut
-                cut = part[half + r * o : half + (r + 1) * o, h * LANES : (h + 1) * LANES]
-                other_ref[r, t + h] = cut
-
-
-def filter_grad_body(scale, taps, s_ref, x_ref, gp_ref, first_ref, second_ref):
-    o = gp_ref.shape[1]
+                out_ref[r, t + h] = cut
+
+
+def filter_grad_body(scale, taps, o, s_ref, x_ref, w_ref, total_ref, mine_ref, first_ref, second_ref):
+    input_grad(mine_ref.shape[1], o, w_ref[: 4 * o], s_ref, mine_ref)
     full = lax.dot_general(
         s_ref[...], x_ref[...], (((1,), (1,)), ((), ())), preferred_element_type=jnp.float32
     )
     full = (full * scale).astype(first_ref.dtype)
     first_ref[...] = full[: taps * o]
     second_ref[: (27 - taps) * o] = full[taps * o :]
-    total = jnp.sum(gp_ref[...].astype(jnp.float32), axis=0)
-    total = jnp.sum(total, axis=1, keepdims=True) * scale
-    second_ref[(27 - taps) * o :] = jnp.broadcast_to(
-        total, (o, second_ref.shape[1])
-    ).astype(second_ref.dtype)
-
-
-def pair_body(a_ref, b_ref, out_ref):
-    out_ref[...] = (a_ref[...].astype(jnp.float32) + b_ref[...].astype(jnp.float32)).astype(
-        out_ref.dtype
-    )
+    row = jnp.concatenate([total_ref[...]] * (second_ref.shape[1] // LANES), axis=1)
+    second_ref[(27 - taps) * o :] = row.astype(second_ref.dtype)
+
+
+def middle_body(*refs):
+    for p in range(3):
+        total = refs[2 * p][...].astype(jnp.float32) + refs[2 * p + 1][...].astype(jnp.float32)
+        refs[6 + p][...] = total.astype(refs[6 + p].dtype)
 
 
 def split_sum_body(a_ref, b_ref, *outs):
@@ -248,14 +271,7 @@
         out[...] = total.astype(out.dtype)
 
 
-def sum_body(*refs):
-    total = refs[0][...].astype(jnp.float32)
-    for ref in refs[1:-1]:
-        total = total + ref[...].astype(jnp.float32)
-    refs[-1][...] = total.astype(refs[-1].dtype)
-
-
-def last_body(taps, a_ref, b_ref, c_ref, d_ref, out_ref, bias_ref):
+def last_body(taps, a_ref, b_ref, c_ref, d_ref, g_ref, h_ref, k_ref, out_ref, bias_ref, grad_ref):
     o = out_ref.shape[1]
     f32 = jnp.float32
     for k in range(27):
@@ -264,6 +280,8 @@
         out_ref[k] = left[cut].astype(f32) + right[cut].astype(f32)
     cut = slice((27 - taps) * o, (28 - taps) * o)
     bias_ref[...] = (c_ref[cut].astype(f32) + d_ref[cut].astype(f32))[:, :LANES]
+    total = g_ref[...] + h_ref[...].astype(f32) + k_ref[...].astype(f32)
+    grad_ref[...] = total.astype(grad_ref.dtype)
 
 
 def rotate(value, axis, step):
@@ -276,13 +294,14 @@
 
 
 def on_device(x_in, weight, bias_vec, grad_out):
-    count = lax.axis_size("chan")
     o, _, c_all = weight.shape
     _, n, rows, depth = x_in.shape
     f32, bf16 = jnp.float32, jnp.bfloat16
     cells = n * rows
+    flops = 2 * 27 * o * c_all * cells * depth
     scale = 1.0 / math.sqrt(lax.axis_size("slab") * cells * depth)
-    me = lax.axis_index("chan").astype(jnp.int32).reshape(1)
+    me = lax.axis_index("chan").astype(jnp.int32)
+    owners = jnp.bitwise_xor(me, jnp.array([0, 2, 4, 6, 1, 3, 5, 7], jnp.int32))
 
     def by_row(a):
         return jnp.transpose(a, (1, 2, 0, 3)).reshape(cells, o, depth)
@@ -291,81 +310,101 @@
         return jnp.transpose(a.reshape(n, rows, o, depth), (2, 0, 1, 3))
 
     x_own = by_row(x_in)
-    blocks = [x_own, swap(x_own, "chan", 1)]
-    for r in range(1, count // 2):
-        far = rotate(x_own, "chan", 2 * r)
-        blocks += [far, swap(far, "chan", 1)]
+    x_a = swap(x_own, "chan", 2)
+    x_b = swap(x_own, "chan", 4)
+    x_side = swap(x_own, "chan", 1)
     w_taps = jnp.transpose(weight, (1, 0, 2))
-    w_back = jnp.transpose(w_taps.reshape(27 * o, c_all))
+    w_flat, w_back, bias = call(
+        prepare_body,
+        [
+            shape_of((27 * o, c_all), bf16),
+            shape_of((c_all, 27 * o), bf16),
+            shape_of((o, LANES), f32),
+        ],
+        [w_taps, bias_vec[:, None]],
+        name="prepare",
+    )
     go = by_row(grad_out)
-    bias = jnp.broadcast_to(bias_vec.astype(f32)[:, None], (o, depth))
+    x_a, w_flat, w_back, bias, go = lax.optimization_barrier((x_a, w_flat, w_back, bias, go))
+    x_a_side = swap(x_a, "chan", 1)
+    x_ab = swap(x_b, "chan", 2)
+    x_b_side = swap(x_b, "chan", 1)
+    go_above = rotate(go[:rows], "slab", -1)
+    go_below = rotate(go[cells - rows :], "slab", 1)
+    x_ab_side = swap(x_ab, "chan", 1)
+    blocks = [x_own, x_a, x_b, x_ab, x_side, x_a_side, x_b_side, x_ab_side]
 
     own, low, high, x_all = call(
-        functools.partial(forward_body, n, rows, o, count),
+        functools.partial(forward_body, n, rows, o),
         [
             shape_of((cells, o, depth), f32),
-            shape_of((rows, o, depth), bf16),
-            shape_of((rows, o, depth), bf16),
+            shape_of((2 * rows, o, depth), bf16),
+            shape_of((2 * rows, o, depth), bf16),
             shape_of((c_all, cells * depth), bf16),
         ],
-        [me, w_taps, *blocks],
-        [SMEM] + [VMEM] * (1 + count),
+        [owners, w_flat, *blocks, go_below, go_above],
+        [SMEM] + [VMEM] * 9 + [pl.BlockSpec(memory_space=pl.ANY)] * 2,
         [pltpu.VMEM((3, n + 2, rows, o, depth), f32)],
-        flops=2 * 27 * o * c_all * cells * depth,
+        flops=flops,
         name="forward",
     )
     above = rotate(low, "slab", -1)
     below = rotate(high, "slab", 1)
-    act, gp = call(
-        functools.partial(activation_body, n, rows),
-        [shape_of((cells, o, depth), bf16)] * 2,
-        [own, below, above, bias, go],
-        name="activation",
-    )
-    gp_above = rotate(gp[:rows], "slab", -1)
-    gp_below = rotate(gp[cells - rows :], "slab", 1)
-    half = (count // 2, cells, o, depth)
-    mine, other, stacked = call(
-        functools.partial(input_grad_body, n, rows, o, count),
-        [
+    half = (4, cells, o, depth)
+    act, total, stacked, w_turned, other = call(
+        functools.partial(gradient_body, n, rows, o, scale),
+        [
+            shape_of((cells, o, depth), bf16),
+            shape_of((o, LANES), f32),
+            shape_of((27 * o, cells * depth), bf16),
+            shape_of((c_all, 27 * o), bf16),
             shape_of(half, bf16),
-            shape_of(half, bf16),
-            shape_of((27 * o, cells * depth), bf16),
-        ],
-        [me, gp, gp_below, gp_above, w_back],
-        [SMEM] + [VMEM] * 4,
-        [pltpu.VMEM((c_all, 27 * o), bf16)],
-        flops=2 * 27 * o * c_all * cells * depth,
-        name="input_grad",
+        ],
+        [owners, own, low, high, below, above, bias, go, go_below, go_above, w_back],
+        [SMEM] + [VMEM] * 10,
+        flops=flops // 2,
+        name="gradient",
     )
     other = swap(other, "chan", 1)
     taps = 14
-    first, second = call(
-        functools.partial(filter_grad_body, scale, taps),
-        [shape_of((taps * o, c_all), bf16), shape_of(((28 - taps) * o, c_all), bf16)],
-        [stacked, x_all, gp],
-        flops=2 * 27 * o * c_all * cells * depth,
+    mine, first, second = call(
+        functools.partial(filter_grad_body, scale, taps, o),
+        [
+            shape_of(half, bf16),
+            shape_of((taps * o, c_all), bf16),
+            shape_of(((28 - taps) * o, c_all), bf16),
+        ],
+        [stacked, x_all, w_turned, total],
+        flops=flops + flops // 2,
         name="filter_grad",
     )
+    g_own, g_a, g_b, g_ab = call(
+        split_sum_body,
+        [shape_of((cells, o, depth), f32)] + [shape_of((cells, o, depth), bf16)] * 3,
+        [mine, other],
+        name="pair_sum",
+    )
+    far = swap(g_ab, "chan", 2)
+    near = swap(g_a, "chan", 2)
     first_far = swap(first, "slab", 1)
     second_far = swap(second, "slab", 2)
-    sums = call(
-        split_sum_body,
-        [shape_of((cells, o, depth), f32)]
-        + [shape_of((cells, o, depth), bf16)] * (count // 2 - 1),
-        [mine, other],
-        name="pair_sum",
-    )
-    far = [rotate(sums[r], "chan", 2 * r) for r in range(1, count // 2)]
-    (first,) = call(pair_body, [shape_of(first.shape, bf16)], [first, first_far], name="first")
-    (second,) = call(pair_body, [shape_of(second.shape, bf16)], [second, second_far], name="second")
+    g_b, first, second = call(
+        middle_body,
+        [shape_of(a.shape, bf16) for a in (g_b, first, second)],
+        [g_b, far, first, first_far, second, second_far],
+        name="middle",
+    )
+    across = swap(g_b, "chan", 4)
     first_far = swap(first, "slab", 2)
     second_far = swap(second, "slab", 1)
-    (grad_in,) = call(sum_body, [shape_of((cells, o, depth), bf16)], [sums[0], *far], name="sum")
-    weight_grad, bias_grad = call(
+    weight_grad, bias_grad, grad_in = call(
         functools.partial(last_body, taps),
-        [shape_of((27, o, c_all), f32), shape_of((o, LANES), f32)],
-        [first, first_far, second, second_far],
+        [
+            shape_of((27, o, c_all), f32),
+            shape_of((o, LANES), f32),
+            shape_of((cells, o, depth), bf16),
+        ],
+        [first, first_far, second, second_far, g_own, near, across],
         name="last",
     )
     return (
@@ -389,7 +428,8 @@
             weight.shape[0] % 32 == 0
             and x_in.shape[3] == LANES
             and lax.axis_size("slab") == 4
-            and lax.axis_size("chan") % 2 == 0
+            and lax.axis_size("chan") == 8
+            and x_in.shape[1] >= 2
         )
         return (on_device if tiled else plain)(x_in, weight, bias_vec, grad_out)
 

time: 61.8 us -> 56.6 us (0.916)
  waiting for transfers between devices: 30.3 us -> 24 us
  starting transfers between devices: 20.7 us -> 18.7 us
  local copies, waits for them, and re-layouts: 4.4 us -> 5.69 us
  Pallas kernels: 5.46 us -> 6.73 us
  other arithmetic: 0 us -> 0.66 us
    ppermute x10 -> x4, waiting for transfers between devices: 22.5 us -> 8.19 us  [rotate(): lax.ppermute(value, axis, [(i, (i + step) % count) for i in range(count)])]
    ppermute x10 -> x4, starting transfers between devices: 16.6 us -> 4.58 us  [rotate(): lax.ppermute(value, axis, [(i, (i + step) % count) for i in range(count)])]
    ppermute x9 -> x15, starting transfers between devices: 4.18 us -> 14.1 us  [swap(): lax.ppermute(value, axis, [(i, i ^ bit) for i in range(lax.axis_size(axis...]
    ppermute x9 -> x15, waiting for transfers between devices: 7.86 us -> 15.8 us  [swap(): lax.ppermute(value, axis, [(i, i ^ bit) for i in range(lax.axis_size(axis...]
    pallas_call x9 -> x7, Pallas kernels: 5.46 us -> 6.73 us  [call(): pl.pallas_call(body, out_shape=out_shape, in_specs=specs or [VMEM] * len(...]
    transpose x2, local copies, waits for them, and re-layouts: 1.01 us -> 1.88 us  [by_row(): return jnp.transpose(a, (1, 2, 0, 3)).reshape(cells, o, depth)]
    broadcast_in_dim x1, local copies, waits for them, and re-layouts: 0.07 us -> 0.75 us  [on_device(): bias_vec[:, None]]
    xor x0 -> x1, other arithmetic: none -> 0.66 us  [on_device(): owners = jnp.bitwise_xor(me, jnp.array([0, 2, 4, 6, 1, 3, 5, 7], jnp.int32))]
  transfers between devices with their start and end apart: 19 -> 19, of which waited for: 12 -> 9; matrix products, arithmetic and copies ran while one was open for 3% -> 5% of each run, Pallas kernels for 4% -> 4%
where the time goes in v2:
time: 56.6 us; the launch traced here: 56.4 us
  waiting for transfers between devices  24 us (42%)
  starting transfers between devices  18.7 us (33%)
  Pallas kernels  6.73 us (12%)
  local copies, waits for them, and re-layouts  5.69 us (10%)
  between operations  0.72 us (1%)
  other arithmetic  0.66 us (1%)
    ppermute x15, waiting for transfers between devices, swap(): lax.ppermute(value, axis, [(i, i ^ bit) for i in range(lax.axis_size(axis...  15.8 us
    ppermute x15, starting transfers between devices, swap(): lax.ppermute(value, axis, [(i, i ^ bit) for i in range(lax.axis_size(axis...  14.1 us
    ppermute x4, waiting for transfers between devices, rotate(): lax.ppermute(value, axis, [(i, (i + step) % count) for i in range(count)])  8.19 us
    pallas_call x7, Pallas kernels, call(): pl.pallas_call(body, out_shape=out_shape, in_specs=specs or [VMEM] * len(...  6.73 us
    ppermute x4, starting transfers between devices, rotate(): lax.ppermute(value, axis, [(i, (i + step) % count) for i in range(count)])  4.58 us
    transpose x2, local copies, waits for them, and re-layouts, by_row(): return jnp.transpose(a, (1, 2, 0, 3)).reshape(cells, o, depth)  1.88 us
    reshape x2, local copies, waits for them, and re-layouts, by_channel(): return jnp.transpose(a.reshape(n, rows, o, depth), (2, 0, 1, 3))  1.42 us
  transfers between devices with their start and end apart: 19, of which 9 were waited for; matrix products, arithmetic and copies ran while one was open for 5% of the time, Pallas kernels for 4%

profile of v2, /device:TPU:0, one launch (start us, length us, event | category | flops | bytes accessed | tf_op | source)
XLA Modules:
  0.0 56.4 jit_solution(10743571800532350509)
XLA Ops:
  0.6 0.9 %copy.14 = bf16[2,8,32,128]{3,2,1,0:T(8,128)(2,1)S(1)} copy(bf16[2,8,32,128]{3,1,0,2:T(8,128)(2,1)} %bitcast.24) | data formatting | bytes 262144 | tf_op jit(solution)/shard_map/transpose | solution.py:307
  1.6 3.1 %collective-permute-start = (bf16[16,32,128]{2,1,0:T(8,128)(2,1)S(1)}, bf16[16,32,128]{2,1,0:T(8,128)(2,1)S(1)}, u32[]{:S(2)}, u32[]{:S(2)}) collective-permute-start(bf16[16,32,128]{2,1,0:T(8,128)(2,1)S(1)} %bitcast.18), channel_id=1, source_target_pairs={{0,2},{1,3},{2,0},{3,1},{4,6},{5,7},{6,4},{7,5},{8,10},{9,11},{10,... | collective-permute-start | bytes 393224 | tf_op jit(solution)/shard_map/ppermute | solution.py:293
  4.7 2.6 %collective-permute-start.1 = (bf16[16,32,128]{2,1,0:T(8,128)(2,1)S(1)}, bf16[16,32,128]{2,1,0:T(8,128)(2,1)S(1)}, u32[]{:S(2)}, u32[]{:S(2)}) collective-permute-start(bf16[16,32,128]{2,1,0:T(8,128)(2,1)S(1)} %bitcast.19), channel_id=1, source_target_pairs={{0,4},{1,5},{2,6},{3,7},{4,0},{5,1},{6,2},{7,3},{8,12},{9,13},{10,... | collective-permute-start | bytes 393224 | tf_op jit(solution)/shard_map/ppermute | solution.py:293
  7.3 0.7 %copy.15.bias_ref = bf16[32,1]{1,0:T(8,128)(2,1)S(1)} copy(bf16[32,1]{0,1:T(2,128)(2,1)} %bitcast.28) | data formatting | bytes 128 | tf_op jit(solution)/shard_map/broadcast_in_dim | solution.py:324
  8.0 0.9 %copy.16 = bf16[2,8,32,128]{3,2,1,0:T(8,128)(2,1)S(1)} copy(bf16[2,8,32,128]{3,1,0,2:T(8,128)(2,1)} %bitcast.25) | data formatting | bytes 262144 | tf_op jit(solution)/shard_map/transpose | solution.py:307
  9.0 1.0 %copy-done = bf16[32,27,256]{2,0,1:T(8,128)(2,1)S(1)} copy-done((bf16[32,27,256]{2,0,1:T(8,128)(2,1)S(1)}, bf16[32,27,256]{2,0,1:T(8,128)(2,1)}, u32[]{:S(2)}) %copy-start) | copy-done | bytes 442392
  10.2 3.2 %collective-permute-done.1.refs_2_ = bf16[16,32,128]{2,1,0:T(8,128)(2,1)S(1)} collective-permute-done((bf16[16,32,128]{2,1,0:T(8,128)(2,1)S(1)}, bf16[16,32,128]{2,1,0:T(8,128)(2,1)S(1)}, u32[]{:S(2)}, u32[]{:S(2)}) %collective-permute-start.1) | collective-permute-done | bytes 131104 | tf_op jit(solution)/shard_map/ppermute | solution.py:293
  13.8 2.5 %collective-permute-start.8 = (bf16[8,32,128]{2,1,0:T(8,128)(2,1)S(1)}, bf16[8,32,128]{2,1,0:T(8,128)(2,1)S(1)}, u32[]{:S(2)}, u32[]{:S(2)}) collective-permute-start(bf16[8,32,128]{2,1,0:T(8,128)(2,1)S(1)} %get-tuple-element.64), channel_id=1, source_target_pairs={{0,24},{8,0},{16,8},{24,16},{1,25},{9,1},{17,9},{25,17},{2,26},{10... | collective-permute-start | bytes 196616 | tf_op jit(solution)/shard_map/ppermute | solution.py:289
  16.9 1.5 %collective-permute-done.2.refs_3_ = bf16[16,32,128]{2,1,0:T(8,128)(2,1)S(1)} collective-permute-done((bf16[16,32,128]{2,1,0:T(8,128)(2,1)S(1)}, bf16[16,32,128]{2,1,0:T(8,128)(2,1)S(1)}, u32[]{:S(2)}, u32[]{:S(2)}) %collective-permute-start.2) | collective-permute-done | bytes 131104 | tf_op jit(solution)/shard_map/ppermute | solution.py:293
  19.0 2.5 %collective-permute-done.7.refs_8_.go_below_ref = bf16[8,32,128]{2,1,0:T(8,128)(2,1)S(1)} collective-permute-done((bf16[8,32,128]{2,1,0:T(8,128)(2,1)S(1)}, bf16[8,32,128]{2,1,0:T(8,128)(2,1)S(1)}, u32[]{:S(2)}, u32[]{:S(2)}) %collective-permute-start.7) | collective-permute-done | bytes 65568 | tf_op jit(solution)/shard_map/ppermute | solution.py:289
  21.5 1.9 %forward.1 = (f32[16,32,128]{2,1,0:T(8,128)S(1)}, bf16[16,32,128]{2,1,0:T(8,128)(2,1)S(1)}, bf16[16,32,128]{2,1,0:T(8,128)(2,1)S(1)}, bf16[256,2048]{1,0:T(8,128)(2,1)S(1)}) custom-call(s32[8]{0:T(128)S(1)} %broadcast_xor_fusion.owner_ref, bf16[864,256]{1,0:T(8,128)(2,1)S(1)} %get-tuple-element.37.w_ref, bf16[16,32,128]{2,1,0:T(8,128)(2,1)S(1)} %bitcast.21, ...), custom_call_target="tpu_custom_call" | custom-call | flops 905969664 | bytes 3194912 | tf_op jit(solution)/shard_map/forward/pallas_call | solution.py:105
  24.1 1.4 %collective-permute-start.9 = (bf16[16,32,128]{2,1,0:T(8,128)(2,1)S(1)}, bf16[16,32,128]{2,1,0:T(8,128)(2,1)S(1)}, u32[]{:S(2)}, u32[]{:S(2)}) collective-permute-start(bf16[16,32,128]{2,1,0:T(8,128)(2,1)S(1)} %get-tuple-element.42.high_ref), channel_id=1, source_target_pairs={{0,8},{8,16},{16,24},{24,0},{1,9},{9,17},{17,25},{25,1},{2,10},{10... | collective-permute-start | bytes 393224 | tf_op jit(solution)/shard_map/ppermute | solution.py:289
  25.5 3.8 %collective-permute-done.10.above_ref = bf16[16,32,128]{2,1,0:T(8,128)(2,1)S(1)} collective-permute-done((bf16[16,32,128]{2,1,0:T(8,128)(2,1)S(1)}, bf16[16,32,128]{2,1,0:T(8,128)(2,1)S(1)}, u32[]{:S(2)}, u32[]{:S(2)}) %collective-permute-start.10) | collective-permute-done | bytes 131104 | tf_op jit(solution)/shard_map/ppermute | solution.py:289
  29.3 1.9 %collective-permute-done.9.below_ref = bf16[16,32,128]{2,1,0:T(8,128)(2,1)S(1)} collective-permute-done((bf16[16,32,128]{2,1,0:T(8,128)(2,1)S(1)}, bf16[16,32,128]{2,1,0:T(8,128)(2,1)S(1)}, u32[]{:S(2)}, u32[]{:S(2)}) %collective-permute-start.9) | collective-permute-done | bytes 131104 | tf_op jit(solution)/shard_map/ppermute | solution.py:289
  31.2 1.7 %gradient.1 = (bf16[16,32,128]{2,1,0:T(8,128)(2,1)S(1)}, f32[32,128]{1,0:T(8,128)S(1)}, bf16[864,2048]{1,0:T(8,128)(2,1)S(1)}, bf16[256,864]{1,0:T(8,128)(2,1)S(1)}, bf16[4,16,32,128]{3,2,1,0:T(8,128)(2,1)S(1)}) custom-call(s32[8]{0:T(128)S(1)} %broadcast_xor_fusion.owner_ref, f32[16,32,128]{2,1,0:T(8,128)S(1)} %get-tuple-element.40.own_ref, ...), custom_call_target="tpu_custom_call" | custom-call | flops 452984832 | bytes 6160416 | tf_op jit(solution)/shard_map/gradient/pallas_call | solution.py:105
  33.0 1.7 %filter_grad.1 = (bf16[4,16,32,128]{3,2,1,0:T(8,128)(2,1)S(1)}, bf16[448,256]{1,0:T(8,128)(2,1)S(1)}, bf16[448,256]{1,0:T(8,128)(2,1)S(1)}) custom-call(bf16[864,2048]{1,0:T(8,128)(2,1)S(1)} %get-tuple-element.46.s_ref, bf16[256,2048]{1,0:T(8,128)(2,1)S(1)} %get-tuple-element.47.x_ref, bf16[256,864]{1,0:T(8,128)(2,1)S(1)} %get-tuple-element.48.w_ref, ...), custom_call_target="tpu_custom_call" | custom-call | flops 1358954496 | bytes 6029312 | tf_op jit(solution)/shard_map/filter_grad/pallas_call | solution.py:105
  34.6 1.3 %collective-permute-start.13 = (bf16[448,256]{1,0:T(8,128)(2,1)S(1)}, bf16[448,256]{1,0:T(8,128)(2,1)S(1)}, u32[]{:S(2)}, u32[]{:S(2)}) collective-permute-start(bf16[448,256]{1,0:T(8,128)(2,1)S(1)} %get-tuple-element.54.refs_2_), channel_id=1, source_target_pairs={{0,8},{8,0},{16,24},{24,16},{1,9},{9,1},{17,25},{25,17},{2,10},{10... | collective-permute-start | bytes 688136 | tf_op jit(solution)/shard_map/ppermute | solution.py:293
  37.3 5.4 %collective-permute-done.13.refs_3_ = bf16[448,256]{1,0:T(8,128)(2,1)S(1)} collective-permute-done((bf16[448,256]{1,0:T(8,128)(2,1)S(1)}, bf16[448,256]{1,0:T(8,128)(2,1)S(1)}, u32[]{:S(2)}, u32[]{:S(2)}) %collective-permute-start.13) | collective-permute-done | bytes 229408 | tf_op jit(solution)/shard_map/ppermute | solution.py:293
  42.7 1.0 %collective-permute-done.14.refs_5_ = bf16[448,256]{1,0:T(8,128)(2,1)S(1)} collective-permute-done((bf16[448,256]{1,0:T(8,128)(2,1)S(1)}, bf16[448,256]{1,0:T(8,128)(2,1)S(1)}, u32[]{:S(2)}, u32[]{:S(2)}) %collective-permute-start.14) | collective-permute-done | bytes 229408 | tf_op jit(solution)/shard_map/ppermute | solution.py:293
  44.4 1.2 %collective-permute-start.16 = (bf16[448,256]{1,0:T(8,128)(2,1)S(1)}, bf16[448,256]{1,0:T(8,128)(2,1)S(1)}, u32[]{:S(2)}, u32[]{:S(2)}) collective-permute-start(bf16[448,256]{1,0:T(8,128)(2,1)S(1)} %get-tuple-element.57.c_ref), channel_id=1, source_target_pairs={{0,8},{8,0},{16,24},{24,16},{1,9},{9,1},{17,25},{25,17},{2,10},{10... | collective-permute-start | bytes 688136 | tf_op jit(solution)/shard_map/ppermute | solution.py:293
  46.4 2.3 %collective-permute-start.18 = (bf16[16,32,128]{2,1,0:T(8,128)(2,1)S(1)}, bf16[16,32,128]{2,1,0:T(8,128)(2,1)S(1)}, u32[]{:S(2)}, u32[]{:S(2)}) collective-permute-start(bf16[16,32,128]{2,1,0:T(8,128)(2,1)S(1)} %get-tuple-element.60), channel_id=1, source_target_pairs={{0,4},{1,5},{2,6},{3,7},{4,0},{5,1},{6,2},{7,3},{8,12},{9,13},{10,... | collective-permute-start | bytes 393224 | tf_op jit(solution)/shard_map/ppermute | solution.py:293
  49.4 2.3 %collective-permute-done.17.h_ref = bf16[16,32,128]{2,1,0:T(8,128)(2,1)S(1)} collective-permute-done((bf16[16,32,128]{2,1,0:T(8,128)(2,1)S(1)}, bf16[16,32,128]{2,1,0:T(8,128)(2,1)S(1)}, u32[]{:S(2)}, u32[]{:S(2)}) %collective-permute-start.17) | collective-permute-done | bytes 131104 | tf_op jit(solution)/shard_map/ppermute | solution.py:293
  51.7 2.3 %collective-permute-done.18.k_ref = bf16[16,32,128]{2,1,0:T(8,128)(2,1)S(1)} collective-permute-done((bf16[16,32,128]{2,1,0:T(8,128)(2,1)S(1)}, bf16[16,32,128]{2,1,0:T(8,128)(2,1)S(1)}, u32[]{:S(2)}, u32[]{:S(2)}) %collective-permute-start.18) | collective-permute-done | bytes 131104 | tf_op jit(solution)/shard_map/ppermute | solution.py:293
  54.1 1.0 %last.1 = (f32[27,32,256]{2,1,0:T(8,128)}, f32[32,128]{1,0:T(8,128)S(1)}, bf16[16,32,128]{2,1,0:T(8,128)(2,1)S(1)}) custom-call(bf16[448,256]{1,0:T(8,128)(2,1)S(1)} %get-tuple-element.56.a_ref, bf16[448,256]{1,0:T(8,128)(2,1)S(1)} %collective-permute-done.15.b_ref, bf16[448,256]{1,0:T(8,128)(2,1)S(1)} %get-tuple-element.57.c_ref, ...), custom_call_target="tpu_custom_call" | custom-call | bytes 2473984 | tf_op jit(solution)/shard_map/last/pallas_call | solution.py:105
  (31 shorter events, 7.4 us)
Async XLA Ops:
  1.6 8.6 %collective-permute-start = (bf16[16,32,128]{2,1,0:T(8,128)(2,1)S(1)}, bf16[16,32,128]{2,1,0:T(8,128)(2,1)S(1)}, u32[]{:S(2)}, u32[]{:S(2)}) collective-permute-start(bf16[16,32,128]{2,1,0:T(8,128)(2,1)S(1)} %bitcast.18), channel_id=1, source_target_pairs={{0,2},{1,3},{2,0},{3,1},{4,6},{5,7},{6,4},{7,5},{8,10},{9,11},{10,... | collective-permute-start | bytes 393224 | tf_op jit(solution)/shard_map/ppermute | solution.py:293
  4.7 8.7 %collective-permute-start.1 = (bf16[16,32,128]{2,1,0:T(8,128)(2,1)S(1)}, bf16[16,32,128]{2,1,0:T(8,128)(2,1)S(1)}, u32[]{:S(2)}, u32[]{:S(2)}) collective-permute-start(bf16[16,32,128]{2,1,0:T(8,128)(2,1)S(1)} %bitcast.19), channel_id=1, source_target_pairs={{0,4},{1,5},{2,6},{3,7},{4,0},{5,1},{6,2},{7,3},{8,12},{9,13},{10,... | collective-permute-start | bytes 393224 | tf_op jit(solution)/shard_map/ppermute | solution.py:293
  7.3 9.1 %collective-permute-start.3 = (bf16[16,32,128]{2,1,0:T(8,128)(2,1)S(1)}, bf16[16,32,128]{2,1,0:T(8,128)(2,1)S(1)}, u32[]{:S(2)}, u32[]{:S(2)}) collective-permute-start(bf16[16,32,128]{2,1,0:T(8,128)(2,1)S(1)} %bitcast.20), channel_id=1, source_target_pairs={{0,1},{1,0},{2,3},{3,2},{4,5},{5,4},{6,7},{7,6},{8,9},{9,8},{10,11... | collective-permute-start | bytes 393224 | tf_op jit(solution)/shard_map/ppermute | solution.py:293
  8.9 1.0 %copy-start = (bf16[32,27,256]{2,0,1:T(8,128)(2,1)S(1)}, bf16[32,27,256]{2,0,1:T(8,128)(2,1)}, u32[]{:S(2)}) copy-start(bf16[32,27,256]{2,0,1:T(8,128)(2,1)} %param.6) | copy-start | bytes 1327108
  13.4 5.0 %collective-permute-start.2 = (bf16[16,32,128]{2,1,0:T(8,128)(2,1)S(1)}, bf16[16,32,128]{2,1,0:T(8,128)(2,1)S(1)}, u32[]{:S(2)}, u32[]{:S(2)}) collective-permute-start(bf16[16,32,128]{2,1,0:T(8,128)(2,1)S(1)} %collective-permute-done.1.refs_2_), channel_id=1, source_target_pairs={{0,2},{1,3},{2,0},{3,1},{4,6},{5,7},{6,4},{7,5},{8,10},{9,11},{10,... | collective-permute-start | bytes 393224 | tf_op jit(solution)/shard_map/ppermute | solution.py:293
  13.8 5.2 %collective-permute-start.8 = (bf16[8,32,128]{2,1,0:T(8,128)(2,1)S(1)}, bf16[8,32,128]{2,1,0:T(8,128)(2,1)S(1)}, u32[]{:S(2)}, u32[]{:S(2)}) collective-permute-start(bf16[8,32,128]{2,1,0:T(8,128)(2,1)S(1)} %get-tuple-element.64), channel_id=1, source_target_pairs={{0,24},{8,0},{16,8},{24,16},{1,25},{9,1},{17,9},{25,17},{2,26},{10... | collective-permute-start | bytes 196616 | tf_op jit(solution)/shard_map/ppermute | solution.py:289
  16.3 5.2 %collective-permute-start.7 = (bf16[8,32,128]{2,1,0:T(8,128)(2,1)S(1)}, bf16[8,32,128]{2,1,0:T(8,128)(2,1)S(1)}, u32[]{:S(2)}, u32[]{:S(2)}) collective-permute-start(bf16[8,32,128]{2,1,0:T(8,128)(2,1)S(1)} %get-tuple-element.65), channel_id=1, source_target_pairs={{0,8},{8,16},{16,24},{24,0},{1,9},{9,17},{17,25},{25,1},{2,10},{10... | collective-permute-start | bytes 196616 | tf_op jit(solution)/shard_map/ppermute | solution.py:289
  16.3 5.2 %collective-permute-start.4 = (bf16[16,32,128]{2,1,0:T(8,128)(2,1)S(1)}, bf16[16,32,128]{2,1,0:T(8,128)(2,1)S(1)}, u32[]{:S(2)}, u32[]{:S(2)}) collective-permute-start(bf16[16,32,128]{2,1,0:T(8,128)(2,1)S(1)} %collective-permute-done.refs_1_), channel_id=1, source_target_pairs={{0,1},{1,0},{2,3},{3,2},{4,5},{5,4},{6,7},{7,6},{8,9},{9,8},{10,11... | collective-permute-start | bytes 393224 | tf_op jit(solution)/shard_map/ppermute | solution.py:293
  16.3 5.2 %collective-permute-start.5 = (bf16[16,32,128]{2,1,0:T(8,128)(2,1)S(1)}, bf16[16,32,128]{2,1,0:T(8,128)(2,1)S(1)}, u32[]{:S(2)}, u32[]{:S(2)}) collective-permute-start(bf16[16,32,128]{2,1,0:T(8,128)(2,1)S(1)} %collective-permute-done.1.refs_2_), channel_id=1, source_target_pairs={{0,1},{1,0},{2,3},{3,2},{4,5},{5,4},{6,7},{7,6},{8,9},{9,8},{10,11... | collective-permute-start | bytes 393224 | tf_op jit(solution)/shard_map/ppermute | solution.py:293
  18.3 3.2 %collective-permute-start.6 = (bf16[16,32,128]{2,1,0:T(8,128)(2,1)S(1)}, bf16[16,32,128]{2,1,0:T(8,128)(2,1)S(1)}, u32[]{:S(2)}, u32[]{:S(2)}) collective-permute-start(bf16[16,32,128]{2,1,0:T(8,128)(2,1)S(1)} %collective-permute-done.2.refs_3_), channel_id=1, source_target_pairs={{0,1},{1,0},{2,3},{3,2},{4,5},{5,4},{6,7},{7,6},{8,9},{9,8},{10,11... | collective-permute-start | bytes 393224 | tf_op jit(solution)/shard_map/ppermute | solution.py:293
  23.4 5.9 %collective-permute-start.10 = (bf16[16,32,128]{2,1,0:T(8,128)(2,1)S(1)}, bf16[16,32,128]{2,1,0:T(8,128)(2,1)S(1)}, u32[]{:S(2)}, u32[]{:S(2)}) collective-permute-start(bf16[16,32,128]{2,1,0:T(8,128)(2,1)S(1)} %get-tuple-element.41.low_ref), channel_id=1, source_target_pairs={{0,24},{8,0},{16,8},{24,16},{1,25},{9,1},{17,9},{25,17},{2,26},{10... | collective-permute-start | bytes 393224 | tf_op jit(solution)/shard_map/ppermute | solution.py:289
  24.1 7.1 %collective-permute-start.9 = (bf16[16,32,128]{2,1,0:T(8,128)(2,1)S(1)}, bf16[16,32,128]{2,1,0:T(8,128)(2,1)S(1)}, u32[]{:S(2)}, u32[]{:S(2)}) collective-permute-start(bf16[16,32,128]{2,1,0:T(8,128)(2,1)S(1)} %get-tuple-element.42.high_ref), channel_id=1, source_target_pairs={{0,8},{8,16},{16,24},{24,0},{1,9},{9,17},{17,25},{25,1},{2,10},{10... | collective-permute-start | bytes 393224 | tf_op jit(solution)/shard_map/ppermute | solution.py:289
  32.9 3.6 %collective-permute-start.11 = (bf16[4,16,32,128]{3,2,1,0:T(8,128)(2,1)S(1)}, bf16[4,16,32,128]{3,2,1,0:T(8,128)(2,1)S(1)}, u32[]{:S(2)}, u32[]{:S(2)}) collective-permute-start(bf16[4,16,32,128]{3,2,1,0:T(8,128)(2,1)S(1)} %get-tuple-element.51), channel_id=1, source_target_pairs={{0,1},{1,0},{2,3},{3,2},{4,5},{5,4},{6,7},{7,6},{8,9},{9,8},{10,11... | collective-permute-start | bytes 1572872 | tf_op jit(solution)/shard_map/ppermute | solution.py:293
  34.6 8.1 %collective-permute-start.13 = (bf16[448,256]{1,0:T(8,128)(2,1)S(1)}, bf16[448,256]{1,0:T(8,128)(2,1)S(1)}, u32[]{:S(2)}, u32[]{:S(2)}) collective-permute-start(bf16[448,256]{1,0:T(8,128)(2,1)S(1)} %get-tuple-element.54.refs_2_), channel_id=1, source_target_pairs={{0,8},{8,0},{16,24},{24,16},{1,9},{9,1},{17,25},{25,17},{2,10},{10... | collective-permute-start | bytes 688136 | tf_op jit(solution)/shard_map/ppermute | solution.py:293
  36.0 7.7 %collective-permute-start.14 = (bf16[448,256]{1,0:T(8,128)(2,1)S(1)}, bf16[448,256]{1,0:T(8,128)(2,1)S(1)}, u32[]{:S(2)}, u32[]{:S(2)}) collective-permute-start(bf16[448,256]{1,0:T(8,128)(2,1)S(1)} %get-tuple-element.55.refs_4_), channel_id=1, source_target_pairs={{0,16},{8,24},{16,0},{24,8},{1,17},{9,25},{17,1},{25,9},{2,18},{10... | collective-permute-start | bytes 688136 | tf_op jit(solution)/shard_map/ppermute | solution.py:293
  36.6 7.1 %collective-permute-start.12 = (bf16[16,32,128]{2,1,0:T(8,128)(2,1)S(1)}, bf16[16,32,128]{2,1,0:T(8,128)(2,1)S(1)}, u32[]{:S(2)}, u32[]{:S(2)}) collective-permute-start(bf16[16,32,128]{2,1,0:T(8,128)(2,1)S(1)} %get-tuple-element.53), channel_id=1, source_target_pairs={{0,2},{1,3},{2,0},{3,1},{4,6},{5,7},{6,4},{7,5},{8,10},{9,11},{10,... | collective-permute-start | bytes 393224 | tf_op jit(solution)/shard_map/ppermute | solution.py:293
  43.8 10.2 %collective-permute-start.15 = (bf16[448,256]{1,0:T(8,128)(2,1)S(1)}, bf16[448,256]{1,0:T(8,128)(2,1)S(1)}, u32[]{:S(2)}, u32[]{:S(2)}) collective-permute-start(bf16[448,256]{1,0:T(8,128)(2,1)S(1)} %get-tuple-element.56.a_ref), channel_id=1, source_target_pairs={{0,16},{8,24},{16,0},{24,8},{1,17},{9,25},{17,1},{25,9},{2,18},{10... | collective-permute-start | bytes 688136 | tf_op jit(solution)/shard_map/ppermute | solution.py:293
  44.4 9.7 %collective-permute-start.16 = (bf16[448,256]{1,0:T(8,128)(2,1)S(1)}, bf16[448,256]{1,0:T(8,128)(2,1)S(1)}, u32[]{:S(2)}, u32[]{:S(2)}) collective-permute-start(bf16[448,256]{1,0:T(8,128)(2,1)S(1)} %get-tuple-element.57.c_ref), channel_id=1, source_target_pairs={{0,8},{8,0},{16,24},{24,16},{1,9},{9,1},{17,25},{25,17},{2,10},{10... | collective-permute-start | bytes 688136 | tf_op jit(solution)/shard_map/ppermute | solution.py:293
  45.7 6.1 %collective-permute-start.17 = (bf16[16,32,128]{2,1,0:T(8,128)(2,1)S(1)}, bf16[16,32,128]{2,1,0:T(8,128)(2,1)S(1)}, u32[]{:S(2)}, u32[]{:S(2)}) collective-permute-start(bf16[16,32,128]{2,1,0:T(8,128)(2,1)S(1)} %get-tuple-element.59), channel_id=1, source_target_pairs={{0,2},{1,3},{2,0},{3,1},{4,6},{5,7},{6,4},{7,5},{8,10},{9,11},{10,... | collective-permute-start | bytes 393224 | tf_op jit(solution)/shard_map/ppermute | solution.py:293
  46.4 7.7 %collective-permute-start.18 = (bf16[16,32,128]{2,1,0:T(8,128)(2,1)S(1)}, bf16[16,32,128]{2,1,0:T(8,128)(2,1)S(1)}, u32[]{:S(2)}, u32[]{:S(2)}) collective-permute-start(bf16[16,32,128]{2,1,0:T(8,128)(2,1)S(1)} %get-tuple-element.60), channel_id=1, source_target_pairs={{0,4},{1,5},{2,6},{3,7},{4,0},{5,1},{6,2},{7,3},{8,12},{9,13},{10,... | collective-permute-start | bytes 393224 | tf_op jit(solution)/shard_map/ppermute | solution.py:293

commit v3 on v2

--- a/solution.py
+++ b/solution.py
@@ -9,6 +9,7 @@
 from jax.sharding import PartitionSpec as P
 
 LANES = 128
+SUM_FLOPS = 20 * 10**8
 VMEM = pl.BlockSpec(memory_space=pltpu.VMEM)
 SMEM = pl.BlockSpec(memory_space=pltpu.SMEM)
 
@@ -120,18 +121,33 @@
     return jax.ShapeDtypeStruct(shape, dtype)
 
 
+def turn_body(in_ref, out_ref, wide_ref):
+    cells, o, _ = out_ref.shape
+    wide_ref[...] = in_ref[...].astype(jnp.float32).reshape(wide_ref.shape)
+    for k in range(cells):
+        out_ref[k] = wide_ref[pl.ds(k, o, stride=cells), :].astype(out_ref.dtype)
+
+
 def prepare_body(w_ref, bias_ref, flat_ref, back_ref, wide_ref):
     flat = w_ref[...].reshape(flat_ref.shape)
     flat_ref[...] = flat
     back_ref[...] = jnp.transpose(flat)
-    wide_ref[...] = jnp.broadcast_to(bias_ref[...].astype(jnp.float32), wide_ref.shape)
-
-
-def forward_body(n, rows, o, owner_ref, w_ref, *refs):
+    o = wide_ref.shape[0]
+    row = jnp.broadcast_to(bias_ref[...].astype(jnp.float32), (o, o))
+    same = lax.broadcasted_iota(jnp.int32, (o, o), 0) == lax.broadcasted_iota(jnp.int32, (o, o), 1)
+    column = jnp.sum(jnp.where(same, row, 0.0), axis=1, keepdims=True)
+    wide_ref[...] = jnp.broadcast_to(column, wide_ref.shape)
+
+
+def owner(me_ref, b):
+    return jnp.bitwise_xor(me_ref[0], 2 * (b % 4) + b // 4)
+
+
+def forward_body(n, rows, o, me_ref, w_ref, *refs):
     blocks = refs[:8]
-    own_ref, low_ref, high_ref, x_ref, acc = refs[10:]
+    own_ref, low_ref, high_ref, x_ref, acc = refs[8:]
     for b in range(8):
-        place = pl.ds(pl.multiple_of(owner_ref[b] * o, o), o)
+        place = pl.ds(pl.multiple_of(owner(me_ref, b) * o, o), o)
         for k in range(n * rows):
             x_ref[place, k * LANES : (k + 1) * LANES] = blocks[b][k]
     w = w_ref[...]
@@ -175,7 +191,7 @@
     rows,
     o,
     scale,
-    owner_ref,
+    me_ref,
     own_ref,
     low_ref,
     high_ref,
@@ -191,10 +207,11 @@
     s_ref,
     w_ref,
     other_ref,
+    wide_ref,
 ):
     f32, bf16 = jnp.float32, jnp.bfloat16
     for b in range(8):
-        place = pl.ds(pl.multiple_of(owner_ref[b] * o, o), o)
+        place = pl.ds(pl.multiple_of(owner(me_ref, b) * o, o), o)
         w_ref[b * o : (b + 1) * o] = back_ref[place]
     total = jnp.zeros((o, LANES), f32)
     for q in range(n + 2):
@@ -218,7 +235,7 @@
             value = (go.astype(f32) * slope).astype(bf16)
             wide = value.astype(f32)
             if 1 <= q <= n:
-                act_ref[(q - 1) * rows + y] = (pre * s).astype(bf16)
+                wide_ref[pl.ds((q - 1) * rows + y, o, stride=n * rows), :] = pre * s
                 total = total + wide
             turned = [
                 pltpu.roll(wide, LANES - 1, 1).astype(bf16),
@@ -230,6 +247,7 @@
                 if 0 <= p < n:
                     at = (p * rows + (y + j - 1) % rows) * LANES
                     s_ref[k * o : (k + 1) * o, at : at + LANES] = turned[l]
+    act_ref[...] = wide_ref[...].reshape(act_ref.shape).astype(bf16)
     total_ref[...] = jnp.broadcast_to(
         jnp.sum(total, axis=1, keepdims=True) * scale, total_ref.shape
     )
@@ -259,10 +277,11 @@
     second_ref[(27 - taps) * o :] = row.astype(second_ref.dtype)
 
 
-def middle_body(*refs):
-    for p in range(3):
+def pair_body(*refs):
+    count = len(refs) // 3
+    for p in range(count):
         total = refs[2 * p][...].astype(jnp.float32) + refs[2 * p + 1][...].astype(jnp.float32)
-        refs[6 + p][...] = total.astype(refs[6 + p].dtype)
+        refs[2 * count + p][...] = total.astype(refs[2 * count + p].dtype)
 
 
 def split_sum_body(a_ref, b_ref, *outs):
@@ -271,7 +290,16 @@
         out[...] = total.astype(out.dtype)
 
 
-def last_body(taps, a_ref, b_ref, c_ref, d_ref, g_ref, h_ref, k_ref, out_ref, bias_ref, grad_ref):
+def sum_body(a_ref, b_ref, c_ref, out_ref, token_ref, wide_ref):
+    token_ref[...] = jnp.zeros_like(token_ref)
+    cells, o, _ = a_ref.shape
+    for k in range(cells):
+        total = a_ref[k] + b_ref[k].astype(jnp.float32) + c_ref[k].astype(jnp.float32)
+        wide_ref[pl.ds(k, o, stride=cells), :] = total
+    out_ref[...] = wide_ref[...].reshape(out_ref.shape).astype(out_ref.dtype)
+
+
+def last_body(taps, a_ref, b_ref, c_ref, d_ref, _, out_ref, bias_ref):
     o = out_ref.shape[1]
     f32 = jnp.float32
     for k in range(27):
@@ -279,9 +307,9 @@
         cut = slice(at * o, (at + 1) * o)
         out_ref[k] = left[cut].astype(f32) + right[cut].astype(f32)
     cut = slice((27 - taps) * o, (28 - taps) * o)
-    bias_ref[...] = (c_ref[cut].astype(f32) + d_ref[cut].astype(f32))[:, :LANES]
-    total = g_ref[...] + h_ref[...].astype(f32) + k_ref[...].astype(f32)
-    grad_ref[...] = total.astype(grad_ref.dtype)
+    column = (c_ref[cut].astype(f32) + d_ref[cut].astype(f32))[:, :o]
+    same = lax.broadcasted_iota(jnp.int32, (o, o), 0) == lax.broadcasted_iota(jnp.int32, (o, o), 1)
+    bias_ref[...] = jnp.sum(jnp.where(same, column, 0.0), axis=0, keepdims=True)
 
 
 def rotate(value, axis, step):
@@ -300,16 +328,14 @@
     cells = n * rows
     flops = 2 * 27 * o * c_all * cells * depth
     scale = 1.0 / math.sqrt(lax.axis_size("slab") * cells * depth)
-    me = lax.axis_index("chan").astype(jnp.int32)
-    owners = jnp.bitwise_xor(me, jnp.array([0, 2, 4, 6, 1, 3, 5, 7], jnp.int32))
-
-    def by_row(a):
-        return jnp.transpose(a, (1, 2, 0, 3)).reshape(cells, o, depth)
-
-    def by_channel(a):
-        return jnp.transpose(a.reshape(n, rows, o, depth), (2, 0, 1, 3))
-
-    x_own = by_row(x_in)
+    me = lax.axis_index("chan").astype(jnp.int32).reshape(1)
+
+    def by_row(a, name):
+        shapes = [shape_of((cells, o, depth), bf16)]
+        scratch = [pltpu.VMEM((o * cells, depth), f32)]
+        return call(turn_body, shapes, [a], scratch=scratch, name=name)[0]
+
+    x_own = by_row(x_in, "turn_x")
     x_a = swap(x_own, "chan", 2)
     x_b = swap(x_own, "chan", 4)
     x_side = swap(x_own, "chan", 1)
@@ -321,16 +347,18 @@
             shape_of((c_all, 27 * o), bf16),
             shape_of((o, LANES), f32),
         ],
-        [w_taps, bias_vec[:, None]],
+        [w_taps, bias_vec[None, :]],
         name="prepare",
     )
-    go = by_row(grad_out)
-    x_a, w_flat, w_back, bias, go = lax.optimization_barrier((x_a, w_flat, w_back, bias, go))
+    go = by_row(grad_out, "turn_go")
+    go_above = rotate(go[:rows], "slab", -1)
+    go_below = rotate(go[cells - rows :], "slab", 1)
     x_a_side = swap(x_a, "chan", 1)
+    x_b, w_flat, w_back, bias, go, go_above, go_below = lax.optimization_barrier(
+        (x_b, w_flat, w_back, bias, go, go_above, go_below)
+    )
     x_ab = swap(x_b, "chan", 2)
     x_b_side = swap(x_b, "chan", 1)
-    go_above = rotate(go[:rows], "slab", -1)
-    go_below = rotate(go[cells - rows :], "slab", 1)
     x_ab_side = swap(x_ab, "chan", 1)
     blocks = [x_own, x_a, x_b, x_ab, x_side, x_a_side, x_b_side, x_ab_side]
 
@@ -342,8 +370,8 @@
             shape_of((2 * rows, o, depth), bf16),
             shape_of((c_all, cells * depth), bf16),
         ],
-        [owners, w_flat, *blocks, go_below, go_above],
-        [SMEM] + [VMEM] * 9 + [pl.BlockSpec(memory_space=pl.ANY)] * 2,
+        [me, w_flat, *blocks],
+        [SMEM] + [VMEM] * 9,
         [pltpu.VMEM((3, n + 2, rows, o, depth), f32)],
         flops=flops,
         name="forward",
@@ -354,14 +382,15 @@
     act, total, stacked, w_turned, other = call(
         functools.partial(gradient_body, n, rows, o, scale),
         [
-            shape_of((cells, o, depth), bf16),
+            shape_of((o, n, rows, depth), bf16),
             shape_of((o, LANES), f32),
             shape_of((27 * o, cells * depth), bf16),
             shape_of((c_all, 27 * o), bf16),
             shape_of(half, bf16),
         ],
-        [owners, own, low, high, below, above, bias, go, go_below, go_above, w_back],
+        [me, own, low, high, below, above, bias, go, go_below, go_above, w_back],
         [SMEM] + [VMEM] * 10,
+        [pltpu.VMEM((o * cells, depth), f32)],
         flops=flops // 2,
         name="gradient",
     )
@@ -388,31 +417,32 @@
     near = swap(g_a, "chan", 2)
     first_far = swap(first, "slab", 1)
     second_far = swap(second, "slab", 2)
-    g_b, first, second = call(
-        middle_body,
-        [shape_of(a.shape, bf16) for a in (g_b, first, second)],
-        [g_b, far, first, first_far, second, second_far],
-        name="middle",
-    )
+    (g_b,) = call(pair_body, [shape_of(g_b.shape, bf16)], [g_b, far], name="far_sum")
     across = swap(g_b, "chan", 4)
+    first, second = call(
+        pair_body,
+        [shape_of(a.shape, bf16) for a in (first, second)],
+        [first, first_far, second, second_far],
+        name="filter_sum",
+    )
     first_far = swap(first, "slab", 2)
     second_far = swap(second, "slab", 1)
-    weight_grad, bias_grad, grad_in = call(
+    grad_in, token = call(
+        sum_body,
+        [shape_of((o, n, rows, depth), bf16), shape_of((8, LANES), f32)],
+        [g_own, near, across],
+        scratch=[pltpu.VMEM((o * cells, depth), f32)],
+        flops=SUM_FLOPS,
+        name="sum",
+    )
+    weight_grad, bias_grad = call(
         functools.partial(last_body, taps),
-        [
-            shape_of((27, o, c_all), f32),
-            shape_of((o, LANES), f32),
-            shape_of((cells, o, depth), bf16),
-        ],
-        [first, first_far, second, second_far, g_own, near, across],
+        [shape_of((27, o, c_all), f32), shape_of((1, o), f32)],
+        [first, first_far, second, second_far, token],
+        [VMEM] * 4 + [pl.BlockSpec(memory_space=pl.ANY)],
         name="last",
     )
-    return (
-        by_channel(act),
-        by_channel(grad_in),
-        jnp.transpose(weight_grad, (1, 0, 2)),
-        bias_grad[:, 0],
-    )
+    return act, grad_in, jnp.transpose(weight_grad, (1, 0, 2)), bias_grad[0]
 
 
 def solution(mesh):

time: 56.6 us -> 53 us (0.936)
  waiting for transfers between devices: 24 us -> 21.1 us
  local copies, waits for them, and re-layouts: 5.69 us -> 3.48 us
  starting transfers between devices: 18.7 us -> 20.3 us
  other arithmetic: 0.66 us -> 0 us
    unnamed x2 -> x8, local copies, waits for them, and re-layouts: 1.01 us -> 3.47 us
    ppermute x15, waiting for transfers between devices: 15.8 us -> 13.8 us  [swap(): lax.ppermute(value, axis, [(i, i ^ bit) for i in range(lax.axis_size(axis...]
    transpose x2 -> x0, local copies, waits for them, and re-layouts: 1.88 us -> none  [by_row(): return jnp.transpose(a, (1, 2, 0, 3)).reshape(cells, o, depth)]
    reshape x2 -> x0, local copies, waits for them, and re-layouts: 1.42 us -> none  [by_channel(): return jnp.transpose(a.reshape(n, rows, o, depth), (2, 0, 1, 3))]
    ppermute x15, starting transfers between devices: 14.1 us -> 15.2 us  [swap(): lax.ppermute(value, axis, [(i, i ^ bit) for i in range(lax.axis_size(axis...]
    ppermute x4, waiting for transfers between devices: 8.19 us -> 7.29 us  [rotate(): lax.ppermute(value, axis, [(i, (i + step) % count) for i in range(count)])]
    broadcast_in_dim x1 -> x0, local copies, waits for them, and re-layouts: 0.75 us -> none  [on_device(): bias_vec[:, None]]
    xor x1 -> x0, other arithmetic: 0.66 us -> none  [on_device(): owners = jnp.bitwise_xor(me, jnp.array([0, 2, 4, 6, 1, 3, 5, 7], jnp.int32))]
  transfers between devices with their start and end apart: 19 -> 19, of which waited for: 9 -> 8; matrix products, arithmetic and copies ran while one was open for 5% -> 0% of each run, Pallas kernels for 4% -> 6%
where the time goes in v3:
time: 53 us; the launch traced here: 52.8 us
  waiting for transfers between devices  21.1 us (40%)
  starting transfers between devices  20.3 us (38%)
  Pallas kernels  7.21 us (14%)
  local copies, waits for them, and re-layouts  3.48 us (7%)
  between operations  0.74 us (1%)
    ppermute x15, starting transfers between devices, swap(): lax.ppermute(value, axis, [(i, i ^ bit) for i in range(lax.axis_size(axis...  15.2 us
    ppermute x15, waiting for transfers between devices, swap(): lax.ppermute(value, axis, [(i, i ^ bit) for i in range(lax.axis_size(axis...  13.8 us
    ppermute x4, waiting for transfers between devices, rotate(): lax.ppermute(value, axis, [(i, (i + step) % count) for i in range(count)])  7.29 us
    pallas_call x11, Pallas kernels, call(): pl.pallas_call(body, out_shape=out_shape, in_specs=specs or [VMEM] * len(...  7.21 us
    ppermute x4, starting transfers between devices, rotate(): lax.ppermute(value, axis, [(i, (i + step) % count) for i in range(count)])  5.05 us
    unnamed x8, local copies, waits for them, and re-layouts  3.47 us
  transfers between devices with their start and end apart: 19, of which 8 were waited for; matrix products, arithmetic and copies ran while one was open for 0% of the time, Pallas kernels for 6%

profile of v3, /device:TPU:0, one launch (start us, length us, event | category | flops | bytes accessed | tf_op | source)
XLA Modules:
  0.0 52.8 jit_solution(13575308187416697618)
XLA Ops:
  1.6 4.1 %collective-permute-start = (bf16[16,32,128]{2,1,0:T(8,128)(2,1)S(1)}, bf16[16,32,128]{2,1,0:T(8,128)(2,1)S(1)}, u32[]{:S(2)}, u32[]{:S(2)}) collective-permute-start(bf16[16,32,128]{2,1,0:T(8,128)(2,1)S(1)} %turn_x.1.refs_0_), channel_id=1, source_target_pairs={{0,4},{1,5},{2,6},{3,7},{4,0},{5,1},{6,2},{7,3},{8,12},{9,13},{10,... | collective-permute-start | bytes 393224 | tf_op jit(solution)/shard_map/ppermute | solution.py:321
  5.7 0.9 %copy-done.2 = bf16[32,2,8,128]{3,2,1,0:T(8,128)(2,1)S(1)} copy-done((bf16[32,2,8,128]{3,2,1,0:T(8,128)(2,1)S(1)}, bf16[32,2,8,128]{3,2,1,0:T(8,128)(2,1)}, u32[]{:S(2)}) %copy-start.2) | copy-done | bytes 131096
  6.8 1.5 %collective-permute-start.2 = (bf16[8,32,128]{2,1,0:T(8,128)(2,1)S(1)}, bf16[8,32,128]{2,1,0:T(8,128)(2,1)S(1)}, u32[]{:S(2)}, u32[]{:S(2)}) collective-permute-start(bf16[8,32,128]{2,1,0:T(8,128)(2,1)S(1)} %get-tuple-element.68), channel_id=1, source_target_pairs={{0,8},{8,16},{16,24},{24,0},{1,9},{9,17},{17,25},{25,1},{2,10},{10... | collective-permute-start | bytes 196616 | tf_op jit(solution)/shard_map/ppermute | solution.py:317
  8.3 1.4 %collective-permute-start.1 = (bf16[8,32,128]{2,1,0:T(8,128)(2,1)S(1)}, bf16[8,32,128]{2,1,0:T(8,128)(2,1)S(1)}, u32[]{:S(2)}, u32[]{:S(2)}) collective-permute-start(bf16[8,32,128]{2,1,0:T(8,128)(2,1)S(1)} %get-tuple-element.69), channel_id=1, source_target_pairs={{0,24},{8,0},{16,8},{24,16},{1,25},{9,1},{17,9},{25,17},{2,26},{10... | collective-permute-start | bytes 196616 | tf_op jit(solution)/shard_map/ppermute | solution.py:317
  9.7 1.6 %collective-permute-start.3 = (bf16[16,32,128]{2,1,0:T(8,128)(2,1)S(1)}, bf16[16,32,128]{2,1,0:T(8,128)(2,1)S(1)}, u32[]{:S(2)}, u32[]{:S(2)}) collective-permute-start(bf16[16,32,128]{2,1,0:T(8,128)(2,1)S(1)} %turn_x.1.refs_0_), channel_id=1, source_target_pairs={{0,2},{1,3},{2,0},{3,1},{4,6},{5,7},{6,4},{7,5},{8,10},{9,11},{10,... | collective-permute-start | bytes 393224 | tf_op jit(solution)/shard_map/ppermute | solution.py:321
  11.3 1.0 %copy-done = bf16[32,27,256]{2,0,1:T(8,128)(2,1)S(1)} copy-done((bf16[32,27,256]{2,0,1:T(8,128)(2,1)S(1)}, bf16[32,27,256]{2,0,1:T(8,128)(2,1)}, u32[]{:S(2)}) %copy-start) | copy-done | bytes 442392
  13.2 1.1 %collective-permute-start.4 = (bf16[16,32,128]{2,1,0:T(8,128)(2,1)S(1)}, bf16[16,32,128]{2,1,0:T(8,128)(2,1)S(1)}, u32[]{:S(2)}, u32[]{:S(2)}) collective-permute-start(bf16[16,32,128]{2,1,0:T(8,128)(2,1)S(1)} %collective-permute-done.refs_2_), channel_id=1, source_target_pairs={{0,2},{1,3},{2,0},{3,1},{4,6},{5,7},{6,4},{7,5},{8,10},{9,11},{10,... | collective-permute-start | bytes 393224 | tf_op jit(solution)/shard_map/ppermute | solution.py:321
  15.1 3.2 %collective-permute-done.4.refs_3_ = bf16[16,32,128]{2,1,0:T(8,128)(2,1)S(1)} collective-permute-done((bf16[16,32,128]{2,1,0:T(8,128)(2,1)S(1)}, bf16[16,32,128]{2,1,0:T(8,128)(2,1)S(1)}, u32[]{:S(2)}, u32[]{:S(2)}) %collective-permute-start.4) | collective-permute-done | bytes 131104 | tf_op jit(solution)/shard_map/ppermute | solution.py:321
  18.3 1.3 %collective-permute-done.8.refs_7_ = bf16[16,32,128]{2,1,0:T(8,128)(2,1)S(1)} collective-permute-done((bf16[16,32,128]{2,1,0:T(8,128)(2,1)S(1)}, bf16[16,32,128]{2,1,0:T(8,128)(2,1)S(1)}, u32[]{:S(2)}, u32[]{:S(2)}) %collective-permute-start.8) | collective-permute-done | bytes 131104 | tf_op jit(solution)/shard_map/ppermute | solution.py:321
  19.6 1.4 %forward.1 = (f32[16,32,128]{2,1,0:T(8,128)S(1)}, bf16[16,32,128]{2,1,0:T(8,128)(2,1)S(1)}, bf16[16,32,128]{2,1,0:T(8,128)(2,1)S(1)}, bf16[256,2048]{1,0:T(8,128)(2,1)S(1)}) custom-call(s32[1]{0:T(128)} %bitcast.me_ref, bf16[864,256]{1,0:T(8,128)(2,1)S(1)} %get-tuple-element.39.w_ref, bf16[16,32,128]{2,1,0:T(8,128)(2,1)S(1)} %turn_x.1.refs_0_, ...), custom_call_target="tpu_custom_call" | custom-call | flops 905969664 | bytes 3063812 | tf_op jit(solution)/shard_map/forward/pallas_call | solution.py:106
  21.0 1.9 %collective-permute-start.10 = (bf16[16,32,128]{2,1,0:T(8,128)(2,1)S(1)}, bf16[16,32,128]{2,1,0:T(8,128)(2,1)S(1)}, u32[]{:S(2)}, u32[]{:S(2)}) collective-permute-start(bf16[16,32,128]{2,1,0:T(8,128)(2,1)S(1)} %get-tuple-element.42.low_ref), channel_id=1, source_target_pairs={{0,24},{8,0},{16,8},{24,16},{1,25},{9,1},{17,9},{25,17},{2,26},{10... | collective-permute-start | bytes 393224 | tf_op jit(solution)/shard_map/ppermute | solution.py:317
  23.0 4.0 %collective-permute-done.10.above_ref = bf16[16,32,128]{2,1,0:T(8,128)(2,1)S(1)} collective-permute-done((bf16[16,32,128]{2,1,0:T(8,128)(2,1)S(1)}, bf16[16,32,128]{2,1,0:T(8,128)(2,1)S(1)}, u32[]{:S(2)}, u32[]{:S(2)}) %collective-permute-start.10) | collective-permute-done | bytes 131104 | tf_op jit(solution)/shard_map/ppermute | solution.py:317
  27.0 3.3 %collective-permute-done.9.below_ref = bf16[16,32,128]{2,1,0:T(8,128)(2,1)S(1)} collective-permute-done((bf16[16,32,128]{2,1,0:T(8,128)(2,1)S(1)}, bf16[16,32,128]{2,1,0:T(8,128)(2,1)S(1)}, u32[]{:S(2)}, u32[]{:S(2)}) %collective-permute-start.9) | collective-permute-done | bytes 131104 | tf_op jit(solution)/shard_map/ppermute | solution.py:317
  30.3 1.7 %gradient.1 = (bf16[32,2,8,128]{3,2,1,0:T(8,128)(2,1)}, f32[32,128]{1,0:T(8,128)S(1)}, bf16[864,2048]{1,0:T(8,128)(2,1)S(1)}, bf16[256,864]{1,0:T(8,128)(2,1)S(1)}, bf16[4,16,32,128]{3,2,1,0:T(8,128)(2,1)S(1)}) custom-call(s32[1]{0:T(128)} %bitcast.me_ref, f32[16,32,128]{2,1,0:T(8,128)S(1)} %get-tuple-element.41.own_ref, ...), custom_call_target="tpu_custom_call" | custom-call | flops 452984832 | bytes 6160388 | tf_op jit(solution)/shard_map/gradient/pallas_call | solution.py:106
  32.0 1.7 %filter_grad.1 = (bf16[4,16,32,128]{3,2,1,0:T(8,128)(2,1)S(1)}, bf16[448,256]{1,0:T(8,128)(2,1)S(1)}, bf16[448,256]{1,0:T(8,128)(2,1)S(1)}) custom-call(bf16[864,2048]{1,0:T(8,128)(2,1)S(1)} %get-tuple-element.50.s_ref, bf16[256,2048]{1,0:T(8,128)(2,1)S(1)} %get-tuple-element.51.x_ref, bf16[256,864]{1,0:T(8,128)(2,1)S(1)} %get-tuple-element.52.w_ref, ...), custom_call_target="tpu_custom_call" | custom-call | flops 1358954496 | bytes 6029312 | tf_op jit(solution)/shard_map/filter_grad/pallas_call | solution.py:106
  33.7 1.0 %collective-permute-start.15 = (bf16[448,256]{1,0:T(8,128)(2,1)S(1)}, bf16[448,256]{1,0:T(8,128)(2,1)S(1)}, u32[]{:S(2)}, u32[]{:S(2)}) collective-permute-start(bf16[448,256]{1,0:T(8,128)(2,1)S(1)} %get-tuple-element.61.refs_0_), channel_id=1, source_target_pairs={{0,8},{8,0},{16,24},{24,16},{1,9},{9,1},{17,25},{25,17},{2,10},{10... | collective-permute-start | bytes 688136 | tf_op jit(solution)/shard_map/ppermute | solution.py:321
  34.7 1.2 %collective-permute-start.16 = (bf16[448,256]{1,0:T(8,128)(2,1)S(1)}, bf16[448,256]{1,0:T(8,128)(2,1)S(1)}, u32[]{:S(2)}, u32[]{:S(2)}) collective-permute-start(bf16[448,256]{1,0:T(8,128)(2,1)S(1)} %get-tuple-element.62.refs_2_), channel_id=1, source_target_pairs={{0,16},{8,24},{16,0},{24,8},{1,17},{9,25},{17,1},{25,9},{2,18},{10... | collective-permute-start | bytes 688136 | tf_op jit(solution)/shard_map/ppermute | solution.py:321
  36.1 1.6 %collective-permute-start.13 = (bf16[16,32,128]{2,1,0:T(8,128)(2,1)S(1)}, bf16[16,32,128]{2,1,0:T(8,128)(2,1)S(1)}, u32[]{:S(2)}, u32[]{:S(2)}) collective-permute-start(bf16[16,32,128]{2,1,0:T(8,128)(2,1)S(1)} %get-tuple-element.59), channel_id=1, source_target_pairs={{0,2},{1,3},{2,0},{3,1},{4,6},{5,7},{6,4},{7,5},{8,10},{9,11},{10,... | collective-permute-start | bytes 393224 | tf_op jit(solution)/shard_map/ppermute | solution.py:321
  38.2 4.3 %collective-permute-done.13.refs_1_ = bf16[16,32,128]{2,1,0:T(8,128)(2,1)S(1)} collective-permute-done((bf16[16,32,128]{2,1,0:T(8,128)(2,1)S(1)}, bf16[16,32,128]{2,1,0:T(8,128)(2,1)S(1)}, u32[]{:S(2)}, u32[]{:S(2)}) %collective-permute-start.13) | collective-permute-done | bytes 131104 | tf_op jit(solution)/shard_map/ppermute | solution.py:321
  42.6 1.5 %collective-permute-start.14 = (bf16[16,32,128]{2,1,0:T(8,128)(2,1)S(1)}, bf16[16,32,128]{2,1,0:T(8,128)(2,1)S(1)}, u32[]{:S(2)}, u32[]{:S(2)}) collective-permute-start(bf16[16,32,128]{2,1,0:T(8,128)(2,1)S(1)} %far_sum.1), channel_id=1, source_target_pairs={{0,4},{1,5},{2,6},{3,7},{4,0},{5,1},{6,2},{7,3},{8,12},{9,13},{10,... | collective-permute-start | bytes 393224 | tf_op jit(solution)/shard_map/ppermute | solution.py:321
  44.2 1.6 %collective-permute-start.17 = (bf16[448,256]{1,0:T(8,128)(2,1)S(1)}, bf16[448,256]{1,0:T(8,128)(2,1)S(1)}, u32[]{:S(2)}, u32[]{:S(2)}) collective-permute-start(bf16[448,256]{1,0:T(8,128)(2,1)S(1)} %get-tuple-element.63.a_ref), channel_id=1, source_target_pairs={{0,16},{8,24},{16,0},{24,8},{1,17},{9,25},{17,1},{25,9},{2,18},{10... | collective-permute-start | bytes 688136 | tf_op jit(solution)/shard_map/ppermute | solution.py:321
  46.3 3.6 %collective-permute-done.14.c_ref = bf16[16,32,128]{2,1,0:T(8,128)(2,1)S(1)} collective-permute-done((bf16[16,32,128]{2,1,0:T(8,128)(2,1)S(1)}, bf16[16,32,128]{2,1,0:T(8,128)(2,1)S(1)}, u32[]{:S(2)}, u32[]{:S(2)}) %collective-permute-start.14) | collective-permute-done | bytes 131104 | tf_op jit(solution)/shard_map/ppermute | solution.py:321
  50.7 1.1 %collective-permute-done.18.d_ref = bf16[448,256]{1,0:T(8,128)(2,1)S(1)} collective-permute-done((bf16[448,256]{1,0:T(8,128)(2,1)S(1)}, bf16[448,256]{1,0:T(8,128)(2,1)S(1)}, u32[]{:S(2)}, u32[]{:S(2)}) %collective-permute-start.18) | collective-permute-done | bytes 229408 | tf_op jit(solution)/shard_map/ppermute | solution.py:321
  51.8 1.0 %last.1 = (f32[27,32,256]{2,1,0:T(8,128)}, f32[1,32]{1,0:T(1,128)}) custom-call(bf16[448,256]{1,0:T(8,128)(2,1)S(1)} %get-tuple-element.63.a_ref, bf16[448,256]{1,0:T(8,128)(2,1)S(1)} %collective-permute-done.17.b_ref, bf16[448,256]{1,0:T(8,128)(2,1)S(1)} %get-tuple-element.64.c_ref, bf16[448,256]{1,0:T(8,128)(2,1)S(1)} %collective-permute-done.18.d_ref, ...), custom_call_target="tpu_custom_call" | custom-call | bytes 1806464 | tf_op jit(solution)/shard_map/last/pallas_call | solution.py:106
  (34 shorter events, 4.9 us)
Async XLA Ops:
  0.6 0.9 %copy-start.1 = (bf16[32,2,8,128]{3,2,1,0:T(8,128)(2,1)S(1)}, bf16[32,2,8,128]{3,2,1,0:T(8,128)(2,1)}, u32[]{:S(2)}) copy-start(bf16[32,2,8,128]{3,2,1,0:T(8,128)(2,1)} %in_ref.2) | copy-start | bytes 393220
  1.6 11.6 %collective-permute-start = (bf16[16,32,128]{2,1,0:T(8,128)(2,1)S(1)}, bf16[16,32,128]{2,1,0:T(8,128)(2,1)S(1)}, u32[]{:S(2)}, u32[]{:S(2)}) collective-permute-start(bf16[16,32,128]{2,1,0:T(8,128)(2,1)S(1)} %turn_x.1.refs_0_), channel_id=1, source_target_pairs={{0,4},{1,5},{2,6},{3,7},{4,0},{5,1},{6,2},{7,3},{8,12},{9,13},{10,... | collective-permute-start | bytes 393224 | tf_op jit(solution)/shard_map/ppermute | solution.py:321
  5.7 0.9 %copy-start.2 = (bf16[32,2,8,128]{3,2,1,0:T(8,128)(2,1)S(1)}, bf16[32,2,8,128]{3,2,1,0:T(8,128)(2,1)}, u32[]{:S(2)}) copy-start(bf16[32,2,8,128]{3,2,1,0:T(8,128)(2,1)} %in_ref.3) | copy-start | bytes 393220
  6.8 6.4 %collective-permute-start.2 = (bf16[8,32,128]{2,1,0:T(8,128)(2,1)S(1)}, bf16[8,32,128]{2,1,0:T(8,128)(2,1)S(1)}, u32[]{:S(2)}, u32[]{:S(2)}) collective-permute-start(bf16[8,32,128]{2,1,0:T(8,128)(2,1)S(1)} %get-tuple-element.68), channel_id=1, source_target_pairs={{0,8},{8,16},{16,24},{24,0},{1,9},{9,17},{17,25},{25,1},{2,10},{10... | collective-permute-start | bytes 196616 | tf_op jit(solution)/shard_map/ppermute | solution.py:317
  8.3 4.9 %collective-permute-start.1 = (bf16[8,32,128]{2,1,0:T(8,128)(2,1)S(1)}, bf16[8,32,128]{2,1,0:T(8,128)(2,1)S(1)}, u32[]{:S(2)}, u32[]{:S(2)}) collective-permute-start(bf16[8,32,128]{2,1,0:T(8,128)(2,1)S(1)} %get-tuple-element.69), channel_id=1, source_target_pairs={{0,24},{8,0},{16,8},{24,16},{1,25},{9,1},{17,9},{25,17},{2,26},{10... | collective-permute-start | bytes 196616 | tf_op jit(solution)/shard_map/ppermute | solution.py:317
  9.7 5.3 %collective-permute-start.3 = (bf16[16,32,128]{2,1,0:T(8,128)(2,1)S(1)}, bf16[16,32,128]{2,1,0:T(8,128)(2,1)S(1)}, u32[]{:S(2)}, u32[]{:S(2)}) collective-permute-start(bf16[16,32,128]{2,1,0:T(8,128)(2,1)S(1)} %turn_x.1.refs_0_), channel_id=1, source_target_pairs={{0,2},{1,3},{2,0},{3,1},{4,6},{5,7},{6,4},{7,5},{8,10},{9,11},{10,... | collective-permute-start | bytes 393224 | tf_op jit(solution)/shard_map/ppermute | solution.py:321
  11.3 1.0 %copy-start = (bf16[32,27,256]{2,0,1:T(8,128)(2,1)S(1)}, bf16[32,27,256]{2,0,1:T(8,128)(2,1)}, u32[]{:S(2)}) copy-start(bf16[32,27,256]{2,0,1:T(8,128)(2,1)} %param.5) | copy-start | bytes 1327108
  12.3 0.7 %copy-start.3 = (bf16[32]{0:T(256)(128)(2,1)S(1)}, bf16[32]{0:T(256)(128)(2,1)}, u32[]{:S(2)}) copy-start(bf16[32]{0:T(256)(128)(2,1)} %param.6) | copy-start | bytes 196
  13.2 5.0 %collective-permute-start.4 = (bf16[16,32,128]{2,1,0:T(8,128)(2,1)S(1)}, bf16[16,32,128]{2,1,0:T(8,128)(2,1)S(1)}, u32[]{:S(2)}, u32[]{:S(2)}) collective-permute-start(bf16[16,32,128]{2,1,0:T(8,128)(2,1)S(1)} %collective-permute-done.refs_2_), channel_id=1, source_target_pairs={{0,2},{1,3},{2,0},{3,1},{4,6},{5,7},{6,4},{7,5},{8,10},{9,11},{10,... | collective-permute-start | bytes 393224 | tf_op jit(solution)/shard_map/ppermute | solution.py:321
  14.3 3.9 %collective-permute-start.5 = (bf16[16,32,128]{2,1,0:T(8,128)(2,1)S(1)}, bf16[16,32,128]{2,1,0:T(8,128)(2,1)S(1)}, u32[]{:S(2)}, u32[]{:S(2)}) collective-permute-start(bf16[16,32,128]{2,1,0:T(8,128)(2,1)S(1)} %turn_x.1.refs_0_), channel_id=1, source_target_pairs={{0,1},{1,0},{2,3},{3,2},{4,5},{5,4},{6,7},{7,6},{8,9},{9,8},{10,11... | collective-permute-start | bytes 393224 | tf_op jit(solution)/shard_map/ppermute | solution.py:321
  14.3 4.0 %collective-permute-start.7 = (bf16[16,32,128]{2,1,0:T(8,128)(2,1)S(1)}, bf16[16,32,128]{2,1,0:T(8,128)(2,1)S(1)}, u32[]{:S(2)}, u32[]{:S(2)}) collective-permute-start(bf16[16,32,128]{2,1,0:T(8,128)(2,1)S(1)} %collective-permute-done.refs_2_), channel_id=1, source_target_pairs={{0,1},{1,0},{2,3},{3,2},{4,5},{5,4},{6,7},{7,6},{8,9},{9,8},{10,11... | collective-permute-start | bytes 393224 | tf_op jit(solution)/shard_map/ppermute | solution.py:321
  15.1 3.2 %collective-permute-start.6 = (bf16[16,32,128]{2,1,0:T(8,128)(2,1)S(1)}, bf16[16,32,128]{2,1,0:T(8,128)(2,1)S(1)}, u32[]{:S(2)}, u32[]{:S(2)}) collective-permute-start(bf16[16,32,128]{2,1,0:T(8,128)(2,1)S(1)} %collective-permute-done.3.refs_1_), channel_id=1, source_target_pairs={{0,1},{1,0},{2,3},{3,2},{4,5},{5,4},{6,7},{7,6},{8,9},{9,8},{10,11... | collective-permute-start | bytes 393224 | tf_op jit(solution)/shard_map/ppermute | solution.py:321
  18.3 1.3 %collective-permute-start.8 = (bf16[16,32,128]{2,1,0:T(8,128)(2,1)S(1)}, bf16[16,32,128]{2,1,0:T(8,128)(2,1)S(1)}, u32[]{:S(2)}, u32[]{:S(2)}) collective-permute-start(bf16[16,32,128]{2,1,0:T(8,128)(2,1)S(1)} %collective-permute-done.4.refs_3_), channel_id=1, source_target_pairs={{0,1},{1,0},{2,3},{3,2},{4,5},{5,4},{6,7},{7,6},{8,9},{9,8},{10,11... | collective-permute-start | bytes 393224 | tf_op jit(solution)/shard_map/ppermute | solution.py:321
  21.0 6.0 %collective-permute-start.10 = (bf16[16,32,128]{2,1,0:T(8,128)(2,1)S(1)}, bf16[16,32,128]{2,1,0:T(8,128)(2,1)S(1)}, u32[]{:S(2)}, u32[]{:S(2)}) collective-permute-start(bf16[16,32,128]{2,1,0:T(8,128)(2,1)S(1)} %get-tuple-element.42.low_ref), channel_id=1, source_target_pairs={{0,24},{8,0},{16,8},{24,16},{1,25},{9,1},{17,9},{25,17},{2,26},{10... | collective-permute-start | bytes 393224 | tf_op jit(solution)/shard_map/ppermute | solution.py:317
  22.9 7.4 %collective-permute-start.9 = (bf16[16,32,128]{2,1,0:T(8,128)(2,1)S(1)}, bf16[16,32,128]{2,1,0:T(8,128)(2,1)S(1)}, u32[]{:S(2)}, u32[]{:S(2)}) collective-permute-start(bf16[16,32,128]{2,1,0:T(8,128)(2,1)S(1)} %get-tuple-element.43.high_ref), channel_id=1, source_target_pairs={{0,8},{8,16},{16,24},{24,0},{1,9},{9,17},{17,25},{25,1},{2,10},{10... | collective-permute-start | bytes 393224 | tf_op jit(solution)/shard_map/ppermute | solution.py:317
  32.0 4.0 %collective-permute-start.11 = (bf16[4,16,32,128]{3,2,1,0:T(8,128)(2,1)S(1)}, bf16[4,16,32,128]{3,2,1,0:T(8,128)(2,1)S(1)}, u32[]{:S(2)}, u32[]{:S(2)}) collective-permute-start(bf16[4,16,32,128]{3,2,1,0:T(8,128)(2,1)S(1)} %get-tuple-element.55), channel_id=1, source_target_pairs={{0,1},{1,0},{2,3},{3,2},{4,5},{5,4},{6,7},{7,6},{8,9},{9,8},{10,11... | collective-permute-start | bytes 1572872 | tf_op jit(solution)/shard_map/ppermute | solution.py:321
  33.7 10.3 %collective-permute-start.15 = (bf16[448,256]{1,0:T(8,128)(2,1)S(1)}, bf16[448,256]{1,0:T(8,128)(2,1)S(1)}, u32[]{:S(2)}, u32[]{:S(2)}) collective-permute-start(bf16[448,256]{1,0:T(8,128)(2,1)S(1)} %get-tuple-element.61.refs_0_), channel_id=1, source_target_pairs={{0,8},{8,0},{16,24},{24,16},{1,9},{9,1},{17,25},{25,17},{2,10},{10... | collective-permute-start | bytes 688136 | tf_op jit(solution)/shard_map/ppermute | solution.py:321
  34.7 9.3 %collective-permute-start.16 = (bf16[448,256]{1,0:T(8,128)(2,1)S(1)}, bf16[448,256]{1,0:T(8,128)(2,1)S(1)}, u32[]{:S(2)}, u32[]{:S(2)}) collective-permute-start(bf16[448,256]{1,0:T(8,128)(2,1)S(1)} %get-tuple-element.62.refs_2_), channel_id=1, source_target_pairs={{0,16},{8,24},{16,0},{24,8},{1,17},{9,25},{17,1},{25,9},{2,18},{10... | collective-permute-start | bytes 688136 | tf_op jit(solution)/shard_map/ppermute | solution.py:321
  36.1 6.4 %collective-permute-start.13 = (bf16[16,32,128]{2,1,0:T(8,128)(2,1)S(1)}, bf16[16,32,128]{2,1,0:T(8,128)(2,1)S(1)}, u32[]{:S(2)}, u32[]{:S(2)}) collective-permute-start(bf16[16,32,128]{2,1,0:T(8,128)(2,1)S(1)} %get-tuple-element.59), channel_id=1, source_target_pairs={{0,2},{1,3},{2,0},{3,1},{4,6},{5,7},{6,4},{7,5},{8,10},{9,11},{10,... | collective-permute-start | bytes 393224 | tf_op jit(solution)/shard_map/ppermute | solution.py:321
  37.8 8.6 %collective-permute-start.12 = (bf16[16,32,128]{2,1,0:T(8,128)(2,1)S(1)}, bf16[16,32,128]{2,1,0:T(8,128)(2,1)S(1)}, u32[]{:S(2)}, u32[]{:S(2)}) collective-permute-start(bf16[16,32,128]{2,1,0:T(8,128)(2,1)S(1)} %get-tuple-element.57), channel_id=1, source_target_pairs={{0,2},{1,3},{2,0},{3,1},{4,6},{5,7},{6,4},{7,5},{8,10},{9,11},{10,... | collective-permute-start | bytes 393224 | tf_op jit(solution)/shard_map/ppermute | solution.py:321
  42.6 7.3 %collective-permute-start.14 = (bf16[16,32,128]{2,1,0:T(8,128)(2,1)S(1)}, bf16[16,32,128]{2,1,0:T(8,128)(2,1)S(1)}, u32[]{:S(2)}, u32[]{:S(2)}) collective-permute-start(bf16[16,32,128]{2,1,0:T(8,128)(2,1)S(1)} %far_sum.1), channel_id=1, source_target_pairs={{0,4},{1,5},{2,6},{3,7},{4,0},{5,1},{6,2},{7,3},{8,12},{9,13},{10,... | collective-permute-start | bytes 393224 | tf_op jit(solution)/shard_map/ppermute | solution.py:321
  44.2 6.5 %collective-permute-start.17 = (bf16[448,256]{1,0:T(8,128)(2,1)S(1)}, bf16[448,256]{1,0:T(8,128)(2,1)S(1)}, u32[]{:S(2)}, u32[]{:S(2)}) collective-permute-start(bf16[448,256]{1,0:T(8,128)(2,1)S(1)} %get-tuple-element.63.a_ref), channel_id=1, source_target_pairs={{0,16},{8,24},{16,0},{24,8},{1,17},{9,25},{17,1},{25,9},{2,18},{10... | collective-permute-start | bytes 688136 | tf_op jit(solution)/shard_map/ppermute | solution.py:321
  45.8 6.0 %collective-permute-start.18 = (bf16[448,256]{1,0:T(8,128)(2,1)S(1)}, bf16[448,256]{1,0:T(8,128)(2,1)S(1)}, u32[]{:S(2)}, u32[]{:S(2)}) collective-permute-start(bf16[448,256]{1,0:T(8,128)(2,1)S(1)} %get-tuple-element.64.c_ref), channel_id=1, source_target_pairs={{0,8},{8,0},{16,24},{24,16},{1,9},{9,1},{17,25},{25,17},{2,10},{10... | collective-permute-start | bytes 688136 | tf_op jit(solution)/shard_map/ppermute | solution.py:321

commit v4 on v3

--- a/solution.py
+++ b/solution.py
@@ -10,7 +10,10 @@
 
 LANES = 128
 SUM_FLOPS = 20 * 10**8
+ASSEMBLE_FLOPS = 0
 VMEM = pl.BlockSpec(memory_space=pltpu.VMEM)
+ANY = pl.BlockSpec(memory_space=pl.ANY)
+HBM = pl.BlockSpec(memory_space=pltpu.HBM)
 SMEM = pl.BlockSpec(memory_space=pltpu.SMEM)
 
 
@@ -100,7 +103,7 @@
     return (activation, grad_in.astype(jnp.bfloat16), weight_grad, bias_grad)
 
 
-def call(body, out_shape, operands, specs=None, scratch=(), flops=0, name=None):
+def call(body, out_shape, operands, specs=None, scratch=(), flops=0, name=None, aliases=None):
     read = sum(math.prod(a.shape) * a.dtype.itemsize for a in operands)
     written = sum(math.prod(a.shape) * a.dtype.itemsize for a in out_shape)
     return pl.pallas_call(
@@ -109,6 +112,7 @@
         in_specs=specs or [VMEM] * len(operands),
         out_specs=[VMEM] * len(out_shape),
         scratch_shapes=list(scratch),
+        input_output_aliases=aliases or {},
         compiler_params=pltpu.CompilerParams(vmem_limit_bytes=24 * 2**20),
         cost_estimate=pl.CostEstimate(
             flops=flops, bytes_accessed=read + written, transcendentals=0
@@ -121,35 +125,77 @@
     return jax.ShapeDtypeStruct(shape, dtype)
 
 
-def turn_body(in_ref, out_ref, wide_ref):
-    cells, o, _ = out_ref.shape
-    wide_ref[...] = in_ref[...].astype(jnp.float32).reshape(wide_ref.shape)
-    for k in range(cells):
-        out_ref[k] = wide_ref[pl.ds(k, o, stride=cells), :].astype(out_ref.dtype)
-
-
-def prepare_body(w_ref, bias_ref, flat_ref, back_ref, wide_ref):
-    flat = w_ref[...].reshape(flat_ref.shape)
+def turned(value, wide_ref):
+    o = value.shape[0]
+    cells = wide_ref.shape[0] // o
+    wide_ref[...] = value.astype(jnp.float32).reshape(wide_ref.shape)
+    return [
+        wide_ref[pl.ds(k, o, stride=cells), :].astype(value.dtype) for k in range(cells)
+    ]
+
+
+def prepare_body(
+    x_hbm,
+    go_hbm,
+    w_hbm,
+    bias_hbm,
+    x_ref,
+    go_ref,
+    flat_ref,
+    back_ref,
+    bias_ref,
+    go_in,
+    w_in,
+    bias_in,
+    wide_ref,
+    sems,
+):
+    copies = [
+        pltpu.make_async_copy(source, target, sems.at[at])
+        for at, (source, target) in enumerate(
+            [(go_hbm, go_in), (w_hbm, w_in), (bias_hbm, bias_in), (x_hbm, x_ref)]
+        )
+    ]
+    for copy in copies:
+        copy.start()
+    copies[0].wait()
+    for k, value in enumerate(turned(go_in[...], wide_ref)):
+        go_ref[k] = value
+    copies[1].wait()
+    copies[2].wait()
+    copies[3].wait()
+    flat = w_in[...].reshape(flat_ref.shape)
     flat_ref[...] = flat
     back_ref[...] = jnp.transpose(flat)
-    o = wide_ref.shape[0]
-    row = jnp.broadcast_to(bias_ref[...].astype(jnp.float32), (o, o))
+    o = bias_ref.shape[0]
+    row = jnp.broadcast_to(bias_in[...].astype(jnp.float32), (o, o))
     same = lax.broadcasted_iota(jnp.int32, (o, o), 0) == lax.broadcasted_iota(jnp.int32, (o, o), 1)
     column = jnp.sum(jnp.where(same, row, 0.0), axis=1, keepdims=True)
-    wide_ref[...] = jnp.broadcast_to(column, wide_ref.shape)
+    bias_ref[...] = jnp.broadcast_to(column, bias_ref.shape)
+
+
+def place_block(me_ref, b, block_ref, x_ref, wide_ref):
+    o = block_ref.shape[0]
+    place = pl.ds(pl.multiple_of(owner(me_ref, b) * o, o), o)
+    for k, value in enumerate(turned(block_ref[...], wide_ref)):
+        x_ref[place, k * LANES : (k + 1) * LANES] = value
+
+
+def assemble_body(places, me_ref, *refs):
+    blocks, (x_ref, wide_ref) = refs[: len(places)], refs[-2:]
+    for b, block in zip(places, blocks):
+        place_block(me_ref, b, block, x_ref, wide_ref)
 
 
 def owner(me_ref, b):
     return jnp.bitwise_xor(me_ref[0], 2 * (b % 4) + b // 4)
 
 
-def forward_body(n, rows, o, me_ref, w_ref, *refs):
-    blocks = refs[:8]
-    own_ref, low_ref, high_ref, x_ref, acc = refs[8:]
-    for b in range(8):
-        place = pl.ds(pl.multiple_of(owner(me_ref, b) * o, o), o)
-        for k in range(n * rows):
-            x_ref[place, k * LANES : (k + 1) * LANES] = blocks[b][k]
+def forward_body(n, rows, o, places, me_ref, w_ref, *refs):
+    blocks = refs[: len(places)]
+    own_ref, low_ref, high_ref, x_ref, acc, wide_ref = refs[len(places) + 1 :]
+    for b, block in zip(places, blocks):
+        place_block(me_ref, b, block, x_ref, wide_ref)
     w = w_ref[...]
     seen = set()
     for p in range(n):
@@ -207,21 +253,25 @@
     s_ref,
     w_ref,
     other_ref,
+    far_ref,
     wide_ref,
+    rim_ref,
 ):
     f32, bf16 = jnp.float32, jnp.bfloat16
     for b in range(8):
         place = pl.ds(pl.multiple_of(owner(me_ref, b) * o, o), o)
         w_ref[b * o : (b + 1) * o] = back_ref[place]
     total = jnp.zeros((o, LANES), f32)
+    go_below = turned(go_below_ref[:, n - 1 :], rim_ref)
+    go_above = turned(go_above_ref[:, :1], rim_ref)
     for q in range(n + 2):
         for y in range(rows):
             if q == 0:
                 pre = below_ref[rows + y].astype(f32) + low_ref[y].astype(f32)
-                go = go_below_ref[y]
+                go = go_below[y]
             elif q == n + 1:
                 pre = above_ref[rows + y].astype(f32) + high_ref[y].astype(f32)
-                go = go_above_ref[y]
+                go = go_above[y]
             else:
                 pre = own_ref[(q - 1) * rows + y]
                 go = go_ref[(q - 1) * rows + y]
@@ -237,7 +287,7 @@
             if 1 <= q <= n:
                 wide_ref[pl.ds((q - 1) * rows + y, o, stride=n * rows), :] = pre * s
                 total = total + wide
-            turned = [
+            shifts = [
                 pltpu.roll(wide, LANES - 1, 1).astype(bf16),
                 value,
                 pltpu.roll(wide, 1, 1).astype(bf16),
@@ -246,27 +296,34 @@
                 p = q - 2 + i
                 if 0 <= p < n:
                     at = (p * rows + (y + j - 1) % rows) * LANES
-                    s_ref[k * o : (k + 1) * o, at : at + LANES] = turned[l]
+                    s_ref[k * o : (k + 1) * o, at : at + LANES] = shifts[l]
     act_ref[...] = wide_ref[...].reshape(act_ref.shape).astype(bf16)
     total_ref[...] = jnp.broadcast_to(
         jnp.sum(total, axis=1, keepdims=True) * scale, total_ref.shape
     )
-    input_grad(n * rows, o, w_ref[4 * o :], s_ref, other_ref)
-
-
-def input_grad(cells, o, w, s_ref, out_ref):
+    input_grad(n * rows, o, w_ref[3 * o :], s_ref, [(far_ref, None)] + [(other_ref, r) for r in range(4)])
+
+
+def input_grad(cells, o, w, s_ref, outs):
     for t in range(0, cells, 2):
         part = jnp.dot(
             w, s_ref[:, t * LANES : (t + 2) * LANES], preferred_element_type=jnp.float32
-        ).astype(out_ref.dtype)
+        ).astype(outs[0][0].dtype)
         for h in range(2):
-            for r in range(4):
+            for r, (out_ref, at) in enumerate(outs):
                 cut = part[r * o : (r + 1) * o, h * LANES : (h + 1) * LANES]
-                out_ref[r, t + h] = cut
-
-
-def filter_grad_body(scale, taps, o, s_ref, x_ref, w_ref, total_ref, mine_ref, first_ref, second_ref):
-    input_grad(mine_ref.shape[1], o, w_ref[: 4 * o], s_ref, mine_ref)
+                if at is None:
+                    out_ref[t + h] = cut
+                else:
+                    out_ref[at, t + h] = cut
+
+
+def rest_body(o, s_ref, w_ref, out_ref):
+    cells = out_ref.shape[1]
+    input_grad(cells, o, w_ref[: 3 * o], s_ref, [(out_ref, r) for r in range(3)])
+
+
+def filter_grad_body(scale, taps, o, s_ref, x_ref, total_ref, first_ref, second_ref):
     full = lax.dot_general(
         s_ref[...], x_ref[...], (((1,), (1,)), ((), ())), preferred_element_type=jnp.float32
     )
@@ -284,10 +341,17 @@
         refs[2 * count + p][...] = total.astype(refs[2 * count + p].dtype)
 
 
-def split_sum_body(a_ref, b_ref, *outs):
-    for r, out in enumerate(outs):
-        total = a_ref[r].astype(jnp.float32) + b_ref[r].astype(jnp.float32)
-        out[...] = total.astype(out.dtype)
+def core_sum_body(mine_ref, other_ref, out_ref):
+    total = mine_ref[...].astype(jnp.float32) + other_ref[3].astype(jnp.float32)
+    out_ref[...] = total.astype(out_ref.dtype)
+
+
+def chip_sum_body(rest_ref, other_ref, far_ref, own_ref, a_ref, b_ref):
+    f32 = jnp.float32
+    own_ref[...] = rest_ref[0].astype(f32) + other_ref[0].astype(f32)
+    a_ref[...] = (rest_ref[1].astype(f32) + other_ref[1].astype(f32)).astype(a_ref.dtype)
+    total = rest_ref[2].astype(f32) + other_ref[2].astype(f32) + far_ref[...].astype(f32)
+    b_ref[...] = total.astype(b_ref.dtype)
 
 
 def sum_body(a_ref, b_ref, c_ref, out_ref, token_ref, wide_ref):
@@ -312,6 +376,10 @@
     bias_ref[...] = jnp.sum(jnp.where(same, column, 0.0), axis=0, keepdims=True)
 
 
+def in_hbm(value):
+    return pltpu.with_memory_space_constraint(value, pltpu.HBM)
+
+
 def rotate(value, axis, step):
     count = lax.axis_size(axis)
     return lax.ppermute(value, axis, [(i, (i + step) % count) for i in range(count)])
@@ -330,94 +398,113 @@
     scale = 1.0 / math.sqrt(lax.axis_size("slab") * cells * depth)
     me = lax.axis_index("chan").astype(jnp.int32).reshape(1)
 
-    def by_row(a, name):
-        shapes = [shape_of((cells, o, depth), bf16)]
-        scratch = [pltpu.VMEM((o * cells, depth), f32)]
-        return call(turn_body, shapes, [a], scratch=scratch, name=name)[0]
-
-    x_own = by_row(x_in, "turn_x")
-    x_a = swap(x_own, "chan", 2)
-    x_b = swap(x_own, "chan", 4)
-    x_side = swap(x_own, "chan", 1)
-    w_taps = jnp.transpose(weight, (1, 0, 2))
-    w_flat, w_back, bias = call(
+    block_wide = [pltpu.VMEM((o * cells, depth), f32)]
+
+    x_b = swap(x_in, "chan", 4)
+    x_a = swap(x_in, "chan", 2)
+    x_side = swap(x_in, "chan", 1)
+    go_above = rotate(grad_out, "slab", -1)
+    go_below = rotate(grad_out, "slab", 1)
+    x_own, go, w_flat, w_back, bias = call(
         prepare_body,
         [
+            shape_of((o, n, rows, depth), bf16),
+            shape_of((cells, o, depth), bf16),
             shape_of((27 * o, c_all), bf16),
             shape_of((c_all, 27 * o), bf16),
             shape_of((o, LANES), f32),
         ],
-        [w_taps, bias_vec[None, :]],
+        [in_hbm(a) for a in (x_in, grad_out, jnp.transpose(weight, (1, 0, 2)), bias_vec[None, :])],
+        [HBM] * 4,
+        [
+            pltpu.VMEM((o, n, rows, depth), bf16),
+            pltpu.VMEM((27, o, c_all), bf16),
+            pltpu.VMEM((1, o), bf16),
+            *block_wide,
+            pltpu.SemaphoreType.DMA((4,)),
+        ],
         name="prepare",
     )
-    go = by_row(grad_out, "turn_go")
-    go_above = rotate(go[:rows], "slab", -1)
-    go_below = rotate(go[cells - rows :], "slab", 1)
+    x_b, w_flat = lax.optimization_barrier((x_b, w_flat))
+    x_ab = swap(x_b, "chan", 2)
     x_a_side = swap(x_a, "chan", 1)
-    x_b, w_flat, w_back, bias, go, go_above, go_below = lax.optimization_barrier(
-        (x_b, w_flat, w_back, bias, go, go_above, go_below)
-    )
-    x_ab = swap(x_b, "chan", 2)
     x_b_side = swap(x_b, "chan", 1)
+    early, late = (0, 1, 2, 4, 5, 6), (3, 7)
+    (x_all,) = call(
+        functools.partial(assemble_body, early),
+        [shape_of((c_all, cells * depth), bf16)],
+        [me, x_own, x_a, x_b, x_side, x_a_side, x_b_side, go_above, go_below],
+        [SMEM] + [VMEM] * 6 + [ANY] * 2,
+        block_wide,
+        flops=ASSEMBLE_FLOPS,
+        name="assemble",
+    )
+    x_ab, x_all = lax.optimization_barrier((x_ab, x_all))
     x_ab_side = swap(x_ab, "chan", 1)
-    blocks = [x_own, x_a, x_b, x_ab, x_side, x_a_side, x_b_side, x_ab_side]
-
     own, low, high, x_all = call(
-        functools.partial(forward_body, n, rows, o),
+        functools.partial(forward_body, n, rows, o, late),
         [
             shape_of((cells, o, depth), f32),
             shape_of((2 * rows, o, depth), bf16),
             shape_of((2 * rows, o, depth), bf16),
             shape_of((c_all, cells * depth), bf16),
         ],
-        [me, w_flat, *blocks],
-        [SMEM] + [VMEM] * 9,
-        [pltpu.VMEM((3, n + 2, rows, o, depth), f32)],
+        [me, w_flat, x_ab, x_ab_side, x_all],
+        [SMEM] + [VMEM] * 4,
+        [pltpu.VMEM((3, n + 2, rows, o, depth), f32), *block_wide],
         flops=flops,
         name="forward",
+        aliases={4: 3},
     )
     above = rotate(low, "slab", -1)
     below = rotate(high, "slab", 1)
-    half = (4, cells, o, depth)
-    act, total, stacked, w_turned, other = call(
+    act, total, stacked, w_turned, other, far = call(
         functools.partial(gradient_body, n, rows, o, scale),
         [
             shape_of((o, n, rows, depth), bf16),
             shape_of((o, LANES), f32),
             shape_of((27 * o, cells * depth), bf16),
             shape_of((c_all, 27 * o), bf16),
-            shape_of(half, bf16),
+            shape_of((4, cells, o, depth), bf16),
+            shape_of((cells, o, depth), bf16),
         ],
         [me, own, low, high, below, above, bias, go, go_below, go_above, w_back],
         [SMEM] + [VMEM] * 10,
-        [pltpu.VMEM((o * cells, depth), f32)],
+        [*block_wide, pltpu.VMEM((o * rows, depth), f32)],
         flops=flops // 2,
         name="gradient",
     )
     other = swap(other, "chan", 1)
     taps = 14
-    mine, first, second = call(
+    first, second = call(
         functools.partial(filter_grad_body, scale, taps, o),
-        [
-            shape_of(half, bf16),
-            shape_of((taps * o, c_all), bf16),
-            shape_of(((28 - taps) * o, c_all), bf16),
-        ],
-        [stacked, x_all, w_turned, total],
-        flops=flops + flops // 2,
+        [shape_of((taps * o, c_all), bf16), shape_of(((28 - taps) * o, c_all), bf16)],
+        [stacked, x_all, total],
+        flops=flops,
         name="filter_grad",
     )
-    g_own, g_a, g_b, g_ab = call(
-        split_sum_body,
-        [shape_of((cells, o, depth), f32)] + [shape_of((cells, o, depth), bf16)] * 3,
-        [mine, other],
-        name="pair_sum",
-    )
-    far = swap(g_ab, "chan", 2)
-    near = swap(g_a, "chan", 2)
     first_far = swap(first, "slab", 1)
     second_far = swap(second, "slab", 2)
-    (g_b,) = call(pair_body, [shape_of(g_b.shape, bf16)], [g_b, far], name="far_sum")
+    (far,) = call(core_sum_body, [shape_of(far.shape, bf16)], [far, other], name="core_sum")
+    far = swap(far, "chan", 2)
+    (rest,) = call(
+        functools.partial(rest_body, o),
+        [shape_of((3, cells, o, depth), bf16)],
+        [stacked, w_turned],
+        flops=flops // 2,
+        name="rest",
+    )
+    g_own, g_a, g_b = call(
+        chip_sum_body,
+        [
+            shape_of((cells, o, depth), f32),
+            shape_of((cells, o, depth), bf16),
+            shape_of((cells, o, depth), bf16),
+        ],
+        [rest, other, far],
+        name="chip_sum",
+    )
+    near = swap(g_a, "chan", 2)
     across = swap(g_b, "chan", 4)
     first, second = call(
         pair_body,
@@ -439,7 +526,7 @@
         functools.partial(last_body, taps),
         [shape_of((27, o, c_all), f32), shape_of((1, o), f32)],
         [first, first_far, second, second_far, token],
-        [VMEM] * 4 + [pl.BlockSpec(memory_space=pl.ANY)],
+        [VMEM] * 4 + [ANY],
         name="last",
     )
     return act, grad_in, jnp.transpose(weight_grad, (1, 0, 2)), bias_grad[0]

time: 53 us -> 53 us (level)
  local copies, waits for them, and re-layouts: 3.48 us -> 0 us
  Pallas kernels: 7.21 us -> 9.18 us
  waiting for transfers between devices: 21.1 us -> 22.8 us
    unnamed x8 -> x0, local copies, waits for them, and re-layouts: 3.47 us -> none
    ppermute x4, waiting for transfers between devices: 7.29 us -> 9.73 us  [rotate(): lax.ppermute(value, axis, [(i, (i + step) % count) for i in range(count)])]
    pallas_call x11, Pallas kernels: 7.21 us -> 9.18 us  [call(): pl.pallas_call(body, out_shape=out_shape, in_specs=specs or [VMEM] * len(...]
    ppermute x15, waiting for transfers between devices: 13.8 us -> 13.1 us  [swap(): lax.ppermute(value, axis, [(i, i ^ bit) for i in range(lax.axis_size(axis...]
  transfers between devices with their start and end apart: 19 -> 19, of which waited for: 8 -> 12; matrix products, arithmetic and copies ran while one was open for 0% -> 0% of each run, Pallas kernels for 6% -> 9%
where the time goes in v4:
time: 53 us; the launch traced here: 52.8 us
  waiting for transfers between devices  22.8 us (43%)
  starting transfers between devices  20.1 us (38%)
  Pallas kernels  9.18 us (17%)
  between operations  0.7 us (1%)
    ppermute x15, starting transfers between devices, swap(): lax.ppermute(value, axis, [(i, i ^ bit) for i in range(lax.axis_size(axis...  15.1 us
    ppermute x15, waiting for transfers between devices, swap(): lax.ppermute(value, axis, [(i, i ^ bit) for i in range(lax.axis_size(axis...  13.1 us
    ppermute x4, waiting for transfers between devices, rotate(): lax.ppermute(value, axis, [(i, (i + step) % count) for i in range(count)])  9.73 us
    pallas_call x11, Pallas kernels, call(): pl.pallas_call(body, out_shape=out_shape, in_specs=specs or [VMEM] * len(...  9.18 us
    ppermute x4, starting transfers between devices, rotate(): lax.ppermute(value, axis, [(i, (i + step) % count) for i in range(count)])  5 us
  transfers between devices with their start and end apart: 19, of which 12 were waited for; matrix products, arithmetic and copies ran while one was open for 0% of the time, Pallas kernels for 9%

profile of v4, /device:TPU:0, one launch (start us, length us, event | category | flops | bytes accessed | tf_op | source)
XLA Modules:
  0.0 52.8 jit_solution(2417665270856341005)
XLA Ops:
  0.6 4.1 %collective-permute-start = (bf16[32,2,8,128]{3,2,1,0:T(8,128)(2,1)}, bf16[32,2,8,128]{3,2,1,0:T(8,128)(2,1)S(1)}, u32[]{:S(2)}, u32[]{:S(2)}) collective-permute-start(bf16[32,2,8,128]{3,2,1,0:T(8,128)(2,1)} %x_hbm.1), channel_id=1, source_target_pairs={{0,4},{1,5},{2,6},{3,7},{4,0},{5,1},{6,2},{7,3},{8,12},{9,13},{10,... | collective-permute-start | bytes 393224 | tf_op jit(solution)/shard_map/ppermute | solution.py:389
  4.7 1.6 %collective-permute-start.2 = (bf16[32,2,8,128]{3,2,1,0:T(8,128)(2,1)}, bf16[32,2,8,128]{3,2,1,0:T(8,128)(2,1)S(1)}, u32[]{:S(2)}, u32[]{:S(2)}) collective-permute-start(bf16[32,2,8,128]{3,2,1,0:T(8,128)(2,1)} %x_hbm.1), channel_id=1, source_target_pairs={{0,2},{1,3},{2,0},{3,1},{4,6},{5,7},{6,4},{7,5},{8,10},{9,11},{10,... | collective-permute-start | bytes 393224 | tf_op jit(solution)/shard_map/ppermute | solution.py:389
  6.3 1.5 %collective-permute-start.7 = (bf16[32,2,8,128]{3,2,1,0:T(8,128)(2,1)}, bf16[32,2,8,128]{3,2,1,0:T(8,128)(2,1)S(1)}, u32[]{:S(2)}, u32[]{:S(2)}) collective-permute-start(bf16[32,2,8,128]{3,2,1,0:T(8,128)(2,1)} %go_hbm.1), channel_id=1, source_target_pairs={{0,8},{8,16},{16,24},{24,0},{1,9},{9,17},{17,25},{25,1},{2,10},{10... | collective-permute-start | bytes 393224 | tf_op jit(solution)/shard_map/ppermute | solution.py:385
  7.8 1.4 %collective-permute-start.6 = (bf16[32,2,8,128]{3,2,1,0:T(8,128)(2,1)}, bf16[32,2,8,128]{3,2,1,0:T(8,128)(2,1)S(1)}, u32[]{:S(2)}, u32[]{:S(2)}) collective-permute-start(bf16[32,2,8,128]{3,2,1,0:T(8,128)(2,1)} %go_hbm.1), channel_id=1, source_target_pairs={{0,24},{8,0},{16,8},{24,16},{1,25},{9,1},{17,9},{25,17},{2,26},{10... | collective-permute-start | bytes 393224 | tf_op jit(solution)/shard_map/ppermute | solution.py:385
  9.2 1.4 %prepare.1 = (bf16[32,2,8,128]{3,2,1,0:T(8,128)(2,1)S(1)}, bf16[16,32,128]{2,1,0:T(8,128)(2,1)S(1)}, bf16[864,256]{1,0:T(8,128)(2,1)S(1)}, bf16[256,864]{1,0:T(8,128)(2,1)S(1)}, f32[32,128]{1,0:T(8,128)S(1)}) custom-call(bf16[32,2,8,128]{3,2,1,0:T(8,128)(2,1)} %x_hbm.1, bf16[32,2,8,128]{3,2,1,0:T(8,128)(2,1)} %go_hbm.1, bf16[27,32,256]{2,1,0:T(8,128)(2,1)} %bitcast.5, ...), custom_call_target="tpu_custom_call" | custom-call | bytes 1867840 | tf_op jit(solution)/shard_map/prepare/pallas_call | solution.py:109
  12.1 1.4 %collective-permute-done.7.refs_7_.go_below_ref = bf16[32,2,8,128]{3,2,1,0:T(8,128)(2,1)S(1)} collective-permute-done((bf16[32,2,8,128]{3,2,1,0:T(8,128)(2,1)}, bf16[32,2,8,128]{3,2,1,0:T(8,128)(2,1)S(1)}, u32[]{:S(2)}, u32[]{:S(2)}) %collective-permute-start.7) | collective-permute-done | bytes 131104 | tf_op jit(solution)/shard_map/ppermute | solution.py:385
  14.0 1.0 %collective-permute-done.6.refs_6_.go_above_ref = bf16[32,2,8,128]{3,2,1,0:T(8,128)(2,1)S(1)} collective-permute-done((bf16[32,2,8,128]{3,2,1,0:T(8,128)(2,1)}, bf16[32,2,8,128]{3,2,1,0:T(8,128)(2,1)S(1)}, u32[]{:S(2)}, u32[]{:S(2)}) %collective-permute-start.6) | collective-permute-done | bytes 131104 | tf_op jit(solution)/shard_map/ppermute | solution.py:385
  15.6 2.9 %collective-permute-done.1.refs_0_ = bf16[32,2,8,128]{3,2,1,0:T(8,128)(2,1)S(1)} collective-permute-done((bf16[32,2,8,128]{3,2,1,0:T(8,128)(2,1)S(1)}, bf16[32,2,8,128]{3,2,1,0:T(8,128)(2,1)S(1)}, u32[]{:S(2)}, u32[]{:S(2)}) %collective-permute-start.1) | collective-permute-done | bytes 131104 | tf_op jit(solution)/shard_map/ppermute | solution.py:389
  18.5 1.3 %collective-permute-done.8.refs_1_ = bf16[32,2,8,128]{3,2,1,0:T(8,128)(2,1)S(1)} collective-permute-done((bf16[32,2,8,128]{3,2,1,0:T(8,128)(2,1)S(1)}, bf16[32,2,8,128]{3,2,1,0:T(8,128)(2,1)S(1)}, u32[]{:S(2)}, u32[]{:S(2)}) %collective-permute-start.8) | collective-permute-done | bytes 131104 | tf_op jit(solution)/shard_map/ppermute | solution.py:389
  19.8 1.4 %forward.1 = (f32[16,32,128]{2,1,0:T(8,128)S(1)}, bf16[16,32,128]{2,1,0:T(8,128)(2,1)S(1)}, bf16[16,32,128]{2,1,0:T(8,128)(2,1)S(1)}, bf16[256,2048]{1,0:T(8,128)(2,1)S(1)}) custom-call(s32[1]{0:T(128)} %bitcast.me_ref, bf16[864,256]{1,0:T(8,128)(2,1)S(1)} %get-tuple-element.35.w_ref, ...), custom_call_target="tpu_custom_call", output_to_operand_aliasing={{3}: (4, {})} | custom-call | flops 905969664 | bytes 3325956 | tf_op jit(solution)/shard_map/forward/pallas_call | solution.py:109
  21.2 1.6 %collective-permute-start.10 = (bf16[16,32,128]{2,1,0:T(8,128)(2,1)S(1)}, bf16[16,32,128]{2,1,0:T(8,128)(2,1)S(1)}, u32[]{:S(2)}, u32[]{:S(2)}) collective-permute-start(bf16[16,32,128]{2,1,0:T(8,128)(2,1)S(1)} %get-tuple-element.41.low_ref), channel_id=1, source_target_pairs={{0,24},{8,0},{16,8},{24,16},{1,25},{9,1},{17,9},{25,17},{2,26},{10... | collective-permute-start | bytes 393224 | tf_op jit(solution)/shard_map/ppermute | solution.py:385
  23.3 4.3 %collective-permute-done.10.above_ref = bf16[16,32,128]{2,1,0:T(8,128)(2,1)S(1)} collective-permute-done((bf16[16,32,128]{2,1,0:T(8,128)(2,1)S(1)}, bf16[16,32,128]{2,1,0:T(8,128)(2,1)S(1)}, u32[]{:S(2)}, u32[]{:S(2)}) %collective-permute-start.10) | collective-permute-done | bytes 131104 | tf_op jit(solution)/shard_map/ppermute | solution.py:385
  27.6 3.0 %collective-permute-done.9.below_ref = bf16[16,32,128]{2,1,0:T(8,128)(2,1)S(1)} collective-permute-done((bf16[16,32,128]{2,1,0:T(8,128)(2,1)S(1)}, bf16[16,32,128]{2,1,0:T(8,128)(2,1)S(1)}, u32[]{:S(2)}, u32[]{:S(2)}) %collective-permute-start.9) | collective-permute-done | bytes 131104 | tf_op jit(solution)/shard_map/ppermute | solution.py:385
  30.6 1.9 %gradient.1 = (bf16[32,2,8,128]{3,2,1,0:T(8,128)(2,1)}, f32[32,128]{1,0:T(8,128)S(1)}, bf16[864,2048]{1,0:T(8,128)(2,1)S(1)}, bf16[256,864]{1,0:T(8,128)(2,1)S(1...) custom-call(s32[1]{0:T(128)} %bitcast.me_ref, f32[16,32,128]{2,1,0:T(8,128)S(1)} %get-tuple-element.40.own_ref, ...), custom_call_target="tpu_custom_call" | custom-call | flops 452984832 | bytes 6422532 | tf_op jit(solution)/shard_map/gradient/pallas_call | solution.py:109
  32.5 1.1 %filter_grad.1 = (bf16[448,256]{1,0:T(8,128)(2,1)S(1)}, bf16[448,256]{1,0:T(8,128)(2,1)S(1)}) custom-call(bf16[864,2048]{1,0:T(8,128)(2,1)S(1)} %get-tuple-element.47.s_ref, bf16[256,2048]{1,0:T(8,128)(2,1)S(1)} %get-tuple-element.55.x_ref, f32[32,128]{1,0:T(8,128)S(1)} %get-tuple-element.56.total_ref), custom_call_target="tpu_custom_call" | custom-call | flops 905969664 | bytes 5062656 | tf_op jit(solution)/shard_map/filter_grad/pallas_call | solution.py:109
  34.8 1.4 %collective-permute-start.12 = (bf16[16,32,128]{2,1,0:T(8,128)(2,1)S(1)}, bf16[16,32,128]{2,1,0:T(8,128)(2,1)S(1)}, u32[]{:S(2)}, u32[]{:S(2)}) collective-permute-start(bf16[16,32,128]{2,1,0:T(8,128)(2,1)S(1)} %core_sum.1), channel_id=1, source_target_pairs={{0,2},{1,3},{2,0},{3,1},{4,6},{5,7},{6,4},{7,5},{8,10},{9,11},{10,... | collective-permute-start | bytes 393224 | tf_op jit(solution)/shard_map/ppermute | solution.py:389
  37.0 3.2 %collective-permute-done.12.far_ref = bf16[16,32,128]{2,1,0:T(8,128)(2,1)S(1)} collective-permute-done((bf16[16,32,128]{2,1,0:T(8,128)(2,1)S(1)}, bf16[16,32,128]{2,1,0:T(8,128)(2,1)S(1)}, u32[]{:S(2)}, u32[]{:S(2)}) %collective-permute-start.12) | collective-permute-done | bytes 131104 | tf_op jit(solution)/shard_map/ppermute | solution.py:389
  40.3 1.4 %collective-permute-start.13 = (bf16[16,32,128]{2,1,0:T(8,128)(2,1)S(1)}, bf16[16,32,128]{2,1,0:T(8,128)(2,1)S(1)}, u32[]{:S(2)}, u32[]{:S(2)}) collective-permute-start(bf16[16,32,128]{2,1,0:T(8,128)(2,1)S(1)} %get-tuple-element.52), channel_id=1, source_target_pairs={{0,2},{1,3},{2,0},{3,1},{4,6},{5,7},{6,4},{7,5},{8,10},{9,11},{10,... | collective-permute-start | bytes 393224 | tf_op jit(solution)/shard_map/ppermute | solution.py:389
  41.7 2.4 %collective-permute-start.14 = (bf16[16,32,128]{2,1,0:T(8,128)(2,1)S(1)}, bf16[16,32,128]{2,1,0:T(8,128)(2,1)S(1)}, u32[]{:S(2)}, u32[]{:S(2)}) collective-permute-start(bf16[16,32,128]{2,1,0:T(8,128)(2,1)S(1)} %get-tuple-element.53), channel_id=1, source_target_pairs={{0,4},{1,5},{2,6},{3,7},{4,0},{5,1},{6,2},{7,3},{8,12},{9,13},{10,... | collective-permute-start | bytes 393224 | tf_op jit(solution)/shard_map/ppermute | solution.py:389
  44.2 1.6 %collective-permute-start.17 = (bf16[448,256]{1,0:T(8,128)(2,1)S(1)}, bf16[448,256]{1,0:T(8,128)(2,1)S(1)}, u32[]{:S(2)}, u32[]{:S(2)}) collective-permute-start(bf16[448,256]{1,0:T(8,128)(2,1)S(1)} %get-tuple-element.59.a_ref), channel_id=1, source_target_pairs={{0,16},{8,24},{16,0},{24,8},{1,17},{9,25},{17,1},{25,9},{2,18},{10... | collective-permute-start | bytes 688136 | tf_op jit(solution)/shard_map/ppermute | solution.py:389
  47.0 2.7 %collective-permute-done.14.c_ref = bf16[16,32,128]{2,1,0:T(8,128)(2,1)S(1)} collective-permute-done((bf16[16,32,128]{2,1,0:T(8,128)(2,1)S(1)}, bf16[16,32,128]{2,1,0:T(8,128)(2,1)S(1)}, u32[]{:S(2)}, u32[]{:S(2)}) %collective-permute-start.14) | collective-permute-done | bytes 131104 | tf_op jit(solution)/shard_map/ppermute | solution.py:389
  49.6 0.8 %sum.1 = (bf16[32,2,8,128]{3,2,1,0:T(8,128)(2,1)}, f32[8,128]{1,0:T(8,128)S(1)}) custom-call(f32[16,32,128]{2,1,0:T(8,128)S(1)} %get-tuple-element.51.a_ref, bf16[16,32,128]{2,1,0:T(8,128)(2,1)S(1)} %collective-permute-done.13.b_ref, bf16[16,32,128]{2,1,0:T(8,128)(2,1)S(1)} %collective-permute-done.14.c_ref), custom_call_target="tpu_custom_call" | custom-call | flops 2000000000 | bytes 659456 | tf_op jit(solution)/shard_map/sum/pallas_call | solution.py:109
  50.4 1.4 %collective-permute-done.18.d_ref = bf16[448,256]{1,0:T(8,128)(2,1)S(1)} collective-permute-done((bf16[448,256]{1,0:T(8,128)(2,1)S(1)}, bf16[448,256]{1,0:T(8,128)(2,1)S(1)}, u32[]{:S(2)}, u32[]{:S(2)}) %collective-permute-start.18) | collective-permute-done | bytes 229408 | tf_op jit(solution)/shard_map/ppermute | solution.py:389
  51.8 1.0 %last.1 = (f32[27,32,256]{2,1,0:T(8,128)}, f32[1,32]{1,0:T(1,128)}) custom-call(bf16[448,256]{1,0:T(8,128)(2,1)S(1)} %get-tuple-element.59.a_ref, bf16[448,256]{1,0:T(8,128)(2,1)S(1)} %collective-permute-done.17.b_ref, bf16[448,256]{1,0:T(8,128)(2,1)S(1)} %get-tuple-element.60.c_ref, bf16[448,256]{1,0:T(8,128)(2,1)S(1)} %collective-permute-done.18.d_ref, ...), custom_call_target="tpu_custom_call" | custom-call | bytes 1806464 | tf_op jit(solution)/shard_map/last/pallas_call | solution.py:109
  (25 shorter events, 6.4 us)
Async XLA Ops:
  0.6 10.7 %collective-permute-start = (bf16[32,2,8,128]{3,2,1,0:T(8,128)(2,1)}, bf16[32,2,8,128]{3,2,1,0:T(8,128)(2,1)S(1)}, u32[]{:S(2)}, u32[]{:S(2)}) collective-permute-start(bf16[32,2,8,128]{3,2,1,0:T(8,128)(2,1)} %x_hbm.1), channel_id=1, source_target_pairs={{0,4},{1,5},{2,6},{3,7},{4,0},{5,1},{6,2},{7,3},{8,12},{9,13},{10,... | collective-permute-start | bytes 393224 | tf_op jit(solution)/shard_map/ppermute | solution.py:389
  4.7 6.8 %collective-permute-start.2 = (bf16[32,2,8,128]{3,2,1,0:T(8,128)(2,1)}, bf16[32,2,8,128]{3,2,1,0:T(8,128)(2,1)S(1)}, u32[]{:S(2)}, u32[]{:S(2)}) collective-permute-start(bf16[32,2,8,128]{3,2,1,0:T(8,128)(2,1)} %x_hbm.1), channel_id=1, source_target_pairs={{0,2},{1,3},{2,0},{3,1},{4,6},{5,7},{6,4},{7,5},{8,10},{9,11},{10,... | collective-permute-start | bytes 393224 | tf_op jit(solution)/shard_map/ppermute | solution.py:389
  6.3 7.2 %collective-permute-start.7 = (bf16[32,2,8,128]{3,2,1,0:T(8,128)(2,1)}, bf16[32,2,8,128]{3,2,1,0:T(8,128)(2,1)S(1)}, u32[]{:S(2)}, u32[]{:S(2)}) collective-permute-start(bf16[32,2,8,128]{3,2,1,0:T(8,128)(2,1)} %go_hbm.1), channel_id=1, source_target_pairs={{0,8},{8,16},{16,24},{24,0},{1,9},{9,17},{17,25},{25,1},{2,10},{10... | collective-permute-start | bytes 393224 | tf_op jit(solution)/shard_map/ppermute | solution.py:385
  7.8 7.2 %collective-permute-start.6 = (bf16[32,2,8,128]{3,2,1,0:T(8,128)(2,1)}, bf16[32,2,8,128]{3,2,1,0:T(8,128)(2,1)S(1)}, u32[]{:S(2)}, u32[]{:S(2)}) collective-permute-start(bf16[32,2,8,128]{3,2,1,0:T(8,128)(2,1)} %go_hbm.1), channel_id=1, source_target_pairs={{0,24},{8,0},{16,8},{24,16},{1,25},{9,1},{17,9},{25,17},{2,26},{10... | collective-permute-start | bytes 393224 | tf_op jit(solution)/shard_map/ppermute | solution.py:385
  9.2 5.7 %collective-permute-start.3 = (bf16[32,2,8,128]{3,2,1,0:T(8,128)(2,1)}, bf16[32,2,8,128]{3,2,1,0:T(8,128)(2,1)S(1)}, u32[]{:S(2)}, u32[]{:S(2)}) collective-permute-start(bf16[32,2,8,128]{3,2,1,0:T(8,128)(2,1)} %x_hbm.1), channel_id=1, source_target_pairs={{0,1},{1,0},{2,3},{3,2},{4,5},{5,4},{6,7},{7,6},{8,9},{9,8},{10,11... | collective-permute-start | bytes 393224 | tf_op jit(solution)/shard_map/ppermute | solution.py:389
  11.6 3.4 %collective-permute-start.4 = (bf16[32,2,8,128]{3,2,1,0:T(8,128)(2,1)S(1)}, bf16[32,2,8,128]{3,2,1,0:T(8,128)(2,1)S(1)}, u32[]{:S(2)}, u32[]{:S(2)}) collective-permute-start(bf16[32,2,8,128]{3,2,1,0:T(8,128)(2,1)S(1)} %collective-permute-done.2.refs_1_), channel_id=1, source_target_pairs={{0,1},{1,0},{2,3},{3,2},{4,5},{5,4},{6,7},{7,6},{8,9},{9,8},{10,11... | collective-permute-start | bytes 393224 | tf_op jit(solution)/shard_map/ppermute | solution.py:389
  11.6 3.4 %collective-permute-start.5 = (bf16[32,2,8,128]{3,2,1,0:T(8,128)(2,1)S(1)}, bf16[32,2,8,128]{3,2,1,0:T(8,128)(2,1)S(1)}, u32[]{:S(2)}, u32[]{:S(2)}) collective-permute-start(bf16[32,2,8,128]{3,2,1,0:T(8,128)(2,1)S(1)} %collective-permute-done.refs_2_), channel_id=1, source_target_pairs={{0,1},{1,0},{2,3},{3,2},{4,5},{5,4},{6,7},{7,6},{8,9},{9,8},{10,11... | collective-permute-start | bytes 393224 | tf_op jit(solution)/shard_map/ppermute | solution.py:389
  13.5 5.0 %collective-permute-start.1 = (bf16[32,2,8,128]{3,2,1,0:T(8,128)(2,1)S(1)}, bf16[32,2,8,128]{3,2,1,0:T(8,128)(2,1)S(1)}, u32[]{:S(2)}, u32[]{:S(2)}) collective-permute-start(bf16[32,2,8,128]{3,2,1,0:T(8,128)(2,1)S(1)} %collective-permute-done.refs_2_), channel_id=1, source_target_pairs={{0,2},{1,3},{2,0},{3,1},{4,6},{5,7},{6,4},{7,5},{8,10},{9,11},{10,... | collective-permute-start | bytes 393224 | tf_op jit(solution)/shard_map/ppermute | solution.py:389
  18.5 1.3 %collective-permute-start.8 = (bf16[32,2,8,128]{3,2,1,0:T(8,128)(2,1)S(1)}, bf16[32,2,8,128]{3,2,1,0:T(8,128)(2,1)S(1)}, u32[]{:S(2)}, u32[]{:S(2)}) collective-permute-start(bf16[32,2,8,128]{3,2,1,0:T(8,128)(2,1)S(1)} %collective-permute-done.1.refs_0_), channel_id=1, source_target_pairs={{0,1},{1,0},{2,3},{3,2},{4,5},{5,4},{6,7},{7,6},{8,9},{9,8},{10,11... | collective-permute-start | bytes 393224 | tf_op jit(solution)/shard_map/ppermute | solution.py:389
  21.2 6.4 %collective-permute-start.10 = (bf16[16,32,128]{2,1,0:T(8,128)(2,1)S(1)}, bf16[16,32,128]{2,1,0:T(8,128)(2,1)S(1)}, u32[]{:S(2)}, u32[]{:S(2)}) collective-permute-start(bf16[16,32,128]{2,1,0:T(8,128)(2,1)S(1)} %get-tuple-element.41.low_ref), channel_id=1, source_target_pairs={{0,24},{8,0},{16,8},{24,16},{1,25},{9,1},{17,9},{25,17},{2,26},{10... | collective-permute-start | bytes 393224 | tf_op jit(solution)/shard_map/ppermute | solution.py:385
  22.8 7.8 %collective-permute-start.9 = (bf16[16,32,128]{2,1,0:T(8,128)(2,1)S(1)}, bf16[16,32,128]{2,1,0:T(8,128)(2,1)S(1)}, u32[]{:S(2)}, u32[]{:S(2)}) collective-permute-start(bf16[16,32,128]{2,1,0:T(8,128)(2,1)S(1)} %get-tuple-element.42.high_ref), channel_id=1, source_target_pairs={{0,8},{8,16},{16,24},{24,0},{1,9},{9,17},{17,25},{25,1},{2,10},{10... | collective-permute-start | bytes 393224 | tf_op jit(solution)/shard_map/ppermute | solution.py:385
  32.5 2.3 %collective-permute-start.11 = (bf16[4,16,32,128]{3,2,1,0:T(8,128)(2,1)S(1)}, bf16[4,16,32,128]{3,2,1,0:T(8,128)(2,1)S(1)}, u32[]{:S(2)}, u32[]{:S(2)}) collective-permute-start(bf16[4,16,32,128]{3,2,1,0:T(8,128)(2,1)S(1)} %get-tuple-element.49), channel_id=1, source_target_pairs={{0,1},{1,0},{2,3},{3,2},{4,5},{5,4},{6,7},{7,6},{8,9},{9,8},{10,11... | collective-permute-start | bytes 1572872 | tf_op jit(solution)/shard_map/ppermute | solution.py:389
  33.6 10.5 %collective-permute-start.15 = (bf16[448,256]{1,0:T(8,128)(2,1)S(1)}, bf16[448,256]{1,0:T(8,128)(2,1)S(1)}, u32[]{:S(2)}, u32[]{:S(2)}) collective-permute-start(bf16[448,256]{1,0:T(8,128)(2,1)S(1)} %get-tuple-element.57.refs_0_), channel_id=1, source_target_pairs={{0,8},{8,0},{16,24},{24,16},{1,9},{9,1},{17,25},{25,17},{2,10},{10... | collective-permute-start | bytes 688136 | tf_op jit(solution)/shard_map/ppermute | solution.py:389
  34.2 9.9 %collective-permute-start.16 = (bf16[448,256]{1,0:T(8,128)(2,1)S(1)}, bf16[448,256]{1,0:T(8,128)(2,1)S(1)}, u32[]{:S(2)}, u32[]{:S(2)}) collective-permute-start(bf16[448,256]{1,0:T(8,128)(2,1)S(1)} %get-tuple-element.58.refs_2_), channel_id=1, source_target_pairs={{0,16},{8,24},{16,0},{24,8},{1,17},{9,25},{17,1},{25,9},{2,18},{10... | collective-permute-start | bytes 688136 | tf_op jit(solution)/shard_map/ppermute | solution.py:389
  34.8 5.4 %collective-permute-start.12 = (bf16[16,32,128]{2,1,0:T(8,128)(2,1)S(1)}, bf16[16,32,128]{2,1,0:T(8,128)(2,1)S(1)}, u32[]{:S(2)}, u32[]{:S(2)}) collective-permute-start(bf16[16,32,128]{2,1,0:T(8,128)(2,1)S(1)} %core_sum.1), channel_id=1, source_target_pairs={{0,2},{1,3},{2,0},{3,1},{4,6},{5,7},{6,4},{7,5},{8,10},{9,11},{10,... | collective-permute-start | bytes 393224 | tf_op jit(solution)/shard_map/ppermute | solution.py:389
  40.3 6.7 %collective-permute-start.13 = (bf16[16,32,128]{2,1,0:T(8,128)(2,1)S(1)}, bf16[16,32,128]{2,1,0:T(8,128)(2,1)S(1)}, u32[]{:S(2)}, u32[]{:S(2)}) collective-permute-start(bf16[16,32,128]{2,1,0:T(8,128)(2,1)S(1)} %get-tuple-element.52), channel_id=1, source_target_pairs={{0,2},{1,3},{2,0},{3,1},{4,6},{5,7},{6,4},{7,5},{8,10},{9,11},{10,... | collective-permute-start | bytes 393224 | tf_op jit(solution)/shard_map/ppermute | solution.py:389
  41.7 7.9 %collective-permute-start.14 = (bf16[16,32,128]{2,1,0:T(8,128)(2,1)S(1)}, bf16[16,32,128]{2,1,0:T(8,128)(2,1)S(1)}, u32[]{:S(2)}, u32[]{:S(2)}) collective-permute-start(bf16[16,32,128]{2,1,0:T(8,128)(2,1)S(1)} %get-tuple-element.53), channel_id=1, source_target_pairs={{0,4},{1,5},{2,6},{3,7},{4,0},{5,1},{6,2},{7,3},{8,12},{9,13},{10,... | collective-permute-start | bytes 393224 | tf_op jit(solution)/shard_map/ppermute | solution.py:389
  44.2 6.2 %collective-permute-start.17 = (bf16[448,256]{1,0:T(8,128)(2,1)S(1)}, bf16[448,256]{1,0:T(8,128)(2,1)S(1)}, u32[]{:S(2)}, u32[]{:S(2)}) collective-permute-start(bf16[448,256]{1,0:T(8,128)(2,1)S(1)} %get-tuple-element.59.a_ref), channel_id=1, source_target_pairs={{0,16},{8,24},{16,0},{24,8},{1,17},{9,25},{17,1},{25,9},{2,18},{10... | collective-permute-start | bytes 688136 | tf_op jit(solution)/shard_map/ppermute | solution.py:389
  45.8 6.0 %collective-permute-start.18 = (bf16[448,256]{1,0:T(8,128)(2,1)S(1)}, bf16[448,256]{1,0:T(8,128)(2,1)S(1)}, u32[]{:S(2)}, u32[]{:S(2)}) collective-permute-start(bf16[448,256]{1,0:T(8,128)(2,1)S(1)} %get-tuple-element.60.c_ref), channel_id=1, source_target_pairs={{0,8},{8,0},{16,24},{24,16},{1,9},{9,1},{17,25},{25,17},{2,10},{10... | collective-permute-start | bytes 688136 | tf_op jit(solution)/shard_map/ppermute | solution.py:389

commit v5 on v4

--- a/solution.py
+++ b/solution.py
@@ -10,7 +10,7 @@
 
 LANES = 128
 SUM_FLOPS = 20 * 10**8
-ASSEMBLE_FLOPS = 0
+FORWARD_FLOPS = 0
 VMEM = pl.BlockSpec(memory_space=pltpu.VMEM)
 ANY = pl.BlockSpec(memory_space=pl.ANY)
 HBM = pl.BlockSpec(memory_space=pltpu.HBM)
@@ -135,12 +135,16 @@
 
 
 def prepare_body(
+    n,
+    rows,
     x_hbm,
     go_hbm,
     w_hbm,
     bias_hbm,
     x_ref,
     go_ref,
+    go_low_ref,
+    go_high_ref,
     flat_ref,
     back_ref,
     bias_ref,
@@ -161,6 +165,10 @@
     copies[0].wait()
     for k, value in enumerate(turned(go_in[...], wide_ref)):
         go_ref[k] = value
+        if k < rows:
+            go_low_ref[k] = value
+        if k >= (n - 1) * rows:
+            go_high_ref[k - (n - 1) * rows] = value
     copies[1].wait()
     copies[2].wait()
     copies[3].wait()
@@ -255,23 +263,20 @@
     other_ref,
     far_ref,
     wide_ref,
-    rim_ref,
 ):
     f32, bf16 = jnp.float32, jnp.bfloat16
     for b in range(8):
         place = pl.ds(pl.multiple_of(owner(me_ref, b) * o, o), o)
         w_ref[b * o : (b + 1) * o] = back_ref[place]
     total = jnp.zeros((o, LANES), f32)
-    go_below = turned(go_below_ref[:, n - 1 :], rim_ref)
-    go_above = turned(go_above_ref[:, :1], rim_ref)
     for q in range(n + 2):
         for y in range(rows):
             if q == 0:
                 pre = below_ref[rows + y].astype(f32) + low_ref[y].astype(f32)
-                go = go_below[y]
+                go = go_below_ref[y]
             elif q == n + 1:
                 pre = above_ref[rows + y].astype(f32) + high_ref[y].astype(f32)
-                go = go_above[y]
+                go = go_above_ref[y]
             else:
                 pre = own_ref[(q - 1) * rows + y]
                 go = go_ref[(q - 1) * rows + y]
@@ -334,11 +339,12 @@
     second_ref[(27 - taps) * o :] = row.astype(second_ref.dtype)
 
 
-def pair_body(*refs):
-    count = len(refs) // 3
-    for p in range(count):
-        total = refs[2 * p][...].astype(jnp.float32) + refs[2 * p + 1][...].astype(jnp.float32)
-        refs[2 * count + p][...] = total.astype(refs[2 * count + p].dtype)
+def second_body(rest_ref, other_ref, a_ref, b_ref, c_ref, d_ref, _, own_ref, near_ref, ab_ref, cd_ref):
+    f32 = jnp.float32
+    ab_ref[...] = (a_ref[...].astype(f32) + b_ref[...].astype(f32)).astype(ab_ref.dtype)
+    cd_ref[...] = (c_ref[...].astype(f32) + d_ref[...].astype(f32)).astype(cd_ref.dtype)
+    own_ref[...] = rest_ref[0].astype(f32) + other_ref[0].astype(f32)
+    near_ref[...] = (rest_ref[1].astype(f32) + other_ref[1].astype(f32)).astype(near_ref.dtype)
 
 
 def core_sum_body(mine_ref, other_ref, out_ref):
@@ -346,26 +352,23 @@
     out_ref[...] = total.astype(out_ref.dtype)
 
 
-def chip_sum_body(rest_ref, other_ref, far_ref, own_ref, a_ref, b_ref):
+def chip_sum_body(rest_ref, other_ref, far_ref, b_ref):
     f32 = jnp.float32
-    own_ref[...] = rest_ref[0].astype(f32) + other_ref[0].astype(f32)
-    a_ref[...] = (rest_ref[1].astype(f32) + other_ref[1].astype(f32)).astype(a_ref.dtype)
     total = rest_ref[2].astype(f32) + other_ref[2].astype(f32) + far_ref[...].astype(f32)
     b_ref[...] = total.astype(b_ref.dtype)
 
 
-def sum_body(a_ref, b_ref, c_ref, out_ref, token_ref, wide_ref):
-    token_ref[...] = jnp.zeros_like(token_ref)
-    cells, o, _ = a_ref.shape
-    for k in range(cells):
-        total = a_ref[k] + b_ref[k].astype(jnp.float32) + c_ref[k].astype(jnp.float32)
-        wide_ref[pl.ds(k, o, stride=cells), :] = total
-    out_ref[...] = wide_ref[...].reshape(out_ref.shape).astype(out_ref.dtype)
-
-
-def last_body(taps, a_ref, b_ref, c_ref, d_ref, _, out_ref, bias_ref):
+def sum_body(a_ref, b_ref, out_ref):
+    out_ref[...] = a_ref[...] + b_ref[...].astype(jnp.float32)
+
+
+def last_body(taps, a_ref, b_ref, c_ref, d_ref, g_ref, h_ref, out_ref, bias_ref, grad_ref, wide_ref):
     o = out_ref.shape[1]
     f32 = jnp.float32
+    cells = g_ref.shape[0]
+    for k in range(cells):
+        wide_ref[pl.ds(k, o, stride=cells), :] = g_ref[k] + h_ref[k].astype(f32)
+    grad_ref[...] = wide_ref[...].reshape(grad_ref.shape).astype(grad_ref.dtype)
     for k in range(27):
         left, right, at = (a_ref, b_ref, k) if k < taps else (c_ref, d_ref, k - taps)
         cut = slice(at * o, (at + 1) * o)
@@ -403,13 +406,13 @@
     x_b = swap(x_in, "chan", 4)
     x_a = swap(x_in, "chan", 2)
     x_side = swap(x_in, "chan", 1)
-    go_above = rotate(grad_out, "slab", -1)
-    go_below = rotate(grad_out, "slab", 1)
-    x_own, go, w_flat, w_back, bias = call(
-        prepare_body,
+    x_own, go, go_low, go_high, w_flat, w_back, bias = call(
+        functools.partial(prepare_body, n, rows),
         [
             shape_of((o, n, rows, depth), bf16),
             shape_of((cells, o, depth), bf16),
+            shape_of((rows, o, depth), bf16),
+            shape_of((rows, o, depth), bf16),
             shape_of((27 * o, c_all), bf16),
             shape_of((c_all, 27 * o), bf16),
             shape_of((o, LANES), f32),
@@ -425,6 +428,8 @@
         ],
         name="prepare",
     )
+    go_above = rotate(go_low, "slab", -1)
+    go_below = rotate(go_high, "slab", 1)
     x_b, w_flat = lax.optimization_barrier((x_b, w_flat))
     x_ab = swap(x_b, "chan", 2)
     x_a_side = swap(x_a, "chan", 1)
@@ -433,10 +438,9 @@
     (x_all,) = call(
         functools.partial(assemble_body, early),
         [shape_of((c_all, cells * depth), bf16)],
-        [me, x_own, x_a, x_b, x_side, x_a_side, x_b_side, go_above, go_below],
-        [SMEM] + [VMEM] * 6 + [ANY] * 2,
+        [me, x_own, x_a, x_b, x_side, x_a_side, x_b_side, go_above],
+        [SMEM] + [VMEM] * 6 + [ANY],
         block_wide,
-        flops=ASSEMBLE_FLOPS,
         name="assemble",
     )
     x_ab, x_all = lax.optimization_barrier((x_ab, x_all))
@@ -452,10 +456,11 @@
         [me, w_flat, x_ab, x_ab_side, x_all],
         [SMEM] + [VMEM] * 4,
         [pltpu.VMEM((3, n + 2, rows, o, depth), f32), *block_wide],
-        flops=flops,
+        flops=FORWARD_FLOPS,
         name="forward",
         aliases={4: 3},
     )
+    low, high, go_below = lax.optimization_barrier((low, high, go_below))
     above = rotate(low, "slab", -1)
     below = rotate(high, "slab", 1)
     act, total, stacked, w_turned, other, far = call(
@@ -470,7 +475,7 @@
         ],
         [me, own, low, high, below, above, bias, go, go_below, go_above, w_back],
         [SMEM] + [VMEM] * 10,
-        [*block_wide, pltpu.VMEM((o * rows, depth), f32)],
+        block_wide,
         flops=flops // 2,
         name="gradient",
     )
@@ -494,39 +499,41 @@
         flops=flops // 2,
         name="rest",
     )
-    g_own, g_a, g_b = call(
-        chip_sum_body,
+    (far,) = call(
+        chip_sum_body, [shape_of((cells, o, depth), bf16)], [rest, other, far], name="chip_sum"
+    )
+    across = swap(far, "chan", 4)
+    own_sum, near, first, second = call(
+        second_body,
         [
             shape_of((cells, o, depth), f32),
             shape_of((cells, o, depth), bf16),
-            shape_of((cells, o, depth), bf16),
-        ],
-        [rest, other, far],
-        name="chip_sum",
-    )
-    near = swap(g_a, "chan", 2)
-    across = swap(g_b, "chan", 4)
-    first, second = call(
-        pair_body,
-        [shape_of(a.shape, bf16) for a in (first, second)],
-        [first, first_far, second, second_far],
-        name="filter_sum",
+            shape_of(first.shape, bf16),
+            shape_of(second.shape, bf16),
+        ],
+        [rest, other, first, first_far, second, second_far, far],
+        [VMEM] * 6 + [ANY],
+        name="second_sum",
     )
     first_far = swap(first, "slab", 2)
     second_far = swap(second, "slab", 1)
-    grad_in, token = call(
+    near = swap(near, "chan", 2)
+    (own_sum,) = call(
         sum_body,
-        [shape_of((o, n, rows, depth), bf16), shape_of((8, LANES), f32)],
-        [g_own, near, across],
-        scratch=[pltpu.VMEM((o * cells, depth), f32)],
+        [shape_of((cells, o, depth), f32)],
+        [own_sum, across],
         flops=SUM_FLOPS,
         name="sum",
     )
-    weight_grad, bias_grad = call(
+    weight_grad, bias_grad, grad_in = call(
         functools.partial(last_body, taps),
-        [shape_of((27, o, c_all), f32), shape_of((1, o), f32)],
-        [first, first_far, second, second_far, token],
-        [VMEM] * 4 + [ANY],
+        [
+            shape_of((27, o, c_all), f32),
+            shape_of((1, o), f32),
+            shape_of((o, n, rows, depth), bf16),
+        ],
+        [first, first_far, second, second_far, own_sum, near],
+        scratch=block_wide,
         name="last",
     )
     return act, grad_in, jnp.transpose(weight_grad, (1, 0, 2)), bias_grad[0]

time: 53 us -> 55.2 us (1.042)
  starting transfers between devices: 20.1 us -> 22.3 us
  waiting for transfers between devices: 22.8 us -> 23.5 us
  Pallas kernels: 9.18 us -> 8.49 us
    ppermute x4, starting transfers between devices: 5 us -> 6.83 us  [rotate(): lax.ppermute(value, axis, [(i, (i + step) % count) for i in range(count)])]
    pallas_call x11, Pallas kernels: 9.18 us -> 8.49 us  [call(): pl.pallas_call(body, out_shape=out_shape, in_specs=specs or [VMEM] * len(...]
  transfers between devices with their start and end apart: 19 -> 19, of which waited for: 12 -> 9; matrix products, arithmetic and copies ran while one was open for 0% -> 0% of each run, Pallas kernels for 9% -> 10%
where the time goes in v5:
time: 55.2 us; the launch traced here: 55 us
  waiting for transfers between devices  23.5 us (43%)
  starting transfers between devices  22.3 us (40%)
  Pallas kernels  8.49 us (15%)
  between operations  0.72 us (1%)
    ppermute x15, starting transfers between devices, swap(): lax.ppermute(value, axis, [(i, i ^ bit) for i in range(lax.axis_size(axis...  15.5 us
    ppermute x15, waiting for transfers between devices, swap(): lax.ppermute(value, axis, [(i, i ^ bit) for i in range(lax.axis_size(axis...  13.2 us
    ppermute x4, waiting for transfers between devices, rotate(): lax.ppermute(value, axis, [(i, (i + step) % count) for i in range(count)])  10.3 us
    pallas_call x11, Pallas kernels, call(): pl.pallas_call(body, out_shape=out_shape, in_specs=specs or [VMEM] * len(...  8.49 us
    ppermute x4, starting transfers between devices, rotate(): lax.ppermute(value, axis, [(i, (i + step) % count) for i in range(count)])  6.83 us
  transfers between devices with their start and end apart: 19, of which 9 were waited for; matrix products, arithmetic and copies ran while one was open for 0% of the time, Pallas kernels for 10%

profile of v5, /device:TPU:0, one launch (start us, length us, event | category | flops | bytes accessed | tf_op | source)
XLA Modules:
  0.0 55.0 jit_solution(6352196461621310385)
XLA Ops:
  0.6 4.1 %collective-permute-start = (bf16[32,2,8,128]{3,2,1,0:T(8,128)(2,1)}, bf16[32,2,8,128]{3,2,1,0:T(8,128)(2,1)S(1)}, u32[]{:S(2)}, u32[]{:S(2)}) collective-permute-start(bf16[32,2,8,128]{3,2,1,0:T(8,128)(2,1)} %x_hbm.1), channel_id=1, source_target_pairs={{0,4},{1,5},{2,6},{3,7},{4,0},{5,1},{6,2},{7,3},{8,12},{9,13},{10,... | collective-permute-start | bytes 393224 | tf_op jit(solution)/shard_map/ppermute | solution.py:392
  4.7 1.6 %collective-permute-start.2 = (bf16[32,2,8,128]{3,2,1,0:T(8,128)(2,1)}, bf16[32,2,8,128]{3,2,1,0:T(8,128)(2,1)S(1)}, u32[]{:S(2)}, u32[]{:S(2)}) collective-permute-start(bf16[32,2,8,128]{3,2,1,0:T(8,128)(2,1)} %x_hbm.1), channel_id=1, source_target_pairs={{0,2},{1,3},{2,0},{3,1},{4,6},{5,7},{6,4},{7,5},{8,10},{9,11},{10,... | collective-permute-start | bytes 393224 | tf_op jit(solution)/shard_map/ppermute | solution.py:392
  6.3 1.4 %prepare.1 = (bf16[32,2,8,128]{3,2,1,0:T(8,128)(2,1)S(1)}, bf16[16,32,128]{2,1,0:T(8,128)(2,1)S(1)}, bf16[8,32,128]{2,1,0:T(8,128)(2,1)S(1)}, bf16[8,32,128]{2,1...) custom-call(bf16[32,2,8,128]{3,2,1,0:T(8,128)(2,1)} %x_hbm.1, ...), custom_call_target="tpu_custom_call" | custom-call | bytes 1998912 | tf_op jit(solution)/shard_map/prepare/pallas_call | solution.py:109
  7.7 3.7 %collective-permute-done.refs_2_ = bf16[32,2,8,128]{3,2,1,0:T(8,128)(2,1)S(1)} collective-permute-done((bf16[32,2,8,128]{3,2,1,0:T(8,128)(2,1)}, bf16[32,2,8,128]{3,2,1,0:T(8,128)(2,1)S(1)}, u32[]{:S(2)}, u32[]{:S(2)}) %collective-permute-start) | collective-permute-done | bytes 131104 | tf_op jit(solution)/shard_map/ppermute | solution.py:392
  12.1 1.4 %collective-permute-start.1 = (bf16[32,2,8,128]{3,2,1,0:T(8,128)(2,1)S(1)}, bf16[32,2,8,128]{3,2,1,0:T(8,128)(2,1)S(1)}, u32[]{:S(2)}, u32[]{:S(2)}) collective-permute-start(bf16[32,2,8,128]{3,2,1,0:T(8,128)(2,1)S(1)} %collective-permute-done.refs_2_), channel_id=1, source_target_pairs={{0,2},{1,3},{2,0},{3,1},{4,6},{5,7},{6,4},{7,5},{8,10},{9,11},{10,... | collective-permute-start | bytes 393224 | tf_op jit(solution)/shard_map/ppermute | solution.py:392
  13.5 2.4 %collective-permute-start.6 = (bf16[8,32,128]{2,1,0:T(8,128)(2,1)S(1)}, bf16[8,32,128]{2,1,0:T(8,128)(2,1)S(1)}, u32[]{:S(2)}, u32[]{:S(2)}) collective-permute-start(bf16[8,32,128]{2,1,0:T(8,128)(2,1)S(1)} %get-tuple-element.41), channel_id=1, source_target_pairs={{0,24},{8,0},{16,8},{24,16},{1,25},{9,1},{17,9},{25,17},{2,26},{10... | collective-permute-start | bytes 196616 | tf_op jit(solution)/shard_map/ppermute | solution.py:388
  16.0 1.9 %collective-permute-done.6.refs_6_.go_above_ref = bf16[8,32,128]{2,1,0:T(8,128)(2,1)S(1)} collective-permute-done((bf16[8,32,128]{2,1,0:T(8,128)(2,1)S(1)}, bf16[8,32,128]{2,1,0:T(8,128)(2,1)S(1)}, u32[]{:S(2)}, u32[]{:S(2)}) %collective-permute-start.6) | collective-permute-done | bytes 65568 | tf_op jit(solution)/shard_map/ppermute | solution.py:388
  18.6 2.4 %collective-permute-start.8 = (bf16[8,32,128]{2,1,0:T(8,128)(2,1)S(1)}, bf16[8,32,128]{2,1,0:T(8,128)(2,1)S(1)}, u32[]{:S(2)}, u32[]{:S(2)}) collective-permute-start(bf16[8,32,128]{2,1,0:T(8,128)(2,1)S(1)} %get-tuple-element.47), channel_id=1, source_target_pairs={{0,8},{8,16},{16,24},{24,0},{1,9},{9,17},{17,25},{25,1},{2,10},{10... | collective-permute-start | bytes 196616 | tf_op jit(solution)/shard_map/ppermute | solution.py:388
  21.0 1.4 %forward.1 = (f32[16,32,128]{2,1,0:T(8,128)S(1)}, bf16[16,32,128]{2,1,0:T(8,128)(2,1)S(1)}, bf16[16,32,128]{2,1,0:T(8,128)(2,1)S(1)}, bf16[256,2048]{1,0:T(8,128)(2,1)S(1)}) custom-call(s32[1]{0:T(128)} %bitcast.me_ref, bf16[864,256]{1,0:T(8,128)(2,1)S(1)} %get-tuple-element.38.w_ref, ...), custom_call_target="tpu_custom_call", output_to_operand_aliasing={{3}: (4, {})} | custom-call | bytes 3325956 | tf_op jit(solution)/shard_map/forward/pallas_call | solution.py:109
  22.3 2.3 %collective-permute-done.8.go_below_ref = bf16[8,32,128]{2,1,0:T(8,128)(2,1)S(1)} collective-permute-done((bf16[8,32,128]{2,1,0:T(8,128)(2,1)S(1)}, bf16[8,32,128]{2,1,0:T(8,128)(2,1)S(1)}, u32[]{:S(2)}, u32[]{:S(2)}) %collective-permute-start.8) | collective-permute-done | bytes 65568 | tf_op jit(solution)/shard_map/ppermute | solution.py:388
  24.6 1.7 %collective-permute-start.10 = (bf16[16,32,128]{2,1,0:T(8,128)(2,1)S(1)}, bf16[16,32,128]{2,1,0:T(8,128)(2,1)S(1)}, u32[]{:S(2)}, u32[]{:S(2)}) collective-permute-start(bf16[16,32,128]{2,1,0:T(8,128)(2,1)S(1)} %get-tuple-element.48.low_ref), channel_id=1, source_target_pairs={{0,24},{8,0},{16,8},{24,16},{1,25},{9,1},{17,9},{25,17},{2,26},{10... | collective-permute-start | bytes 393224 | tf_op jit(solution)/shard_map/ppermute | solution.py:388
  26.6 4.4 %collective-permute-done.10.above_ref = bf16[16,32,128]{2,1,0:T(8,128)(2,1)S(1)} collective-permute-done((bf16[16,32,128]{2,1,0:T(8,128)(2,1)S(1)}, bf16[16,32,128]{2,1,0:T(8,128)(2,1)S(1)}, u32[]{:S(2)}, u32[]{:S(2)}) %collective-permute-start.10) | collective-permute-done | bytes 131104 | tf_op jit(solution)/shard_map/ppermute | solution.py:388
  31.0 1.7 %collective-permute-done.9.below_ref = bf16[16,32,128]{2,1,0:T(8,128)(2,1)S(1)} collective-permute-done((bf16[16,32,128]{2,1,0:T(8,128)(2,1)S(1)}, bf16[16,32,128]{2,1,0:T(8,128)(2,1)S(1)}, u32[]{:S(2)}, u32[]{:S(2)}) %collective-permute-start.9) | collective-permute-done | bytes 131104 | tf_op jit(solution)/shard_map/ppermute | solution.py:388
  32.7 1.8 %gradient.1 = (bf16[32,2,8,128]{3,2,1,0:T(8,128)(2,1)}, f32[32,128]{1,0:T(8,128)S(1)}, bf16[864,2048]{1,0:T(8,128)(2,1)S(1)}, bf16[256,864]{1,0:T(8,128)(2,1)S(1...) custom-call(s32[1]{0:T(128)} %bitcast.me_ref, f32[16,32,128]{2,1,0:T(8,128)S(1)} %get-tuple-element.44.own_ref, ...), custom_call_target="tpu_custom_call" | custom-call | flops 452984832 | bytes 6291460 | tf_op jit(solution)/shard_map/gradient/pallas_call | solution.py:109
  34.6 1.1 %filter_grad.1 = (bf16[448,256]{1,0:T(8,128)(2,1)S(1)}, bf16[448,256]{1,0:T(8,128)(2,1)S(1)}) custom-call(bf16[864,2048]{1,0:T(8,128)(2,1)S(1)} %get-tuple-element.55.s_ref, bf16[256,2048]{1,0:T(8,128)(2,1)S(1)} %get-tuple-element.58.x_ref, f32[32,128]{1,0:T(8,128)S(1)} %get-tuple-element.59.total_ref), custom_call_target="tpu_custom_call" | custom-call | flops 905969664 | bytes 5062656 | tf_op jit(solution)/shard_map/filter_grad/pallas_call | solution.py:109
  35.7 1.6 %collective-permute-start.12 = (bf16[448,256]{1,0:T(8,128)(2,1)S(1)}, bf16[448,256]{1,0:T(8,128)(2,1)S(1)}, u32[]{:S(2)}, u32[]{:S(2)}) collective-permute-start(bf16[448,256]{1,0:T(8,128)(2,1)S(1)} %get-tuple-element.60.a_ref), channel_id=1, source_target_pairs={{0,8},{8,0},{16,24},{24,16},{1,9},{9,1},{17,25},{25,17},{2,10},{10... | collective-permute-start | bytes 688136 | tf_op jit(solution)/shard_map/ppermute | solution.py:392
  37.8 0.7 %collective-permute-start.14 = (bf16[16,32,128]{2,1,0:T(8,128)(2,1)S(1)}, bf16[16,32,128]{2,1,0:T(8,128)(2,1)S(1)}, u32[]{:S(2)}, u32[]{:S(2)}) collective-permute-start(bf16[16,32,128]{2,1,0:T(8,128)(2,1)S(1)} %core_sum.1), channel_id=1, source_target_pairs={{0,2},{1,3},{2,0},{3,1},{4,6},{5,7},{6,4},{7,5},{8,10},{9,11},{10,... | collective-permute-start | bytes 393224 | tf_op jit(solution)/shard_map/ppermute | solution.py:392
  38.5 0.8 %rest.1.rest_ref = bf16[3,16,32,128]{3,2,1,0:T(8,128)(2,1)S(1)} custom-call(bf16[864,2048]{1,0:T(8,128)(2,1)S(1)} %get-tuple-element.55.s_ref, bf16[256,864]{1,0:T(8,128)(2,1)S(1)} %get-tuple-element.56.w_ref), custom_call_target="tpu_custom_call" | custom-call | flops 452984832 | bytes 4374528 | tf_op jit(solution)/shard_map/rest/pallas_call | solution.py:109
  39.3 3.9 %collective-permute-done.14.far_ref = bf16[16,32,128]{2,1,0:T(8,128)(2,1)S(1)} collective-permute-done((bf16[16,32,128]{2,1,0:T(8,128)(2,1)S(1)}, bf16[16,32,128]{2,1,0:T(8,128)(2,1)S(1)}, u32[]{:S(2)}, u32[]{:S(2)}) %collective-permute-start.14) | collective-permute-done | bytes 131104 | tf_op jit(solution)/shard_map/ppermute | solution.py:392
  43.3 2.4 %collective-permute-start.17 = (bf16[16,32,128]{2,1,0:T(8,128)(2,1)S(1)}, bf16[16,32,128]{2,1,0:T(8,128)(2,1)S(1)}, u32[]{:S(2)}, u32[]{:S(2)}) collective-permute-start(bf16[16,32,128]{2,1,0:T(8,128)(2,1)S(1)} %chip_sum.1._), channel_id=1, source_target_pairs={{0,4},{1,5},{2,6},{3,7},{4,0},{5,1},{6,2},{7,3},{8,12},{9,13},{10,... | collective-permute-start | bytes 393224 | tf_op jit(solution)/shard_map/ppermute | solution.py:392
  45.9 1.6 %collective-permute-start.15 = (bf16[448,256]{1,0:T(8,128)(2,1)S(1)}, bf16[448,256]{1,0:T(8,128)(2,1)S(1)}, u32[]{:S(2)}, u32[]{:S(2)}) collective-permute-start(bf16[448,256]{1,0:T(8,128)(2,1)S(1)} %get-tuple-element.63.a_ref), channel_id=1, source_target_pairs={{0,16},{8,24},{16,0},{24,8},{1,17},{9,25},{17,1},{25,9},{2,18},{10... | collective-permute-start | bytes 688136 | tf_op jit(solution)/shard_map/ppermute | solution.py:392
  48.5 3.1 %collective-permute-done.17.b_ref = bf16[16,32,128]{2,1,0:T(8,128)(2,1)S(1)} collective-permute-done((bf16[16,32,128]{2,1,0:T(8,128)(2,1)S(1)}, bf16[16,32,128]{2,1,0:T(8,128)(2,1)S(1)}, u32[]{:S(2)}, u32[]{:S(2)}) %collective-permute-start.17) | collective-permute-done | bytes 131104 | tf_op jit(solution)/shard_map/ppermute | solution.py:392
  51.7 2.2 %collective-permute-done.18.h_ref = bf16[16,32,128]{2,1,0:T(8,128)(2,1)S(1)} collective-permute-done((bf16[16,32,128]{2,1,0:T(8,128)(2,1)S(1)}, bf16[16,32,128]{2,1,0:T(8,128)(2,1)S(1)}, u32[]{:S(2)}, u32[]{:S(2)}) %collective-permute-start.18) | collective-permute-done | bytes 131104 | tf_op jit(solution)/shard_map/ppermute | solution.py:392
  53.9 1.1 %last.1 = (f32[27,32,256]{2,1,0:T(8,128)}, f32[1,32]{1,0:T(1,128)}, bf16[32,2,8,128]{3,2,1,0:T(8,128)(2,1)}) custom-call(bf16[448,256]{1,0:T(8,128)(2,1)S(1)} %get-tuple-element.63.a_ref, bf16[448,256]{1,0:T(8,128)(2,1)S(1)} %collective-permute-done.15.b_ref, bf16[448,256]{1,0:T(8,128)(2,1)S(1)} %get-tuple-element.64.c_ref, ...), custom_call_target="tpu_custom_call" | custom-call | bytes 2326656 | tf_op jit(solution)/shard_map/last/pallas_call | solution.py:109
  (25 shorter events, 3.5 us)
Async XLA Ops:
  0.6 10.7 %collective-permute-start = (bf16[32,2,8,128]{3,2,1,0:T(8,128)(2,1)}, bf16[32,2,8,128]{3,2,1,0:T(8,128)(2,1)S(1)}, u32[]{:S(2)}, u32[]{:S(2)}) collective-permute-start(bf16[32,2,8,128]{3,2,1,0:T(8,128)(2,1)} %x_hbm.1), channel_id=1, source_target_pairs={{0,4},{1,5},{2,6},{3,7},{4,0},{5,1},{6,2},{7,3},{8,12},{9,13},{10,... | collective-permute-start | bytes 393224 | tf_op jit(solution)/shard_map/ppermute | solution.py:392
  4.7 6.8 %collective-permute-start.2 = (bf16[32,2,8,128]{3,2,1,0:T(8,128)(2,1)}, bf16[32,2,8,128]{3,2,1,0:T(8,128)(2,1)S(1)}, u32[]{:S(2)}, u32[]{:S(2)}) collective-permute-start(bf16[32,2,8,128]{3,2,1,0:T(8,128)(2,1)} %x_hbm.1), channel_id=1, source_target_pairs={{0,2},{1,3},{2,0},{3,1},{4,6},{5,7},{6,4},{7,5},{8,10},{9,11},{10,... | collective-permute-start | bytes 393224 | tf_op jit(solution)/shard_map/ppermute | solution.py:392
  6.3 11.6 %collective-permute-start.3 = (bf16[32,2,8,128]{3,2,1,0:T(8,128)(2,1)}, bf16[32,2,8,128]{3,2,1,0:T(8,128)(2,1)S(1)}, u32[]{:S(2)}, u32[]{:S(2)}) collective-permute-start(bf16[32,2,8,128]{3,2,1,0:T(8,128)(2,1)} %x_hbm.1), channel_id=1, source_target_pairs={{0,1},{1,0},{2,3},{3,2},{4,5},{5,4},{6,7},{7,6},{8,9},{9,8},{10,11... | collective-permute-start | bytes 393224 | tf_op jit(solution)/shard_map/ppermute | solution.py:392
  11.6 6.3 %collective-permute-start.4 = (bf16[32,2,8,128]{3,2,1,0:T(8,128)(2,1)S(1)}, bf16[32,2,8,128]{3,2,1,0:T(8,128)(2,1)S(1)}, u32[]{:S(2)}, u32[]{:S(2)}) collective-permute-start(bf16[32,2,8,128]{3,2,1,0:T(8,128)(2,1)S(1)} %collective-permute-done.2.refs_1_), channel_id=1, source_target_pairs={{0,1},{1,0},{2,3},{3,2},{4,5},{5,4},{6,7},{7,6},{8,9},{9,8},{10,11... | collective-permute-start | bytes 393224 | tf_op jit(solution)/shard_map/ppermute | solution.py:392
  11.6 6.3 %collective-permute-start.5 = (bf16[32,2,8,128]{3,2,1,0:T(8,128)(2,1)S(1)}, bf16[32,2,8,128]{3,2,1,0:T(8,128)(2,1)S(1)}, u32[]{:S(2)}, u32[]{:S(2)}) collective-permute-start(bf16[32,2,8,128]{3,2,1,0:T(8,128)(2,1)S(1)} %collective-permute-done.refs_2_), channel_id=1, source_target_pairs={{0,1},{1,0},{2,3},{3,2},{4,5},{5,4},{6,7},{7,6},{8,9},{9,8},{10,11... | collective-permute-start | bytes 393224 | tf_op jit(solution)/shard_map/ppermute | solution.py:392
  12.1 6.4 %collective-permute-start.1 = (bf16[32,2,8,128]{3,2,1,0:T(8,128)(2,1)S(1)}, bf16[32,2,8,128]{3,2,1,0:T(8,128)(2,1)S(1)}, u32[]{:S(2)}, u32[]{:S(2)}) collective-permute-start(bf16[32,2,8,128]{3,2,1,0:T(8,128)(2,1)S(1)} %collective-permute-done.refs_2_), channel_id=1, source_target_pairs={{0,2},{1,3},{2,0},{3,1},{4,6},{5,7},{6,4},{7,5},{8,10},{9,11},{10,... | collective-permute-start | bytes 393224 | tf_op jit(solution)/shard_map/ppermute | solution.py:392
  13.5 4.4 %collective-permute-start.6 = (bf16[8,32,128]{2,1,0:T(8,128)(2,1)S(1)}, bf16[8,32,128]{2,1,0:T(8,128)(2,1)S(1)}, u32[]{:S(2)}, u32[]{:S(2)}) collective-permute-start(bf16[8,32,128]{2,1,0:T(8,128)(2,1)S(1)} %get-tuple-element.41), channel_id=1, source_target_pairs={{0,24},{8,0},{16,8},{24,16},{1,25},{9,1},{17,9},{25,17},{2,26},{10... | collective-permute-start | bytes 196616 | tf_op jit(solution)/shard_map/ppermute | solution.py:388
  18.5 2.4 %collective-permute-start.7 = (bf16[32,2,8,128]{3,2,1,0:T(8,128)(2,1)S(1)}, bf16[32,2,8,128]{3,2,1,0:T(8,128)(2,1)S(1)}, u32[]{:S(2)}, u32[]{:S(2)}) collective-permute-start(bf16[32,2,8,128]{3,2,1,0:T(8,128)(2,1)S(1)} %collective-permute-done.1.refs_0_), channel_id=1, source_target_pairs={{0,1},{1,0},{2,3},{3,2},{4,5},{5,4},{6,7},{7,6},{8,9},{9,8},{10,11... | collective-permute-start | bytes 393224 | tf_op jit(solution)/shard_map/ppermute | solution.py:392
  18.6 6.0 %collective-permute-start.8 = (bf16[8,32,128]{2,1,0:T(8,128)(2,1)S(1)}, bf16[8,32,128]{2,1,0:T(8,128)(2,1)S(1)}, u32[]{:S(2)}, u32[]{:S(2)}) collective-permute-start(bf16[8,32,128]{2,1,0:T(8,128)(2,1)S(1)} %get-tuple-element.47), channel_id=1, source_target_pairs={{0,8},{8,16},{16,24},{24,0},{1,9},{9,17},{17,25},{25,1},{2,10},{10... | collective-permute-start | bytes 196616 | tf_op jit(solution)/shard_map/ppermute | solution.py:388
  24.6 6.4 %collective-permute-start.10 = (bf16[16,32,128]{2,1,0:T(8,128)(2,1)S(1)}, bf16[16,32,128]{2,1,0:T(8,128)(2,1)S(1)}, u32[]{:S(2)}, u32[]{:S(2)}) collective-permute-start(bf16[16,32,128]{2,1,0:T(8,128)(2,1)S(1)} %get-tuple-element.48.low_ref), channel_id=1, source_target_pairs={{0,24},{8,0},{16,8},{24,16},{1,25},{9,1},{17,9},{25,17},{2,26},{10... | collective-permute-start | bytes 393224 | tf_op jit(solution)/shard_map/ppermute | solution.py:388
  26.4 6.4 %collective-permute-start.9 = (bf16[16,32,128]{2,1,0:T(8,128)(2,1)S(1)}, bf16[16,32,128]{2,1,0:T(8,128)(2,1)S(1)}, u32[]{:S(2)}, u32[]{:S(2)}) collective-permute-start(bf16[16,32,128]{2,1,0:T(8,128)(2,1)S(1)} %get-tuple-element.49.high_ref), channel_id=1, source_target_pairs={{0,8},{8,16},{16,24},{24,0},{1,9},{9,17},{17,25},{25,1},{2,10},{10... | collective-permute-start | bytes 393224 | tf_op jit(solution)/shard_map/ppermute | solution.py:388
  34.6 3.2 %collective-permute-start.11 = (bf16[4,16,32,128]{3,2,1,0:T(8,128)(2,1)S(1)}, bf16[4,16,32,128]{3,2,1,0:T(8,128)(2,1)S(1)}, u32[]{:S(2)}, u32[]{:S(2)}) collective-permute-start(bf16[4,16,32,128]{3,2,1,0:T(8,128)(2,1)S(1)} %get-tuple-element.57), channel_id=1, source_target_pairs={{0,1},{1,0},{2,3},{3,2},{4,5},{5,4},{6,7},{7,6},{8,9},{9,8},{10,11... | collective-permute-start | bytes 1572872 | tf_op jit(solution)/shard_map/ppermute | solution.py:392
  35.7 10.0 %collective-permute-start.12 = (bf16[448,256]{1,0:T(8,128)(2,1)S(1)}, bf16[448,256]{1,0:T(8,128)(2,1)S(1)}, u32[]{:S(2)}, u32[]{:S(2)}) collective-permute-start(bf16[448,256]{1,0:T(8,128)(2,1)S(1)} %get-tuple-element.60.a_ref), channel_id=1, source_target_pairs={{0,8},{8,0},{16,24},{24,16},{1,9},{9,1},{17,25},{25,17},{2,10},{10... | collective-permute-start | bytes 688136 | tf_op jit(solution)/shard_map/ppermute | solution.py:392
  37.3 8.4 %collective-permute-start.13 = (bf16[448,256]{1,0:T(8,128)(2,1)S(1)}, bf16[448,256]{1,0:T(8,128)(2,1)S(1)}, u32[]{:S(2)}, u32[]{:S(2)}) collective-permute-start(bf16[448,256]{1,0:T(8,128)(2,1)S(1)} %get-tuple-element.61.c_ref), channel_id=1, source_target_pairs={{0,16},{8,24},{16,0},{24,8},{1,17},{9,25},{17,1},{25,9},{2,18},{10... | collective-permute-start | bytes 688136 | tf_op jit(solution)/shard_map/ppermute | solution.py:392
  37.8 5.4 %collective-permute-start.14 = (bf16[16,32,128]{2,1,0:T(8,128)(2,1)S(1)}, bf16[16,32,128]{2,1,0:T(8,128)(2,1)S(1)}, u32[]{:S(2)}, u32[]{:S(2)}) collective-permute-start(bf16[16,32,128]{2,1,0:T(8,128)(2,1)S(1)} %core_sum.1), channel_id=1, source_target_pairs={{0,2},{1,3},{2,0},{3,1},{4,6},{5,7},{6,4},{7,5},{8,10},{9,11},{10,... | collective-permute-start | bytes 393224 | tf_op jit(solution)/shard_map/ppermute | solution.py:392
  43.3 8.4 %collective-permute-start.17 = (bf16[16,32,128]{2,1,0:T(8,128)(2,1)S(1)}, bf16[16,32,128]{2,1,0:T(8,128)(2,1)S(1)}, u32[]{:S(2)}, u32[]{:S(2)}) collective-permute-start(bf16[16,32,128]{2,1,0:T(8,128)(2,1)S(1)} %chip_sum.1._), channel_id=1, source_target_pairs={{0,4},{1,5},{2,6},{3,7},{4,0},{5,1},{6,2},{7,3},{8,12},{9,13},{10,... | collective-permute-start | bytes 393224 | tf_op jit(solution)/shard_map/ppermute | solution.py:392
  45.9 8.0 %collective-permute-start.15 = (bf16[448,256]{1,0:T(8,128)(2,1)S(1)}, bf16[448,256]{1,0:T(8,128)(2,1)S(1)}, u32[]{:S(2)}, u32[]{:S(2)}) collective-permute-start(bf16[448,256]{1,0:T(8,128)(2,1)S(1)} %get-tuple-element.63.a_ref), channel_id=1, source_target_pairs={{0,16},{8,24},{16,0},{24,8},{1,17},{9,25},{17,1},{25,9},{2,18},{10... | collective-permute-start | bytes 688136 | tf_op jit(solution)/shard_map/ppermute | solution.py:392
  47.5 6.5 %collective-permute-start.16 = (bf16[448,256]{1,0:T(8,128)(2,1)S(1)}, bf16[448,256]{1,0:T(8,128)(2,1)S(1)}, u32[]{:S(2)}, u32[]{:S(2)}) collective-permute-start(bf16[448,256]{1,0:T(8,128)(2,1)S(1)} %get-tuple-element.64.c_ref), channel_id=1, source_target_pairs={{0,8},{8,0},{16,24},{24,16},{1,9},{9,1},{17,25},{25,17},{2,10},{10... | collective-permute-start | bytes 688136 | tf_op jit(solution)/shard_map/ppermute | solution.py:392
  48.0 5.9 %collective-permute-start.18 = (bf16[16,32,128]{2,1,0:T(8,128)(2,1)S(1)}, bf16[16,32,128]{2,1,0:T(8,128)(2,1)S(1)}, u32[]{:S(2)}, u32[]{:S(2)}) collective-permute-start(bf16[16,32,128]{2,1,0:T(8,128)(2,1)S(1)} %get-tuple-element.66), channel_id=1, source_target_pairs={{0,2},{1,3},{2,0},{3,1},{4,6},{5,7},{6,4},{7,5},{8,10},{9,11},{10,... | collective-permute-start | bytes 393224 | tf_op jit(solution)/shard_map/ppermute | solution.py:392

commit v6 on v5

--- a/solution.py
+++ b/solution.py
@@ -10,7 +10,8 @@
 
 LANES = 128
 SUM_FLOPS = 20 * 10**8
-FORWARD_FLOPS = 0
+FORWARD_FLOPS = 9 * 10**8
+ASSEMBLE_FLOPS = 40 * 10**8
 VMEM = pl.BlockSpec(memory_space=pltpu.VMEM)
 ANY = pl.BlockSpec(memory_space=pl.ANY)
 HBM = pl.BlockSpec(memory_space=pltpu.HBM)
@@ -432,18 +433,19 @@
     go_below = rotate(go_high, "slab", 1)
     x_b, w_flat = lax.optimization_barrier((x_b, w_flat))
     x_ab = swap(x_b, "chan", 2)
+    late_b, go_above, go_below = lax.optimization_barrier((x_b, go_above, go_below))
     x_a_side = swap(x_a, "chan", 1)
-    x_b_side = swap(x_b, "chan", 1)
-    early, late = (0, 1, 2, 4, 5, 6), (3, 7)
+    x_b_side = swap(late_b, "chan", 1)
+    early, late = (0, 1, 2, 3, 4, 5, 6), (7,)
     (x_all,) = call(
         functools.partial(assemble_body, early),
         [shape_of((c_all, cells * depth), bf16)],
-        [me, x_own, x_a, x_b, x_side, x_a_side, x_b_side, go_above],
-        [SMEM] + [VMEM] * 6 + [ANY],
+        [me, x_own, x_a, x_b, x_ab, x_side, x_a_side, x_b_side],
+        [SMEM] + [VMEM] * 7,
         block_wide,
+        flops=ASSEMBLE_FLOPS,
         name="assemble",
     )
-    x_ab, x_all = lax.optimization_barrier((x_ab, x_all))
     x_ab_side = swap(x_ab, "chan", 1)
     own, low, high, x_all = call(
         functools.partial(forward_body, n, rows, o, late),
@@ -453,14 +455,13 @@
             shape_of((2 * rows, o, depth), bf16),
             shape_of((c_all, cells * depth), bf16),
         ],
-        [me, w_flat, x_ab, x_ab_side, x_all],
-        [SMEM] + [VMEM] * 4,
+        [me, w_flat, x_ab_side, x_all],
+        [SMEM] + [VMEM] * 3,
         [pltpu.VMEM((3, n + 2, rows, o, depth), f32), *block_wide],
         flops=FORWARD_FLOPS,
         name="forward",
-        aliases={4: 3},
-    )
-    low, high, go_below = lax.optimization_barrier((low, high, go_below))
+        aliases={3: 3},
+    )
     above = rotate(low, "slab", -1)
     below = rotate(high, "slab", 1)
     act, total, stacked, w_turned, other, far = call(

time: 55.2 us -> 50.7 us (0.918)
  waiting for transfers between devices: 23.5 us -> 19.6 us
    ppermute x15, waiting for transfers between devices: 13.2 us -> 9.65 us  [swap(): lax.ppermute(value, axis, [(i, i ^ bit) for i in range(lax.axis_size(axis...]
    ppermute x4, starting transfers between devices: 6.83 us -> 5.25 us  [rotate(): lax.ppermute(value, axis, [(i, (i + step) % count) for i in range(count)])]
    ppermute x15, starting transfers between devices: 15.5 us -> 16.5 us  [swap(): lax.ppermute(value, axis, [(i, i ^ bit) for i in range(lax.axis_size(axis...]
  transfers between devices with their start and end apart: 19 -> 19, of which waited for: 9 -> 13; matrix products, arithmetic and copies ran while one was open for 0% -> 0% of each run, Pallas kernels for 10% -> 8%
where the time goes in v6:
time: 50.7 us; the launch traced here: 50.6 us
  starting transfers between devices  21.8 us (43%)
  waiting for transfers between devices  19.6 us (39%)
  Pallas kernels  8.52 us (17%)
  between operations  0.7 us (1%)
    ppermute x15, starting transfers between devices, swap(): lax.ppermute(value, axis, [(i, i ^ bit) for i in range(lax.axis_size(axis...  16.5 us
    ppermute x4, waiting for transfers between devices, rotate(): lax.ppermute(value, axis, [(i, (i + step) % count) for i in range(count)])  9.92 us
    ppermute x15, waiting for transfers between devices, swap(): lax.ppermute(value, axis, [(i, i ^ bit) for i in range(lax.axis_size(axis...  9.65 us
    pallas_call x11, Pallas kernels, call(): pl.pallas_call(body, out_shape=out_shape, in_specs=specs or [VMEM] * len(...  8.52 us
    ppermute x4, starting transfers between devices, rotate(): lax.ppermute(value, axis, [(i, (i + step) % count) for i in range(count)])  5.25 us
  transfers between devices with their start and end apart: 19, of which 13 were waited for; matrix products, arithmetic and copies ran while one was open for 0% of the time, Pallas kernels for 8%

profile of v6, /device:TPU:0, one launch (start us, length us, event | category | flops | bytes accessed | tf_op | source)
XLA Modules:
  0.0 50.6 jit_solution(5136832497878440699)
XLA Ops:
  0.6 4.1 %collective-permute-start = (bf16[32,2,8,128]{3,2,1,0:T(8,128)(2,1)}, bf16[32,2,8,128]{3,2,1,0:T(8,128)(2,1)S(1)}, u32[]{:S(2)}, u32[]{:S(2)}) collective-permute-start(bf16[32,2,8,128]{3,2,1,0:T(8,128)(2,1)} %x_hbm.1), channel_id=1, source_target_pairs={{0,4},{1,5},{2,6},{3,7},{4,0},{5,1},{6,2},{7,3},{8,12},{9,13},{10,... | collective-permute-start | bytes 393224 | tf_op jit(solution)/shard_map/ppermute | solution.py:393
  4.7 1.6 %collective-permute-start.3 = (bf16[32,2,8,128]{3,2,1,0:T(8,128)(2,1)}, bf16[32,2,8,128]{3,2,1,0:T(8,128)(2,1)S(1)}, u32[]{:S(2)}, u32[]{:S(2)}) collective-permute-start(bf16[32,2,8,128]{3,2,1,0:T(8,128)(2,1)} %x_hbm.1), channel_id=1, source_target_pairs={{0,2},{1,3},{2,0},{3,1},{4,6},{5,7},{6,4},{7,5},{8,10},{9,11},{10,... | collective-permute-start | bytes 393224 | tf_op jit(solution)/shard_map/ppermute | solution.py:393
  6.3 1.4 %prepare.1 = (bf16[32,2,8,128]{3,2,1,0:T(8,128)(2,1)S(1)}, bf16[16,32,128]{2,1,0:T(8,128)(2,1)S(1)}, bf16[8,32,128]{2,1,0:T(8,128)(2,1)S(1)}, bf16[8,32,128]{2,1...) custom-call(bf16[32,2,8,128]{3,2,1,0:T(8,128)(2,1)} %x_hbm.1, ...), custom_call_target="tpu_custom_call" | custom-call | bytes 1998912 | tf_op jit(solution)/shard_map/prepare/pallas_call | solution.py:110
  7.7 2.5 %collective-permute-start.6 = (bf16[8,32,128]{2,1,0:T(8,128)(2,1)S(1)}, bf16[8,32,128]{2,1,0:T(8,128)(2,1)S(1)}, u32[]{:S(2)}, u32[]{:S(2)}) collective-permute-start(bf16[8,32,128]{2,1,0:T(8,128)(2,1)S(1)} %get-tuple-element.39), channel_id=1, source_target_pairs={{0,24},{8,0},{16,8},{24,16},{1,25},{9,1},{17,9},{25,17},{2,26},{10... | collective-permute-start | bytes 196616 | tf_op jit(solution)/shard_map/ppermute | solution.py:389
  10.2 1.2 %collective-permute-done.refs_2_ = bf16[32,2,8,128]{3,2,1,0:T(8,128)(2,1)S(1)} collective-permute-done((bf16[32,2,8,128]{3,2,1,0:T(8,128)(2,1)}, bf16[32,2,8,128]{3,2,1,0:T(8,128)(2,1)S(1)}, u32[]{:S(2)}, u32[]{:S(2)}) %collective-permute-start) | collective-permute-done | bytes 131104 | tf_op jit(solution)/shard_map/ppermute | solution.py:393
  11.4 0.7 %collective-permute-start.1 = (bf16[32,2,8,128]{3,2,1,0:T(8,128)(2,1)S(1)}, bf16[32,2,8,128]{3,2,1,0:T(8,128)(2,1)S(1)}, u32[]{:S(2)}, u32[]{:S(2)}) collective-permute-start(bf16[32,2,8,128]{3,2,1,0:T(8,128)(2,1)S(1)} %collective-permute-done.refs_2_), channel_id=1, source_target_pairs={{0,2},{1,3},{2,0},{3,1},{4,6},{5,7},{6,4},{7,5},{8,10},{9,11},{10,... | collective-permute-start | bytes 393224 | tf_op jit(solution)/shard_map/ppermute | solution.py:393
  12.4 3.0 %collective-permute-done.7.go_below_ref = bf16[8,32,128]{2,1,0:T(8,128)(2,1)S(1)} collective-permute-done((bf16[8,32,128]{2,1,0:T(8,128)(2,1)S(1)}, bf16[8,32,128]{2,1,0:T(8,128)(2,1)S(1)}, u32[]{:S(2)}, u32[]{:S(2)}) %collective-permute-start.7) | collective-permute-done | bytes 65568 | tf_op jit(solution)/shard_map/ppermute | solution.py:389
  16.9 0.7 %assemble.1.refs_1_ = bf16[256,2048]{1,0:T(8,128)(2,1)S(1)} custom-call(s32[1]{0:T(128)} %bitcast.me_ref, bf16[32,2,8,128]{3,2,1,0:T(8,128)(2,1)S(1)} %get-tuple-element.38.refs_0_, bf16[32,2,8,128]{3,2,1,0:T(8,128)(2,1)S(1)} %collective-permute-done.3.refs_1_, bf16[32,2,8,128]{3,2,1,0:T(8,128)(2,1)S(1)} %collective-permute-done.refs_2_, ...), custom_call_target="tpu_custom_call" | custom-call | flops 4000000000 | bytes 1966084 | tf_op jit(solution)/shard_map/assemble/pallas_call | solution.py:110
  17.7 1.3 %forward.1 = (f32[16,32,128]{2,1,0:T(8,128)S(1)}, bf16[16,32,128]{2,1,0:T(8,128)(2,1)S(1)}, bf16[16,32,128]{2,1,0:T(8,128)(2,1)S(1)}, bf16[256,2048]{1,0:T(8,128)(2,1)S(1)}) custom-call(s32[1]{0:T(128)} %bitcast.me_ref, bf16[864,256]{1,0:T(8,128)(2,1)S(1)} %get-tuple-element.36.w_ref, ...), custom_call_target="tpu_custom_call", output_to_operand_aliasing={{3}: (3, {})} | custom-call | flops 900000000 | bytes 3194884 | tf_op jit(solution)/shard_map/forward/pallas_call | solution.py:110
  19.0 2.8 %collective-permute-start.10 = (bf16[16,32,128]{2,1,0:T(8,128)(2,1)S(1)}, bf16[16,32,128]{2,1,0:T(8,128)(2,1)S(1)}, u32[]{:S(2)}, u32[]{:S(2)}) collective-permute-start(bf16[16,32,128]{2,1,0:T(8,128)(2,1)S(1)} %get-tuple-element.43.low_ref), channel_id=1, source_target_pairs={{0,24},{8,0},{16,8},{24,16},{1,25},{9,1},{17,9},{25,17},{2,26},{10... | collective-permute-start | bytes 393224 | tf_op jit(solution)/shard_map/ppermute | solution.py:389
  21.7 3.9 %collective-permute-done.10.above_ref = bf16[16,32,128]{2,1,0:T(8,128)(2,1)S(1)} collective-permute-done((bf16[16,32,128]{2,1,0:T(8,128)(2,1)S(1)}, bf16[16,32,128]{2,1,0:T(8,128)(2,1)S(1)}, u32[]{:S(2)}, u32[]{:S(2)}) %collective-permute-start.10) | collective-permute-done | bytes 131104 | tf_op jit(solution)/shard_map/ppermute | solution.py:389
  25.6 2.8 %collective-permute-done.9.below_ref = bf16[16,32,128]{2,1,0:T(8,128)(2,1)S(1)} collective-permute-done((bf16[16,32,128]{2,1,0:T(8,128)(2,1)S(1)}, bf16[16,32,128]{2,1,0:T(8,128)(2,1)S(1)}, u32[]{:S(2)}, u32[]{:S(2)}) %collective-permute-start.9) | collective-permute-done | bytes 131104 | tf_op jit(solution)/shard_map/ppermute | solution.py:389
  28.4 1.8 %gradient.1 = (bf16[32,2,8,128]{3,2,1,0:T(8,128)(2,1)}, f32[32,128]{1,0:T(8,128)S(1)}, bf16[864,2048]{1,0:T(8,128)(2,1)S(1)}, bf16[256,864]{1,0:T(8,128)(2,1)S(1...) custom-call(s32[1]{0:T(128)} %bitcast.me_ref, f32[16,32,128]{2,1,0:T(8,128)S(1)} %get-tuple-element.42.own_ref, ...), custom_call_target="tpu_custom_call" | custom-call | flops 452984832 | bytes 6291460 | tf_op jit(solution)/shard_map/gradient/pallas_call | solution.py:110
  30.2 1.1 %filter_grad.1 = (bf16[448,256]{1,0:T(8,128)(2,1)S(1)}, bf16[448,256]{1,0:T(8,128)(2,1)S(1)}) custom-call(bf16[864,2048]{1,0:T(8,128)(2,1)S(1)} %get-tuple-element.51.s_ref, bf16[256,2048]{1,0:T(8,128)(2,1)S(1)} %get-tuple-element.54.x_ref, f32[32,128]{1,0:T(8,128)S(1)} %get-tuple-element.55.total_ref), custom_call_target="tpu_custom_call" | custom-call | flops 905969664 | bytes 5062656 | tf_op jit(solution)/shard_map/filter_grad/pallas_call | solution.py:110
  31.4 1.8 %collective-permute-start.12 = (bf16[448,256]{1,0:T(8,128)(2,1)S(1)}, bf16[448,256]{1,0:T(8,128)(2,1)S(1)}, u32[]{:S(2)}, u32[]{:S(2)}) collective-permute-start(bf16[448,256]{1,0:T(8,128)(2,1)S(1)} %get-tuple-element.56.a_ref), channel_id=1, source_target_pairs={{0,8},{8,0},{16,24},{24,16},{1,9},{9,1},{17,25},{25,17},{2,10},{10... | collective-permute-start | bytes 688136 | tf_op jit(solution)/shard_map/ppermute | solution.py:393
  33.7 1.0 %collective-permute-start.14 = (bf16[16,32,128]{2,1,0:T(8,128)(2,1)S(1)}, bf16[16,32,128]{2,1,0:T(8,128)(2,1)S(1)}, u32[]{:S(2)}, u32[]{:S(2)}) collective-permute-start(bf16[16,32,128]{2,1,0:T(8,128)(2,1)S(1)} %core_sum.1), channel_id=1, source_target_pairs={{0,2},{1,3},{2,0},{3,1},{4,6},{5,7},{6,4},{7,5},{8,10},{9,11},{10,... | collective-permute-start | bytes 393224 | tf_op jit(solution)/shard_map/ppermute | solution.py:393
  34.6 0.8 %rest.1.rest_ref = bf16[3,16,32,128]{3,2,1,0:T(8,128)(2,1)S(1)} custom-call(bf16[864,2048]{1,0:T(8,128)(2,1)S(1)} %get-tuple-element.51.s_ref, bf16[256,864]{1,0:T(8,128)(2,1)S(1)} %get-tuple-element.52.w_ref), custom_call_target="tpu_custom_call" | custom-call | flops 452984832 | bytes 4374528 | tf_op jit(solution)/shard_map/rest/pallas_call | solution.py:110
  35.4 3.6 %collective-permute-done.14.far_ref = bf16[16,32,128]{2,1,0:T(8,128)(2,1)S(1)} collective-permute-done((bf16[16,32,128]{2,1,0:T(8,128)(2,1)S(1)}, bf16[16,32,128]{2,1,0:T(8,128)(2,1)S(1)}, u32[]{:S(2)}, u32[]{:S(2)}) %collective-permute-start.14) | collective-permute-done | bytes 131104 | tf_op jit(solution)/shard_map/ppermute | solution.py:393
  39.1 2.5 %collective-permute-start.17 = (bf16[16,32,128]{2,1,0:T(8,128)(2,1)S(1)}, bf16[16,32,128]{2,1,0:T(8,128)(2,1)S(1)}, u32[]{:S(2)}, u32[]{:S(2)}) collective-permute-start(bf16[16,32,128]{2,1,0:T(8,128)(2,1)S(1)} %chip_sum.1._), channel_id=1, source_target_pairs={{0,4},{1,5},{2,6},{3,7},{4,0},{5,1},{6,2},{7,3},{8,12},{9,13},{10,... | collective-permute-start | bytes 393224 | tf_op jit(solution)/shard_map/ppermute | solution.py:393
  41.8 1.6 %collective-permute-start.15 = (bf16[448,256]{1,0:T(8,128)(2,1)S(1)}, bf16[448,256]{1,0:T(8,128)(2,1)S(1)}, u32[]{:S(2)}, u32[]{:S(2)}) collective-permute-start(bf16[448,256]{1,0:T(8,128)(2,1)S(1)} %get-tuple-element.59.a_ref), channel_id=1, source_target_pairs={{0,16},{8,24},{16,0},{24,8},{1,17},{9,25},{17,1},{25,9},{2,18},{10... | collective-permute-start | bytes 688136 | tf_op jit(solution)/shard_map/ppermute | solution.py:393
  43.9 1.7 %collective-permute-start.18 = (bf16[16,32,128]{2,1,0:T(8,128)(2,1)S(1)}, bf16[16,32,128]{2,1,0:T(8,128)(2,1)S(1)}, u32[]{:S(2)}, u32[]{:S(2)}) collective-permute-start(bf16[16,32,128]{2,1,0:T(8,128)(2,1)S(1)} %get-tuple-element.62), channel_id=1, source_target_pairs={{0,2},{1,3},{2,0},{3,1},{4,6},{5,7},{6,4},{7,5},{8,10},{9,11},{10,... | collective-permute-start | bytes 393224 | tf_op jit(solution)/shard_map/ppermute | solution.py:393
  45.7 1.8 %collective-permute-done.17.b_ref = bf16[16,32,128]{2,1,0:T(8,128)(2,1)S(1)} collective-permute-done((bf16[16,32,128]{2,1,0:T(8,128)(2,1)S(1)}, bf16[16,32,128]{2,1,0:T(8,128)(2,1)S(1)}, u32[]{:S(2)}, u32[]{:S(2)}) %collective-permute-start.17) | collective-permute-done | bytes 131104 | tf_op jit(solution)/shard_map/ppermute | solution.py:393
  47.5 1.7 %collective-permute-done.18.h_ref = bf16[16,32,128]{2,1,0:T(8,128)(2,1)S(1)} collective-permute-done((bf16[16,32,128]{2,1,0:T(8,128)(2,1)S(1)}, bf16[16,32,128]{2,1,0:T(8,128)(2,1)S(1)}, u32[]{:S(2)}, u32[]{:S(2)}) %collective-permute-start.18) | collective-permute-done | bytes 131104 | tf_op jit(solution)/shard_map/ppermute | solution.py:393
  49.5 1.1 %last.1 = (f32[27,32,256]{2,1,0:T(8,128)}, f32[1,32]{1,0:T(1,128)}, bf16[32,2,8,128]{3,2,1,0:T(8,128)(2,1)}) custom-call(bf16[448,256]{1,0:T(8,128)(2,1)S(1)} %get-tuple-element.59.a_ref, bf16[448,256]{1,0:T(8,128)(2,1)S(1)} %collective-permute-done.15.b_ref, bf16[448,256]{1,0:T(8,128)(2,1)S(1)} %get-tuple-element.60.c_ref, ...), custom_call_target="tpu_custom_call" | custom-call | bytes 2326656 | tf_op jit(solution)/shard_map/last/pallas_call | solution.py:110
  (25 shorter events, 3.4 us)
Async XLA Ops:
  0.6 10.7 %collective-permute-start = (bf16[32,2,8,128]{3,2,1,0:T(8,128)(2,1)}, bf16[32,2,8,128]{3,2,1,0:T(8,128)(2,1)S(1)}, u32[]{:S(2)}, u32[]{:S(2)}) collective-permute-start(bf16[32,2,8,128]{3,2,1,0:T(8,128)(2,1)} %x_hbm.1), channel_id=1, source_target_pairs={{0,4},{1,5},{2,6},{3,7},{4,0},{5,1},{6,2},{7,3},{8,12},{9,13},{10,... | collective-permute-start | bytes 393224 | tf_op jit(solution)/shard_map/ppermute | solution.py:393
  4.7 10.6 %collective-permute-start.3 = (bf16[32,2,8,128]{3,2,1,0:T(8,128)(2,1)}, bf16[32,2,8,128]{3,2,1,0:T(8,128)(2,1)S(1)}, u32[]{:S(2)}, u32[]{:S(2)}) collective-permute-start(bf16[32,2,8,128]{3,2,1,0:T(8,128)(2,1)} %x_hbm.1), channel_id=1, source_target_pairs={{0,2},{1,3},{2,0},{3,1},{4,6},{5,7},{6,4},{7,5},{8,10},{9,11},{10,... | collective-permute-start | bytes 393224 | tf_op jit(solution)/shard_map/ppermute | solution.py:393
  7.7 4.7 %collective-permute-start.6 = (bf16[8,32,128]{2,1,0:T(8,128)(2,1)S(1)}, bf16[8,32,128]{2,1,0:T(8,128)(2,1)S(1)}, u32[]{:S(2)}, u32[]{:S(2)}) collective-permute-start(bf16[8,32,128]{2,1,0:T(8,128)(2,1)S(1)} %get-tuple-element.39), channel_id=1, source_target_pairs={{0,24},{8,0},{16,8},{24,16},{1,25},{9,1},{17,9},{25,17},{2,26},{10... | collective-permute-start | bytes 196616 | tf_op jit(solution)/shard_map/ppermute | solution.py:389
  10.2 5.2 %collective-permute-start.7 = (bf16[8,32,128]{2,1,0:T(8,128)(2,1)S(1)}, bf16[8,32,128]{2,1,0:T(8,128)(2,1)S(1)}, u32[]{:S(2)}, u32[]{:S(2)}) collective-permute-start(bf16[8,32,128]{2,1,0:T(8,128)(2,1)S(1)} %get-tuple-element.40), channel_id=1, source_target_pairs={{0,8},{8,16},{16,24},{24,0},{1,9},{9,17},{17,25},{25,1},{2,10},{10... | collective-permute-start | bytes 196616 | tf_op jit(solution)/shard_map/ppermute | solution.py:389
  10.2 6.2 %collective-permute-start.4 = (bf16[32,2,8,128]{3,2,1,0:T(8,128)(2,1)}, bf16[32,2,8,128]{3,2,1,0:T(8,128)(2,1)S(1)}, u32[]{:S(2)}, u32[]{:S(2)}) collective-permute-start(bf16[32,2,8,128]{3,2,1,0:T(8,128)(2,1)} %x_hbm.1), channel_id=1, source_target_pairs={{0,1},{1,0},{2,3},{3,2},{4,5},{5,4},{6,7},{7,6},{8,9},{9,8},{10,11... | collective-permute-start | bytes 393224 | tf_op jit(solution)/shard_map/ppermute | solution.py:393
  11.4 5.0 %collective-permute-start.1 = (bf16[32,2,8,128]{3,2,1,0:T(8,128)(2,1)S(1)}, bf16[32,2,8,128]{3,2,1,0:T(8,128)(2,1)S(1)}, u32[]{:S(2)}, u32[]{:S(2)}) collective-permute-start(bf16[32,2,8,128]{3,2,1,0:T(8,128)(2,1)S(1)} %collective-permute-done.refs_2_), channel_id=1, source_target_pairs={{0,2},{1,3},{2,0},{3,1},{4,6},{5,7},{6,4},{7,5},{8,10},{9,11},{10,... | collective-permute-start | bytes 393224 | tf_op jit(solution)/shard_map/ppermute | solution.py:393
  15.3 1.3 %collective-permute-start.5 = (bf16[32,2,8,128]{3,2,1,0:T(8,128)(2,1)S(1)}, bf16[32,2,8,128]{3,2,1,0:T(8,128)(2,1)S(1)}, u32[]{:S(2)}, u32[]{:S(2)}) collective-permute-start(bf16[32,2,8,128]{3,2,1,0:T(8,128)(2,1)S(1)} %collective-permute-done.3.refs_1_), channel_id=1, source_target_pairs={{0,1},{1,0},{2,3},{3,2},{4,5},{5,4},{6,7},{7,6},{8,9},{9,8},{10,11... | collective-permute-start | bytes 393224 | tf_op jit(solution)/shard_map/ppermute | solution.py:393
  15.4 1.5 %collective-permute-start.8 = (bf16[32,2,8,128]{3,2,1,0:T(8,128)(2,1)S(1)}, bf16[32,2,8,128]{3,2,1,0:T(8,128)(2,1)S(1)}, u32[]{:S(2)}, u32[]{:S(2)}) collective-permute-start(bf16[32,2,8,128]{3,2,1,0:T(8,128)(2,1)S(1)} %collective-permute-done.refs_2_), channel_id=1, source_target_pairs={{0,1},{1,0},{2,3},{3,2},{4,5},{5,4},{6,7},{7,6},{8,9},{9,8},{10,11... | collective-permute-start | bytes 393224 | tf_op jit(solution)/shard_map/ppermute | solution.py:393
  16.3 1.3 %collective-permute-start.2 = (bf16[32,2,8,128]{3,2,1,0:T(8,128)(2,1)S(1)}, bf16[32,2,8,128]{3,2,1,0:T(8,128)(2,1)S(1)}, u32[]{:S(2)}, u32[]{:S(2)}) collective-permute-start(bf16[32,2,8,128]{3,2,1,0:T(8,128)(2,1)S(1)} %collective-permute-done.1.refs_3_), channel_id=1, source_target_pairs={{0,1},{1,0},{2,3},{3,2},{4,5},{5,4},{6,7},{7,6},{8,9},{9,8},{10,11... | collective-permute-start | bytes 393224 | tf_op jit(solution)/shard_map/ppermute | solution.py:393
  19.0 6.6 %collective-permute-start.10 = (bf16[16,32,128]{2,1,0:T(8,128)(2,1)S(1)}, bf16[16,32,128]{2,1,0:T(8,128)(2,1)S(1)}, u32[]{:S(2)}, u32[]{:S(2)}) collective-permute-start(bf16[16,32,128]{2,1,0:T(8,128)(2,1)S(1)} %get-tuple-element.43.low_ref), channel_id=1, source_target_pairs={{0,24},{8,0},{16,8},{24,16},{1,25},{9,1},{17,9},{25,17},{2,26},{10... | collective-permute-start | bytes 393224 | tf_op jit(solution)/shard_map/ppermute | solution.py:389
  21.7 6.7 %collective-permute-start.9 = (bf16[16,32,128]{2,1,0:T(8,128)(2,1)S(1)}, bf16[16,32,128]{2,1,0:T(8,128)(2,1)S(1)}, u32[]{:S(2)}, u32[]{:S(2)}) collective-permute-start(bf16[16,32,128]{2,1,0:T(8,128)(2,1)S(1)} %get-tuple-element.44.high_ref), channel_id=1, source_target_pairs={{0,8},{8,16},{16,24},{24,0},{1,9},{9,17},{17,25},{25,1},{2,10},{10... | collective-permute-start | bytes 393224 | tf_op jit(solution)/shard_map/ppermute | solution.py:389
  30.2 3.4 %collective-permute-start.11 = (bf16[4,16,32,128]{3,2,1,0:T(8,128)(2,1)S(1)}, bf16[4,16,32,128]{3,2,1,0:T(8,128)(2,1)S(1)}, u32[]{:S(2)}, u32[]{:S(2)}) collective-permute-start(bf16[4,16,32,128]{3,2,1,0:T(8,128)(2,1)S(1)} %get-tuple-element.53), channel_id=1, source_target_pairs={{0,1},{1,0},{2,3},{3,2},{4,5},{5,4},{6,7},{7,6},{8,9},{9,8},{10,11... | collective-permute-start | bytes 1572872 | tf_op jit(solution)/shard_map/ppermute | solution.py:393
  31.4 10.3 %collective-permute-start.12 = (bf16[448,256]{1,0:T(8,128)(2,1)S(1)}, bf16[448,256]{1,0:T(8,128)(2,1)S(1)}, u32[]{:S(2)}, u32[]{:S(2)}) collective-permute-start(bf16[448,256]{1,0:T(8,128)(2,1)S(1)} %get-tuple-element.56.a_ref), channel_id=1, source_target_pairs={{0,8},{8,0},{16,24},{24,16},{1,9},{9,1},{17,25},{25,17},{2,10},{10... | collective-permute-start | bytes 688136 | tf_op jit(solution)/shard_map/ppermute | solution.py:393
  33.1 8.5 %collective-permute-start.13 = (bf16[448,256]{1,0:T(8,128)(2,1)S(1)}, bf16[448,256]{1,0:T(8,128)(2,1)S(1)}, u32[]{:S(2)}, u32[]{:S(2)}) collective-permute-start(bf16[448,256]{1,0:T(8,128)(2,1)S(1)} %get-tuple-element.57.c_ref), channel_id=1, source_target_pairs={{0,16},{8,24},{16,0},{24,8},{1,17},{9,25},{17,1},{25,9},{2,18},{10... | collective-permute-start | bytes 688136 | tf_op jit(solution)/shard_map/ppermute | solution.py:393
  33.7 5.4 %collective-permute-start.14 = (bf16[16,32,128]{2,1,0:T(8,128)(2,1)S(1)}, bf16[16,32,128]{2,1,0:T(8,128)(2,1)S(1)}, u32[]{:S(2)}, u32[]{:S(2)}) collective-permute-start(bf16[16,32,128]{2,1,0:T(8,128)(2,1)S(1)} %core_sum.1), channel_id=1, source_target_pairs={{0,2},{1,3},{2,0},{3,1},{4,6},{5,7},{6,4},{7,5},{8,10},{9,11},{10,... | collective-permute-start | bytes 393224 | tf_op jit(solution)/shard_map/ppermute | solution.py:393
  39.1 8.4 %collective-permute-start.17 = (bf16[16,32,128]{2,1,0:T(8,128)(2,1)S(1)}, bf16[16,32,128]{2,1,0:T(8,128)(2,1)S(1)}, u32[]{:S(2)}, u32[]{:S(2)}) collective-permute-start(bf16[16,32,128]{2,1,0:T(8,128)(2,1)S(1)} %chip_sum.1._), channel_id=1, source_target_pairs={{0,4},{1,5},{2,6},{3,7},{4,0},{5,1},{6,2},{7,3},{8,12},{9,13},{10,... | collective-permute-start | bytes 393224 | tf_op jit(solution)/shard_map/ppermute | solution.py:393
  41.8 7.4 %collective-permute-start.15 = (bf16[448,256]{1,0:T(8,128)(2,1)S(1)}, bf16[448,256]{1,0:T(8,128)(2,1)S(1)}, u32[]{:S(2)}, u32[]{:S(2)}) collective-permute-start(bf16[448,256]{1,0:T(8,128)(2,1)S(1)} %get-tuple-element.59.a_ref), channel_id=1, source_target_pairs={{0,16},{8,24},{16,0},{24,8},{1,17},{9,25},{17,1},{25,9},{2,18},{10... | collective-permute-start | bytes 688136 | tf_op jit(solution)/shard_map/ppermute | solution.py:393
  43.4 6.0 %collective-permute-start.16 = (bf16[448,256]{1,0:T(8,128)(2,1)S(1)}, bf16[448,256]{1,0:T(8,128)(2,1)S(1)}, u32[]{:S(2)}, u32[]{:S(2)}) collective-permute-start(bf16[448,256]{1,0:T(8,128)(2,1)S(1)} %get-tuple-element.60.c_ref), channel_id=1, source_target_pairs={{0,8},{8,0},{16,24},{24,16},{1,9},{9,1},{17,25},{25,17},{2,10},{10... | collective-permute-start | bytes 688136 | tf_op jit(solution)/shard_map/ppermute | solution.py:393
  43.9 5.3 %collective-permute-start.18 = (bf16[16,32,128]{2,1,0:T(8,128)(2,1)S(1)}, bf16[16,32,128]{2,1,0:T(8,128)(2,1)S(1)}, u32[]{:S(2)}, u32[]{:S(2)}) collective-permute-start(bf16[16,32,128]{2,1,0:T(8,128)(2,1)S(1)} %get-tuple-element.62), channel_id=1, source_target_pairs={{0,2},{1,3},{2,0},{3,1},{4,6},{5,7},{6,4},{7,5},{8,10},{9,11},{10,... | collective-permute-start | bytes 393224 | tf_op jit(solution)/shard_map/ppermute | solution.py:393

commit v7 on v6

--- a/solution.py
+++ b/solution.py
@@ -9,8 +9,8 @@
 from jax.sharding import PartitionSpec as P
 
 LANES = 128
+FORWARD_FLOPS = 9 * 10**8
 SUM_FLOPS = 20 * 10**8
-FORWARD_FLOPS = 9 * 10**8
 ASSEMBLE_FLOPS = 40 * 10**8
 VMEM = pl.BlockSpec(memory_space=pltpu.VMEM)
 ANY = pl.BlockSpec(memory_space=pl.ANY)
@@ -260,9 +260,9 @@
     act_ref,
     total_ref,
     s_ref,
+    other_ref,
+    mine_ref,
     w_ref,
-    other_ref,
-    far_ref,
     wide_ref,
 ):
     f32, bf16 = jnp.float32, jnp.bfloat16
@@ -307,7 +307,7 @@
     total_ref[...] = jnp.broadcast_to(
         jnp.sum(total, axis=1, keepdims=True) * scale, total_ref.shape
     )
-    input_grad(n * rows, o, w_ref[3 * o :], s_ref, [(far_ref, None)] + [(other_ref, r) for r in range(4)])
+    input_grad(n * rows, o, w_ref[...], s_ref, [(ref, r) for ref in (mine_ref, other_ref) for r in range(4)])
 
 
 def input_grad(cells, o, w, s_ref, outs):
@@ -318,15 +318,7 @@
         for h in range(2):
             for r, (out_ref, at) in enumerate(outs):
                 cut = part[r * o : (r + 1) * o, h * LANES : (h + 1) * LANES]
-                if at is None:
-                    out_ref[t + h] = cut
-                else:
-                    out_ref[at, t + h] = cut
-
-
-def rest_body(o, s_ref, w_ref, out_ref):
-    cells = out_ref.shape[1]
-    input_grad(cells, o, w_ref[: 3 * o], s_ref, [(out_ref, r) for r in range(3)])
+                out_ref[at, t + h] = cut
 
 
 def filter_grad_body(scale, taps, o, s_ref, x_ref, total_ref, first_ref, second_ref):
@@ -340,35 +332,32 @@
     second_ref[(27 - taps) * o :] = row.astype(second_ref.dtype)
 
 
-def second_body(rest_ref, other_ref, a_ref, b_ref, c_ref, d_ref, _, own_ref, near_ref, ab_ref, cd_ref):
+def pair_body(a_ref, b_ref, c_ref, d_ref, _, ab_ref, cd_ref):
     f32 = jnp.float32
     ab_ref[...] = (a_ref[...].astype(f32) + b_ref[...].astype(f32)).astype(ab_ref.dtype)
     cd_ref[...] = (c_ref[...].astype(f32) + d_ref[...].astype(f32)).astype(cd_ref.dtype)
-    own_ref[...] = rest_ref[0].astype(f32) + other_ref[0].astype(f32)
-    near_ref[...] = (rest_ref[1].astype(f32) + other_ref[1].astype(f32)).astype(near_ref.dtype)
-
-
-def core_sum_body(mine_ref, other_ref, out_ref):
-    total = mine_ref[...].astype(jnp.float32) + other_ref[3].astype(jnp.float32)
-    out_ref[...] = total.astype(out_ref.dtype)
-
-
-def chip_sum_body(rest_ref, other_ref, far_ref, b_ref):
+
+
+def core_sum_body(mine_ref, other_ref, *outs):
+    for r, out_ref in enumerate(outs):
+        total = mine_ref[r].astype(jnp.float32) + other_ref[r].astype(jnp.float32)
+        out_ref[...] = total.astype(out_ref.dtype)
+
+
+def sum_body(a_ref, b_ref, c_ref, d_ref, out_ref):
     f32 = jnp.float32
-    total = rest_ref[2].astype(f32) + other_ref[2].astype(f32) + far_ref[...].astype(f32)
-    b_ref[...] = total.astype(b_ref.dtype)
-
-
-def sum_body(a_ref, b_ref, out_ref):
-    out_ref[...] = a_ref[...] + b_ref[...].astype(jnp.float32)
-
-
-def last_body(taps, a_ref, b_ref, c_ref, d_ref, g_ref, h_ref, out_ref, bias_ref, grad_ref, wide_ref):
+    total = b_ref[...].astype(f32) + c_ref[...].astype(f32) + d_ref[...].astype(f32)
+    out_ref[...] = a_ref[...] + total
+
+
+def last_body(
+    taps, a_ref, b_ref, c_ref, d_ref, g_ref, out_ref, bias_ref, grad_ref, wide_ref
+):
     o = out_ref.shape[1]
     f32 = jnp.float32
     cells = g_ref.shape[0]
     for k in range(cells):
-        wide_ref[pl.ds(k, o, stride=cells), :] = g_ref[k] + h_ref[k].astype(f32)
+        wide_ref[pl.ds(k, o, stride=cells), :] = g_ref[k]
     grad_ref[...] = wide_ref[...].reshape(grad_ref.shape).astype(grad_ref.dtype)
     for k in range(27):
         left, right, at = (a_ref, b_ref, k) if k < taps else (c_ref, d_ref, k - taps)
@@ -404,6 +393,7 @@
 
     block_wide = [pltpu.VMEM((o * cells, depth), f32)]
 
+    x_ab = swap(x_in, "chan", 6)
     x_b = swap(x_in, "chan", 4)
     x_a = swap(x_in, "chan", 2)
     x_side = swap(x_in, "chan", 1)
@@ -432,10 +422,9 @@
     go_above = rotate(go_low, "slab", -1)
     go_below = rotate(go_high, "slab", 1)
     x_b, w_flat = lax.optimization_barrier((x_b, w_flat))
-    x_ab = swap(x_b, "chan", 2)
-    late_b, go_above, go_below = lax.optimization_barrier((x_b, go_above, go_below))
+    late_ab, go_above, go_below = lax.optimization_barrier((x_ab, go_above, go_below))
     x_a_side = swap(x_a, "chan", 1)
-    x_b_side = swap(late_b, "chan", 1)
+    x_b_side = swap(x_b, "chan", 1)
     early, late = (0, 1, 2, 3, 4, 5, 6), (7,)
     (x_all,) = call(
         functools.partial(assemble_body, early),
@@ -446,7 +435,7 @@
         flops=ASSEMBLE_FLOPS,
         name="assemble",
     )
-    x_ab_side = swap(x_ab, "chan", 1)
+    x_ab_side = swap(late_ab, "chan", 1)
     own, low, high, x_all = call(
         functools.partial(forward_body, n, rows, o, late),
         [
@@ -464,20 +453,19 @@
     )
     above = rotate(low, "slab", -1)
     below = rotate(high, "slab", 1)
-    act, total, stacked, w_turned, other, far = call(
+    act, total, stacked, other, mine = call(
         functools.partial(gradient_body, n, rows, o, scale),
         [
             shape_of((o, n, rows, depth), bf16),
             shape_of((o, LANES), f32),
             shape_of((27 * o, cells * depth), bf16),
-            shape_of((c_all, 27 * o), bf16),
             shape_of((4, cells, o, depth), bf16),
-            shape_of((cells, o, depth), bf16),
+            shape_of((4, cells, o, depth), bf16),
         ],
         [me, own, low, high, below, above, bias, go, go_below, go_above, w_back],
         [SMEM] + [VMEM] * 10,
-        block_wide,
-        flops=flops // 2,
+        [pltpu.VMEM((c_all, 27 * o), bf16), *block_wide],
+        flops=flops,
         name="gradient",
     )
     other = swap(other, "chan", 1)
@@ -491,38 +479,28 @@
     )
     first_far = swap(first, "slab", 1)
     second_far = swap(second, "slab", 2)
-    (far,) = call(core_sum_body, [shape_of(far.shape, bf16)], [far, other], name="core_sum")
-    far = swap(far, "chan", 2)
-    (rest,) = call(
-        functools.partial(rest_body, o),
-        [shape_of((3, cells, o, depth), bf16)],
-        [stacked, w_turned],
-        flops=flops // 2,
-        name="rest",
-    )
-    (far,) = call(
-        chip_sum_body, [shape_of((cells, o, depth), bf16)], [rest, other, far], name="chip_sum"
-    )
-    across = swap(far, "chan", 4)
-    own_sum, near, first, second = call(
-        second_body,
-        [
-            shape_of((cells, o, depth), f32),
-            shape_of((cells, o, depth), bf16),
-            shape_of(first.shape, bf16),
-            shape_of(second.shape, bf16),
-        ],
-        [rest, other, first, first_far, second, second_far, far],
-        [VMEM] * 6 + [ANY],
-        name="second_sum",
+    g_own, g_a, g_b, g_ab = call(
+        core_sum_body,
+        [shape_of((cells, o, depth), f32)] + [shape_of((cells, o, depth), bf16)] * 3,
+        [mine, other],
+        name="core_sum",
+    )
+    g_ab = swap(g_ab, "chan", 6)
+    g_b = swap(g_b, "chan", 4)
+    g_a = swap(g_a, "chan", 2)
+    first, second = call(
+        pair_body,
+        [shape_of(first.shape, bf16), shape_of(second.shape, bf16)],
+        [first, first_far, second, second_far, g_own],
+        [VMEM] * 4 + [ANY],
+        name="pair_sum",
     )
     first_far = swap(first, "slab", 2)
     second_far = swap(second, "slab", 1)
-    near = swap(near, "chan", 2)
-    (own_sum,) = call(
+    (g_own,) = call(
         sum_body,
         [shape_of((cells, o, depth), f32)],
-        [own_sum, across],
+        [g_own, g_ab, g_b, g_a],
         flops=SUM_FLOPS,
         name="sum",
     )
@@ -533,7 +511,7 @@
             shape_of((1, o), f32),
             shape_of((o, n, rows, depth), bf16),
         ],
-        [first, first_far, second, second_far, own_sum, near],
+        [first, first_far, second, second_far, g_own],
         scratch=block_wide,
         name="last",
     )

time: 50.7 us -> 50.7 us (level)
  waiting for transfers between devices: 19.6 us -> 20.7 us
  Pallas kernels: 8.52 us -> 7.61 us
    ppermute x15, starting transfers between devices: 16.5 us -> 14.4 us  [swap(): lax.ppermute(value, axis, [(i, i ^ bit) for i in range(lax.axis_size(axis...]
    ppermute x4, starting transfers between devices: 5.25 us -> 7.02 us  [rotate(): lax.ppermute(value, axis, [(i, (i + step) % count) for i in range(count)])]
    pallas_call x11 -> x9, Pallas kernels: 8.52 us -> 7.61 us  [call(): pl.pallas_call(body, out_shape=out_shape, in_specs=specs or [VMEM] * len(...]
    ppermute x15, waiting for transfers between devices: 9.65 us -> 10.5 us  [swap(): lax.ppermute(value, axis, [(i, i ^ bit) for i in range(lax.axis_size(axis...]
  transfers between devices with their start and end apart: 19 -> 19, of which waited for: 13 -> 9; matrix products, arithmetic and copies ran while one was open for 0% -> 0% of each run, Pallas kernels for 8% -> 7%
where the time goes in v7:
time: 50.7 us; the launch traced here: 50.5 us
  starting transfers between devices  21.4 us (42%)
  waiting for transfers between devices  20.7 us (41%)
  Pallas kernels  7.61 us (15%)
  between operations  0.74 us (1%)
    ppermute x15, starting transfers between devices, swap(): lax.ppermute(value, axis, [(i, i ^ bit) for i in range(lax.axis_size(axis...  14.4 us
    ppermute x15, waiting for transfers between devices, swap(): lax.ppermute(value, axis, [(i, i ^ bit) for i in range(lax.axis_size(axis...  10.5 us
    ppermute x4, waiting for transfers between devices, rotate(): lax.ppermute(value, axis, [(i, (i + step) % count) for i in range(count)])  10.2 us
    pallas_call x9, Pallas kernels, call(): pl.pallas_call(body, out_shape=out_shape, in_specs=specs or [VMEM] * len(...  7.61 us
    ppermute x4, starting transfers between devices, rotate(): lax.ppermute(value, axis, [(i, (i + step) % count) for i in range(count)])  7.02 us
  transfers between devices with their start and end apart: 19, of which 9 were waited for; matrix products, arithmetic and copies ran while one was open for 0% of the time, Pallas kernels for 7%

profile of v7, /device:TPU:0, one launch (start us, length us, event | category | flops | bytes accessed | tf_op | source)
XLA Modules:
  0.0 50.5 jit_solution(1639003171961039968)
XLA Ops:
  0.6 4.1 %collective-permute-start = (bf16[32,2,8,128]{3,2,1,0:T(8,128)(2,1)}, bf16[32,2,8,128]{3,2,1,0:T(8,128)(2,1)S(1)}, u32[]{:S(2)}, u32[]{:S(2)}) collective-permute-start(bf16[32,2,8,128]{3,2,1,0:T(8,128)(2,1)} %x_hbm.1), channel_id=1, source_target_pairs={{0,4},{1,5},{2,6},{3,7},{4,0},{5,1},{6,2},{7,3},{8,12},{9,13},{10,... | collective-permute-start | bytes 393224 | tf_op jit(solution)/shard_map/ppermute | solution.py:382
  4.7 1.6 %collective-permute-start.5 = (bf16[32,2,8,128]{3,2,1,0:T(8,128)(2,1)}, bf16[32,2,8,128]{3,2,1,0:T(8,128)(2,1)S(1)}, u32[]{:S(2)}, u32[]{:S(2)}) collective-permute-start(bf16[32,2,8,128]{3,2,1,0:T(8,128)(2,1)} %x_hbm.1), channel_id=1, source_target_pairs={{0,2},{1,3},{2,0},{3,1},{4,6},{5,7},{6,4},{7,5},{8,10},{9,11},{10,... | collective-permute-start | bytes 393224 | tf_op jit(solution)/shard_map/ppermute | solution.py:382
  6.3 1.4 %prepare.1 = (bf16[32,2,8,128]{3,2,1,0:T(8,128)(2,1)S(1)}, bf16[16,32,128]{2,1,0:T(8,128)(2,1)S(1)}, bf16[8,32,128]{2,1,0:T(8,128)(2,1)S(1)}, bf16[8,32,128]{2,1...) custom-call(bf16[32,2,8,128]{3,2,1,0:T(8,128)(2,1)} %x_hbm.1, ...), custom_call_target="tpu_custom_call" | custom-call | bytes 1998912 | tf_op jit(solution)/shard_map/prepare/pallas_call | solution.py:110
  7.7 2.5 %collective-permute-start.2 = (bf16[8,32,128]{2,1,0:T(8,128)(2,1)S(1)}, bf16[8,32,128]{2,1,0:T(8,128)(2,1)S(1)}, u32[]{:S(2)}, u32[]{:S(2)}) collective-permute-start(bf16[8,32,128]{2,1,0:T(8,128)(2,1)S(1)} %get-tuple-element.38), channel_id=1, source_target_pairs={{0,24},{8,0},{16,8},{24,16},{1,25},{9,1},{17,9},{25,17},{2,26},{10... | collective-permute-start | bytes 196616 | tf_op jit(solution)/shard_map/ppermute | solution.py:378
  10.4 1.0 %collective-permute-done.refs_2_ = bf16[32,2,8,128]{3,2,1,0:T(8,128)(2,1)S(1)} collective-permute-done((bf16[32,2,8,128]{3,2,1,0:T(8,128)(2,1)}, bf16[32,2,8,128]{3,2,1,0:T(8,128)(2,1)S(1)}, u32[]{:S(2)}, u32[]{:S(2)}) %collective-permute-start) | collective-permute-done | bytes 131104 | tf_op jit(solution)/shard_map/ppermute | solution.py:382
  12.1 2.4 %collective-permute-start.3 = (bf16[8,32,128]{2,1,0:T(8,128)(2,1)S(1)}, bf16[8,32,128]{2,1,0:T(8,128)(2,1)S(1)}, u32[]{:S(2)}, u32[]{:S(2)}) collective-permute-start(bf16[8,32,128]{2,1,0:T(8,128)(2,1)S(1)} %get-tuple-element.39), channel_id=1, source_target_pairs={{0,8},{8,16},{16,24},{24,0},{1,9},{9,17},{17,25},{25,1},{2,10},{10... | collective-permute-start | bytes 196616 | tf_op jit(solution)/shard_map/ppermute | solution.py:378
  14.5 3.2 %collective-permute-done.3.go_below_ref = bf16[8,32,128]{2,1,0:T(8,128)(2,1)S(1)} collective-permute-done((bf16[8,32,128]{2,1,0:T(8,128)(2,1)S(1)}, bf16[8,32,128]{2,1,0:T(8,128)(2,1)S(1)}, u32[]{:S(2)}, u32[]{:S(2)}) %collective-permute-start.3) | collective-permute-done | bytes 65568 | tf_op jit(solution)/shard_map/ppermute | solution.py:378
  17.8 0.7 %assemble.1.refs_1_ = bf16[256,2048]{1,0:T(8,128)(2,1)S(1)} custom-call(s32[1]{0:T(128)} %bitcast.me_ref, bf16[32,2,8,128]{3,2,1,0:T(8,128)(2,1)S(1)} %get-tuple-element.41.refs_0_, bf16[32,2,8,128]{3,2,1,0:T(8,128)(2,1)S(1)} %collective-permute-done.5.refs_1_, bf16[32,2,8,128]{3,2,1,0:T(8,128)(2,1)S(1)} %collective-permute-done.refs_2_, ...), custom_call_target="tpu_custom_call" | custom-call | flops 4000000000 | bytes 1966084 | tf_op jit(solution)/shard_map/assemble/pallas_call | solution.py:110
  18.5 0.6 %collective-permute-done.4.refs_0_ = bf16[32,2,8,128]{3,2,1,0:T(8,128)(2,1)S(1)} collective-permute-done((bf16[32,2,8,128]{3,2,1,0:T(8,128)(2,1)S(1)}, bf16[32,2,8,128]{3,2,1,0:T(8,128)(2,1)S(1)}, u32[]{:S(2)}, u32[]{:S(2)}) %collective-permute-start.4) | collective-permute-done | bytes 131104 | tf_op jit(solution)/shard_map/ppermute | solution.py:382
  19.1 1.3 %forward.1 = (f32[16,32,128]{2,1,0:T(8,128)S(1)}, bf16[16,32,128]{2,1,0:T(8,128)(2,1)S(1)}, bf16[16,32,128]{2,1,0:T(8,128)(2,1)S(1)}, bf16[256,2048]{1,0:T(8,128)(2,1)S(1)}) custom-call(s32[1]{0:T(128)} %bitcast.me_ref, bf16[864,256]{1,0:T(8,128)(2,1)S(1)} %get-tuple-element.37.w_ref, ...), custom_call_target="tpu_custom_call", output_to_operand_aliasing={{3}: (3, {})} | custom-call | flops 900000000 | bytes 3194884 | tf_op jit(solution)/shard_map/forward/pallas_call | solution.py:110
  20.4 2.1 %collective-permute-start.10 = (bf16[16,32,128]{2,1,0:T(8,128)(2,1)S(1)}, bf16[16,32,128]{2,1,0:T(8,128)(2,1)S(1)}, u32[]{:S(2)}, u32[]{:S(2)}) collective-permute-start(bf16[16,32,128]{2,1,0:T(8,128)(2,1)S(1)} %get-tuple-element.44.low_ref), channel_id=1, source_target_pairs={{0,24},{8,0},{16,8},{24,16},{1,25},{9,1},{17,9},{25,17},{2,26},{10... | collective-permute-start | bytes 393224 | tf_op jit(solution)/shard_map/ppermute | solution.py:378
  22.5 4.3 %collective-permute-done.10.above_ref = bf16[16,32,128]{2,1,0:T(8,128)(2,1)S(1)} collective-permute-done((bf16[16,32,128]{2,1,0:T(8,128)(2,1)S(1)}, bf16[16,32,128]{2,1,0:T(8,128)(2,1)S(1)}, u32[]{:S(2)}, u32[]{:S(2)}) %collective-permute-start.10) | collective-permute-done | bytes 131104 | tf_op jit(solution)/shard_map/ppermute | solution.py:378
  26.8 2.7 %collective-permute-done.9.below_ref = bf16[16,32,128]{2,1,0:T(8,128)(2,1)S(1)} collective-permute-done((bf16[16,32,128]{2,1,0:T(8,128)(2,1)S(1)}, bf16[16,32,128]{2,1,0:T(8,128)(2,1)S(1)}, u32[]{:S(2)}, u32[]{:S(2)}) %collective-permute-start.9) | collective-permute-done | bytes 131104 | tf_op jit(solution)/shard_map/ppermute | solution.py:378
  29.4 1.7 %gradient.1 = (bf16[32,2,8,128]{3,2,1,0:T(8,128)(2,1)}, f32[32,128]{1,0:T(8,128)S(1)}, bf16[864,2048]{1,0:T(8,128)(2,1)S(1)}, bf16[4,16,32,128]{3,2,1,0:T(8,128)(2,1)S(1)}, bf16[4,16,32,128]{3,2,1,0:T(8,128)(2,1)S(1)}) custom-call(s32[1]{0:T(128)} %bitcast.me_ref, f32[16,32,128]{2,1,0:T(8,128)S(1)} %get-tuple-element.43.own_ref, ...), custom_call_target="tpu_custom_call" | custom-call | flops 905969664 | bytes 6242308 | tf_op jit(solution)/shard_map/gradient/pallas_call | solution.py:110
  31.2 1.1 %filter_grad.1 = (bf16[448,256]{1,0:T(8,128)(2,1)S(1)}, bf16[448,256]{1,0:T(8,128)(2,1)S(1)}) custom-call(bf16[864,2048]{1,0:T(8,128)(2,1)S(1)} %get-tuple-element.52.s_ref, bf16[256,2048]{1,0:T(8,128)(2,1)S(1)} %get-tuple-element.53.x_ref, f32[32,128]{1,0:T(8,128)S(1)} %get-tuple-element.54.total_ref), custom_call_target="tpu_custom_call" | custom-call | flops 905969664 | bytes 5062656 | tf_op jit(solution)/shard_map/filter_grad/pallas_call | solution.py:110
  32.4 1.4 %collective-permute-start.11 = (bf16[448,256]{1,0:T(8,128)(2,1)S(1)}, bf16[448,256]{1,0:T(8,128)(2,1)S(1)}, u32[]{:S(2)}, u32[]{:S(2)}) collective-permute-start(bf16[448,256]{1,0:T(8,128)(2,1)S(1)} %get-tuple-element.55.a_ref), channel_id=1, source_target_pairs={{0,8},{8,0},{16,24},{24,16},{1,9},{9,1},{17,25},{25,17},{2,10},{10... | collective-permute-start | bytes 688136 | tf_op jit(solution)/shard_map/ppermute | solution.py:382
  34.4 3.6 %collective-permute-start.16 = (bf16[16,32,128]{2,1,0:T(8,128)(2,1)S(1)}, bf16[16,32,128]{2,1,0:T(8,128)(2,1)S(1)}, u32[]{:S(2)}, u32[]{:S(2)}) collective-permute-start(bf16[16,32,128]{2,1,0:T(8,128)(2,1)S(1)} %get-tuple-element.62), channel_id=1, source_target_pairs={{0,6},{1,7},{2,4},{3,5},{4,2},{5,3},{6,0},{7,1},{8,14},{9,15},{10,... | collective-permute-start | bytes 393224 | tf_op jit(solution)/shard_map/ppermute | solution.py:382
  38.0 0.9 %collective-permute-start.18 = (bf16[16,32,128]{2,1,0:T(8,128)(2,1)S(1)}, bf16[16,32,128]{2,1,0:T(8,128)(2,1)S(1)}, u32[]{:S(2)}, u32[]{:S(2)}) collective-permute-start(bf16[16,32,128]{2,1,0:T(8,128)(2,1)S(1)} %get-tuple-element.64), channel_id=1, source_target_pairs={{0,2},{1,3},{2,0},{3,1},{4,6},{5,7},{6,4},{7,5},{8,10},{9,11},{10,... | collective-permute-start | bytes 393224 | tf_op jit(solution)/shard_map/ppermute | solution.py:382
  38.9 1.6 %collective-permute-done.11.b_ref = bf16[448,256]{1,0:T(8,128)(2,1)S(1)} collective-permute-done((bf16[448,256]{1,0:T(8,128)(2,1)S(1)}, bf16[448,256]{1,0:T(8,128)(2,1)S(1)}, u32[]{:S(2)}, u32[]{:S(2)}) %collective-permute-start.11) | collective-permute-done | bytes 229408 | tf_op jit(solution)/shard_map/ppermute | solution.py:382
  40.4 1.1 %collective-permute-done.12.d_ref = bf16[448,256]{1,0:T(8,128)(2,1)S(1)} collective-permute-done((bf16[448,256]{1,0:T(8,128)(2,1)S(1)}, bf16[448,256]{1,0:T(8,128)(2,1)S(1)}, u32[]{:S(2)}, u32[]{:S(2)}) %collective-permute-start.12) | collective-permute-done | bytes 229408 | tf_op jit(solution)/shard_map/ppermute | solution.py:382
  41.6 0.6 %collective-permute-start.14 = (bf16[448,256]{1,0:T(8,128)(2,1)S(1)}, bf16[448,256]{1,0:T(8,128)(2,1)S(1)}, u32[]{:S(2)}, u32[]{:S(2)}) collective-permute-start(bf16[448,256]{1,0:T(8,128)(2,1)S(1)} %get-tuple-element.60.a_ref), channel_id=1, source_target_pairs={{0,16},{8,24},{16,0},{24,8},{1,17},{9,25},{17,1},{25,9},{2,18},{10... | collective-permute-start | bytes 688136 | tf_op jit(solution)/shard_map/ppermute | solution.py:382
  42.2 1.0 %collective-permute-start.15 = (bf16[448,256]{1,0:T(8,128)(2,1)S(1)}, bf16[448,256]{1,0:T(8,128)(2,1)S(1)}, u32[]{:S(2)}, u32[]{:S(2)}) collective-permute-start(bf16[448,256]{1,0:T(8,128)(2,1)S(1)} %get-tuple-element.61.c_ref), channel_id=1, source_target_pairs={{0,8},{8,0},{16,24},{24,16},{1,9},{9,1},{17,25},{25,17},{2,10},{10... | collective-permute-start | bytes 688136 | tf_op jit(solution)/shard_map/ppermute | solution.py:382
  43.2 6.1 %collective-permute-done.17.c_ref = bf16[16,32,128]{2,1,0:T(8,128)(2,1)S(1)} collective-permute-done((bf16[16,32,128]{2,1,0:T(8,128)(2,1)S(1)}, bf16[16,32,128]{2,1,0:T(8,128)(2,1)S(1)}, u32[]{:S(2)}, u32[]{:S(2)}) %collective-permute-start.17) | collective-permute-done | bytes 131104 | tf_op jit(solution)/shard_map/ppermute | solution.py:382
  49.4 1.1 %last.1 = (f32[27,32,256]{2,1,0:T(8,128)}, f32[1,32]{1,0:T(1,128)}, bf16[32,2,8,128]{3,2,1,0:T(8,128)(2,1)}) custom-call(bf16[448,256]{1,0:T(8,128)(2,1)S(1)} %get-tuple-element.60.a_ref, bf16[448,256]{1,0:T(8,128)(2,1)S(1)} %collective-permute-done.14.b_ref, bf16[448,256]{1,0:T(8,128)(2,1)S(1)} %get-tuple-element.61.c_ref, ...), custom_call_target="tpu_custom_call" | custom-call | bytes 2195584 | tf_op jit(solution)/shard_map/last/pallas_call | solution.py:110
  (23 shorter events, 1.8 us)
Async XLA Ops:
  0.6 10.7 %collective-permute-start = (bf16[32,2,8,128]{3,2,1,0:T(8,128)(2,1)}, bf16[32,2,8,128]{3,2,1,0:T(8,128)(2,1)S(1)}, u32[]{:S(2)}, u32[]{:S(2)}) collective-permute-start(bf16[32,2,8,128]{3,2,1,0:T(8,128)(2,1)} %x_hbm.1), channel_id=1, source_target_pairs={{0,4},{1,5},{2,6},{3,7},{4,0},{5,1},{6,2},{7,3},{8,12},{9,13},{10,... | collective-permute-start | bytes 393224 | tf_op jit(solution)/shard_map/ppermute | solution.py:382
  4.7 6.8 %collective-permute-start.5 = (bf16[32,2,8,128]{3,2,1,0:T(8,128)(2,1)}, bf16[32,2,8,128]{3,2,1,0:T(8,128)(2,1)S(1)}, u32[]{:S(2)}, u32[]{:S(2)}) collective-permute-start(bf16[32,2,8,128]{3,2,1,0:T(8,128)(2,1)} %x_hbm.1), channel_id=1, source_target_pairs={{0,2},{1,3},{2,0},{3,1},{4,6},{5,7},{6,4},{7,5},{8,10},{9,11},{10,... | collective-permute-start | bytes 393224 | tf_op jit(solution)/shard_map/ppermute | solution.py:382
  7.7 4.4 %collective-permute-start.2 = (bf16[8,32,128]{2,1,0:T(8,128)(2,1)S(1)}, bf16[8,32,128]{2,1,0:T(8,128)(2,1)S(1)}, u32[]{:S(2)}, u32[]{:S(2)}) collective-permute-start(bf16[8,32,128]{2,1,0:T(8,128)(2,1)S(1)} %get-tuple-element.38), channel_id=1, source_target_pairs={{0,24},{8,0},{16,8},{24,16},{1,25},{9,1},{17,9},{25,17},{2,26},{10... | collective-permute-start | bytes 196616 | tf_op jit(solution)/shard_map/ppermute | solution.py:378
  10.2 7.6 %collective-permute-start.1 = (bf16[32,2,8,128]{3,2,1,0:T(8,128)(2,1)}, bf16[32,2,8,128]{3,2,1,0:T(8,128)(2,1)S(1)}, u32[]{:S(2)}, u32[]{:S(2)}) collective-permute-start(bf16[32,2,8,128]{3,2,1,0:T(8,128)(2,1)} %x_hbm.1), channel_id=1, source_target_pairs={{0,6},{1,7},{2,4},{3,5},{4,2},{5,3},{6,0},{7,1},{8,14},{9,15},{10,... | collective-permute-start | bytes 393224 | tf_op jit(solution)/shard_map/ppermute | solution.py:382
  10.4 7.3 %collective-permute-start.6 = (bf16[32,2,8,128]{3,2,1,0:T(8,128)(2,1)}, bf16[32,2,8,128]{3,2,1,0:T(8,128)(2,1)S(1)}, u32[]{:S(2)}, u32[]{:S(2)}) collective-permute-start(bf16[32,2,8,128]{3,2,1,0:T(8,128)(2,1)} %x_hbm.1), channel_id=1, source_target_pairs={{0,1},{1,0},{2,3},{3,2},{4,5},{5,4},{6,7},{7,6},{8,9},{9,8},{10,11... | collective-permute-start | bytes 393224 | tf_op jit(solution)/shard_map/ppermute | solution.py:382
  11.6 6.2 %collective-permute-start.7 = (bf16[32,2,8,128]{3,2,1,0:T(8,128)(2,1)S(1)}, bf16[32,2,8,128]{3,2,1,0:T(8,128)(2,1)S(1)}, u32[]{:S(2)}, u32[]{:S(2)}) collective-permute-start(bf16[32,2,8,128]{3,2,1,0:T(8,128)(2,1)S(1)} %collective-permute-done.5.refs_1_), channel_id=1, source_target_pairs={{0,1},{1,0},{2,3},{3,2},{4,5},{5,4},{6,7},{7,6},{8,9},{9,8},{10,11... | collective-permute-start | bytes 393224 | tf_op jit(solution)/shard_map/ppermute | solution.py:382
  11.6 6.2 %collective-permute-start.8 = (bf16[32,2,8,128]{3,2,1,0:T(8,128)(2,1)S(1)}, bf16[32,2,8,128]{3,2,1,0:T(8,128)(2,1)S(1)}, u32[]{:S(2)}, u32[]{:S(2)}) collective-permute-start(bf16[32,2,8,128]{3,2,1,0:T(8,128)(2,1)S(1)} %collective-permute-done.refs_2_), channel_id=1, source_target_pairs={{0,1},{1,0},{2,3},{3,2},{4,5},{5,4},{6,7},{7,6},{8,9},{9,8},{10,11... | collective-permute-start | bytes 393224 | tf_op jit(solution)/shard_map/ppermute | solution.py:382
  12.1 5.7 %collective-permute-start.3 = (bf16[8,32,128]{2,1,0:T(8,128)(2,1)S(1)}, bf16[8,32,128]{2,1,0:T(8,128)(2,1)S(1)}, u32[]{:S(2)}, u32[]{:S(2)}) collective-permute-start(bf16[8,32,128]{2,1,0:T(8,128)(2,1)S(1)} %get-tuple-element.39), channel_id=1, source_target_pairs={{0,8},{8,16},{16,24},{24,0},{1,9},{9,17},{17,25},{25,1},{2,10},{10... | collective-permute-start | bytes 196616 | tf_op jit(solution)/shard_map/ppermute | solution.py:378
  17.7 1.3 %collective-permute-start.4 = (bf16[32,2,8,128]{3,2,1,0:T(8,128)(2,1)S(1)}, bf16[32,2,8,128]{3,2,1,0:T(8,128)(2,1)S(1)}, u32[]{:S(2)}, u32[]{:S(2)}) collective-permute-start(bf16[32,2,8,128]{3,2,1,0:T(8,128)(2,1)S(1)} %collective-permute-done.1.refs_3_), channel_id=1, source_target_pairs={{0,1},{1,0},{2,3},{3,2},{4,5},{5,4},{6,7},{7,6},{8,9},{9,8},{10,11... | collective-permute-start | bytes 393224 | tf_op jit(solution)/shard_map/ppermute | solution.py:382
  20.4 6.4 %collective-permute-start.10 = (bf16[16,32,128]{2,1,0:T(8,128)(2,1)S(1)}, bf16[16,32,128]{2,1,0:T(8,128)(2,1)S(1)}, u32[]{:S(2)}, u32[]{:S(2)}) collective-permute-start(bf16[16,32,128]{2,1,0:T(8,128)(2,1)S(1)} %get-tuple-element.44.low_ref), channel_id=1, source_target_pairs={{0,24},{8,0},{16,8},{24,16},{1,25},{9,1},{17,9},{25,17},{2,26},{10... | collective-permute-start | bytes 393224 | tf_op jit(solution)/shard_map/ppermute | solution.py:378
  22.4 7.0 %collective-permute-start.9 = (bf16[16,32,128]{2,1,0:T(8,128)(2,1)S(1)}, bf16[16,32,128]{2,1,0:T(8,128)(2,1)S(1)}, u32[]{:S(2)}, u32[]{:S(2)}) collective-permute-start(bf16[16,32,128]{2,1,0:T(8,128)(2,1)S(1)} %get-tuple-element.45.high_ref), channel_id=1, source_target_pairs={{0,8},{8,16},{16,24},{24,0},{1,9},{9,17},{17,25},{25,1},{2,10},{10... | collective-permute-start | bytes 393224 | tf_op jit(solution)/shard_map/ppermute | solution.py:378
  31.2 3.1 %collective-permute-start.13 = (bf16[4,16,32,128]{3,2,1,0:T(8,128)(2,1)S(1)}, bf16[4,16,32,128]{3,2,1,0:T(8,128)(2,1)S(1)}, u32[]{:S(2)}, u32[]{:S(2)}) collective-permute-start(bf16[4,16,32,128]{3,2,1,0:T(8,128)(2,1)S(1)} %get-tuple-element.58), channel_id=1, source_target_pairs={{0,1},{1,0},{2,3},{3,2},{4,5},{5,4},{6,7},{7,6},{8,9},{9,8},{10,11... | collective-permute-start | bytes 1572872 | tf_op jit(solution)/shard_map/ppermute | solution.py:382
  32.4 8.1 %collective-permute-start.11 = (bf16[448,256]{1,0:T(8,128)(2,1)S(1)}, bf16[448,256]{1,0:T(8,128)(2,1)S(1)}, u32[]{:S(2)}, u32[]{:S(2)}) collective-permute-start(bf16[448,256]{1,0:T(8,128)(2,1)S(1)} %get-tuple-element.55.a_ref), channel_id=1, source_target_pairs={{0,8},{8,0},{16,24},{24,16},{1,9},{9,1},{17,25},{25,17},{2,10},{10... | collective-permute-start | bytes 688136 | tf_op jit(solution)/shard_map/ppermute | solution.py:382
  33.8 7.7 %collective-permute-start.12 = (bf16[448,256]{1,0:T(8,128)(2,1)S(1)}, bf16[448,256]{1,0:T(8,128)(2,1)S(1)}, u32[]{:S(2)}, u32[]{:S(2)}) collective-permute-start(bf16[448,256]{1,0:T(8,128)(2,1)S(1)} %get-tuple-element.56.c_ref), channel_id=1, source_target_pairs={{0,16},{8,24},{16,0},{24,8},{1,17},{9,25},{17,1},{25,9},{2,18},{10... | collective-permute-start | bytes 688136 | tf_op jit(solution)/shard_map/ppermute | solution.py:382
  34.4 8.8 %collective-permute-start.16 = (bf16[16,32,128]{2,1,0:T(8,128)(2,1)S(1)}, bf16[16,32,128]{2,1,0:T(8,128)(2,1)S(1)}, u32[]{:S(2)}, u32[]{:S(2)}) collective-permute-start(bf16[16,32,128]{2,1,0:T(8,128)(2,1)S(1)} %get-tuple-element.62), channel_id=1, source_target_pairs={{0,6},{1,7},{2,4},{3,5},{4,2},{5,3},{6,0},{7,1},{8,14},{9,15},{10,... | collective-permute-start | bytes 393224 | tf_op jit(solution)/shard_map/ppermute | solution.py:382
  38.0 11.3 %collective-permute-start.17 = (bf16[16,32,128]{2,1,0:T(8,128)(2,1)S(1)}, bf16[16,32,128]{2,1,0:T(8,128)(2,1)S(1)}, u32[]{:S(2)}, u32[]{:S(2)}) collective-permute-start(bf16[16,32,128]{2,1,0:T(8,128)(2,1)S(1)} %get-tuple-element.63), channel_id=1, source_target_pairs={{0,4},{1,5},{2,6},{3,7},{4,0},{5,1},{6,2},{7,3},{8,12},{9,13},{10,... | collective-permute-start | bytes 393224 | tf_op jit(solution)/shard_map/ppermute | solution.py:382
  38.0 11.3 %collective-permute-start.18 = (bf16[16,32,128]{2,1,0:T(8,128)(2,1)S(1)}, bf16[16,32,128]{2,1,0:T(8,128)(2,1)S(1)}, u32[]{:S(2)}, u32[]{:S(2)}) collective-permute-start(bf16[16,32,128]{2,1,0:T(8,128)(2,1)S(1)} %get-tuple-element.64), channel_id=1, source_target_pairs={{0,2},{1,3},{2,0},{3,1},{4,6},{5,7},{6,4},{7,5},{8,10},{9,11},{10,... | collective-permute-start | bytes 393224 | tf_op jit(solution)/shard_map/ppermute | solution.py:382
  41.6 7.7 %collective-permute-start.14 = (bf16[448,256]{1,0:T(8,128)(2,1)S(1)}, bf16[448,256]{1,0:T(8,128)(2,1)S(1)}, u32[]{:S(2)}, u32[]{:S(2)}) collective-permute-start(bf16[448,256]{1,0:T(8,128)(2,1)S(1)} %get-tuple-element.60.a_ref), channel_id=1, source_target_pairs={{0,16},{8,24},{16,0},{24,8},{1,17},{9,25},{17,1},{25,9},{2,18},{10... | collective-permute-start | bytes 688136 | tf_op jit(solution)/shard_map/ppermute | solution.py:382
  42.2 7.2 %collective-permute-start.15 = (bf16[448,256]{1,0:T(8,128)(2,1)S(1)}, bf16[448,256]{1,0:T(8,128)(2,1)S(1)}, u32[]{:S(2)}, u32[]{:S(2)}) collective-permute-start(bf16[448,256]{1,0:T(8,128)(2,1)S(1)} %get-tuple-element.61.c_ref), channel_id=1, source_target_pairs={{0,8},{8,0},{16,24},{24,16},{1,9},{9,1},{17,25},{25,17},{2,10},{10... | collective-permute-start | bytes 688136 | tf_op jit(solution)/shard_map/ppermute | solution.py:382

commit v8 on v7

--- a/solution.py
+++ b/solution.py
@@ -10,7 +10,7 @@
 
 LANES = 128
 FORWARD_FLOPS = 9 * 10**8
-SUM_FLOPS = 20 * 10**8
+SUM_FLOPS = 50 * 10**8
 ASSEMBLE_FLOPS = 40 * 10**8
 VMEM = pl.BlockSpec(memory_space=pltpu.VMEM)
 ANY = pl.BlockSpec(memory_space=pl.ANY)
@@ -321,21 +321,18 @@
                 out_ref[at, t + h] = cut
 
 
-def filter_grad_body(scale, taps, o, s_ref, x_ref, total_ref, first_ref, second_ref):
+def filter_grad_body(scale, o, s_ref, x_ref, total_ref, out_ref):
     full = lax.dot_general(
         s_ref[...], x_ref[...], (((1,), (1,)), ((), ())), preferred_element_type=jnp.float32
     )
-    full = (full * scale).astype(first_ref.dtype)
-    first_ref[...] = full[: taps * o]
-    second_ref[: (27 - taps) * o] = full[taps * o :]
-    row = jnp.concatenate([total_ref[...]] * (second_ref.shape[1] // LANES), axis=1)
-    second_ref[(27 - taps) * o :] = row.astype(second_ref.dtype)
-
-
-def pair_body(a_ref, b_ref, c_ref, d_ref, _, ab_ref, cd_ref):
+    out_ref[: 27 * o] = (full * scale).astype(out_ref.dtype)
+    row = jnp.concatenate([total_ref[...]] * (out_ref.shape[1] // LANES), axis=1)
+    out_ref[27 * o :] = row.astype(out_ref.dtype)
+
+
+def pair_body(a_ref, b_ref, _, out_ref):
     f32 = jnp.float32
-    ab_ref[...] = (a_ref[...].astype(f32) + b_ref[...].astype(f32)).astype(ab_ref.dtype)
-    cd_ref[...] = (c_ref[...].astype(f32) + d_ref[...].astype(f32)).astype(cd_ref.dtype)
+    out_ref[...] = (a_ref[...].astype(f32) + b_ref[...].astype(f32)).astype(out_ref.dtype)
 
 
 def core_sum_body(mine_ref, other_ref, *outs):
@@ -350,9 +347,7 @@
     out_ref[...] = a_ref[...] + total
 
 
-def last_body(
-    taps, a_ref, b_ref, c_ref, d_ref, g_ref, out_ref, bias_ref, grad_ref, wide_ref
-):
+def last_body(a_ref, b_ref, g_ref, out_ref, bias_ref, grad_ref, wide_ref):
     o = out_ref.shape[1]
     f32 = jnp.float32
     cells = g_ref.shape[0]
@@ -360,11 +355,10 @@
         wide_ref[pl.ds(k, o, stride=cells), :] = g_ref[k]
     grad_ref[...] = wide_ref[...].reshape(grad_ref.shape).astype(grad_ref.dtype)
     for k in range(27):
-        left, right, at = (a_ref, b_ref, k) if k < taps else (c_ref, d_ref, k - taps)
-        cut = slice(at * o, (at + 1) * o)
-        out_ref[k] = left[cut].astype(f32) + right[cut].astype(f32)
-    cut = slice((27 - taps) * o, (28 - taps) * o)
-    column = (c_ref[cut].astype(f32) + d_ref[cut].astype(f32))[:, :o]
+        cut = slice(k * o, (k + 1) * o)
+        out_ref[k] = a_ref[cut].astype(f32) + b_ref[cut].astype(f32)
+    cut = slice(27 * o, 28 * o)
+    column = (a_ref[cut].astype(f32) + b_ref[cut].astype(f32))[:, :o]
     same = lax.broadcasted_iota(jnp.int32, (o, o), 0) == lax.broadcasted_iota(jnp.int32, (o, o), 1)
     bias_ref[...] = jnp.sum(jnp.where(same, column, 0.0), axis=0, keepdims=True)
 
@@ -380,6 +374,16 @@
 
 def swap(value, axis, bit):
     return lax.ppermute(value, axis, [(i, i ^ bit) for i in range(lax.axis_size(axis))])
+
+
+def cross(value, phase):
+    slabs, chans = lax.axis_size("slab"), lax.axis_size("chan")
+    pairs = [
+        (s * chans + c, (s ^ (1 + (c + phase) % 2)) * chans + c)
+        for s in range(slabs)
+        for c in range(chans)
+    ]
+    return lax.ppermute(value, ("slab", "chan"), pairs)
 
 
 def on_device(x_in, weight, bias_vec, grad_out):
@@ -393,7 +397,6 @@
 
     block_wide = [pltpu.VMEM((o * cells, depth), f32)]
 
-    x_ab = swap(x_in, "chan", 6)
     x_b = swap(x_in, "chan", 4)
     x_a = swap(x_in, "chan", 2)
     x_side = swap(x_in, "chan", 1)
@@ -422,9 +425,10 @@
     go_above = rotate(go_low, "slab", -1)
     go_below = rotate(go_high, "slab", 1)
     x_b, w_flat = lax.optimization_barrier((x_b, w_flat))
-    late_ab, go_above, go_below = lax.optimization_barrier((x_ab, go_above, go_below))
+    x_ab = swap(x_b, "chan", 2)
+    late_b, go_above, go_below = lax.optimization_barrier((x_b, go_above, go_below))
     x_a_side = swap(x_a, "chan", 1)
-    x_b_side = swap(x_b, "chan", 1)
+    x_b_side = swap(late_b, "chan", 1)
     early, late = (0, 1, 2, 3, 4, 5, 6), (7,)
     (x_all,) = call(
         functools.partial(assemble_body, early),
@@ -435,7 +439,7 @@
         flops=ASSEMBLE_FLOPS,
         name="assemble",
     )
-    x_ab_side = swap(late_ab, "chan", 1)
+    x_ab_side = swap(x_ab, "chan", 1)
     own, low, high, x_all = call(
         functools.partial(forward_body, n, rows, o, late),
         [
@@ -469,16 +473,14 @@
         name="gradient",
     )
     other = swap(other, "chan", 1)
-    taps = 14
-    first, second = call(
-        functools.partial(filter_grad_body, scale, taps, o),
-        [shape_of((taps * o, c_all), bf16), shape_of(((28 - taps) * o, c_all), bf16)],
+    (filters,) = call(
+        functools.partial(filter_grad_body, scale, o),
+        [shape_of((28 * o, c_all), bf16)],
         [stacked, x_all, total],
         flops=flops,
         name="filter_grad",
     )
-    first_far = swap(first, "slab", 1)
-    second_far = swap(second, "slab", 2)
+    filters_far = cross(filters, 0)
     g_own, g_a, g_b, g_ab = call(
         core_sum_body,
         [shape_of((cells, o, depth), f32)] + [shape_of((cells, o, depth), bf16)] * 3,
@@ -488,15 +490,14 @@
     g_ab = swap(g_ab, "chan", 6)
     g_b = swap(g_b, "chan", 4)
     g_a = swap(g_a, "chan", 2)
-    first, second = call(
+    (filters,) = call(
         pair_body,
-        [shape_of(first.shape, bf16), shape_of(second.shape, bf16)],
-        [first, first_far, second, second_far, g_own],
-        [VMEM] * 4 + [ANY],
+        [shape_of(filters.shape, bf16)],
+        [filters, filters_far, g_own],
+        [VMEM] * 2 + [ANY],
         name="pair_sum",
     )
-    first_far = swap(first, "slab", 2)
-    second_far = swap(second, "slab", 1)
+    filters_far = cross(filters, 1)
     (g_own,) = call(
         sum_body,
         [shape_of((cells, o, depth), f32)],
@@ -505,13 +506,13 @@
         name="sum",
     )
     weight_grad, bias_grad, grad_in = call(
-        functools.partial(last_body, taps),
+        last_body,
         [
             shape_of((27, o, c_all), f32),
             shape_of((1, o), f32),
             shape_of((o, n, rows, depth), bf16),
         ],
-        [first, first_far, second, second_far, g_own],
+        [filters, filters_far, g_own],
         scratch=block_wide,
         name="last",
     )

time: 50.7 us -> 49.8 us (0.982)
  starting transfers between devices: 21.4 us -> 19.1 us
  waiting for transfers between devices: 20.7 us -> 22.2 us
    ppermute x0 -> x2, waiting for transfers between devices: none -> 3.51 us  [cross(): return lax.ppermute(value, ('slab', 'chan'), pairs)]
    ppermute x15 -> x11, starting transfers between devices: 14.4 us -> 11.4 us  [swap(): lax.ppermute(value, axis, [(i, i ^ bit) for i in range(lax.axis_size(axis...]
    ppermute x0 -> x2, starting transfers between devices: none -> 2.44 us  [cross(): return lax.ppermute(value, ('slab', 'chan'), pairs)]
    ppermute x15 -> x11, waiting for transfers between devices: 10.5 us -> 8.75 us  [swap(): lax.ppermute(value, axis, [(i, i ^ bit) for i in range(lax.axis_size(axis...]
    ppermute x4, starting transfers between devices: 7.02 us -> 5.25 us  [rotate(): lax.ppermute(value, axis, [(i, (i + step) % count) for i in range(count)])]
  transfers between devices with their start and end apart: 19 -> 17, of which waited for: 9 -> 13; matrix products, arithmetic and copies ran while one was open for 0% -> 0% of each run, Pallas kernels for 7% -> 7%
where the time goes in v8:
time: 49.8 us; the launch traced here: 49.6 us
  waiting for transfers between devices  22.2 us (45%)
  starting transfers between devices  19.1 us (38%)
  Pallas kernels  7.62 us (15%)
  between operations  0.7 us (1%)
    ppermute x11, starting transfers between devices, swap(): lax.ppermute(value, axis, [(i, i ^ bit) for i in range(lax.axis_size(axis...  11.4 us
    ppermute x4, waiting for transfers between devices, rotate(): lax.ppermute(value, axis, [(i, (i + step) % count) for i in range(count)])  9.92 us
    ppermute x11, waiting for transfers between devices, swap(): lax.ppermute(value, axis, [(i, i ^ bit) for i in range(lax.axis_size(axis...  8.75 us
    pallas_call x9, Pallas kernels, call(): pl.pallas_call(body, out_shape=out_shape, in_specs=specs or [VMEM] * len(...  7.62 us
    ppermute x4, starting transfers between devices, rotate(): lax.ppermute(value, axis, [(i, (i + step) % count) for i in range(count)])  5.25 us
    ppermute x2, waiting for transfers between devices, cross(): return lax.ppermute(value, ('slab', 'chan'), pairs)  3.51 us
    ppermute x2, starting transfers between devices, cross(): return lax.ppermute(value, ('slab', 'chan'), pairs)  2.44 us
  transfers between devices with their start and end apart: 17, of which 13 were waited for; matrix products, arithmetic and copies ran while one was open for 0% of the time, Pallas kernels for 7%

profile of v8, /device:TPU:0, one launch (start us, length us, event | category | flops | bytes accessed | tf_op | source)
XLA Modules:
  0.0 49.6 jit_solution(1461951361993738897)
XLA Ops:
  0.6 4.1 %collective-permute-start = (bf16[32,2,8,128]{3,2,1,0:T(8,128)(2,1)}, bf16[32,2,8,128]{3,2,1,0:T(8,128)(2,1)S(1)}, u32[]{:S(2)}, u32[]{:S(2)}) collective-permute-start(bf16[32,2,8,128]{3,2,1,0:T(8,128)(2,1)} %x_hbm.1), channel_id=1, source_target_pairs={{0,4},{1,5},{2,6},{3,7},{4,0},{5,1},{6,2},{7,3},{8,12},{9,13},{10,... | collective-permute-start | bytes 393224 | tf_op jit(solution)/shard_map/ppermute | solution.py:376
  4.7 1.6 %collective-permute-start.3 = (bf16[32,2,8,128]{3,2,1,0:T(8,128)(2,1)}, bf16[32,2,8,128]{3,2,1,0:T(8,128)(2,1)S(1)}, u32[]{:S(2)}, u32[]{:S(2)}) collective-permute-start(bf16[32,2,8,128]{3,2,1,0:T(8,128)(2,1)} %x_hbm.1), channel_id=1, source_target_pairs={{0,2},{1,3},{2,0},{3,1},{4,6},{5,7},{6,4},{7,5},{8,10},{9,11},{10,... | collective-permute-start | bytes 393224 | tf_op jit(solution)/shard_map/ppermute | solution.py:376
  6.3 1.4 %prepare.1 = (bf16[32,2,8,128]{3,2,1,0:T(8,128)(2,1)S(1)}, bf16[16,32,128]{2,1,0:T(8,128)(2,1)S(1)}, bf16[8,32,128]{2,1,0:T(8,128)(2,1)S(1)}, bf16[8,32,128]{2,1...) custom-call(bf16[32,2,8,128]{3,2,1,0:T(8,128)(2,1)} %x_hbm.1, ...), custom_call_target="tpu_custom_call" | custom-call | bytes 1998912 | tf_op jit(solution)/shard_map/prepare/pallas_call | solution.py:110
  7.7 2.5 %collective-permute-start.6 = (bf16[8,32,128]{2,1,0:T(8,128)(2,1)S(1)}, bf16[8,32,128]{2,1,0:T(8,128)(2,1)S(1)}, u32[]{:S(2)}, u32[]{:S(2)}) collective-permute-start(bf16[8,32,128]{2,1,0:T(8,128)(2,1)S(1)} %get-tuple-element.36), channel_id=1, source_target_pairs={{0,24},{8,0},{16,8},{24,16},{1,25},{9,1},{17,9},{25,17},{2,26},{10... | collective-permute-start | bytes 196616 | tf_op jit(solution)/shard_map/ppermute | solution.py:372
  10.2 1.2 %collective-permute-done.refs_2_ = bf16[32,2,8,128]{3,2,1,0:T(8,128)(2,1)S(1)} collective-permute-done((bf16[32,2,8,128]{3,2,1,0:T(8,128)(2,1)}, bf16[32,2,8,128]{3,2,1,0:T(8,128)(2,1)S(1)}, u32[]{:S(2)}, u32[]{:S(2)}) %collective-permute-start) | collective-permute-done | bytes 131104 | tf_op jit(solution)/shard_map/ppermute | solution.py:376
  11.4 0.7 %collective-permute-start.1 = (bf16[32,2,8,128]{3,2,1,0:T(8,128)(2,1)S(1)}, bf16[32,2,8,128]{3,2,1,0:T(8,128)(2,1)S(1)}, u32[]{:S(2)}, u32[]{:S(2)}) collective-permute-start(bf16[32,2,8,128]{3,2,1,0:T(8,128)(2,1)S(1)} %collective-permute-done.refs_2_), channel_id=1, source_target_pairs={{0,2},{1,3},{2,0},{3,1},{4,6},{5,7},{6,4},{7,5},{8,10},{9,11},{10,... | collective-permute-start | bytes 393224 | tf_op jit(solution)/shard_map/ppermute | solution.py:376
  12.4 3.0 %collective-permute-done.7.go_below_ref = bf16[8,32,128]{2,1,0:T(8,128)(2,1)S(1)} collective-permute-done((bf16[8,32,128]{2,1,0:T(8,128)(2,1)S(1)}, bf16[8,32,128]{2,1,0:T(8,128)(2,1)S(1)}, u32[]{:S(2)}, u32[]{:S(2)}) %collective-permute-start.7) | collective-permute-done | bytes 65568 | tf_op jit(solution)/shard_map/ppermute | solution.py:372
  15.4 0.5 %collective-permute-start.8 = (bf16[32,2,8,128]{3,2,1,0:T(8,128)(2,1)S(1)}, bf16[32,2,8,128]{3,2,1,0:T(8,128)(2,1)S(1)}, u32[]{:S(2)}, u32[]{:S(2)}) collective-permute-start(bf16[32,2,8,128]{3,2,1,0:T(8,128)(2,1)S(1)} %collective-permute-done.refs_2_), channel_id=1, source_target_pairs={{0,1},{1,0},{2,3},{3,2},{4,5},{5,4},{6,7},{7,6},{8,9},{9,8},{10,11... | collective-permute-start | bytes 393224 | tf_op jit(solution)/shard_map/ppermute | solution.py:376
  16.9 0.7 %assemble.1.refs_1_ = bf16[256,2048]{1,0:T(8,128)(2,1)S(1)} custom-call(s32[1]{0:T(128)} %bitcast.me_ref, bf16[32,2,8,128]{3,2,1,0:T(8,128)(2,1)S(1)} %get-tuple-element.35.refs_0_, bf16[32,2,8,128]{3,2,1,0:T(8,128)(2,1)S(1)} %collective-permute-done.3.refs_1_, bf16[32,2,8,128]{3,2,1,0:T(8,128)(2,1)S(1)} %collective-permute-done.refs_2_, ...), custom_call_target="tpu_custom_call" | custom-call | flops 4000000000 | bytes 1966084 | tf_op jit(solution)/shard_map/assemble/pallas_call | solution.py:110
  17.7 1.3 %forward.1 = (f32[16,32,128]{2,1,0:T(8,128)S(1)}, bf16[16,32,128]{2,1,0:T(8,128)(2,1)S(1)}, bf16[16,32,128]{2,1,0:T(8,128)(2,1)S(1)}, bf16[256,2048]{1,0:T(8,128)(2,1)S(1)}) custom-call(s32[1]{0:T(128)} %bitcast.me_ref, bf16[864,256]{1,0:T(8,128)(2,1)S(1)} %get-tuple-element.33.w_ref, ...), custom_call_target="tpu_custom_call", output_to_operand_aliasing={{3}: (3, {})} | custom-call | flops 900000000 | bytes 3194884 | tf_op jit(solution)/shard_map/forward/pallas_call | solution.py:110
  19.0 2.8 %collective-permute-start.10 = (bf16[16,32,128]{2,1,0:T(8,128)(2,1)S(1)}, bf16[16,32,128]{2,1,0:T(8,128)(2,1)S(1)}, u32[]{:S(2)}, u32[]{:S(2)}) collective-permute-start(bf16[16,32,128]{2,1,0:T(8,128)(2,1)S(1)} %get-tuple-element.40.low_ref), channel_id=1, source_target_pairs={{0,24},{8,0},{16,8},{24,16},{1,25},{9,1},{17,9},{25,17},{2,26},{10... | collective-permute-start | bytes 393224 | tf_op jit(solution)/shard_map/ppermute | solution.py:372
  21.7 3.9 %collective-permute-done.10.above_ref = bf16[16,32,128]{2,1,0:T(8,128)(2,1)S(1)} collective-permute-done((bf16[16,32,128]{2,1,0:T(8,128)(2,1)S(1)}, bf16[16,32,128]{2,1,0:T(8,128)(2,1)S(1)}, u32[]{:S(2)}, u32[]{:S(2)}) %collective-permute-start.10) | collective-permute-done | bytes 131104 | tf_op jit(solution)/shard_map/ppermute | solution.py:372
  25.6 2.8 %collective-permute-done.9.below_ref = bf16[16,32,128]{2,1,0:T(8,128)(2,1)S(1)} collective-permute-done((bf16[16,32,128]{2,1,0:T(8,128)(2,1)S(1)}, bf16[16,32,128]{2,1,0:T(8,128)(2,1)S(1)}, u32[]{:S(2)}, u32[]{:S(2)}) %collective-permute-start.9) | collective-permute-done | bytes 131104 | tf_op jit(solution)/shard_map/ppermute | solution.py:372
  28.4 1.7 %gradient.1 = (bf16[32,2,8,128]{3,2,1,0:T(8,128)(2,1)}, f32[32,128]{1,0:T(8,128)S(1)}, bf16[864,2048]{1,0:T(8,128)(2,1)S(1)}, bf16[4,16,32,128]{3,2,1,0:T(8,128)(2,1)S(1)}, bf16[4,16,32,128]{3,2,1,0:T(8,128)(2,1)S(1)}) custom-call(s32[1]{0:T(128)} %bitcast.me_ref, f32[16,32,128]{2,1,0:T(8,128)S(1)} %get-tuple-element.39.own_ref, ...), custom_call_target="tpu_custom_call" | custom-call | flops 905969664 | bytes 6242308 | tf_op jit(solution)/shard_map/gradient/pallas_call | solution.py:110
  30.2 1.1 %filter_grad.1.a_ref = bf16[896,256]{1,0:T(8,128)(2,1)S(1)} custom-call(bf16[864,2048]{1,0:T(8,128)(2,1)S(1)} %get-tuple-element.48.s_ref, bf16[256,2048]{1,0:T(8,128)(2,1)S(1)} %get-tuple-element.49.x_ref, f32[32,128]{1,0:T(8,128)S(1)} %get-tuple-element.50.total_ref), custom_call_target="tpu_custom_call" | custom-call | flops 905969664 | bytes 5062656 | tf_op jit(solution)/shard_map/filter_grad/pallas_call | solution.py:110
  31.3 1.8 %collective-permute-start.11 = (bf16[896,256]{1,0:T(8,128)(2,1)S(1)}, bf16[896,256]{1,0:T(8,128)(2,1)S(1)}, u32[]{:S(2)}, u32[]{:S(2)}) collective-permute-start(bf16[896,256]{1,0:T(8,128)(2,1)S(1)} %filter_grad.1.a_ref), channel_id=1, source_target_pairs={{0,8},{1,17},{2,10},{3,19},{4,12},{5,21},{6,14},{7,23},{8,0},{9,25... | collective-permute-start | bytes 1376264 | tf_op jit(solution)/shard_map/ppermute | solution.py:386
  33.2 3.7 %collective-permute-start.14 = (bf16[16,32,128]{2,1,0:T(8,128)(2,1)S(1)}, bf16[16,32,128]{2,1,0:T(8,128)(2,1)S(1)}, u32[]{:S(2)}, u32[]{:S(2)}) collective-permute-start(bf16[16,32,128]{2,1,0:T(8,128)(2,1)S(1)} %get-tuple-element.54), channel_id=1, source_target_pairs={{0,6},{1,7},{2,4},{3,5},{4,2},{5,3},{6,0},{7,1},{8,14},{9,15},{10,... | collective-permute-start | bytes 393224 | tf_op jit(solution)/shard_map/ppermute | solution.py:376
  36.9 0.8 %collective-permute-start.16 = (bf16[16,32,128]{2,1,0:T(8,128)(2,1)S(1)}, bf16[16,32,128]{2,1,0:T(8,128)(2,1)S(1)}, u32[]{:S(2)}, u32[]{:S(2)}) collective-permute-start(bf16[16,32,128]{2,1,0:T(8,128)(2,1)S(1)} %get-tuple-element.56), channel_id=1, source_target_pairs={{0,2},{1,3},{2,0},{3,1},{4,6},{5,7},{6,4},{7,5},{8,10},{9,11},{10,... | collective-permute-start | bytes 393224 | tf_op jit(solution)/shard_map/ppermute | solution.py:376
  37.7 2.2 %collective-permute-done.11.b_ref = bf16[896,256]{1,0:T(8,128)(2,1)S(1)} collective-permute-done((bf16[896,256]{1,0:T(8,128)(2,1)S(1)}, bf16[896,256]{1,0:T(8,128)(2,1)S(1)}, u32[]{:S(2)}, u32[]{:S(2)}) %collective-permute-start.11) | collective-permute-done | bytes 458784 | tf_op jit(solution)/shard_map/ppermute | solution.py:386
  40.0 0.7 %collective-permute-start.13 = (bf16[896,256]{1,0:T(8,128)(2,1)S(1)}, bf16[896,256]{1,0:T(8,128)(2,1)S(1)}, u32[]{:S(2)}, u32[]{:S(2)}) collective-permute-start(bf16[896,256]{1,0:T(8,128)(2,1)S(1)} %pair_sum.1.a_ref), channel_id=1, source_target_pairs={{0,16},{1,9},{2,18},{3,11},{4,20},{5,13},{6,22},{7,15},{8,24},{9,1... | collective-permute-start | bytes 1376264 | tf_op jit(solution)/shard_map/ppermute | solution.py:386
  40.6 0.9 %collective-permute-done.14.b_ref = bf16[16,32,128]{2,1,0:T(8,128)(2,1)S(1)} collective-permute-done((bf16[16,32,128]{2,1,0:T(8,128)(2,1)S(1)}, bf16[16,32,128]{2,1,0:T(8,128)(2,1)S(1)}, u32[]{:S(2)}, u32[]{:S(2)}) %collective-permute-start.14) | collective-permute-done | bytes 131104 | tf_op jit(solution)/shard_map/ppermute | solution.py:376
  41.5 5.6 %collective-permute-done.15.c_ref = bf16[16,32,128]{2,1,0:T(8,128)(2,1)S(1)} collective-permute-done((bf16[16,32,128]{2,1,0:T(8,128)(2,1)S(1)}, bf16[16,32,128]{2,1,0:T(8,128)(2,1)S(1)}, u32[]{:S(2)}, u32[]{:S(2)}) %collective-permute-start.15) | collective-permute-done | bytes 131104 | tf_op jit(solution)/shard_map/ppermute | solution.py:376
  47.2 1.3 %collective-permute-done.13.b_ref = bf16[896,256]{1,0:T(8,128)(2,1)S(1)} collective-permute-done((bf16[896,256]{1,0:T(8,128)(2,1)S(1)}, bf16[896,256]{1,0:T(8,128)(2,1)S(1)}, u32[]{:S(2)}, u32[]{:S(2)}) %collective-permute-start.13) | collective-permute-done | bytes 458784 | tf_op jit(solution)/shard_map/ppermute | solution.py:386
  48.5 1.1 %last.1 = (f32[27,32,256]{2,1,0:T(8,128)}, f32[1,32]{1,0:T(1,128)}, bf16[32,2,8,128]{3,2,1,0:T(8,128)(2,1)}) custom-call(bf16[896,256]{1,0:T(8,128)(2,1)S(1)} %pair_sum.1.a_ref, bf16[896,256]{1,0:T(8,128)(2,1)S(1)} %collective-permute-done.13.b_ref, f32[16,32,128]{2,1,0:T(8,128)S(1)} %sum.1.g_ref), custom_call_target="tpu_custom_call" | custom-call | bytes 2195584 | tf_op jit(solution)/shard_map/last/pallas_call | solution.py:110
  (19 shorter events, 1.7 us)
Async XLA Ops:
  0.6 10.7 %collective-permute-start = (bf16[32,2,8,128]{3,2,1,0:T(8,128)(2,1)}, bf16[32,2,8,128]{3,2,1,0:T(8,128)(2,1)S(1)}, u32[]{:S(2)}, u32[]{:S(2)}) collective-permute-start(bf16[32,2,8,128]{3,2,1,0:T(8,128)(2,1)} %x_hbm.1), channel_id=1, source_target_pairs={{0,4},{1,5},{2,6},{3,7},{4,0},{5,1},{6,2},{7,3},{8,12},{9,13},{10,... | collective-permute-start | bytes 393224 | tf_op jit(solution)/shard_map/ppermute | solution.py:376
  4.7 10.6 %collective-permute-start.3 = (bf16[32,2,8,128]{3,2,1,0:T(8,128)(2,1)}, bf16[32,2,8,128]{3,2,1,0:T(8,128)(2,1)S(1)}, u32[]{:S(2)}, u32[]{:S(2)}) collective-permute-start(bf16[32,2,8,128]{3,2,1,0:T(8,128)(2,1)} %x_hbm.1), channel_id=1, source_target_pairs={{0,2},{1,3},{2,0},{3,1},{4,6},{5,7},{6,4},{7,5},{8,10},{9,11},{10,... | collective-permute-start | bytes 393224 | tf_op jit(solution)/shard_map/ppermute | solution.py:376
  7.7 4.7 %collective-permute-start.6 = (bf16[8,32,128]{2,1,0:T(8,128)(2,1)S(1)}, bf16[8,32,128]{2,1,0:T(8,128)(2,1)S(1)}, u32[]{:S(2)}, u32[]{:S(2)}) collective-permute-start(bf16[8,32,128]{2,1,0:T(8,128)(2,1)S(1)} %get-tuple-element.36), channel_id=1, source_target_pairs={{0,24},{8,0},{16,8},{24,16},{1,25},{9,1},{17,9},{25,17},{2,26},{10... | collective-permute-start | bytes 196616 | tf_op jit(solution)/shard_map/ppermute | solution.py:372
  10.2 5.2 %collective-permute-start.7 = (bf16[8,32,128]{2,1,0:T(8,128)(2,1)S(1)}, bf16[8,32,128]{2,1,0:T(8,128)(2,1)S(1)}, u32[]{:S(2)}, u32[]{:S(2)}) collective-permute-start(bf16[8,32,128]{2,1,0:T(8,128)(2,1)S(1)} %get-tuple-element.37), channel_id=1, source_target_pairs={{0,8},{8,16},{16,24},{24,0},{1,9},{9,17},{17,25},{25,1},{2,10},{10... | collective-permute-start | bytes 196616 | tf_op jit(solution)/shard_map/ppermute | solution.py:372
  10.2 6.2 %collective-permute-start.4 = (bf16[32,2,8,128]{3,2,1,0:T(8,128)(2,1)}, bf16[32,2,8,128]{3,2,1,0:T(8,128)(2,1)S(1)}, u32[]{:S(2)}, u32[]{:S(2)}) collective-permute-start(bf16[32,2,8,128]{3,2,1,0:T(8,128)(2,1)} %x_hbm.1), channel_id=1, source_target_pairs={{0,1},{1,0},{2,3},{3,2},{4,5},{5,4},{6,7},{7,6},{8,9},{9,8},{10,11... | collective-permute-start | bytes 393224 | tf_op jit(solution)/shard_map/ppermute | solution.py:376
  11.4 5.0 %collective-permute-start.1 = (bf16[32,2,8,128]{3,2,1,0:T(8,128)(2,1)S(1)}, bf16[32,2,8,128]{3,2,1,0:T(8,128)(2,1)S(1)}, u32[]{:S(2)}, u32[]{:S(2)}) collective-permute-start(bf16[32,2,8,128]{3,2,1,0:T(8,128)(2,1)S(1)} %collective-permute-done.refs_2_), channel_id=1, source_target_pairs={{0,2},{1,3},{2,0},{3,1},{4,6},{5,7},{6,4},{7,5},{8,10},{9,11},{10,... | collective-permute-start | bytes 393224 | tf_op jit(solution)/shard_map/ppermute | solution.py:376
  15.3 1.3 %collective-permute-start.5 = (bf16[32,2,8,128]{3,2,1,0:T(8,128)(2,1)S(1)}, bf16[32,2,8,128]{3,2,1,0:T(8,128)(2,1)S(1)}, u32[]{:S(2)}, u32[]{:S(2)}) collective-permute-start(bf16[32,2,8,128]{3,2,1,0:T(8,128)(2,1)S(1)} %collective-permute-done.3.refs_1_), channel_id=1, source_target_pairs={{0,1},{1,0},{2,3},{3,2},{4,5},{5,4},{6,7},{7,6},{8,9},{9,8},{10,11... | collective-permute-start | bytes 393224 | tf_op jit(solution)/shard_map/ppermute | solution.py:376
  15.4 1.5 %collective-permute-start.8 = (bf16[32,2,8,128]{3,2,1,0:T(8,128)(2,1)S(1)}, bf16[32,2,8,128]{3,2,1,0:T(8,128)(2,1)S(1)}, u32[]{:S(2)}, u32[]{:S(2)}) collective-permute-start(bf16[32,2,8,128]{3,2,1,0:T(8,128)(2,1)S(1)} %collective-permute-done.refs_2_), channel_id=1, source_target_pairs={{0,1},{1,0},{2,3},{3,2},{4,5},{5,4},{6,7},{7,6},{8,9},{9,8},{10,11... | collective-permute-start | bytes 393224 | tf_op jit(solution)/shard_map/ppermute | solution.py:376
  16.3 1.3 %collective-permute-start.2 = (bf16[32,2,8,128]{3,2,1,0:T(8,128)(2,1)S(1)}, bf16[32,2,8,128]{3,2,1,0:T(8,128)(2,1)S(1)}, u32[]{:S(2)}, u32[]{:S(2)}) collective-permute-start(bf16[32,2,8,128]{3,2,1,0:T(8,128)(2,1)S(1)} %collective-permute-done.1.refs_3_), channel_id=1, source_target_pairs={{0,1},{1,0},{2,3},{3,2},{4,5},{5,4},{6,7},{7,6},{8,9},{9,8},{10,11... | collective-permute-start | bytes 393224 | tf_op jit(solution)/shard_map/ppermute | solution.py:376
  19.0 6.6 %collective-permute-start.10 = (bf16[16,32,128]{2,1,0:T(8,128)(2,1)S(1)}, bf16[16,32,128]{2,1,0:T(8,128)(2,1)S(1)}, u32[]{:S(2)}, u32[]{:S(2)}) collective-permute-start(bf16[16,32,128]{2,1,0:T(8,128)(2,1)S(1)} %get-tuple-element.40.low_ref), channel_id=1, source_target_pairs={{0,24},{8,0},{16,8},{24,16},{1,25},{9,1},{17,9},{25,17},{2,26},{10... | collective-permute-start | bytes 393224 | tf_op jit(solution)/shard_map/ppermute | solution.py:372
  21.7 6.7 %collective-permute-start.9 = (bf16[16,32,128]{2,1,0:T(8,128)(2,1)S(1)}, bf16[16,32,128]{2,1,0:T(8,128)(2,1)S(1)}, u32[]{:S(2)}, u32[]{:S(2)}) collective-permute-start(bf16[16,32,128]{2,1,0:T(8,128)(2,1)S(1)} %get-tuple-element.41.high_ref), channel_id=1, source_target_pairs={{0,8},{8,16},{16,24},{24,0},{1,9},{9,17},{17,25},{25,1},{2,10},{10... | collective-permute-start | bytes 393224 | tf_op jit(solution)/shard_map/ppermute | solution.py:372
  30.1 3.0 %collective-permute-start.12 = (bf16[4,16,32,128]{3,2,1,0:T(8,128)(2,1)S(1)}, bf16[4,16,32,128]{3,2,1,0:T(8,128)(2,1)S(1)}, u32[]{:S(2)}, u32[]{:S(2)}) collective-permute-start(bf16[4,16,32,128]{3,2,1,0:T(8,128)(2,1)S(1)} %get-tuple-element.52), channel_id=1, source_target_pairs={{0,1},{1,0},{2,3},{3,2},{4,5},{5,4},{6,7},{7,6},{8,9},{9,8},{10,11... | collective-permute-start | bytes 1572872 | tf_op jit(solution)/shard_map/ppermute | solution.py:376
  31.3 8.5 %collective-permute-start.11 = (bf16[896,256]{1,0:T(8,128)(2,1)S(1)}, bf16[896,256]{1,0:T(8,128)(2,1)S(1)}, u32[]{:S(2)}, u32[]{:S(2)}) collective-permute-start(bf16[896,256]{1,0:T(8,128)(2,1)S(1)} %filter_grad.1.a_ref), channel_id=1, source_target_pairs={{0,8},{1,17},{2,10},{3,19},{4,12},{5,21},{6,14},{7,23},{8,0},{9,25... | collective-permute-start | bytes 1376264 | tf_op jit(solution)/shard_map/ppermute | solution.py:386
  33.2 8.3 %collective-permute-start.14 = (bf16[16,32,128]{2,1,0:T(8,128)(2,1)S(1)}, bf16[16,32,128]{2,1,0:T(8,128)(2,1)S(1)}, u32[]{:S(2)}, u32[]{:S(2)}) collective-permute-start(bf16[16,32,128]{2,1,0:T(8,128)(2,1)S(1)} %get-tuple-element.54), channel_id=1, source_target_pairs={{0,6},{1,7},{2,4},{3,5},{4,2},{5,3},{6,0},{7,1},{8,14},{9,15},{10,... | collective-permute-start | bytes 393224 | tf_op jit(solution)/shard_map/ppermute | solution.py:376
  36.9 10.2 %collective-permute-start.15 = (bf16[16,32,128]{2,1,0:T(8,128)(2,1)S(1)}, bf16[16,32,128]{2,1,0:T(8,128)(2,1)S(1)}, u32[]{:S(2)}, u32[]{:S(2)}) collective-permute-start(bf16[16,32,128]{2,1,0:T(8,128)(2,1)S(1)} %get-tuple-element.55), channel_id=1, source_target_pairs={{0,4},{1,5},{2,6},{3,7},{4,0},{5,1},{6,2},{7,3},{8,12},{9,13},{10,... | collective-permute-start | bytes 393224 | tf_op jit(solution)/shard_map/ppermute | solution.py:376
  36.9 10.2 %collective-permute-start.16 = (bf16[16,32,128]{2,1,0:T(8,128)(2,1)S(1)}, bf16[16,32,128]{2,1,0:T(8,128)(2,1)S(1)}, u32[]{:S(2)}, u32[]{:S(2)}) collective-permute-start(bf16[16,32,128]{2,1,0:T(8,128)(2,1)S(1)} %get-tuple-element.56), channel_id=1, source_target_pairs={{0,2},{1,3},{2,0},{3,1},{4,6},{5,7},{6,4},{7,5},{8,10},{9,11},{10,... | collective-permute-start | bytes 393224 | tf_op jit(solution)/shard_map/ppermute | solution.py:376
  40.0 8.5 %collective-permute-start.13 = (bf16[896,256]{1,0:T(8,128)(2,1)S(1)}, bf16[896,256]{1,0:T(8,128)(2,1)S(1)}, u32[]{:S(2)}, u32[]{:S(2)}) collective-permute-start(bf16[896,256]{1,0:T(8,128)(2,1)S(1)} %pair_sum.1.a_ref), channel_id=1, source_target_pairs={{0,16},{1,9},{2,18},{3,11},{4,20},{5,13},{6,22},{7,15},{8,24},{9,1... | collective-permute-start | bytes 1376264 | tf_op jit(solution)/shard_map/ppermute | solution.py:386

commit v9 on v7

--- a/solution.py
+++ b/solution.py
@@ -10,7 +10,7 @@
 
 LANES = 128
 FORWARD_FLOPS = 9 * 10**8
-SUM_FLOPS = 20 * 10**8
+SUM_FLOPS = 24 * 10**8
 ASSEMBLE_FLOPS = 40 * 10**8
 VMEM = pl.BlockSpec(memory_space=pltpu.VMEM)
 ANY = pl.BlockSpec(memory_space=pl.ANY)
@@ -138,6 +138,7 @@
 def prepare_body(
     n,
     rows,
+    me_ref,
     x_hbm,
     go_hbm,
     w_hbm,
@@ -152,6 +153,7 @@
     go_in,
     w_in,
     bias_in,
+    back_in,
     wide_ref,
     sems,
 ):
@@ -175,8 +177,11 @@
     copies[3].wait()
     flat = w_in[...].reshape(flat_ref.shape)
     flat_ref[...] = flat
-    back_ref[...] = jnp.transpose(flat)
     o = bias_ref.shape[0]
+    back_in[...] = jnp.transpose(flat)
+    for b in range(8):
+        place = pl.ds(pl.multiple_of(owner(me_ref, b) * o, o), o)
+        back_ref[b * o : (b + 1) * o] = back_in[place]
     row = jnp.broadcast_to(bias_in[...].astype(jnp.float32), (o, o))
     same = lax.broadcasted_iota(jnp.int32, (o, o), 0) == lax.broadcasted_iota(jnp.int32, (o, o), 1)
     column = jnp.sum(jnp.where(same, row, 0.0), axis=1, keepdims=True)
@@ -246,7 +251,6 @@
     rows,
     o,
     scale,
-    me_ref,
     own_ref,
     low_ref,
     high_ref,
@@ -256,22 +260,19 @@
     go_ref,
     go_below_ref,
     go_above_ref,
-    back_ref,
+    w_ref,
     act_ref,
     total_ref,
     s_ref,
     other_ref,
     mine_ref,
-    w_ref,
     wide_ref,
 ):
     f32, bf16 = jnp.float32, jnp.bfloat16
-    for b in range(8):
-        place = pl.ds(pl.multiple_of(owner(me_ref, b) * o, o), o)
-        w_ref[b * o : (b + 1) * o] = back_ref[place]
     total = jnp.zeros((o, LANES), f32)
-    for q in range(n + 2):
-        for y in range(rows):
+
+    def shift_row(y, total):
+        for q in range(n + 2):
             if q == 0:
                 pre = below_ref[rows + y].astype(f32) + low_ref[y].astype(f32)
                 go = go_below_ref[y]
@@ -303,22 +304,30 @@
                 if 0 <= p < n:
                     at = (p * rows + (y + j - 1) % rows) * LANES
                     s_ref[k * o : (k + 1) * o, at : at + LANES] = shifts[l]
+        return total
+
+    def multiply(t):
+        at = t * LANES
+        part = jnp.dot(
+            w_ref[...], s_ref[:, at : at + 2 * LANES], preferred_element_type=f32
+        ).astype(bf16)
+        for h in range(2):
+            for b in range(8):
+                cut = part[b * o : (b + 1) * o, h * LANES : (h + 1) * LANES]
+                (mine_ref if b < 4 else other_ref)[b % 4, t + h] = cut
+
+    total = shift_row(rows - 1, total)
+    total = shift_row(0, total)
+    for t in range(0, rows, 2):
+        for y in (t + 1, t + 2):
+            if y < rows - 1:
+                total = shift_row(y, total)
+        for p in range(n):
+            multiply(p * rows + t)
     act_ref[...] = wide_ref[...].reshape(act_ref.shape).astype(bf16)
     total_ref[...] = jnp.broadcast_to(
         jnp.sum(total, axis=1, keepdims=True) * scale, total_ref.shape
     )
-    input_grad(n * rows, o, w_ref[...], s_ref, [(ref, r) for ref in (mine_ref, other_ref) for r in range(4)])
-
-
-def input_grad(cells, o, w, s_ref, outs):
-    for t in range(0, cells, 2):
-        part = jnp.dot(
-            w, s_ref[:, t * LANES : (t + 2) * LANES], preferred_element_type=jnp.float32
-        ).astype(outs[0][0].dtype)
-        for h in range(2):
-            for r, (out_ref, at) in enumerate(outs):
-                cut = part[r * o : (r + 1) * o, h * LANES : (h + 1) * LANES]
-                out_ref[at, t + h] = cut
 
 
 def filter_grad_body(scale, taps, o, s_ref, x_ref, total_ref, first_ref, second_ref):
@@ -332,10 +341,9 @@
     second_ref[(27 - taps) * o :] = row.astype(second_ref.dtype)
 
 
-def pair_body(a_ref, b_ref, c_ref, d_ref, _, ab_ref, cd_ref):
+def pair_body(a_ref, b_ref, _, out_ref):
     f32 = jnp.float32
-    ab_ref[...] = (a_ref[...].astype(f32) + b_ref[...].astype(f32)).astype(ab_ref.dtype)
-    cd_ref[...] = (c_ref[...].astype(f32) + d_ref[...].astype(f32)).astype(cd_ref.dtype)
+    out_ref[...] = (a_ref[...].astype(f32) + b_ref[...].astype(f32)).astype(out_ref.dtype)
 
 
 def core_sum_body(mine_ref, other_ref, *outs):
@@ -344,21 +352,19 @@
         out_ref[...] = total.astype(out_ref.dtype)
 
 
-def sum_body(a_ref, b_ref, c_ref, d_ref, out_ref):
+def sum_body(a_ref, b_ref, c_ref, d_ref, out_ref, token_ref, wide_ref):
     f32 = jnp.float32
-    total = b_ref[...].astype(f32) + c_ref[...].astype(f32) + d_ref[...].astype(f32)
-    out_ref[...] = a_ref[...] + total
-
-
-def last_body(
-    taps, a_ref, b_ref, c_ref, d_ref, g_ref, out_ref, bias_ref, grad_ref, wide_ref
-):
+    cells, o, _ = a_ref.shape
+    for k in range(cells):
+        total = a_ref[k] + b_ref[k].astype(f32) + c_ref[k].astype(f32) + d_ref[k].astype(f32)
+        wide_ref[pl.ds(k, o, stride=cells), :] = total
+    out_ref[...] = wide_ref[...].reshape(out_ref.shape).astype(out_ref.dtype)
+    token_ref[...] = jnp.zeros_like(token_ref)
+
+
+def last_body(taps, a_ref, b_ref, c_ref, d_ref, _, out_ref, bias_ref):
     o = out_ref.shape[1]
     f32 = jnp.float32
-    cells = g_ref.shape[0]
-    for k in range(cells):
-        wide_ref[pl.ds(k, o, stride=cells), :] = g_ref[k]
-    grad_ref[...] = wide_ref[...].reshape(grad_ref.shape).astype(grad_ref.dtype)
     for k in range(27):
         left, right, at = (a_ref, b_ref, k) if k < taps else (c_ref, d_ref, k - taps)
         cut = slice(at * o, (at + 1) * o)
@@ -382,6 +388,16 @@
     return lax.ppermute(value, axis, [(i, i ^ bit) for i in range(lax.axis_size(axis))])
 
 
+def cross(value, phase):
+    slabs, chans = lax.axis_size("slab"), lax.axis_size("chan")
+    pairs = [
+        (s * chans + c, (s ^ (1 + (c + phase) % 2)) * chans + c)
+        for s in range(slabs)
+        for c in range(chans)
+    ]
+    return lax.ppermute(value, ("slab", "chan"), pairs)
+
+
 def on_device(x_in, weight, bias_vec, grad_out):
     o, _, c_all = weight.shape
     _, n, rows, depth = x_in.shape
@@ -393,7 +409,6 @@
 
     block_wide = [pltpu.VMEM((o * cells, depth), f32)]
 
-    x_ab = swap(x_in, "chan", 6)
     x_b = swap(x_in, "chan", 4)
     x_a = swap(x_in, "chan", 2)
     x_side = swap(x_in, "chan", 1)
@@ -408,12 +423,13 @@
             shape_of((c_all, 27 * o), bf16),
             shape_of((o, LANES), f32),
         ],
-        [in_hbm(a) for a in (x_in, grad_out, jnp.transpose(weight, (1, 0, 2)), bias_vec[None, :])],
-        [HBM] * 4,
+        [me] + [in_hbm(a) for a in (x_in, grad_out, jnp.transpose(weight, (1, 0, 2)), bias_vec[None, :])],
+        [SMEM] + [HBM] * 4,
         [
             pltpu.VMEM((o, n, rows, depth), bf16),
             pltpu.VMEM((27, o, c_all), bf16),
             pltpu.VMEM((1, o), bf16),
+            pltpu.VMEM((c_all, 27 * o), bf16),
             *block_wide,
             pltpu.SemaphoreType.DMA((4,)),
         ],
@@ -422,9 +438,10 @@
     go_above = rotate(go_low, "slab", -1)
     go_below = rotate(go_high, "slab", 1)
     x_b, w_flat = lax.optimization_barrier((x_b, w_flat))
-    late_ab, go_above, go_below = lax.optimization_barrier((x_ab, go_above, go_below))
+    x_ab = swap(x_b, "chan", 2)
+    late_b, go_above, go_below = lax.optimization_barrier((x_b, go_above, go_below))
     x_a_side = swap(x_a, "chan", 1)
-    x_b_side = swap(x_b, "chan", 1)
+    x_b_side = swap(late_b, "chan", 1)
     early, late = (0, 1, 2, 3, 4, 5, 6), (7,)
     (x_all,) = call(
         functools.partial(assemble_body, early),
@@ -435,7 +452,7 @@
         flops=ASSEMBLE_FLOPS,
         name="assemble",
     )
-    x_ab_side = swap(late_ab, "chan", 1)
+    x_ab_side = swap(x_ab, "chan", 1)
     own, low, high, x_all = call(
         functools.partial(forward_body, n, rows, o, late),
         [
@@ -462,9 +479,9 @@
             shape_of((4, cells, o, depth), bf16),
             shape_of((4, cells, o, depth), bf16),
         ],
-        [me, own, low, high, below, above, bias, go, go_below, go_above, w_back],
-        [SMEM] + [VMEM] * 10,
-        [pltpu.VMEM((c_all, 27 * o), bf16), *block_wide],
+        [own, low, high, below, above, bias, go, go_below, go_above, w_back],
+        [VMEM] * 10,
+        block_wide,
         flops=flops,
         name="gradient",
     )
@@ -477,8 +494,8 @@
         flops=flops,
         name="filter_grad",
     )
-    first_far = swap(first, "slab", 1)
-    second_far = swap(second, "slab", 2)
+    first_far = cross(first, 0)
+    second_far = cross(second, 0)
     g_own, g_a, g_b, g_ab = call(
         core_sum_body,
         [shape_of((cells, o, depth), f32)] + [shape_of((cells, o, depth), bf16)] * 3,
@@ -488,31 +505,31 @@
     g_ab = swap(g_ab, "chan", 6)
     g_b = swap(g_b, "chan", 4)
     g_a = swap(g_a, "chan", 2)
-    first, second = call(
-        pair_body,
-        [shape_of(first.shape, bf16), shape_of(second.shape, bf16)],
-        [first, first_far, second, second_far, g_own],
-        [VMEM] * 4 + [ANY],
-        name="pair_sum",
-    )
-    first_far = swap(first, "slab", 2)
-    second_far = swap(second, "slab", 1)
-    (g_own,) = call(
+    first, second = (
+        call(
+            pair_body,
+            [shape_of(a.shape, bf16)],
+            [a, b, g_own],
+            [VMEM] * 2 + [ANY],
+            name="pair_sum",
+        )[0]
+        for a, b in ((first, first_far), (second, second_far))
+    )
+    first_far = cross(first, 1)
+    second_far = cross(second, 1)
+    grad_in, token = call(
         sum_body,
-        [shape_of((cells, o, depth), f32)],
+        [shape_of((o, n, rows, depth), bf16), shape_of((8, LANES), f32)],
         [g_own, g_ab, g_b, g_a],
+        scratch=block_wide,
         flops=SUM_FLOPS,
         name="sum",
     )
-    weight_grad, bias_grad, grad_in = call(
+    weight_grad, bias_grad = call(
         functools.partial(last_body, taps),
-        [
-            shape_of((27, o, c_all), f32),
-            shape_of((1, o), f32),
-            shape_of((o, n, rows, depth), bf16),
-        ],
-        [first, first_far, second, second_far, g_own],
-        scratch=block_wide,
+        [shape_of((27, o, c_all), f32), shape_of((1, o), f32)],
+        [first, first_far, second, second_far, token],
+        [VMEM] * 4 + [ANY],
         name="last",
     )
     return act, grad_in, jnp.transpose(weight_grad, (1, 0, 2)), bias_grad[0]

time: 50.7 us -> 50.6 us (level)
  starting transfers between devices: 21.4 us -> 20.2 us
  Pallas kernels: 7.61 us -> 8.71 us
    ppermute x0 -> x4, starting transfers between devices: none -> 3.43 us  [cross(): return lax.ppermute(value, ('slab', 'chan'), pairs)]
    ppermute x15 -> x11, starting transfers between devices: 14.4 us -> 11.5 us  [swap(): lax.ppermute(value, axis, [(i, i ^ bit) for i in range(lax.axis_size(axis...]
    ppermute x4, starting transfers between devices: 7.02 us -> 5.28 us  [rotate(): lax.ppermute(value, axis, [(i, (i + step) % count) for i in range(count)])]
    ppermute x0 -> x4, waiting for transfers between devices: none -> 1.11 us  [cross(): return lax.ppermute(value, ('slab', 'chan'), pairs)]
    pallas_call x9 -> x10, Pallas kernels: 7.61 us -> 8.71 us  [call(): pl.pallas_call(body, out_shape=out_shape, in_specs=specs or [VMEM] * len(...]
    ppermute x15 -> x11, waiting for transfers between devices: 10.5 us -> 9.83 us  [swap(): lax.ppermute(value, axis, [(i, i ^ bit) for i in range(lax.axis_size(axis...]
  transfers between devices with their start and end apart: 19 -> 19, of which waited for: 9 -> 11; matrix products, arithmetic and copies ran while one was open for 0% -> 0% of each run, Pallas kernels for 7% -> 9%
where the time goes in v9:
time: 50.6 us; the launch traced here: 50.4 us
  waiting for transfers between devices  20.9 us (41%)
  starting transfers between devices  20.2 us (40%)
  Pallas kernels  8.71 us (17%)
  between operations  0.69 us (1%)
    ppermute x11, starting transfers between devices, swap(): lax.ppermute(value, axis, [(i, i ^ bit) for i in range(lax.axis_size(axis...  11.5 us
    ppermute x4, waiting for transfers between devices, rotate(): lax.ppermute(value, axis, [(i, (i + step) % count) for i in range(count)])  9.92 us
    ppermute x11, waiting for transfers between devices, swap(): lax.ppermute(value, axis, [(i, i ^ bit) for i in range(lax.axis_size(axis...  9.83 us
    pallas_call x10, Pallas kernels, call(): pl.pallas_call(body, out_shape=out_shape, in_specs=specs or [VMEM] * len(...  8.71 us
    ppermute x4, starting transfers between devices, rotate(): lax.ppermute(value, axis, [(i, (i + step) % count) for i in range(count)])  5.28 us
    ppermute x4, starting transfers between devices, cross(): return lax.ppermute(value, ('slab', 'chan'), pairs)  3.43 us
    ppermute x4, waiting for transfers between devices, cross(): return lax.ppermute(value, ('slab', 'chan'), pairs)  1.11 us
  transfers between devices with their start and end apart: 19, of which 11 were waited for; matrix products, arithmetic and copies ran while one was open for 0% of the time, Pallas kernels for 9%

profile of v9, /device:TPU:0, one launch (start us, length us, event | category | flops | bytes accessed | tf_op | source)
XLA Modules:
  0.0 50.4 jit_solution(6933087076768298976)
XLA Ops:
  0.6 4.1 %collective-permute-start = (bf16[32,2,8,128]{3,2,1,0:T(8,128)(2,1)}, bf16[32,2,8,128]{3,2,1,0:T(8,128)(2,1)S(1)}, u32[]{:S(2)}, u32[]{:S(2)}) collective-permute-start(bf16[32,2,8,128]{3,2,1,0:T(8,128)(2,1)} %x_hbm.1), channel_id=1, source_target_pairs={{0,4},{1,5},{2,6},{3,7},{4,0},{5,1},{6,2},{7,3},{8,12},{9,13},{10,... | collective-permute-start | bytes 393224 | tf_op jit(solution)/shard_map/ppermute | solution.py:388
  4.7 1.6 %collective-permute-start.3 = (bf16[32,2,8,128]{3,2,1,0:T(8,128)(2,1)}, bf16[32,2,8,128]{3,2,1,0:T(8,128)(2,1)S(1)}, u32[]{:S(2)}, u32[]{:S(2)}) collective-permute-start(bf16[32,2,8,128]{3,2,1,0:T(8,128)(2,1)} %x_hbm.1), channel_id=1, source_target_pairs={{0,2},{1,3},{2,0},{3,1},{4,6},{5,7},{6,4},{7,5},{8,10},{9,11},{10,... | collective-permute-start | bytes 393224 | tf_op jit(solution)/shard_map/ppermute | solution.py:388
  6.3 1.4 %prepare.1 = (bf16[32,2,8,128]{3,2,1,0:T(8,128)(2,1)S(1)}, bf16[16,32,128]{2,1,0:T(8,128)(2,1)S(1)}, bf16[8,32,128]{2,1,0:T(8,128)(2,1)S(1)}, bf16[8,32,128]{2,1...) custom-call(s32[1]{0:T(128)} %bitcast.me_ref, ...), custom_call_target="tpu_custom_call" | custom-call | bytes 1998916 | tf_op jit(solution)/shard_map/prepare/pallas_call | solution.py:110
  7.7 2.5 %collective-permute-start.6 = (bf16[8,32,128]{2,1,0:T(8,128)(2,1)S(1)}, bf16[8,32,128]{2,1,0:T(8,128)(2,1)S(1)}, u32[]{:S(2)}, u32[]{:S(2)}) collective-permute-start(bf16[8,32,128]{2,1,0:T(8,128)(2,1)S(1)} %get-tuple-element.39), channel_id=1, source_target_pairs={{0,24},{8,0},{16,8},{24,16},{1,25},{9,1},{17,9},{25,17},{2,26},{10... | collective-permute-start | bytes 196616 | tf_op jit(solution)/shard_map/ppermute | solution.py:384
  10.2 1.1 %collective-permute-done.refs_2_ = bf16[32,2,8,128]{3,2,1,0:T(8,128)(2,1)S(1)} collective-permute-done((bf16[32,2,8,128]{3,2,1,0:T(8,128)(2,1)}, bf16[32,2,8,128]{3,2,1,0:T(8,128)(2,1)S(1)}, u32[]{:S(2)}, u32[]{:S(2)}) %collective-permute-start) | collective-permute-done | bytes 131104 | tf_op jit(solution)/shard_map/ppermute | solution.py:388
  11.4 0.7 %collective-permute-start.1 = (bf16[32,2,8,128]{3,2,1,0:T(8,128)(2,1)S(1)}, bf16[32,2,8,128]{3,2,1,0:T(8,128)(2,1)S(1)}, u32[]{:S(2)}, u32[]{:S(2)}) collective-permute-start(bf16[32,2,8,128]{3,2,1,0:T(8,128)(2,1)S(1)} %collective-permute-done.refs_2_), channel_id=1, source_target_pairs={{0,2},{1,3},{2,0},{3,1},{4,6},{5,7},{6,4},{7,5},{8,10},{9,11},{10,... | collective-permute-start | bytes 393224 | tf_op jit(solution)/shard_map/ppermute | solution.py:388
  12.4 3.0 %collective-permute-done.7.go_below_ref = bf16[8,32,128]{2,1,0:T(8,128)(2,1)S(1)} collective-permute-done((bf16[8,32,128]{2,1,0:T(8,128)(2,1)S(1)}, bf16[8,32,128]{2,1,0:T(8,128)(2,1)S(1)}, u32[]{:S(2)}, u32[]{:S(2)}) %collective-permute-start.7) | collective-permute-done | bytes 65568 | tf_op jit(solution)/shard_map/ppermute | solution.py:384
  16.9 0.7 %assemble.1.refs_1_ = bf16[256,2048]{1,0:T(8,128)(2,1)S(1)} custom-call(s32[1]{0:T(128)} %bitcast.me_ref, bf16[32,2,8,128]{3,2,1,0:T(8,128)(2,1)S(1)} %get-tuple-element.38.refs_0_, bf16[32,2,8,128]{3,2,1,0:T(8,128)(2,1)S(1)} %collective-permute-done.3.refs_1_, bf16[32,2,8,128]{3,2,1,0:T(8,128)(2,1)S(1)} %collective-permute-done.refs_2_, ...), custom_call_target="tpu_custom_call" | custom-call | flops 4000000000 | bytes 1966084 | tf_op jit(solution)/shard_map/assemble/pallas_call | solution.py:110
  17.7 1.3 %forward.1 = (f32[16,32,128]{2,1,0:T(8,128)S(1)}, bf16[16,32,128]{2,1,0:T(8,128)(2,1)S(1)}, bf16[16,32,128]{2,1,0:T(8,128)(2,1)S(1)}, bf16[256,2048]{1,0:T(8,128)(2,1)S(1)}) custom-call(s32[1]{0:T(128)} %bitcast.me_ref, bf16[864,256]{1,0:T(8,128)(2,1)S(1)} %get-tuple-element.36.w_ref, ...), custom_call_target="tpu_custom_call", output_to_operand_aliasing={{3}: (3, {})} | custom-call | flops 900000000 | bytes 3194884 | tf_op jit(solution)/shard_map/forward/pallas_call | solution.py:110
  19.0 2.8 %collective-permute-start.10 = (bf16[16,32,128]{2,1,0:T(8,128)(2,1)S(1)}, bf16[16,32,128]{2,1,0:T(8,128)(2,1)S(1)}, u32[]{:S(2)}, u32[]{:S(2)}) collective-permute-start(bf16[16,32,128]{2,1,0:T(8,128)(2,1)S(1)} %get-tuple-element.43.low_ref), channel_id=1, source_target_pairs={{0,24},{8,0},{16,8},{24,16},{1,25},{9,1},{17,9},{25,17},{2,26},{10... | collective-permute-start | bytes 393224 | tf_op jit(solution)/shard_map/ppermute | solution.py:384
  21.8 3.9 %collective-permute-done.10.above_ref = bf16[16,32,128]{2,1,0:T(8,128)(2,1)S(1)} collective-permute-done((bf16[16,32,128]{2,1,0:T(8,128)(2,1)S(1)}, bf16[16,32,128]{2,1,0:T(8,128)(2,1)S(1)}, u32[]{:S(2)}, u32[]{:S(2)}) %collective-permute-start.10) | collective-permute-done | bytes 131104 | tf_op jit(solution)/shard_map/ppermute | solution.py:384
  25.6 2.8 %collective-permute-done.9.below_ref = bf16[16,32,128]{2,1,0:T(8,128)(2,1)S(1)} collective-permute-done((bf16[16,32,128]{2,1,0:T(8,128)(2,1)S(1)}, bf16[16,32,128]{2,1,0:T(8,128)(2,1)S(1)}, u32[]{:S(2)}, u32[]{:S(2)}) %collective-permute-start.9) | collective-permute-done | bytes 131104 | tf_op jit(solution)/shard_map/ppermute | solution.py:384
  28.4 2.1 %gradient.1 = (bf16[32,2,8,128]{3,2,1,0:T(8,128)(2,1)}, f32[32,128]{1,0:T(8,128)S(1)}, bf16[864,2048]{1,0:T(8,128)(2,1)S(1)}, bf16[4,16,32,128]{3,2,1,0:T(8,128)(2,1)S(1)}, bf16[4,16,32,128]{3,2,1,0:T(8,128)(2,1)S(1)}) custom-call(f32[16,32,128]{2,1,0:T(8,128)S(1)} %get-tuple-element.42.own_ref, bf16[16,32,128]{2,1,0:T(8,128)(2,1)S(1)} %get-tuple-element.43.low_ref, ...), custom_call_target="tpu_custom_call" | custom-call | flops 905969664 | bytes 6242304 | tf_op jit(solution)/shard_map/gradient/pallas_call | solution.py:110
  30.5 1.1 %filter_grad.1 = (bf16[448,256]{1,0:T(8,128)(2,1)S(1)}, bf16[448,256]{1,0:T(8,128)(2,1)S(1)}) custom-call(bf16[864,2048]{1,0:T(8,128)(2,1)S(1)} %get-tuple-element.58.s_ref, bf16[256,2048]{1,0:T(8,128)(2,1)S(1)} %get-tuple-element.59.x_ref, f32[32,128]{1,0:T(8,128)S(1)} %get-tuple-element.60.total_ref), custom_call_target="tpu_custom_call" | custom-call | flops 905969664 | bytes 5062656 | tf_op jit(solution)/shard_map/filter_grad/pallas_call | solution.py:110
  31.6 1.8 %collective-permute-start.15 = (bf16[448,256]{1,0:T(8,128)(2,1)S(1)}, bf16[448,256]{1,0:T(8,128)(2,1)S(1)}, u32[]{:S(2)}, u32[]{:S(2)}) collective-permute-start(bf16[448,256]{1,0:T(8,128)(2,1)S(1)} %get-tuple-element.61.a_ref), channel_id=1, source_target_pairs={{0,8},{1,17},{2,10},{3,19},{4,12},{5,21},{6,14},{7,23},{8,0},{9,25... | collective-permute-start | bytes 688136 | tf_op jit(solution)/shard_map/ppermute | solution.py:398
  33.9 3.9 %collective-permute-start.12 = (bf16[16,32,128]{2,1,0:T(8,128)(2,1)S(1)}, bf16[16,32,128]{2,1,0:T(8,128)(2,1)S(1)}, u32[]{:S(2)}, u32[]{:S(2)}) collective-permute-start(bf16[16,32,128]{2,1,0:T(8,128)(2,1)S(1)} %get-tuple-element.54), channel_id=1, source_target_pairs={{0,6},{1,7},{2,4},{3,5},{4,2},{5,3},{6,0},{7,1},{8,14},{9,15},{10,... | collective-permute-start | bytes 393224 | tf_op jit(solution)/shard_map/ppermute | solution.py:388
  37.8 0.6 %collective-permute-start.14 = (bf16[16,32,128]{2,1,0:T(8,128)(2,1)S(1)}, bf16[16,32,128]{2,1,0:T(8,128)(2,1)S(1)}, u32[]{:S(2)}, u32[]{:S(2)}) collective-permute-start(bf16[16,32,128]{2,1,0:T(8,128)(2,1)S(1)} %get-tuple-element.56), channel_id=1, source_target_pairs={{0,2},{1,3},{2,0},{3,1},{4,6},{5,7},{6,4},{7,5},{8,10},{9,11},{10,... | collective-permute-start | bytes 393224 | tf_op jit(solution)/shard_map/ppermute | solution.py:388
  38.5 0.6 %collective-permute-start.16 = (bf16[448,256]{1,0:T(8,128)(2,1)S(1)}, bf16[448,256]{1,0:T(8,128)(2,1)S(1)}, u32[]{:S(2)}, u32[]{:S(2)}) collective-permute-start(bf16[448,256]{1,0:T(8,128)(2,1)S(1)} %pair_sum.2.a_ref), channel_id=1, source_target_pairs={{0,16},{1,9},{2,18},{3,11},{4,20},{5,13},{6,22},{7,15},{8,24},{9,1... | collective-permute-start | bytes 688136 | tf_op jit(solution)/shard_map/ppermute | solution.py:398
  39.1 1.1 %collective-permute-done.17.b_ref = bf16[448,256]{1,0:T(8,128)(2,1)S(1)} collective-permute-done((bf16[448,256]{1,0:T(8,128)(2,1)S(1)}, bf16[448,256]{1,0:T(8,128)(2,1)S(1)}, u32[]{:S(2)}, u32[]{:S(2)}) %collective-permute-start.17) | collective-permute-done | bytes 229408 | tf_op jit(solution)/shard_map/ppermute | solution.py:398
  40.2 0.7 %collective-permute-start.18 = (bf16[448,256]{1,0:T(8,128)(2,1)S(1)}, bf16[448,256]{1,0:T(8,128)(2,1)S(1)}, u32[]{:S(2)}, u32[]{:S(2)}) collective-permute-start(bf16[448,256]{1,0:T(8,128)(2,1)S(1)} %pair_sum.3.c_ref), channel_id=1, source_target_pairs={{0,16},{1,9},{2,18},{3,11},{4,20},{5,13},{6,22},{7,15},{8,24},{9,1... | collective-permute-start | bytes 688136 | tf_op jit(solution)/shard_map/ppermute | solution.py:398
  41.0 1.2 %collective-permute-done.12.b_ref = bf16[16,32,128]{2,1,0:T(8,128)(2,1)S(1)} collective-permute-done((bf16[16,32,128]{2,1,0:T(8,128)(2,1)S(1)}, bf16[16,32,128]{2,1,0:T(8,128)(2,1)S(1)}, u32[]{:S(2)}, u32[]{:S(2)}) %collective-permute-start.12) | collective-permute-done | bytes 131104 | tf_op jit(solution)/shard_map/ppermute | solution.py:388
  42.2 6.4 %collective-permute-done.13.c_ref = bf16[16,32,128]{2,1,0:T(8,128)(2,1)S(1)} collective-permute-done((bf16[16,32,128]{2,1,0:T(8,128)(2,1)S(1)}, bf16[16,32,128]{2,1,0:T(8,128)(2,1)S(1)}, u32[]{:S(2)}, u32[]{:S(2)}) %collective-permute-start.13) | collective-permute-done | bytes 131104 | tf_op jit(solution)/shard_map/ppermute | solution.py:388
  48.6 0.8 %sum.1 = (bf16[32,2,8,128]{3,2,1,0:T(8,128)(2,1)}, f32[8,128]{1,0:T(8,128)S(1)}) custom-call(f32[16,32,128]{2,1,0:T(8,128)S(1)} %get-tuple-element.53.a_ref._, bf16[16,32,128]{2,1,0:T(8,128)(2,1)S(1)} %collective-permute-done.12.b_ref, bf16[16,32,128]{2,1,0:T(8,128)(2,1)S(1)} %collective-permute-done.13.c_ref, ...), custom_call_target="tpu_custom_call" | custom-call | flops 2400000000 | bytes 790528 | tf_op jit(solution)/shard_map/sum/pallas_call | solution.py:110
  49.4 1.0 %last.1 = (f32[27,32,256]{2,1,0:T(8,128)}, f32[1,32]{1,0:T(1,128)}) custom-call(bf16[448,256]{1,0:T(8,128)(2,1)S(1)} %pair_sum.2.a_ref, bf16[448,256]{1,0:T(8,128)(2,1)S(1)} %collective-permute-done.16.b_ref, bf16[448,256]{1,0:T(8,128)(2,1)S(1)} %pair_sum.3.c_ref, bf16[448,256]{1,0:T(8,128)(2,1)S(1)} %collective-permute-done.18.d_ref, ...), custom_call_target="tpu_custom_call" | custom-call | bytes 1806464 | tf_op jit(solution)/shard_map/last/pallas_call | solution.py:110
  (24 shorter events, 2.4 us)
Async XLA Ops:
  0.6 10.7 %collective-permute-start = (bf16[32,2,8,128]{3,2,1,0:T(8,128)(2,1)}, bf16[32,2,8,128]{3,2,1,0:T(8,128)(2,1)S(1)}, u32[]{:S(2)}, u32[]{:S(2)}) collective-permute-start(bf16[32,2,8,128]{3,2,1,0:T(8,128)(2,1)} %x_hbm.1), channel_id=1, source_target_pairs={{0,4},{1,5},{2,6},{3,7},{4,0},{5,1},{6,2},{7,3},{8,12},{9,13},{10,... | collective-permute-start | bytes 393224 | tf_op jit(solution)/shard_map/ppermute | solution.py:388
  4.7 10.7 %collective-permute-start.3 = (bf16[32,2,8,128]{3,2,1,0:T(8,128)(2,1)}, bf16[32,2,8,128]{3,2,1,0:T(8,128)(2,1)S(1)}, u32[]{:S(2)}, u32[]{:S(2)}) collective-permute-start(bf16[32,2,8,128]{3,2,1,0:T(8,128)(2,1)} %x_hbm.1), channel_id=1, source_target_pairs={{0,2},{1,3},{2,0},{3,1},{4,6},{5,7},{6,4},{7,5},{8,10},{9,11},{10,... | collective-permute-start | bytes 393224 | tf_op jit(solution)/shard_map/ppermute | solution.py:388
  7.7 4.7 %collective-permute-start.6 = (bf16[8,32,128]{2,1,0:T(8,128)(2,1)S(1)}, bf16[8,32,128]{2,1,0:T(8,128)(2,1)S(1)}, u32[]{:S(2)}, u32[]{:S(2)}) collective-permute-start(bf16[8,32,128]{2,1,0:T(8,128)(2,1)S(1)} %get-tuple-element.39), channel_id=1, source_target_pairs={{0,24},{8,0},{16,8},{24,16},{1,25},{9,1},{17,9},{25,17},{2,26},{10... | collective-permute-start | bytes 196616 | tf_op jit(solution)/shard_map/ppermute | solution.py:384
  10.2 5.2 %collective-permute-start.7 = (bf16[8,32,128]{2,1,0:T(8,128)(2,1)S(1)}, bf16[8,32,128]{2,1,0:T(8,128)(2,1)S(1)}, u32[]{:S(2)}, u32[]{:S(2)}) collective-permute-start(bf16[8,32,128]{2,1,0:T(8,128)(2,1)S(1)} %get-tuple-element.40), channel_id=1, source_target_pairs={{0,8},{8,16},{16,24},{24,0},{1,9},{9,17},{17,25},{25,1},{2,10},{10... | collective-permute-start | bytes 196616 | tf_op jit(solution)/shard_map/ppermute | solution.py:384
  10.2 6.1 %collective-permute-start.4 = (bf16[32,2,8,128]{3,2,1,0:T(8,128)(2,1)}, bf16[32,2,8,128]{3,2,1,0:T(8,128)(2,1)S(1)}, u32[]{:S(2)}, u32[]{:S(2)}) collective-permute-start(bf16[32,2,8,128]{3,2,1,0:T(8,128)(2,1)} %x_hbm.1), channel_id=1, source_target_pairs={{0,1},{1,0},{2,3},{3,2},{4,5},{5,4},{6,7},{7,6},{8,9},{9,8},{10,11... | collective-permute-start | bytes 393224 | tf_op jit(solution)/shard_map/ppermute | solution.py:388
  11.4 5.0 %collective-permute-start.1 = (bf16[32,2,8,128]{3,2,1,0:T(8,128)(2,1)S(1)}, bf16[32,2,8,128]{3,2,1,0:T(8,128)(2,1)S(1)}, u32[]{:S(2)}, u32[]{:S(2)}) collective-permute-start(bf16[32,2,8,128]{3,2,1,0:T(8,128)(2,1)S(1)} %collective-permute-done.refs_2_), channel_id=1, source_target_pairs={{0,2},{1,3},{2,0},{3,1},{4,6},{5,7},{6,4},{7,5},{8,10},{9,11},{10,... | collective-permute-start | bytes 393224 | tf_op jit(solution)/shard_map/ppermute | solution.py:388
  15.4 1.3 %collective-permute-start.5 = (bf16[32,2,8,128]{3,2,1,0:T(8,128)(2,1)S(1)}, bf16[32,2,8,128]{3,2,1,0:T(8,128)(2,1)S(1)}, u32[]{:S(2)}, u32[]{:S(2)}) collective-permute-start(bf16[32,2,8,128]{3,2,1,0:T(8,128)(2,1)S(1)} %collective-permute-done.3.refs_1_), channel_id=1, source_target_pairs={{0,1},{1,0},{2,3},{3,2},{4,5},{5,4},{6,7},{7,6},{8,9},{9,8},{10,11... | collective-permute-start | bytes 393224 | tf_op jit(solution)/shard_map/ppermute | solution.py:388
  15.4 1.5 %collective-permute-start.8 = (bf16[32,2,8,128]{3,2,1,0:T(8,128)(2,1)S(1)}, bf16[32,2,8,128]{3,2,1,0:T(8,128)(2,1)S(1)}, u32[]{:S(2)}, u32[]{:S(2)}) collective-permute-start(bf16[32,2,8,128]{3,2,1,0:T(8,128)(2,1)S(1)} %collective-permute-done.refs_2_), channel_id=1, source_target_pairs={{0,1},{1,0},{2,3},{3,2},{4,5},{5,4},{6,7},{7,6},{8,9},{9,8},{10,11... | collective-permute-start | bytes 393224 | tf_op jit(solution)/shard_map/ppermute | solution.py:388
  16.3 1.3 %collective-permute-start.2 = (bf16[32,2,8,128]{3,2,1,0:T(8,128)(2,1)S(1)}, bf16[32,2,8,128]{3,2,1,0:T(8,128)(2,1)S(1)}, u32[]{:S(2)}, u32[]{:S(2)}) collective-permute-start(bf16[32,2,8,128]{3,2,1,0:T(8,128)(2,1)S(1)} %collective-permute-done.1.refs_3_), channel_id=1, source_target_pairs={{0,1},{1,0},{2,3},{3,2},{4,5},{5,4},{6,7},{7,6},{8,9},{9,8},{10,11... | collective-permute-start | bytes 393224 | tf_op jit(solution)/shard_map/ppermute | solution.py:388
  19.0 6.6 %collective-permute-start.10 = (bf16[16,32,128]{2,1,0:T(8,128)(2,1)S(1)}, bf16[16,32,128]{2,1,0:T(8,128)(2,1)S(1)}, u32[]{:S(2)}, u32[]{:S(2)}) collective-permute-start(bf16[16,32,128]{2,1,0:T(8,128)(2,1)S(1)} %get-tuple-element.43.low_ref), channel_id=1, source_target_pairs={{0,24},{8,0},{16,8},{24,16},{1,25},{9,1},{17,9},{25,17},{2,26},{10... | collective-permute-start | bytes 393224 | tf_op jit(solution)/shard_map/ppermute | solution.py:384
  21.7 6.6 %collective-permute-start.9 = (bf16[16,32,128]{2,1,0:T(8,128)(2,1)S(1)}, bf16[16,32,128]{2,1,0:T(8,128)(2,1)S(1)}, u32[]{:S(2)}, u32[]{:S(2)}) collective-permute-start(bf16[16,32,128]{2,1,0:T(8,128)(2,1)S(1)} %get-tuple-element.44.high_ref), channel_id=1, source_target_pairs={{0,8},{8,16},{16,24},{24,0},{1,9},{9,17},{17,25},{25,1},{2,10},{10... | collective-permute-start | bytes 393224 | tf_op jit(solution)/shard_map/ppermute | solution.py:384
  30.5 3.2 %collective-permute-start.11 = (bf16[4,16,32,128]{3,2,1,0:T(8,128)(2,1)S(1)}, bf16[4,16,32,128]{3,2,1,0:T(8,128)(2,1)S(1)}, u32[]{:S(2)}, u32[]{:S(2)}) collective-permute-start(bf16[4,16,32,128]{3,2,1,0:T(8,128)(2,1)S(1)} %get-tuple-element.52), channel_id=1, source_target_pairs={{0,1},{1,0},{2,3},{3,2},{4,5},{5,4},{6,7},{7,6},{8,9},{9,8},{10,11... | collective-permute-start | bytes 1572872 | tf_op jit(solution)/shard_map/ppermute | solution.py:388
  31.6 6.8 %collective-permute-start.15 = (bf16[448,256]{1,0:T(8,128)(2,1)S(1)}, bf16[448,256]{1,0:T(8,128)(2,1)S(1)}, u32[]{:S(2)}, u32[]{:S(2)}) collective-permute-start(bf16[448,256]{1,0:T(8,128)(2,1)S(1)} %get-tuple-element.61.a_ref), channel_id=1, source_target_pairs={{0,8},{1,17},{2,10},{3,19},{4,12},{5,21},{6,14},{7,23},{8,0},{9,25... | collective-permute-start | bytes 688136 | tf_op jit(solution)/shard_map/ppermute | solution.py:398
  33.4 6.7 %collective-permute-start.17 = (bf16[448,256]{1,0:T(8,128)(2,1)S(1)}, bf16[448,256]{1,0:T(8,128)(2,1)S(1)}, u32[]{:S(2)}, u32[]{:S(2)}) collective-permute-start(bf16[448,256]{1,0:T(8,128)(2,1)S(1)} %get-tuple-element.62.a_ref), channel_id=1, source_target_pairs={{0,8},{1,17},{2,10},{3,19},{4,12},{5,21},{6,14},{7,23},{8,0},{9,25... | collective-permute-start | bytes 688136 | tf_op jit(solution)/shard_map/ppermute | solution.py:398
  33.9 8.3 %collective-permute-start.12 = (bf16[16,32,128]{2,1,0:T(8,128)(2,1)S(1)}, bf16[16,32,128]{2,1,0:T(8,128)(2,1)S(1)}, u32[]{:S(2)}, u32[]{:S(2)}) collective-permute-start(bf16[16,32,128]{2,1,0:T(8,128)(2,1)S(1)} %get-tuple-element.54), channel_id=1, source_target_pairs={{0,6},{1,7},{2,4},{3,5},{4,2},{5,3},{6,0},{7,1},{8,14},{9,15},{10,... | collective-permute-start | bytes 393224 | tf_op jit(solution)/shard_map/ppermute | solution.py:388
  37.7 10.9 %collective-permute-start.13 = (bf16[16,32,128]{2,1,0:T(8,128)(2,1)S(1)}, bf16[16,32,128]{2,1,0:T(8,128)(2,1)S(1)}, u32[]{:S(2)}, u32[]{:S(2)}) collective-permute-start(bf16[16,32,128]{2,1,0:T(8,128)(2,1)S(1)} %get-tuple-element.55), channel_id=1, source_target_pairs={{0,4},{1,5},{2,6},{3,7},{4,0},{5,1},{6,2},{7,3},{8,12},{9,13},{10,... | collective-permute-start | bytes 393224 | tf_op jit(solution)/shard_map/ppermute | solution.py:388
  37.8 10.9 %collective-permute-start.14 = (bf16[16,32,128]{2,1,0:T(8,128)(2,1)S(1)}, bf16[16,32,128]{2,1,0:T(8,128)(2,1)S(1)}, u32[]{:S(2)}, u32[]{:S(2)}) collective-permute-start(bf16[16,32,128]{2,1,0:T(8,128)(2,1)S(1)} %get-tuple-element.56), channel_id=1, source_target_pairs={{0,2},{1,3},{2,0},{3,1},{4,6},{5,7},{6,4},{7,5},{8,10},{9,11},{10,... | collective-permute-start | bytes 393224 | tf_op jit(solution)/shard_map/ppermute | solution.py:388
  38.5 11.0 %collective-permute-start.16 = (bf16[448,256]{1,0:T(8,128)(2,1)S(1)}, bf16[448,256]{1,0:T(8,128)(2,1)S(1)}, u32[]{:S(2)}, u32[]{:S(2)}) collective-permute-start(bf16[448,256]{1,0:T(8,128)(2,1)S(1)} %pair_sum.2.a_ref), channel_id=1, source_target_pairs={{0,16},{1,9},{2,18},{3,11},{4,20},{5,13},{6,22},{7,15},{8,24},{9,1... | collective-permute-start | bytes 688136 | tf_op jit(solution)/shard_map/ppermute | solution.py:398
  40.2 9.2 %collective-permute-start.18 = (bf16[448,256]{1,0:T(8,128)(2,1)S(1)}, bf16[448,256]{1,0:T(8,128)(2,1)S(1)}, u32[]{:S(2)}, u32[]{:S(2)}) collective-permute-start(bf16[448,256]{1,0:T(8,128)(2,1)S(1)} %pair_sum.3.c_ref), channel_id=1, source_target_pairs={{0,16},{1,9},{2,18},{3,11},{4,20},{5,13},{6,22},{7,15},{8,24},{9,1... | collective-permute-start | bytes 688136 | tf_op jit(solution)/shard_map/ppermute | solution.py:398

commit v10 on v9

--- a/solution.py
+++ b/solution.py
@@ -316,29 +316,28 @@
                 cut = part[b * o : (b + 1) * o, h * LANES : (h + 1) * LANES]
                 (mine_ref if b < 4 else other_ref)[b % 4, t + h] = cut
 
-    total = shift_row(rows - 1, total)
-    total = shift_row(0, total)
-    for t in range(0, rows, 2):
-        for y in (t + 1, t + 2):
-            if y < rows - 1:
-                total = shift_row(y, total)
-        for p in range(n):
-            multiply(p * rows + t)
+    for y in range(rows):
+        total = shift_row(y, total)
+    for t in range(0, n * rows, 2):
+        multiply(t)
     act_ref[...] = wide_ref[...].reshape(act_ref.shape).astype(bf16)
     total_ref[...] = jnp.broadcast_to(
         jnp.sum(total, axis=1, keepdims=True) * scale, total_ref.shape
     )
 
 
-def filter_grad_body(scale, taps, o, s_ref, x_ref, total_ref, first_ref, second_ref):
-    full = lax.dot_general(
-        s_ref[...], x_ref[...], (((1,), (1,)), ((), ())), preferred_element_type=jnp.float32
-    )
-    full = (full * scale).astype(first_ref.dtype)
-    first_ref[...] = full[: taps * o]
-    second_ref[: (27 - taps) * o] = full[taps * o :]
-    row = jnp.concatenate([total_ref[...]] * (second_ref.shape[1] // LANES), axis=1)
-    second_ref[(27 - taps) * o :] = row.astype(second_ref.dtype)
+def filter_grad_body(scale, start, o, s_ref, x_ref, total_ref, _, out_ref):
+    taps = min(27 - start, out_ref.shape[0] // o)
+    part = lax.dot_general(
+        s_ref[start * o : (start + taps) * o],
+        x_ref[...],
+        (((1,), (1,)), ((), ())),
+        preferred_element_type=jnp.float32,
+    )
+    out_ref[: taps * o] = (part * scale).astype(out_ref.dtype)
+    if out_ref.shape[0] > taps * o:
+        row = jnp.concatenate([total_ref[...]] * (out_ref.shape[1] // LANES), axis=1)
+        out_ref[taps * o :] = row.astype(out_ref.dtype)
 
 
 def pair_body(a_ref, b_ref, _, out_ref):
@@ -352,19 +351,21 @@
         out_ref[...] = total.astype(out_ref.dtype)
 
 
-def sum_body(a_ref, b_ref, c_ref, d_ref, out_ref, token_ref, wide_ref):
+def sum_body(a_ref, b_ref, c_ref, d_ref, out_ref):
     f32 = jnp.float32
-    cells, o, _ = a_ref.shape
-    for k in range(cells):
-        total = a_ref[k] + b_ref[k].astype(f32) + c_ref[k].astype(f32) + d_ref[k].astype(f32)
-        wide_ref[pl.ds(k, o, stride=cells), :] = total
-    out_ref[...] = wide_ref[...].reshape(out_ref.shape).astype(out_ref.dtype)
-    token_ref[...] = jnp.zeros_like(token_ref)
-
-
-def last_body(taps, a_ref, b_ref, c_ref, d_ref, _, out_ref, bias_ref):
+    total = b_ref[...].astype(f32) + c_ref[...].astype(f32) + d_ref[...].astype(f32)
+    out_ref[...] = a_ref[...] + total
+
+
+def last_body(
+    taps, a_ref, b_ref, c_ref, d_ref, g_ref, out_ref, bias_ref, grad_ref, wide_ref
+):
     o = out_ref.shape[1]
     f32 = jnp.float32
+    cells = g_ref.shape[0]
+    for k in range(cells):
+        wide_ref[pl.ds(k, o, stride=cells), :] = g_ref[k]
+    grad_ref[...] = wide_ref[...].reshape(grad_ref.shape).astype(grad_ref.dtype)
     for k in range(27):
         left, right, at = (a_ref, b_ref, k) if k < taps else (c_ref, d_ref, k - taps)
         cut = slice(at * o, (at + 1) * o)
@@ -487,21 +488,26 @@
     )
     other = swap(other, "chan", 1)
     taps = 14
-    first, second = call(
-        functools.partial(filter_grad_body, scale, taps, o),
-        [shape_of((taps * o, c_all), bf16), shape_of(((28 - taps) * o, c_all), bf16)],
-        [stacked, x_all, total],
-        flops=flops,
-        name="filter_grad",
-    )
+    def filter_grad(start, taps, after, name):
+        return call(
+            functools.partial(filter_grad_body, scale, start, o),
+            [shape_of((taps * o, c_all), bf16)],
+            [stacked, x_all, total, after],
+            [VMEM] * 3 + [ANY],
+            flops=flops // 2,
+            name=name,
+        )[0]
+
+    first = filter_grad(0, taps, total, "filter_first")
     first_far = cross(first, 0)
-    second_far = cross(second, 0)
     g_own, g_a, g_b, g_ab = call(
         core_sum_body,
         [shape_of((cells, o, depth), f32)] + [shape_of((cells, o, depth), bf16)] * 3,
         [mine, other],
         name="core_sum",
     )
+    second = filter_grad(taps, 28 - taps, g_own, "filter_second")
+    second_far = cross(second, 0)
     g_ab = swap(g_ab, "chan", 6)
     g_b = swap(g_b, "chan", 4)
     g_a = swap(g_a, "chan", 2)
@@ -517,19 +523,22 @@
     )
     first_far = cross(first, 1)
     second_far = cross(second, 1)
-    grad_in, token = call(
+    (g_own,) = call(
         sum_body,
-        [shape_of((o, n, rows, depth), bf16), shape_of((8, LANES), f32)],
+        [shape_of((cells, o, depth), f32)],
         [g_own, g_ab, g_b, g_a],
-        scratch=block_wide,
         flops=SUM_FLOPS,
         name="sum",
     )
-    weight_grad, bias_grad = call(
+    weight_grad, bias_grad, grad_in = call(
         functools.partial(last_body, taps),
-        [shape_of((27, o, c_all), f32), shape_of((1, o), f32)],
-        [first, first_far, second, second_far, token],
-        [VMEM] * 4 + [ANY],
+        [
+            shape_of((27, o, c_all), f32),
+            shape_of((1, o), f32),
+            shape_of((o, n, rows, depth), bf16),
+        ],
+        [first, first_far, second, second_far, g_own],
+        scratch=block_wide,
         name="last",
     )
     return act, grad_in, jnp.transpose(weight_grad, (1, 0, 2)), bias_grad[0]

time: 50.6 us -> 50.2 us (level)
  starting transfers between devices: 20.2 us -> 21.8 us
  waiting for transfers between devices: 20.9 us -> 19.3 us
    ppermute x4, starting transfers between devices: 3.43 us -> 5.18 us  [cross(): return lax.ppermute(value, ('slab', 'chan'), pairs)]
    ppermute x4, waiting for transfers between devices: 1.11 us -> 0.01 us  [cross(): return lax.ppermute(value, ('slab', 'chan'), pairs)]
    pallas_call x10 -> x11, Pallas kernels: 8.71 us -> 8.31 us  [call(): pl.pallas_call(body, out_shape=out_shape, in_specs=specs or [VMEM] * len(...]
  transfers between devices with their start and end apart: 19 -> 19, of which waited for: 11 -> 10; matrix products, arithmetic and copies ran while one was open for 0% -> 0% of each run, Pallas kernels for 9% -> 7%
where the time goes in v10:
time: 50.2 us; the launch traced here: 50 us
  starting transfers between devices  21.8 us (43%)
  waiting for transfers between devices  19.3 us (38%)
  Pallas kernels  8.31 us (17%)
  between operations  0.72 us (1%)
    ppermute x11, starting transfers between devices, swap(): lax.ppermute(value, axis, [(i, i ^ bit) for i in range(lax.axis_size(axis...  11.3 us
    ppermute x4, waiting for transfers between devices, rotate(): lax.ppermute(value, axis, [(i, (i + step) % count) for i in range(count)])  9.92 us
    ppermute x11, waiting for transfers between devices, swap(): lax.ppermute(value, axis, [(i, i ^ bit) for i in range(lax.axis_size(axis...  9.32 us
    pallas_call x11, Pallas kernels, call(): pl.pallas_call(body, out_shape=out_shape, in_specs=specs or [VMEM] * len(...  8.31 us
    ppermute x4, starting transfers between devices, rotate(): lax.ppermute(value, axis, [(i, (i + step) % count) for i in range(count)])  5.28 us
    ppermute x4, starting transfers between devices, cross(): return lax.ppermute(value, ('slab', 'chan'), pairs)  5.18 us
  transfers between devices with their start and end apart: 19, of which 10 were waited for; matrix products, arithmetic and copies ran while one was open for 0% of the time, Pallas kernels for 7%

profile of v10, /device:TPU:0, one launch (start us, length us, event | category | flops | bytes accessed | tf_op | source)
XLA Modules:
  0.0 50.0 jit_solution(6771884881919398702)
XLA Ops:
  0.6 4.1 %collective-permute-start = (bf16[32,2,8,128]{3,2,1,0:T(8,128)(2,1)}, bf16[32,2,8,128]{3,2,1,0:T(8,128)(2,1)S(1)}, u32[]{:S(2)}, u32[]{:S(2)}) collective-permute-start(bf16[32,2,8,128]{3,2,1,0:T(8,128)(2,1)} %x_hbm.1), channel_id=1, source_target_pairs={{0,4},{1,5},{2,6},{3,7},{4,0},{5,1},{6,2},{7,3},{8,12},{9,13},{10,... | collective-permute-start | bytes 393224 | tf_op jit(solution)/shard_map/ppermute | solution.py:389
  4.7 1.6 %collective-permute-start.3 = (bf16[32,2,8,128]{3,2,1,0:T(8,128)(2,1)}, bf16[32,2,8,128]{3,2,1,0:T(8,128)(2,1)S(1)}, u32[]{:S(2)}, u32[]{:S(2)}) collective-permute-start(bf16[32,2,8,128]{3,2,1,0:T(8,128)(2,1)} %x_hbm.1), channel_id=1, source_target_pairs={{0,2},{1,3},{2,0},{3,1},{4,6},{5,7},{6,4},{7,5},{8,10},{9,11},{10,... | collective-permute-start | bytes 393224 | tf_op jit(solution)/shard_map/ppermute | solution.py:389
  6.3 1.4 %prepare.1 = (bf16[32,2,8,128]{3,2,1,0:T(8,128)(2,1)S(1)}, bf16[16,32,128]{2,1,0:T(8,128)(2,1)S(1)}, bf16[8,32,128]{2,1,0:T(8,128)(2,1)S(1)}, bf16[8,32,128]{2,1...) custom-call(s32[1]{0:T(128)} %bitcast.me_ref, ...), custom_call_target="tpu_custom_call" | custom-call | bytes 1998916 | tf_op jit(solution)/shard_map/prepare/pallas_call | solution.py:110
  7.7 2.5 %collective-permute-start.6 = (bf16[8,32,128]{2,1,0:T(8,128)(2,1)S(1)}, bf16[8,32,128]{2,1,0:T(8,128)(2,1)S(1)}, u32[]{:S(2)}, u32[]{:S(2)}) collective-permute-start(bf16[8,32,128]{2,1,0:T(8,128)(2,1)S(1)} %get-tuple-element.36), channel_id=1, source_target_pairs={{0,24},{8,0},{16,8},{24,16},{1,25},{9,1},{17,9},{25,17},{2,26},{10... | collective-permute-start | bytes 196616 | tf_op jit(solution)/shard_map/ppermute | solution.py:385
  10.2 1.1 %collective-permute-done.refs_2_ = bf16[32,2,8,128]{3,2,1,0:T(8,128)(2,1)S(1)} collective-permute-done((bf16[32,2,8,128]{3,2,1,0:T(8,128)(2,1)}, bf16[32,2,8,128]{3,2,1,0:T(8,128)(2,1)S(1)}, u32[]{:S(2)}, u32[]{:S(2)}) %collective-permute-start) | collective-permute-done | bytes 131104 | tf_op jit(solution)/shard_map/ppermute | solution.py:389
  11.4 0.7 %collective-permute-start.1 = (bf16[32,2,8,128]{3,2,1,0:T(8,128)(2,1)S(1)}, bf16[32,2,8,128]{3,2,1,0:T(8,128)(2,1)S(1)}, u32[]{:S(2)}, u32[]{:S(2)}) collective-permute-start(bf16[32,2,8,128]{3,2,1,0:T(8,128)(2,1)S(1)} %collective-permute-done.refs_2_), channel_id=1, source_target_pairs={{0,2},{1,3},{2,0},{3,1},{4,6},{5,7},{6,4},{7,5},{8,10},{9,11},{10,... | collective-permute-start | bytes 393224 | tf_op jit(solution)/shard_map/ppermute | solution.py:389
  12.4 3.0 %collective-permute-done.7.go_below_ref = bf16[8,32,128]{2,1,0:T(8,128)(2,1)S(1)} collective-permute-done((bf16[8,32,128]{2,1,0:T(8,128)(2,1)S(1)}, bf16[8,32,128]{2,1,0:T(8,128)(2,1)S(1)}, u32[]{:S(2)}, u32[]{:S(2)}) %collective-permute-start.7) | collective-permute-done | bytes 65568 | tf_op jit(solution)/shard_map/ppermute | solution.py:385
  16.9 0.7 %assemble.1.refs_1_ = bf16[256,2048]{1,0:T(8,128)(2,1)S(1)} custom-call(s32[1]{0:T(128)} %bitcast.me_ref, bf16[32,2,8,128]{3,2,1,0:T(8,128)(2,1)S(1)} %get-tuple-element.35.refs_0_, bf16[32,2,8,128]{3,2,1,0:T(8,128)(2,1)S(1)} %collective-permute-done.3.refs_1_, bf16[32,2,8,128]{3,2,1,0:T(8,128)(2,1)S(1)} %collective-permute-done.refs_2_, ...), custom_call_target="tpu_custom_call" | custom-call | flops 4000000000 | bytes 1966084 | tf_op jit(solution)/shard_map/assemble/pallas_call | solution.py:110
  17.7 1.3 %forward.1 = (f32[16,32,128]{2,1,0:T(8,128)S(1)}, bf16[16,32,128]{2,1,0:T(8,128)(2,1)S(1)}, bf16[16,32,128]{2,1,0:T(8,128)(2,1)S(1)}, bf16[256,2048]{1,0:T(8,128)(2,1)S(1)}) custom-call(s32[1]{0:T(128)} %bitcast.me_ref, bf16[864,256]{1,0:T(8,128)(2,1)S(1)} %get-tuple-element.33.w_ref, ...), custom_call_target="tpu_custom_call", output_to_operand_aliasing={{3}: (3, {})} | custom-call | flops 900000000 | bytes 3194884 | tf_op jit(solution)/shard_map/forward/pallas_call | solution.py:110
  19.0 2.8 %collective-permute-start.10 = (bf16[16,32,128]{2,1,0:T(8,128)(2,1)S(1)}, bf16[16,32,128]{2,1,0:T(8,128)(2,1)S(1)}, u32[]{:S(2)}, u32[]{:S(2)}) collective-permute-start(bf16[16,32,128]{2,1,0:T(8,128)(2,1)S(1)} %get-tuple-element.40.low_ref), channel_id=1, source_target_pairs={{0,24},{8,0},{16,8},{24,16},{1,25},{9,1},{17,9},{25,17},{2,26},{10... | collective-permute-start | bytes 393224 | tf_op jit(solution)/shard_map/ppermute | solution.py:385
  21.8 3.9 %collective-permute-done.10.above_ref = bf16[16,32,128]{2,1,0:T(8,128)(2,1)S(1)} collective-permute-done((bf16[16,32,128]{2,1,0:T(8,128)(2,1)S(1)}, bf16[16,32,128]{2,1,0:T(8,128)(2,1)S(1)}, u32[]{:S(2)}, u32[]{:S(2)}) %collective-permute-start.10) | collective-permute-done | bytes 131104 | tf_op jit(solution)/shard_map/ppermute | solution.py:385
  25.6 2.8 %collective-permute-done.9.below_ref = bf16[16,32,128]{2,1,0:T(8,128)(2,1)S(1)} collective-permute-done((bf16[16,32,128]{2,1,0:T(8,128)(2,1)S(1)}, bf16[16,32,128]{2,1,0:T(8,128)(2,1)S(1)}, u32[]{:S(2)}, u32[]{:S(2)}) %collective-permute-start.9) | collective-permute-done | bytes 131104 | tf_op jit(solution)/shard_map/ppermute | solution.py:385
  28.4 2.2 %gradient.1 = (bf16[32,2,8,128]{3,2,1,0:T(8,128)(2,1)}, f32[32,128]{1,0:T(8,128)S(1)}, bf16[864,2048]{1,0:T(8,128)(2,1)S(1)}, bf16[4,16,32,128]{3,2,1,0:T(8,128)(2,1)S(1)}, bf16[4,16,32,128]{3,2,1,0:T(8,128)(2,1)S(1)}) custom-call(f32[16,32,128]{2,1,0:T(8,128)S(1)} %get-tuple-element.39.own_ref, bf16[16,32,128]{2,1,0:T(8,128)(2,1)S(1)} %get-tuple-element.40.low_ref, ...), custom_call_target="tpu_custom_call" | custom-call | flops 905969664 | bytes 6242304 | tf_op jit(solution)/shard_map/gradient/pallas_call | solution.py:110
  30.5 0.7 %filter_first.1.a_ref = bf16[448,256]{1,0:T(8,128)(2,1)S(1)} custom-call(bf16[864,2048]{1,0:T(8,128)(2,1)S(1)} %get-tuple-element.48.s_ref, bf16[256,2048]{1,0:T(8,128)(2,1)S(1)} %get-tuple-element.49.x_ref, f32[32,128]{1,0:T(8,128)S(1)} %get-tuple-element.50.total_ref._, f32[32,128]{1,0:T(8,128)S(1)} %get-tuple-element.50.total_ref._), custom_call_target="tpu_custom_call" | custom-call | flops 452984832 | bytes 4849664 | tf_op jit(solution)/shard_map/filter_first/pallas_call | solution.py:110
  31.2 1.8 %collective-permute-start.11 = (bf16[448,256]{1,0:T(8,128)(2,1)S(1)}, bf16[448,256]{1,0:T(8,128)(2,1)S(1)}, u32[]{:S(2)}, u32[]{:S(2)}) collective-permute-start(bf16[448,256]{1,0:T(8,128)(2,1)S(1)} %filter_first.1.a_ref), channel_id=1, source_target_pairs={{0,8},{1,17},{2,10},{3,19},{4,12},{5,21},{6,14},{7,23},{8,0},{9,25... | collective-permute-start | bytes 688136 | tf_op jit(solution)/shard_map/ppermute | solution.py:399
  33.1 0.6 %filter_second.1.a_ref = bf16[448,256]{1,0:T(8,128)(2,1)S(1)} custom-call(bf16[864,2048]{1,0:T(8,128)(2,1)S(1)} %get-tuple-element.48.s_ref, bf16[256,2048]{1,0:T(8,128)(2,1)S(1)} %get-tuple-element.49.x_ref, f32[32,128]{1,0:T(8,128)S(1)} %get-tuple-element.50.total_ref._, f32[16,32,128]{2,1,0:T(8,128)S(1)} %get-tuple-element.53._.a_ref), custom_call_target="tpu_custom_call" | custom-call | flops 452984832 | bytes 5095424 | tf_op jit(solution)/shard_map/filter_second/pallas_call | solution.py:110
  33.8 1.2 %collective-permute-start.14 = (bf16[448,256]{1,0:T(8,128)(2,1)S(1)}, bf16[448,256]{1,0:T(8,128)(2,1)S(1)}, u32[]{:S(2)}, u32[]{:S(2)}) collective-permute-start(bf16[448,256]{1,0:T(8,128)(2,1)S(1)} %filter_second.1.a_ref), channel_id=1, source_target_pairs={{0,8},{1,17},{2,10},{3,19},{4,12},{5,21},{6,14},{7,23},{8,0},{9,25... | collective-permute-start | bytes 688136 | tf_op jit(solution)/shard_map/ppermute | solution.py:399
  35.0 3.6 %collective-permute-start.16 = (bf16[16,32,128]{2,1,0:T(8,128)(2,1)S(1)}, bf16[16,32,128]{2,1,0:T(8,128)(2,1)S(1)}, u32[]{:S(2)}, u32[]{:S(2)}) collective-permute-start(bf16[16,32,128]{2,1,0:T(8,128)(2,1)S(1)} %get-tuple-element.54), channel_id=1, source_target_pairs={{0,6},{1,7},{2,4},{3,5},{4,2},{5,3},{6,0},{7,1},{8,14},{9,15},{10,... | collective-permute-start | bytes 393224 | tf_op jit(solution)/shard_map/ppermute | solution.py:389
  38.6 0.8 %collective-permute-start.18 = (bf16[16,32,128]{2,1,0:T(8,128)(2,1)S(1)}, bf16[16,32,128]{2,1,0:T(8,128)(2,1)S(1)}, u32[]{:S(2)}, u32[]{:S(2)}) collective-permute-start(bf16[16,32,128]{2,1,0:T(8,128)(2,1)S(1)} %get-tuple-element.56), channel_id=1, source_target_pairs={{0,2},{1,3},{2,0},{3,1},{4,6},{5,7},{6,4},{7,5},{8,10},{9,11},{10,... | collective-permute-start | bytes 393224 | tf_op jit(solution)/shard_map/ppermute | solution.py:389
  39.5 0.6 %collective-permute-start.13 = (bf16[448,256]{1,0:T(8,128)(2,1)S(1)}, bf16[448,256]{1,0:T(8,128)(2,1)S(1)}, u32[]{:S(2)}, u32[]{:S(2)}) collective-permute-start(bf16[448,256]{1,0:T(8,128)(2,1)S(1)} %pair_sum.2.a_ref), channel_id=1, source_target_pairs={{0,16},{1,9},{2,18},{3,11},{4,20},{5,13},{6,22},{7,15},{8,24},{9,1... | collective-permute-start | bytes 688136 | tf_op jit(solution)/shard_map/ppermute | solution.py:399
  40.1 1.6 %collective-permute-start.15 = (bf16[448,256]{1,0:T(8,128)(2,1)S(1)}, bf16[448,256]{1,0:T(8,128)(2,1)S(1)}, u32[]{:S(2)}, u32[]{:S(2)}) collective-permute-start(bf16[448,256]{1,0:T(8,128)(2,1)S(1)} %pair_sum.3.c_ref), channel_id=1, source_target_pairs={{0,16},{1,9},{2,18},{3,11},{4,20},{5,13},{6,22},{7,15},{8,24},{9,1... | collective-permute-start | bytes 688136 | tf_op jit(solution)/shard_map/ppermute | solution.py:399
  41.7 1.6 %collective-permute-done.16.b_ref = bf16[16,32,128]{2,1,0:T(8,128)(2,1)S(1)} collective-permute-done((bf16[16,32,128]{2,1,0:T(8,128)(2,1)S(1)}, bf16[16,32,128]{2,1,0:T(8,128)(2,1)S(1)}, u32[]{:S(2)}, u32[]{:S(2)}) %collective-permute-start.16) | collective-permute-done | bytes 131104 | tf_op jit(solution)/shard_map/ppermute | solution.py:389
  43.2 5.6 %collective-permute-done.17.c_ref = bf16[16,32,128]{2,1,0:T(8,128)(2,1)S(1)} collective-permute-done((bf16[16,32,128]{2,1,0:T(8,128)(2,1)S(1)}, bf16[16,32,128]{2,1,0:T(8,128)(2,1)S(1)}, u32[]{:S(2)}, u32[]{:S(2)}) %collective-permute-start.17) | collective-permute-done | bytes 131104 | tf_op jit(solution)/shard_map/ppermute | solution.py:389
  48.9 1.1 %last.1 = (f32[27,32,256]{2,1,0:T(8,128)}, f32[1,32]{1,0:T(1,128)}, bf16[32,2,8,128]{3,2,1,0:T(8,128)(2,1)}) custom-call(bf16[448,256]{1,0:T(8,128)(2,1)S(1)} %pair_sum.2.a_ref, bf16[448,256]{1,0:T(8,128)(2,1)S(1)} %collective-permute-done.13.b_ref, bf16[448,256]{1,0:T(8,128)(2,1)S(1)} %pair_sum.3.c_ref, bf16[448,256]{1,0:T(8,128)(2,1)S(1)} %collective-permute-done.15.d_ref, ...), custom_call_target="tpu_custom_call" | custom-call | bytes 2195584 | tf_op jit(solution)/shard_map/last/pallas_call | solution.py:110
  (25 shorter events, 2.2 us)
Async XLA Ops:
  0.6 10.7 %collective-permute-start = (bf16[32,2,8,128]{3,2,1,0:T(8,128)(2,1)}, bf16[32,2,8,128]{3,2,1,0:T(8,128)(2,1)S(1)}, u32[]{:S(2)}, u32[]{:S(2)}) collective-permute-start(bf16[32,2,8,128]{3,2,1,0:T(8,128)(2,1)} %x_hbm.1), channel_id=1, source_target_pairs={{0,4},{1,5},{2,6},{3,7},{4,0},{5,1},{6,2},{7,3},{8,12},{9,13},{10,... | collective-permute-start | bytes 393224 | tf_op jit(solution)/shard_map/ppermute | solution.py:389
  4.7 10.7 %collective-permute-start.3 = (bf16[32,2,8,128]{3,2,1,0:T(8,128)(2,1)}, bf16[32,2,8,128]{3,2,1,0:T(8,128)(2,1)S(1)}, u32[]{:S(2)}, u32[]{:S(2)}) collective-permute-start(bf16[32,2,8,128]{3,2,1,0:T(8,128)(2,1)} %x_hbm.1), channel_id=1, source_target_pairs={{0,2},{1,3},{2,0},{3,1},{4,6},{5,7},{6,4},{7,5},{8,10},{9,11},{10,... | collective-permute-start | bytes 393224 | tf_op jit(solution)/shard_map/ppermute | solution.py:389
  7.7 4.7 %collective-permute-start.6 = (bf16[8,32,128]{2,1,0:T(8,128)(2,1)S(1)}, bf16[8,32,128]{2,1,0:T(8,128)(2,1)S(1)}, u32[]{:S(2)}, u32[]{:S(2)}) collective-permute-start(bf16[8,32,128]{2,1,0:T(8,128)(2,1)S(1)} %get-tuple-element.36), channel_id=1, source_target_pairs={{0,24},{8,0},{16,8},{24,16},{1,25},{9,1},{17,9},{25,17},{2,26},{10... | collective-permute-start | bytes 196616 | tf_op jit(solution)/shard_map/ppermute | solution.py:385
  10.2 5.2 %collective-permute-start.7 = (bf16[8,32,128]{2,1,0:T(8,128)(2,1)S(1)}, bf16[8,32,128]{2,1,0:T(8,128)(2,1)S(1)}, u32[]{:S(2)}, u32[]{:S(2)}) collective-permute-start(bf16[8,32,128]{2,1,0:T(8,128)(2,1)S(1)} %get-tuple-element.37), channel_id=1, source_target_pairs={{0,8},{8,16},{16,24},{24,0},{1,9},{9,17},{17,25},{25,1},{2,10},{10... | collective-permute-start | bytes 196616 | tf_op jit(solution)/shard_map/ppermute | solution.py:385
  10.2 6.1 %collective-permute-start.4 = (bf16[32,2,8,128]{3,2,1,0:T(8,128)(2,1)}, bf16[32,2,8,128]{3,2,1,0:T(8,128)(2,1)S(1)}, u32[]{:S(2)}, u32[]{:S(2)}) collective-permute-start(bf16[32,2,8,128]{3,2,1,0:T(8,128)(2,1)} %x_hbm.1), channel_id=1, source_target_pairs={{0,1},{1,0},{2,3},{3,2},{4,5},{5,4},{6,7},{7,6},{8,9},{9,8},{10,11... | collective-permute-start | bytes 393224 | tf_op jit(solution)/shard_map/ppermute | solution.py:389
  11.4 5.0 %collective-permute-start.1 = (bf16[32,2,8,128]{3,2,1,0:T(8,128)(2,1)S(1)}, bf16[32,2,8,128]{3,2,1,0:T(8,128)(2,1)S(1)}, u32[]{:S(2)}, u32[]{:S(2)}) collective-permute-start(bf16[32,2,8,128]{3,2,1,0:T(8,128)(2,1)S(1)} %collective-permute-done.refs_2_), channel_id=1, source_target_pairs={{0,2},{1,3},{2,0},{3,1},{4,6},{5,7},{6,4},{7,5},{8,10},{9,11},{10,... | collective-permute-start | bytes 393224 | tf_op jit(solution)/shard_map/ppermute | solution.py:389
  15.4 1.3 %collective-permute-start.5 = (bf16[32,2,8,128]{3,2,1,0:T(8,128)(2,1)S(1)}, bf16[32,2,8,128]{3,2,1,0:T(8,128)(2,1)S(1)}, u32[]{:S(2)}, u32[]{:S(2)}) collective-permute-start(bf16[32,2,8,128]{3,2,1,0:T(8,128)(2,1)S(1)} %collective-permute-done.3.refs_1_), channel_id=1, source_target_pairs={{0,1},{1,0},{2,3},{3,2},{4,5},{5,4},{6,7},{7,6},{8,9},{9,8},{10,11... | collective-permute-start | bytes 393224 | tf_op jit(solution)/shard_map/ppermute | solution.py:389
  15.4 1.5 %collective-permute-start.8 = (bf16[32,2,8,128]{3,2,1,0:T(8,128)(2,1)S(1)}, bf16[32,2,8,128]{3,2,1,0:T(8,128)(2,1)S(1)}, u32[]{:S(2)}, u32[]{:S(2)}) collective-permute-start(bf16[32,2,8,128]{3,2,1,0:T(8,128)(2,1)S(1)} %collective-permute-done.refs_2_), channel_id=1, source_target_pairs={{0,1},{1,0},{2,3},{3,2},{4,5},{5,4},{6,7},{7,6},{8,9},{9,8},{10,11... | collective-permute-start | bytes 393224 | tf_op jit(solution)/shard_map/ppermute | solution.py:389
  16.3 1.3 %collective-permute-start.2 = (bf16[32,2,8,128]{3,2,1,0:T(8,128)(2,1)S(1)}, bf16[32,2,8,128]{3,2,1,0:T(8,128)(2,1)S(1)}, u32[]{:S(2)}, u32[]{:S(2)}) collective-permute-start(bf16[32,2,8,128]{3,2,1,0:T(8,128)(2,1)S(1)} %collective-permute-done.1.refs_3_), channel_id=1, source_target_pairs={{0,1},{1,0},{2,3},{3,2},{4,5},{5,4},{6,7},{7,6},{8,9},{9,8},{10,11... | collective-permute-start | bytes 393224 | tf_op jit(solution)/shard_map/ppermute | solution.py:389
  19.0 6.6 %collective-permute-start.10 = (bf16[16,32,128]{2,1,0:T(8,128)(2,1)S(1)}, bf16[16,32,128]{2,1,0:T(8,128)(2,1)S(1)}, u32[]{:S(2)}, u32[]{:S(2)}) collective-permute-start(bf16[16,32,128]{2,1,0:T(8,128)(2,1)S(1)} %get-tuple-element.40.low_ref), channel_id=1, source_target_pairs={{0,24},{8,0},{16,8},{24,16},{1,25},{9,1},{17,9},{25,17},{2,26},{10... | collective-permute-start | bytes 393224 | tf_op jit(solution)/shard_map/ppermute | solution.py:385
  21.7 6.6 %collective-permute-start.9 = (bf16[16,32,128]{2,1,0:T(8,128)(2,1)S(1)}, bf16[16,32,128]{2,1,0:T(8,128)(2,1)S(1)}, u32[]{:S(2)}, u32[]{:S(2)}) collective-permute-start(bf16[16,32,128]{2,1,0:T(8,128)(2,1)S(1)} %get-tuple-element.41.high_ref), channel_id=1, source_target_pairs={{0,8},{8,16},{16,24},{24,0},{1,9},{9,17},{17,25},{25,1},{2,10},{10... | collective-permute-start | bytes 393224 | tf_op jit(solution)/shard_map/ppermute | solution.py:385
  30.5 2.5 %collective-permute-start.12 = (bf16[4,16,32,128]{3,2,1,0:T(8,128)(2,1)S(1)}, bf16[4,16,32,128]{3,2,1,0:T(8,128)(2,1)S(1)}, u32[]{:S(2)}, u32[]{:S(2)}) collective-permute-start(bf16[4,16,32,128]{3,2,1,0:T(8,128)(2,1)S(1)} %get-tuple-element.52), channel_id=1, source_target_pairs={{0,1},{1,0},{2,3},{3,2},{4,5},{5,4},{6,7},{7,6},{8,9},{9,8},{10,11... | collective-permute-start | bytes 1572872 | tf_op jit(solution)/shard_map/ppermute | solution.py:389
  31.2 8.2 %collective-permute-start.11 = (bf16[448,256]{1,0:T(8,128)(2,1)S(1)}, bf16[448,256]{1,0:T(8,128)(2,1)S(1)}, u32[]{:S(2)}, u32[]{:S(2)}) collective-permute-start(bf16[448,256]{1,0:T(8,128)(2,1)S(1)} %filter_first.1.a_ref), channel_id=1, source_target_pairs={{0,8},{1,17},{2,10},{3,19},{4,12},{5,21},{6,14},{7,23},{8,0},{9,25... | collective-permute-start | bytes 688136 | tf_op jit(solution)/shard_map/ppermute | solution.py:399
  33.8 6.3 %collective-permute-start.14 = (bf16[448,256]{1,0:T(8,128)(2,1)S(1)}, bf16[448,256]{1,0:T(8,128)(2,1)S(1)}, u32[]{:S(2)}, u32[]{:S(2)}) collective-permute-start(bf16[448,256]{1,0:T(8,128)(2,1)S(1)} %filter_second.1.a_ref), channel_id=1, source_target_pairs={{0,8},{1,17},{2,10},{3,19},{4,12},{5,21},{6,14},{7,23},{8,0},{9,25... | collective-permute-start | bytes 688136 | tf_op jit(solution)/shard_map/ppermute | solution.py:399
  35.0 8.2 %collective-permute-start.16 = (bf16[16,32,128]{2,1,0:T(8,128)(2,1)S(1)}, bf16[16,32,128]{2,1,0:T(8,128)(2,1)S(1)}, u32[]{:S(2)}, u32[]{:S(2)}) collective-permute-start(bf16[16,32,128]{2,1,0:T(8,128)(2,1)S(1)} %get-tuple-element.54), channel_id=1, source_target_pairs={{0,6},{1,7},{2,4},{3,5},{4,2},{5,3},{6,0},{7,1},{8,14},{9,15},{10,... | collective-permute-start | bytes 393224 | tf_op jit(solution)/shard_map/ppermute | solution.py:389
  38.6 10.2 %collective-permute-start.17 = (bf16[16,32,128]{2,1,0:T(8,128)(2,1)S(1)}, bf16[16,32,128]{2,1,0:T(8,128)(2,1)S(1)}, u32[]{:S(2)}, u32[]{:S(2)}) collective-permute-start(bf16[16,32,128]{2,1,0:T(8,128)(2,1)S(1)} %get-tuple-element.55), channel_id=1, source_target_pairs={{0,4},{1,5},{2,6},{3,7},{4,0},{5,1},{6,2},{7,3},{8,12},{9,13},{10,... | collective-permute-start | bytes 393224 | tf_op jit(solution)/shard_map/ppermute | solution.py:389
  38.6 10.2 %collective-permute-start.18 = (bf16[16,32,128]{2,1,0:T(8,128)(2,1)S(1)}, bf16[16,32,128]{2,1,0:T(8,128)(2,1)S(1)}, u32[]{:S(2)}, u32[]{:S(2)}) collective-permute-start(bf16[16,32,128]{2,1,0:T(8,128)(2,1)S(1)} %get-tuple-element.56), channel_id=1, source_target_pairs={{0,2},{1,3},{2,0},{3,1},{4,6},{5,7},{6,4},{7,5},{8,10},{9,11},{10,... | collective-permute-start | bytes 393224 | tf_op jit(solution)/shard_map/ppermute | solution.py:389
  39.5 9.4 %collective-permute-start.13 = (bf16[448,256]{1,0:T(8,128)(2,1)S(1)}, bf16[448,256]{1,0:T(8,128)(2,1)S(1)}, u32[]{:S(2)}, u32[]{:S(2)}) collective-permute-start(bf16[448,256]{1,0:T(8,128)(2,1)S(1)} %pair_sum.2.a_ref), channel_id=1, source_target_pairs={{0,16},{1,9},{2,18},{3,11},{4,20},{5,13},{6,22},{7,15},{8,24},{9,1... | collective-permute-start | bytes 688136 | tf_op jit(solution)/shard_map/ppermute | solution.py:399
  40.1 8.8 %collective-permute-start.15 = (bf16[448,256]{1,0:T(8,128)(2,1)S(1)}, bf16[448,256]{1,0:T(8,128)(2,1)S(1)}, u32[]{:S(2)}, u32[]{:S(2)}) collective-permute-start(bf16[448,256]{1,0:T(8,128)(2,1)S(1)} %pair_sum.3.c_ref), channel_id=1, source_target_pairs={{0,16},{1,9},{2,18},{3,11},{4,20},{5,13},{6,22},{7,15},{8,24},{9,1... | collective-permute-start | bytes 688136 | tf_op jit(solution)/shard_map/ppermute | solution.py:399

commit v11 on v10

--- a/solution.py
+++ b/solution.py
@@ -138,7 +138,6 @@
 def prepare_body(
     n,
     rows,
-    me_ref,
     x_hbm,
     go_hbm,
     w_hbm,
@@ -153,7 +152,6 @@
     go_in,
     w_in,
     bias_in,
-    back_in,
     wide_ref,
     sems,
 ):
@@ -177,20 +175,23 @@
     copies[3].wait()
     flat = w_in[...].reshape(flat_ref.shape)
     flat_ref[...] = flat
+    back_ref[...] = jnp.transpose(flat)
     o = bias_ref.shape[0]
-    back_in[...] = jnp.transpose(flat)
-    for b in range(8):
-        place = pl.ds(pl.multiple_of(owner(me_ref, b) * o, o), o)
-        back_ref[b * o : (b + 1) * o] = back_in[place]
     row = jnp.broadcast_to(bias_in[...].astype(jnp.float32), (o, o))
     same = lax.broadcasted_iota(jnp.int32, (o, o), 0) == lax.broadcasted_iota(jnp.int32, (o, o), 1)
     column = jnp.sum(jnp.where(same, row, 0.0), axis=1, keepdims=True)
     bias_ref[...] = jnp.broadcast_to(column, bias_ref.shape)
 
 
+def by_core(even, odd, me_ref):
+    core = lax.rem(me_ref[0], 2)
+    return (1 - core) * owner(me_ref, even) + core * owner(me_ref, odd)
+
+
 def place_block(me_ref, b, block_ref, x_ref, wide_ref):
     o = block_ref.shape[0]
-    place = pl.ds(pl.multiple_of(owner(me_ref, b) * o, o), o)
+    at = b(me_ref) if callable(b) else owner(me_ref, b)
+    place = pl.ds(pl.multiple_of(at * o, o), o)
     for k, value in enumerate(turned(block_ref[...], wide_ref)):
         x_ref[place, k * LANES : (k + 1) * LANES] = value
 
@@ -205,12 +206,18 @@
     return jnp.bitwise_xor(me_ref[0], 2 * (b % 4) + b // 4)
 
 
-def forward_body(n, rows, o, places, me_ref, w_ref, *refs):
-    blocks = refs[: len(places)]
-    own_ref, low_ref, high_ref, x_ref, acc, wide_ref = refs[len(places) + 1 :]
-    for b, block in zip(places, blocks):
-        place_block(me_ref, b, block, x_ref, wide_ref)
-    w = w_ref[...]
+def forward_body(n, rows, o, me_ref, w_ref, *refs):
+    blocks = refs[:4]
+    own_ref, low_ref, high_ref, x_ref, acc, w_copy, wide_ref = refs[5:]
+    w_copy[...] = w_ref[...]
+    for core, pair in enumerate((blocks[:2], blocks[2:])):
+
+        @pl.when(lax.rem(me_ref[0], 2) == core)
+        def _():
+            for b, block in zip((3, 7), pair):
+                place_block(me_ref, b, block, x_ref, wide_ref)
+
+    w = w_copy[...]
     seen = set()
     for p in range(n):
         for t in range(0, rows, 2):
@@ -251,6 +258,7 @@
     rows,
     o,
     scale,
+    me_ref,
     own_ref,
     low_ref,
     high_ref,
@@ -260,19 +268,22 @@
     go_ref,
     go_below_ref,
     go_above_ref,
-    w_ref,
+    back_ref,
     act_ref,
     total_ref,
     s_ref,
     other_ref,
     mine_ref,
+    w_ref,
     wide_ref,
 ):
     f32, bf16 = jnp.float32, jnp.bfloat16
+    for b in range(8):
+        place = pl.ds(pl.multiple_of(owner(me_ref, b) * o, o), o)
+        w_ref[b * o : (b + 1) * o] = back_ref[place]
     total = jnp.zeros((o, LANES), f32)
-
-    def shift_row(y, total):
-        for q in range(n + 2):
+    for q in range(n + 2):
+        for y in range(rows):
             if q == 0:
                 pre = below_ref[rows + y].astype(f32) + low_ref[y].astype(f32)
                 go = go_below_ref[y]
@@ -304,26 +315,22 @@
                 if 0 <= p < n:
                     at = (p * rows + (y + j - 1) % rows) * LANES
                     s_ref[k * o : (k + 1) * o, at : at + LANES] = shifts[l]
-        return total
-
-    def multiply(t):
-        at = t * LANES
-        part = jnp.dot(
-            w_ref[...], s_ref[:, at : at + 2 * LANES], preferred_element_type=f32
-        ).astype(bf16)
-        for h in range(2):
-            for b in range(8):
-                cut = part[b * o : (b + 1) * o, h * LANES : (h + 1) * LANES]
-                (mine_ref if b < 4 else other_ref)[b % 4, t + h] = cut
-
-    for y in range(rows):
-        total = shift_row(y, total)
-    for t in range(0, n * rows, 2):
-        multiply(t)
     act_ref[...] = wide_ref[...].reshape(act_ref.shape).astype(bf16)
     total_ref[...] = jnp.broadcast_to(
         jnp.sum(total, axis=1, keepdims=True) * scale, total_ref.shape
     )
+    input_grad(n * rows, o, w_ref[...], s_ref, [(ref, r) for ref in (mine_ref, other_ref) for r in range(4)])
+
+
+def input_grad(cells, o, w, s_ref, outs):
+    for t in range(0, cells, 2):
+        part = jnp.dot(
+            w, s_ref[:, t * LANES : (t + 2) * LANES], preferred_element_type=jnp.float32
+        ).astype(outs[0][0].dtype)
+        for h in range(2):
+            for r, (out_ref, at) in enumerate(outs):
+                cut = part[r * o : (r + 1) * o, h * LANES : (h + 1) * LANES]
+                out_ref[at, t + h] = cut
 
 
 def filter_grad_body(scale, start, o, s_ref, x_ref, total_ref, _, out_ref):
@@ -389,6 +396,12 @@
     return lax.ppermute(value, axis, [(i, i ^ bit) for i in range(lax.axis_size(axis))])
 
 
+def core_swap(value, even, odd):
+    steps = (even, odd)
+    pairs = [(c, c ^ steps[c % 2]) for c in range(lax.axis_size("chan")) if steps[c % 2]]
+    return lax.ppermute(value, "chan", pairs)
+
+
 def cross(value, phase):
     slabs, chans = lax.axis_size("slab"), lax.axis_size("chan")
     pairs = [
@@ -410,8 +423,8 @@
 
     block_wide = [pltpu.VMEM((o * cells, depth), f32)]
 
-    x_b = swap(x_in, "chan", 4)
-    x_a = swap(x_in, "chan", 2)
+    x_1 = core_swap(x_in, 4, 2)
+    x_2 = core_swap(x_in, 2, 4)
     x_side = swap(x_in, "chan", 1)
     x_own, go, go_low, go_high, w_flat, w_back, bias = call(
         functools.partial(prepare_body, n, rows),
@@ -424,13 +437,12 @@
             shape_of((c_all, 27 * o), bf16),
             shape_of((o, LANES), f32),
         ],
-        [me] + [in_hbm(a) for a in (x_in, grad_out, jnp.transpose(weight, (1, 0, 2)), bias_vec[None, :])],
-        [SMEM] + [HBM] * 4,
+        [in_hbm(a) for a in (x_in, grad_out, jnp.transpose(weight, (1, 0, 2)), bias_vec[None, :])],
+        [HBM] * 4,
         [
             pltpu.VMEM((o, n, rows, depth), bf16),
             pltpu.VMEM((27, o, c_all), bf16),
             pltpu.VMEM((1, o), bf16),
-            pltpu.VMEM((c_all, 27 * o), bf16),
             *block_wide,
             pltpu.SemaphoreType.DMA((4,)),
         ],
@@ -438,36 +450,49 @@
     )
     go_above = rotate(go_low, "slab", -1)
     go_below = rotate(go_high, "slab", 1)
-    x_b, w_flat = lax.optimization_barrier((x_b, w_flat))
-    x_ab = swap(x_b, "chan", 2)
-    late_b, go_above, go_below = lax.optimization_barrier((x_b, go_above, go_below))
-    x_a_side = swap(x_a, "chan", 1)
-    x_b_side = swap(late_b, "chan", 1)
-    early, late = (0, 1, 2, 3, 4, 5, 6), (7,)
+    x_1, w_flat = lax.optimization_barrier((x_1, w_flat))
+    ab_0 = core_swap(x_1, 2, None)
+    ab_1 = core_swap(x_2, None, 2)
+    late_2, go_above, go_below = lax.optimization_barrier((x_2, go_above, go_below))
+    x_1_side = swap(x_1, "chan", 1)
+    x_2_side = swap(late_2, "chan", 1)
+    ab_0_side = core_swap(ab_0, 1, None)
+    ab_1_side = core_swap(ab_1, None, 1)
+    early = [
+        0,
+        functools.partial(by_core, 2, 1),
+        functools.partial(by_core, 1, 2),
+        4,
+        functools.partial(by_core, 5, 6),
+        functools.partial(by_core, 6, 5),
+    ]
     (x_all,) = call(
         functools.partial(assemble_body, early),
         [shape_of((c_all, cells * depth), bf16)],
-        [me, x_own, x_a, x_b, x_ab, x_side, x_a_side, x_b_side],
-        [SMEM] + [VMEM] * 7,
+        [me, x_own, x_1, x_2, x_side, x_1_side, x_2_side],
+        [SMEM] + [VMEM] * 6,
         block_wide,
         flops=ASSEMBLE_FLOPS,
         name="assemble",
     )
-    x_ab_side = swap(x_ab, "chan", 1)
     own, low, high, x_all = call(
-        functools.partial(forward_body, n, rows, o, late),
+        functools.partial(forward_body, n, rows, o),
         [
             shape_of((cells, o, depth), f32),
             shape_of((2 * rows, o, depth), bf16),
             shape_of((2 * rows, o, depth), bf16),
             shape_of((c_all, cells * depth), bf16),
         ],
-        [me, w_flat, x_ab_side, x_all],
-        [SMEM] + [VMEM] * 3,
-        [pltpu.VMEM((3, n + 2, rows, o, depth), f32), *block_wide],
+        [me, w_flat, ab_0, ab_1_side, ab_1, ab_0_side, x_all],
+        [SMEM] + [VMEM] * 6,
+        [
+            pltpu.VMEM((3, n + 2, rows, o, depth), f32),
+            pltpu.VMEM((27 * o, c_all), bf16),
+            *block_wide,
+        ],
         flops=FORWARD_FLOPS,
         name="forward",
-        aliases={3: 3},
+        aliases={6: 3},
     )
     above = rotate(low, "slab", -1)
     below = rotate(high, "slab", 1)
@@ -480,9 +505,9 @@
             shape_of((4, cells, o, depth), bf16),
             shape_of((4, cells, o, depth), bf16),
         ],
-        [own, low, high, below, above, bias, go, go_below, go_above, w_back],
-        [VMEM] * 10,
-        block_wide,
+        [me, own, low, high, below, above, bias, go, go_below, go_above, w_back],
+        [SMEM] + [VMEM] * 10,
+        [pltpu.VMEM((c_all, 27 * o), bf16), *block_wide],
         flops=flops,
         name="gradient",
     )

time: 50.2 us -> 55 us (1.096)
  starting transfers between devices: 21.8 us -> 28.7 us
  waiting for transfers between devices: 19.3 us -> 17.4 us
    ppermute x0 -> x6, starting transfers between devices: none -> 12.9 us  [core_swap(): return lax.ppermute(value, 'chan', pairs)]
    ppermute x11 -> x7, starting transfers between devices: 11.3 us -> 4.97 us  [swap(): lax.ppermute(value, axis, [(i, i ^ bit) for i in range(lax.axis_size(axis...]
    ppermute x0 -> x6, waiting for transfers between devices: none -> 3.83 us  [core_swap(): return lax.ppermute(value, 'chan', pairs)]
    ppermute x11 -> x7, waiting for transfers between devices: 9.32 us -> 6.38 us  [swap(): lax.ppermute(value, axis, [(i, i ^ bit) for i in range(lax.axis_size(axis...]
    ppermute x4, waiting for transfers between devices: 9.92 us -> 7.2 us  [rotate(): lax.ppermute(value, axis, [(i, (i + step) % count) for i in range(count)])]
  transfers between devices with their start and end apart: 19 -> 21, of which waited for: 10 -> 8; matrix products, arithmetic and copies ran while one was open for 0% -> 0% of each run, Pallas kernels for 7% -> 7%
where the time goes in v11:
time: 55 us; the launch traced here: 54.8 us
  starting transfers between devices  28.7 us (52%)
  waiting for transfers between devices  17.4 us (32%)
  Pallas kernels  7.85 us (14%)
  between operations  0.8 us (1%)
    ppermute x6, starting transfers between devices, core_swap(): return lax.ppermute(value, 'chan', pairs)  12.9 us
    pallas_call x11, Pallas kernels, call(): pl.pallas_call(body, out_shape=out_shape, in_specs=specs or [VMEM] * len(...  7.85 us
    ppermute x4, waiting for transfers between devices, rotate(): lax.ppermute(value, axis, [(i, (i + step) % count) for i in range(count)])  7.2 us
    ppermute x7, waiting for transfers between devices, swap(): lax.ppermute(value, axis, [(i, i ^ bit) for i in range(lax.axis_size(axis...  6.38 us
    ppermute x4, starting transfers between devices, rotate(): lax.ppermute(value, axis, [(i, (i + step) % count) for i in range(count)])  5.69 us
    ppermute x4, starting transfers between devices, cross(): return lax.ppermute(value, ('slab', 'chan'), pairs)  5.17 us
    ppermute x7, starting transfers between devices, swap(): lax.ppermute(value, axis, [(i, i ^ bit) for i in range(lax.axis_size(axis...  4.97 us
    ppermute x6, waiting for transfers between devices, core_swap(): return lax.ppermute(value, 'chan', pairs)  3.83 us
  transfers between devices with their start and end apart: 21, of which 8 were waited for; matrix products, arithmetic and copies ran while one was open for 0% of the time, Pallas kernels for 7%

profile of v11, /device:TPU:0, one launch (start us, length us, event | category | flops | bytes accessed | tf_op | source)
XLA Modules:
  0.0 54.8 jit_solution(12238940422324520936)
XLA Ops:
  0.6 4.1 %collective-permute-start = (bf16[32,2,8,128]{3,2,1,0:T(8,128)(2,1)}, bf16[32,2,8,128]{3,2,1,0:T(8,128)(2,1)S(1)}, u32[]{:S(2)}, u32[]{:S(2)}) collective-permute-start(bf16[32,2,8,128]{3,2,1,0:T(8,128)(2,1)} %x_hbm.1), channel_id=1, source_target_pairs={{0,4},{1,3},{2,6},{3,1},{4,0},{5,7},{6,2},{7,5},{8,12},{9,11},{10,... | collective-permute-start | bytes 393224 | tf_op jit(solution)/shard_map/ppermute | solution.py:402
  4.7 1.6 %collective-permute-start.2 = (bf16[32,2,8,128]{3,2,1,0:T(8,128)(2,1)}, bf16[32,2,8,128]{3,2,1,0:T(8,128)(2,1)S(1)}, u32[]{:S(2)}, u32[]{:S(2)}) collective-permute-start(bf16[32,2,8,128]{3,2,1,0:T(8,128)(2,1)} %x_hbm.1), channel_id=1, source_target_pairs={{0,2},{1,5},{2,0},{3,7},{4,6},{5,1},{6,4},{7,3},{8,10},{9,13},{10,... | collective-permute-start | bytes 393224 | tf_op jit(solution)/shard_map/ppermute | solution.py:402
  6.3 1.4 %prepare.1 = (bf16[32,2,8,128]{3,2,1,0:T(8,128)(2,1)S(1)}, bf16[16,32,128]{2,1,0:T(8,128)(2,1)S(1)}, bf16[8,32,128]{2,1,0:T(8,128)(2,1)S(1)}, bf16[8,32,128]{2,1...) custom-call(bf16[32,2,8,128]{3,2,1,0:T(8,128)(2,1)} %x_hbm.1, ...), custom_call_target="tpu_custom_call" | custom-call | bytes 1998912 | tf_op jit(solution)/shard_map/prepare/pallas_call | solution.py:110
  7.7 2.5 %collective-permute-start.8 = (bf16[8,32,128]{2,1,0:T(8,128)(2,1)S(1)}, bf16[8,32,128]{2,1,0:T(8,128)(2,1)S(1)}, u32[]{:S(2)}, u32[]{:S(2)}) collective-permute-start(bf16[8,32,128]{2,1,0:T(8,128)(2,1)S(1)} %get-tuple-element.36), channel_id=1, source_target_pairs={{0,24},{8,0},{16,8},{24,16},{1,25},{9,1},{17,9},{25,17},{2,26},{10... | collective-permute-start | bytes 196616 | tf_op jit(solution)/shard_map/ppermute | solution.py:392
  10.2 1.5 %collective-permute-done.refs_1_ = bf16[32,2,8,128]{3,2,1,0:T(8,128)(2,1)S(1)} collective-permute-done((bf16[32,2,8,128]{3,2,1,0:T(8,128)(2,1)}, bf16[32,2,8,128]{3,2,1,0:T(8,128)(2,1)S(1)}, u32[]{:S(2)}, u32[]{:S(2)}) %collective-permute-start) | collective-permute-done | bytes 131104 | tf_op jit(solution)/shard_map/ppermute | solution.py:402
  11.7 2.6 %collective-permute-start.1 = (bf16[32,2,8,128]{3,2,1,0:T(8,128)(2,1)S(1)}, bf16[32,2,8,128]{3,2,1,0:T(8,128)(2,1)S(1)}, u32[]{:S(2)}, u32[]{:S(2)}) collective-permute-start(bf16[32,2,8,128]{3,2,1,0:T(8,128)(2,1)S(1)} %collective-permute-done.refs_1_), channel_id=1, source_target_pairs={{0,2},{2,0},{4,6},{6,4},{8,10},{10,8},{12,14},{14,12},{16,18},{18,... | collective-permute-start | bytes 393224 | tf_op jit(solution)/shard_map/ppermute | solution.py:402
  14.3 0.7 %collective-permute-start.3 = (bf16[32,2,8,128]{3,2,1,0:T(8,128)(2,1)S(1)}, bf16[32,2,8,128]{3,2,1,0:T(8,128)(2,1)S(1)}, u32[]{:S(2)}, u32[]{:S(2)}) collective-permute-start(bf16[32,2,8,128]{3,2,1,0:T(8,128)(2,1)S(1)} %collective-permute-done.2.refs_2_), channel_id=1, source_target_pairs={{1,3},{3,1},{5,7},{7,5},{9,11},{11,9},{13,15},{15,13},{17,19},{19,... | collective-permute-start | bytes 393224 | tf_op jit(solution)/shard_map/ppermute | solution.py:402
  15.9 1.3 %collective-permute-start.4 = (bf16[32,2,8,128]{3,2,1,0:T(8,128)(2,1)S(1)}, bf16[32,2,8,128]{3,2,1,0:T(8,128)(2,1)S(1)}, u32[]{:S(2)}, u32[]{:S(2)}) collective-permute-start(bf16[32,2,8,128]{3,2,1,0:T(8,128)(2,1)S(1)} %collective-permute-done.3.refs_2_), channel_id=1, source_target_pairs={{1,0},{3,2},{5,4},{7,6},{9,8},{11,10},{13,12},{15,14},{17,16},{19,... | collective-permute-start | bytes 393224 | tf_op jit(solution)/shard_map/ppermute | solution.py:402
  17.1 2.1 %collective-permute-done.1.refs_0_ = bf16[32,2,8,128]{3,2,1,0:T(8,128)(2,1)S(1)} collective-permute-done((bf16[32,2,8,128]{3,2,1,0:T(8,128)(2,1)S(1)}, bf16[32,2,8,128]{3,2,1,0:T(8,128)(2,1)S(1)}, u32[]{:S(2)}, u32[]{:S(2)}) %collective-permute-start.1) | collective-permute-done | bytes 131104 | tf_op jit(solution)/shard_map/ppermute | solution.py:402
  19.2 2.7 %collective-permute-start.5 = (bf16[32,2,8,128]{3,2,1,0:T(8,128)(2,1)S(1)}, bf16[32,2,8,128]{3,2,1,0:T(8,128)(2,1)S(1)}, u32[]{:S(2)}, u32[]{:S(2)}) collective-permute-start(bf16[32,2,8,128]{3,2,1,0:T(8,128)(2,1)S(1)} %collective-permute-done.1.refs_0_), channel_id=1, source_target_pairs={{0,1},{2,3},{4,5},{6,7},{8,9},{10,11},{12,13},{14,15},{16,17},{18,... | collective-permute-start | bytes 393224 | tf_op jit(solution)/shard_map/ppermute | solution.py:402
  22.8 1.4 %forward.1 = (f32[16,32,128]{2,1,0:T(8,128)S(1)}, bf16[16,32,128]{2,1,0:T(8,128)(2,1)S(1)}, bf16[16,32,128]{2,1,0:T(8,128)(2,1)S(1)}, bf16[256,2048]{1,0:T(8,128)(2,1)S(1)}) custom-call(s32[1]{0:T(128)} %bitcast.me_ref, bf16[864,256]{1,0:T(8,128)(2,1)S(1)} %get-tuple-element.33.w_ref, ...), custom_call_target="tpu_custom_call", output_to_operand_aliasing={{3}: (6, {})} | custom-call | flops 900000000 | bytes 3588100 | tf_op jit(solution)/shard_map/forward/pallas_call | solution.py:110
  24.3 3.2 %collective-permute-start.12 = (bf16[16,32,128]{2,1,0:T(8,128)(2,1)S(1)}, bf16[16,32,128]{2,1,0:T(8,128)(2,1)S(1)}, u32[]{:S(2)}, u32[]{:S(2)}) collective-permute-start(bf16[16,32,128]{2,1,0:T(8,128)(2,1)S(1)} %get-tuple-element.40.low_ref), channel_id=1, source_target_pairs={{0,24},{8,0},{16,8},{24,16},{1,25},{9,1},{17,9},{25,17},{2,26},{10... | collective-permute-start | bytes 393224 | tf_op jit(solution)/shard_map/ppermute | solution.py:392
  27.5 3.8 %collective-permute-done.12.above_ref = bf16[16,32,128]{2,1,0:T(8,128)(2,1)S(1)} collective-permute-done((bf16[16,32,128]{2,1,0:T(8,128)(2,1)S(1)}, bf16[16,32,128]{2,1,0:T(8,128)(2,1)S(1)}, u32[]{:S(2)}, u32[]{:S(2)}) %collective-permute-start.12) | collective-permute-done | bytes 131104 | tf_op jit(solution)/shard_map/ppermute | solution.py:392
  31.3 3.0 %collective-permute-done.11.below_ref = bf16[16,32,128]{2,1,0:T(8,128)(2,1)S(1)} collective-permute-done((bf16[16,32,128]{2,1,0:T(8,128)(2,1)S(1)}, bf16[16,32,128]{2,1,0:T(8,128)(2,1)S(1)}, u32[]{:S(2)}, u32[]{:S(2)}) %collective-permute-start.11) | collective-permute-done | bytes 131104 | tf_op jit(solution)/shard_map/ppermute | solution.py:392
  34.3 1.7 %gradient.1 = (bf16[32,2,8,128]{3,2,1,0:T(8,128)(2,1)}, f32[32,128]{1,0:T(8,128)S(1)}, bf16[864,2048]{1,0:T(8,128)(2,1)S(1)}, bf16[4,16,32,128]{3,2,1,0:T(8,128)(2,1)S(1)}, bf16[4,16,32,128]{3,2,1,0:T(8,128)(2,1)S(1)}) custom-call(s32[1]{0:T(128)} %bitcast.me_ref, f32[16,32,128]{2,1,0:T(8,128)S(1)} %get-tuple-element.39.own_ref, ...), custom_call_target="tpu_custom_call" | custom-call | flops 905969664 | bytes 6242308 | tf_op jit(solution)/shard_map/gradient/pallas_call | solution.py:110
  36.1 0.7 %filter_first.1.a_ref = bf16[448,256]{1,0:T(8,128)(2,1)S(1)} custom-call(bf16[864,2048]{1,0:T(8,128)(2,1)S(1)} %get-tuple-element.48.s_ref, bf16[256,2048]{1,0:T(8,128)(2,1)S(1)} %get-tuple-element.49.x_ref, f32[32,128]{1,0:T(8,128)S(1)} %get-tuple-element.50.total_ref._, f32[32,128]{1,0:T(8,128)S(1)} %get-tuple-element.50.total_ref._), custom_call_target="tpu_custom_call" | custom-call | flops 452984832 | bytes 4849664 | tf_op jit(solution)/shard_map/filter_first/pallas_call | solution.py:110
  36.7 1.8 %collective-permute-start.13 = (bf16[448,256]{1,0:T(8,128)(2,1)S(1)}, bf16[448,256]{1,0:T(8,128)(2,1)S(1)}, u32[]{:S(2)}, u32[]{:S(2)}) collective-permute-start(bf16[448,256]{1,0:T(8,128)(2,1)S(1)} %filter_first.1.a_ref), channel_id=1, source_target_pairs={{0,8},{1,17},{2,10},{3,19},{4,12},{5,21},{6,14},{7,23},{8,0},{9,25... | collective-permute-start | bytes 688136 | tf_op jit(solution)/shard_map/ppermute | solution.py:412
  39.3 1.2 %collective-permute-start.16 = (bf16[448,256]{1,0:T(8,128)(2,1)S(1)}, bf16[448,256]{1,0:T(8,128)(2,1)S(1)}, u32[]{:S(2)}, u32[]{:S(2)}) collective-permute-start(bf16[448,256]{1,0:T(8,128)(2,1)S(1)} %filter_second.1.a_ref), channel_id=1, source_target_pairs={{0,8},{1,17},{2,10},{3,19},{4,12},{5,21},{6,14},{7,23},{8,0},{9,25... | collective-permute-start | bytes 688136 | tf_op jit(solution)/shard_map/ppermute | solution.py:412
  41.2 1.3 %collective-permute-start.19 = (bf16[16,32,128]{2,1,0:T(8,128)(2,1)S(1)}, bf16[16,32,128]{2,1,0:T(8,128)(2,1)S(1)}, u32[]{:S(2)}, u32[]{:S(2)}) collective-permute-start(bf16[16,32,128]{2,1,0:T(8,128)(2,1)S(1)} %get-tuple-element.55), channel_id=1, source_target_pairs={{0,4},{1,5},{2,6},{3,7},{4,0},{5,1},{6,2},{7,3},{8,12},{9,13},{10,... | collective-permute-start | bytes 393224 | tf_op jit(solution)/shard_map/ppermute | solution.py:396
  42.5 2.4 %collective-permute-start.20 = (bf16[16,32,128]{2,1,0:T(8,128)(2,1)S(1)}, bf16[16,32,128]{2,1,0:T(8,128)(2,1)S(1)}, u32[]{:S(2)}, u32[]{:S(2)}) collective-permute-start(bf16[16,32,128]{2,1,0:T(8,128)(2,1)S(1)} %get-tuple-element.56), channel_id=1, source_target_pairs={{0,2},{1,3},{2,0},{3,1},{4,6},{5,7},{6,4},{7,5},{8,10},{9,11},{10,... | collective-permute-start | bytes 393224 | tf_op jit(solution)/shard_map/ppermute | solution.py:396
  45.6 1.6 %collective-permute-start.17 = (bf16[448,256]{1,0:T(8,128)(2,1)S(1)}, bf16[448,256]{1,0:T(8,128)(2,1)S(1)}, u32[]{:S(2)}, u32[]{:S(2)}) collective-permute-start(bf16[448,256]{1,0:T(8,128)(2,1)S(1)} %pair_sum.3.c_ref), channel_id=1, source_target_pairs={{0,16},{1,9},{2,18},{3,11},{4,20},{5,13},{6,22},{7,15},{8,24},{9,1... | collective-permute-start | bytes 688136 | tf_op jit(solution)/shard_map/ppermute | solution.py:412
  47.2 1.6 %collective-permute-done.18.b_ref = bf16[16,32,128]{2,1,0:T(8,128)(2,1)S(1)} collective-permute-done((bf16[16,32,128]{2,1,0:T(8,128)(2,1)S(1)}, bf16[16,32,128]{2,1,0:T(8,128)(2,1)S(1)}, u32[]{:S(2)}, u32[]{:S(2)}) %collective-permute-start.18) | collective-permute-done | bytes 131104 | tf_op jit(solution)/shard_map/ppermute | solution.py:396
  48.8 4.8 %collective-permute-done.19.c_ref = bf16[16,32,128]{2,1,0:T(8,128)(2,1)S(1)} collective-permute-done((bf16[16,32,128]{2,1,0:T(8,128)(2,1)S(1)}, bf16[16,32,128]{2,1,0:T(8,128)(2,1)S(1)}, u32[]{:S(2)}, u32[]{:S(2)}) %collective-permute-start.19) | collective-permute-done | bytes 131104 | tf_op jit(solution)/shard_map/ppermute | solution.py:396
  53.7 1.1 %last.1 = (f32[27,32,256]{2,1,0:T(8,128)}, f32[1,32]{1,0:T(1,128)}, bf16[32,2,8,128]{3,2,1,0:T(8,128)(2,1)}) custom-call(bf16[448,256]{1,0:T(8,128)(2,1)S(1)} %pair_sum.2.a_ref, bf16[448,256]{1,0:T(8,128)(2,1)S(1)} %collective-permute-done.15.b_ref, bf16[448,256]{1,0:T(8,128)(2,1)S(1)} %pair_sum.3.c_ref, bf16[448,256]{1,0:T(8,128)(2,1)S(1)} %collective-permute-done.17.d_ref, ...), custom_call_target="tpu_custom_call" | custom-call | bytes 2195584 | tf_op jit(solution)/shard_map/last/pallas_call | solution.py:110
  (29 shorter events, 4.1 us)
Async XLA Ops:
  0.6 11.0 %collective-permute-start = (bf16[32,2,8,128]{3,2,1,0:T(8,128)(2,1)}, bf16[32,2,8,128]{3,2,1,0:T(8,128)(2,1)S(1)}, u32[]{:S(2)}, u32[]{:S(2)}) collective-permute-start(bf16[32,2,8,128]{3,2,1,0:T(8,128)(2,1)} %x_hbm.1), channel_id=1, source_target_pairs={{0,4},{1,3},{2,6},{3,1},{4,0},{5,7},{6,2},{7,5},{8,12},{9,11},{10,... | collective-permute-start | bytes 393224 | tf_op jit(solution)/shard_map/ppermute | solution.py:402
  4.7 9.5 %collective-permute-start.2 = (bf16[32,2,8,128]{3,2,1,0:T(8,128)(2,1)}, bf16[32,2,8,128]{3,2,1,0:T(8,128)(2,1)S(1)}, u32[]{:S(2)}, u32[]{:S(2)}) collective-permute-start(bf16[32,2,8,128]{3,2,1,0:T(8,128)(2,1)} %x_hbm.1), channel_id=1, source_target_pairs={{0,2},{1,5},{2,0},{3,7},{4,6},{5,1},{6,4},{7,3},{8,10},{9,13},{10,... | collective-permute-start | bytes 393224 | tf_op jit(solution)/shard_map/ppermute | solution.py:402
  7.7 7.3 %collective-permute-start.8 = (bf16[8,32,128]{2,1,0:T(8,128)(2,1)S(1)}, bf16[8,32,128]{2,1,0:T(8,128)(2,1)S(1)}, u32[]{:S(2)}, u32[]{:S(2)}) collective-permute-start(bf16[8,32,128]{2,1,0:T(8,128)(2,1)S(1)} %get-tuple-element.36), channel_id=1, source_target_pairs={{0,24},{8,0},{16,8},{24,16},{1,25},{9,1},{17,9},{25,17},{2,26},{10... | collective-permute-start | bytes 196616 | tf_op jit(solution)/shard_map/ppermute | solution.py:392
  10.2 5.2 %collective-permute-start.9 = (bf16[8,32,128]{2,1,0:T(8,128)(2,1)S(1)}, bf16[8,32,128]{2,1,0:T(8,128)(2,1)S(1)}, u32[]{:S(2)}, u32[]{:S(2)}) collective-permute-start(bf16[8,32,128]{2,1,0:T(8,128)(2,1)S(1)} %get-tuple-element.37), channel_id=1, source_target_pairs={{0,8},{8,16},{16,24},{24,0},{1,9},{9,17},{17,25},{25,1},{2,10},{10... | collective-permute-start | bytes 196616 | tf_op jit(solution)/shard_map/ppermute | solution.py:392
  10.2 11.7 %collective-permute-start.6 = (bf16[32,2,8,128]{3,2,1,0:T(8,128)(2,1)}, bf16[32,2,8,128]{3,2,1,0:T(8,128)(2,1)S(1)}, u32[]{:S(2)}, u32[]{:S(2)}) collective-permute-start(bf16[32,2,8,128]{3,2,1,0:T(8,128)(2,1)} %x_hbm.1), channel_id=1, source_target_pairs={{0,1},{1,0},{2,3},{3,2},{4,5},{5,4},{6,7},{7,6},{8,9},{9,8},{10,11... | collective-permute-start | bytes 393224 | tf_op jit(solution)/shard_map/ppermute | solution.py:396
  11.7 7.5 %collective-permute-start.1 = (bf16[32,2,8,128]{3,2,1,0:T(8,128)(2,1)S(1)}, bf16[32,2,8,128]{3,2,1,0:T(8,128)(2,1)S(1)}, u32[]{:S(2)}, u32[]{:S(2)}) collective-permute-start(bf16[32,2,8,128]{3,2,1,0:T(8,128)(2,1)S(1)} %collective-permute-done.refs_1_), channel_id=1, source_target_pairs={{0,2},{2,0},{4,6},{6,4},{8,10},{10,8},{12,14},{14,12},{16,18},{18,... | collective-permute-start | bytes 393224 | tf_op jit(solution)/shard_map/ppermute | solution.py:402
  14.3 1.6 %collective-permute-start.3 = (bf16[32,2,8,128]{3,2,1,0:T(8,128)(2,1)S(1)}, bf16[32,2,8,128]{3,2,1,0:T(8,128)(2,1)S(1)}, u32[]{:S(2)}, u32[]{:S(2)}) collective-permute-start(bf16[32,2,8,128]{3,2,1,0:T(8,128)(2,1)S(1)} %collective-permute-done.2.refs_2_), channel_id=1, source_target_pairs={{1,3},{3,1},{5,7},{7,5},{9,11},{11,9},{13,15},{15,13},{17,19},{19,... | collective-permute-start | bytes 393224 | tf_op jit(solution)/shard_map/ppermute | solution.py:402
  15.3 6.5 %collective-permute-start.10 = (bf16[32,2,8,128]{3,2,1,0:T(8,128)(2,1)S(1)}, bf16[32,2,8,128]{3,2,1,0:T(8,128)(2,1)S(1)}, u32[]{:S(2)}, u32[]{:S(2)}) collective-permute-start(bf16[32,2,8,128]{3,2,1,0:T(8,128)(2,1)S(1)} %collective-permute-done.2.refs_2_), channel_id=1, source_target_pairs={{0,1},{1,0},{2,3},{3,2},{4,5},{5,4},{6,7},{7,6},{8,9},{9,8},{10,11... | collective-permute-start | bytes 393224 | tf_op jit(solution)/shard_map/ppermute | solution.py:396
  15.3 6.6 %collective-permute-start.7 = (bf16[32,2,8,128]{3,2,1,0:T(8,128)(2,1)S(1)}, bf16[32,2,8,128]{3,2,1,0:T(8,128)(2,1)S(1)}, u32[]{:S(2)}, u32[]{:S(2)}) collective-permute-start(bf16[32,2,8,128]{3,2,1,0:T(8,128)(2,1)S(1)} %collective-permute-done.refs_1_), channel_id=1, source_target_pairs={{0,1},{1,0},{2,3},{3,2},{4,5},{5,4},{6,7},{7,6},{8,9},{9,8},{10,11... | collective-permute-start | bytes 393224 | tf_op jit(solution)/shard_map/ppermute | solution.py:396
  15.9 6.7 %collective-permute-start.4 = (bf16[32,2,8,128]{3,2,1,0:T(8,128)(2,1)S(1)}, bf16[32,2,8,128]{3,2,1,0:T(8,128)(2,1)S(1)}, u32[]{:S(2)}, u32[]{:S(2)}) collective-permute-start(bf16[32,2,8,128]{3,2,1,0:T(8,128)(2,1)S(1)} %collective-permute-done.3.refs_2_), channel_id=1, source_target_pairs={{1,0},{3,2},{5,4},{7,6},{9,8},{11,10},{13,12},{15,14},{17,16},{19,... | collective-permute-start | bytes 393224 | tf_op jit(solution)/shard_map/ppermute | solution.py:402
  19.2 3.6 %collective-permute-start.5 = (bf16[32,2,8,128]{3,2,1,0:T(8,128)(2,1)S(1)}, bf16[32,2,8,128]{3,2,1,0:T(8,128)(2,1)S(1)}, u32[]{:S(2)}, u32[]{:S(2)}) collective-permute-start(bf16[32,2,8,128]{3,2,1,0:T(8,128)(2,1)S(1)} %collective-permute-done.1.refs_0_), channel_id=1, source_target_pairs={{0,1},{2,3},{4,5},{6,7},{8,9},{10,11},{12,13},{14,15},{16,17},{18,... | collective-permute-start | bytes 393224 | tf_op jit(solution)/shard_map/ppermute | solution.py:402
  24.3 7.0 %collective-permute-start.12 = (bf16[16,32,128]{2,1,0:T(8,128)(2,1)S(1)}, bf16[16,32,128]{2,1,0:T(8,128)(2,1)S(1)}, u32[]{:S(2)}, u32[]{:S(2)}) collective-permute-start(bf16[16,32,128]{2,1,0:T(8,128)(2,1)S(1)} %get-tuple-element.40.low_ref), channel_id=1, source_target_pairs={{0,24},{8,0},{16,8},{24,16},{1,25},{9,1},{17,9},{25,17},{2,26},{10... | collective-permute-start | bytes 393224 | tf_op jit(solution)/shard_map/ppermute | solution.py:392
  27.4 6.8 %collective-permute-start.11 = (bf16[16,32,128]{2,1,0:T(8,128)(2,1)S(1)}, bf16[16,32,128]{2,1,0:T(8,128)(2,1)S(1)}, u32[]{:S(2)}, u32[]{:S(2)}) collective-permute-start(bf16[16,32,128]{2,1,0:T(8,128)(2,1)S(1)} %get-tuple-element.41.high_ref), channel_id=1, source_target_pairs={{0,8},{8,16},{16,24},{24,0},{1,9},{9,17},{17,25},{25,1},{2,10},{10... | collective-permute-start | bytes 393224 | tf_op jit(solution)/shard_map/ppermute | solution.py:392
  36.0 2.6 %collective-permute-start.14 = (bf16[4,16,32,128]{3,2,1,0:T(8,128)(2,1)S(1)}, bf16[4,16,32,128]{3,2,1,0:T(8,128)(2,1)S(1)}, u32[]{:S(2)}, u32[]{:S(2)}) collective-permute-start(bf16[4,16,32,128]{3,2,1,0:T(8,128)(2,1)S(1)} %get-tuple-element.52), channel_id=1, source_target_pairs={{0,1},{1,0},{2,3},{3,2},{4,5},{5,4},{6,7},{7,6},{8,9},{9,8},{10,11... | collective-permute-start | bytes 1572872 | tf_op jit(solution)/shard_map/ppermute | solution.py:396
  36.7 8.2 %collective-permute-start.13 = (bf16[448,256]{1,0:T(8,128)(2,1)S(1)}, bf16[448,256]{1,0:T(8,128)(2,1)S(1)}, u32[]{:S(2)}, u32[]{:S(2)}) collective-permute-start(bf16[448,256]{1,0:T(8,128)(2,1)S(1)} %filter_first.1.a_ref), channel_id=1, source_target_pairs={{0,8},{1,17},{2,10},{3,19},{4,12},{5,21},{6,14},{7,23},{8,0},{9,25... | collective-permute-start | bytes 688136 | tf_op jit(solution)/shard_map/ppermute | solution.py:412
  39.3 6.2 %collective-permute-start.16 = (bf16[448,256]{1,0:T(8,128)(2,1)S(1)}, bf16[448,256]{1,0:T(8,128)(2,1)S(1)}, u32[]{:S(2)}, u32[]{:S(2)}) collective-permute-start(bf16[448,256]{1,0:T(8,128)(2,1)S(1)} %filter_second.1.a_ref), channel_id=1, source_target_pairs={{0,8},{1,17},{2,10},{3,19},{4,12},{5,21},{6,14},{7,23},{8,0},{9,25... | collective-permute-start | bytes 688136 | tf_op jit(solution)/shard_map/ppermute | solution.py:412
  40.5 8.2 %collective-permute-start.18 = (bf16[16,32,128]{2,1,0:T(8,128)(2,1)S(1)}, bf16[16,32,128]{2,1,0:T(8,128)(2,1)S(1)}, u32[]{:S(2)}, u32[]{:S(2)}) collective-permute-start(bf16[16,32,128]{2,1,0:T(8,128)(2,1)S(1)} %get-tuple-element.54), channel_id=1, source_target_pairs={{0,6},{1,7},{2,4},{3,5},{4,2},{5,3},{6,0},{7,1},{8,14},{9,15},{10,... | collective-permute-start | bytes 393224 | tf_op jit(solution)/shard_map/ppermute | solution.py:396
  41.2 12.4 %collective-permute-start.19 = (bf16[16,32,128]{2,1,0:T(8,128)(2,1)S(1)}, bf16[16,32,128]{2,1,0:T(8,128)(2,1)S(1)}, u32[]{:S(2)}, u32[]{:S(2)}) collective-permute-start(bf16[16,32,128]{2,1,0:T(8,128)(2,1)S(1)} %get-tuple-element.55), channel_id=1, source_target_pairs={{0,4},{1,5},{2,6},{3,7},{4,0},{5,1},{6,2},{7,3},{8,12},{9,13},{10,... | collective-permute-start | bytes 393224 | tf_op jit(solution)/shard_map/ppermute | solution.py:396
  42.5 11.1 %collective-permute-start.20 = (bf16[16,32,128]{2,1,0:T(8,128)(2,1)S(1)}, bf16[16,32,128]{2,1,0:T(8,128)(2,1)S(1)}, u32[]{:S(2)}, u32[]{:S(2)}) collective-permute-start(bf16[16,32,128]{2,1,0:T(8,128)(2,1)S(1)} %get-tuple-element.56), channel_id=1, source_target_pairs={{0,2},{1,3},{2,0},{3,1},{4,6},{5,7},{6,4},{7,5},{8,10},{9,11},{10,... | collective-permute-start | bytes 393224 | tf_op jit(solution)/shard_map/ppermute | solution.py:396
  45.0 8.7 %collective-permute-start.15 = (bf16[448,256]{1,0:T(8,128)(2,1)S(1)}, bf16[448,256]{1,0:T(8,128)(2,1)S(1)}, u32[]{:S(2)}, u32[]{:S(2)}) collective-permute-start(bf16[448,256]{1,0:T(8,128)(2,1)S(1)} %pair_sum.2.a_ref), channel_id=1, source_target_pairs={{0,16},{1,9},{2,18},{3,11},{4,20},{5,13},{6,22},{7,15},{8,24},{9,1... | collective-permute-start | bytes 688136 | tf_op jit(solution)/shard_map/ppermute | solution.py:412
  45.6 8.0 %collective-permute-start.17 = (bf16[448,256]{1,0:T(8,128)(2,1)S(1)}, bf16[448,256]{1,0:T(8,128)(2,1)S(1)}, u32[]{:S(2)}, u32[]{:S(2)}) collective-permute-start(bf16[448,256]{1,0:T(8,128)(2,1)S(1)} %pair_sum.3.c_ref), channel_id=1, source_target_pairs={{0,16},{1,9},{2,18},{3,11},{4,20},{5,13},{6,22},{7,15},{8,24},{9,1... | collective-permute-start | bytes 688136 | tf_op jit(solution)/shard_map/ppermute | solution.py:412

commit v12 on v7

--- a/solution.py
+++ b/solution.py
@@ -10,7 +10,7 @@
 
 LANES = 128
 FORWARD_FLOPS = 9 * 10**8
-SUM_FLOPS = 20 * 10**8
+SUM_FLOPS = 24 * 10**8
 ASSEMBLE_FLOPS = 40 * 10**8
 VMEM = pl.BlockSpec(memory_space=pltpu.VMEM)
 ANY = pl.BlockSpec(memory_space=pl.ANY)
@@ -332,10 +332,9 @@
     second_ref[(27 - taps) * o :] = row.astype(second_ref.dtype)
 
 
-def pair_body(a_ref, b_ref, c_ref, d_ref, _, ab_ref, cd_ref):
+def pair_body(a_ref, b_ref, _, out_ref):
     f32 = jnp.float32
-    ab_ref[...] = (a_ref[...].astype(f32) + b_ref[...].astype(f32)).astype(ab_ref.dtype)
-    cd_ref[...] = (c_ref[...].astype(f32) + d_ref[...].astype(f32)).astype(cd_ref.dtype)
+    out_ref[...] = (a_ref[...].astype(f32) + b_ref[...].astype(f32)).astype(out_ref.dtype)
 
 
 def core_sum_body(mine_ref, other_ref, *outs):
@@ -382,6 +381,16 @@
     return lax.ppermute(value, axis, [(i, i ^ bit) for i in range(lax.axis_size(axis))])
 
 
+def cross(value, phase):
+    slabs, chans = lax.axis_size("slab"), lax.axis_size("chan")
+    pairs = [
+        (s * chans + c, (s ^ (1 + (c + phase) % 2)) * chans + c)
+        for s in range(slabs)
+        for c in range(chans)
+    ]
+    return lax.ppermute(value, ("slab", "chan"), pairs)
+
+
 def on_device(x_in, weight, bias_vec, grad_out):
     o, _, c_all = weight.shape
     _, n, rows, depth = x_in.shape
@@ -393,7 +402,6 @@
 
     block_wide = [pltpu.VMEM((o * cells, depth), f32)]
 
-    x_ab = swap(x_in, "chan", 6)
     x_b = swap(x_in, "chan", 4)
     x_a = swap(x_in, "chan", 2)
     x_side = swap(x_in, "chan", 1)
@@ -422,9 +430,10 @@
     go_above = rotate(go_low, "slab", -1)
     go_below = rotate(go_high, "slab", 1)
     x_b, w_flat = lax.optimization_barrier((x_b, w_flat))
-    late_ab, go_above, go_below = lax.optimization_barrier((x_ab, go_above, go_below))
+    x_ab = swap(x_b, "chan", 2)
+    late_b, go_above, go_below = lax.optimization_barrier((x_b, go_above, go_below))
     x_a_side = swap(x_a, "chan", 1)
-    x_b_side = swap(x_b, "chan", 1)
+    x_b_side = swap(late_b, "chan", 1)
     early, late = (0, 1, 2, 3, 4, 5, 6), (7,)
     (x_all,) = call(
         functools.partial(assemble_body, early),
@@ -435,7 +444,7 @@
         flops=ASSEMBLE_FLOPS,
         name="assemble",
     )
-    x_ab_side = swap(late_ab, "chan", 1)
+    x_ab_side = swap(x_ab, "chan", 1)
     own, low, high, x_all = call(
         functools.partial(forward_body, n, rows, o, late),
         [
@@ -477,8 +486,8 @@
         flops=flops,
         name="filter_grad",
     )
-    first_far = swap(first, "slab", 1)
-    second_far = swap(second, "slab", 2)
+    first_far = cross(first, 0)
+    second_far = cross(second, 0)
     g_own, g_a, g_b, g_ab = call(
         core_sum_body,
         [shape_of((cells, o, depth), f32)] + [shape_of((cells, o, depth), bf16)] * 3,
@@ -488,19 +497,22 @@
     g_ab = swap(g_ab, "chan", 6)
     g_b = swap(g_b, "chan", 4)
     g_a = swap(g_a, "chan", 2)
-    first, second = call(
-        pair_body,
-        [shape_of(first.shape, bf16), shape_of(second.shape, bf16)],
-        [first, first_far, second, second_far, g_own],
-        [VMEM] * 4 + [ANY],
-        name="pair_sum",
-    )
-    first_far = swap(first, "slab", 2)
-    second_far = swap(second, "slab", 1)
+    first, second = (
+        call(
+            pair_body,
+            [shape_of(a.shape, bf16)],
+            [a, b, g_own],
+            [VMEM] * 2 + [ANY],
+            name="pair_sum",
+        )[0]
+        for a, b in ((first, first_far), (second, second_far))
+    )
+    first_far = cross(first, 1)
+    second_far = cross(second, 1)
     (g_own,) = call(
         sum_body,
         [shape_of((cells, o, depth), f32)],
-        [g_own, g_ab, g_b, g_a],
+        [g_own, g_a, g_b, g_ab],
         flops=SUM_FLOPS,
         name="sum",
     )

time: 50.7 us -> 49.3 us (0.972)
  starting transfers between devices: 21.4 us -> 20.1 us
    ppermute x0 -> x4, starting transfers between devices: none -> 3.4 us  [cross(): return lax.ppermute(value, ('slab', 'chan'), pairs)]
    ppermute x15 -> x11, starting transfers between devices: 14.4 us -> 11.5 us  [swap(): lax.ppermute(value, axis, [(i, i ^ bit) for i in range(lax.axis_size(axis...]
    ppermute x4, starting transfers between devices: 7.02 us -> 5.25 us  [rotate(): lax.ppermute(value, axis, [(i, (i + step) % count) for i in range(count)])]
    ppermute x0 -> x4, waiting for transfers between devices: none -> 1.15 us  [cross(): return lax.ppermute(value, ('slab', 'chan'), pairs)]
    ppermute x15 -> x11, waiting for transfers between devices: 10.5 us -> 9.64 us  [swap(): lax.ppermute(value, axis, [(i, i ^ bit) for i in range(lax.axis_size(axis...]
    pallas_call x9 -> x10, Pallas kernels: 7.61 us -> 7.61 us  [call(): pl.pallas_call(body, out_shape=out_shape, in_specs=specs or [VMEM] * len(...]
  transfers between devices with their start and end apart: 19 -> 19, of which waited for: 9 -> 12; matrix products, arithmetic and copies ran while one was open for 0% -> 0% of each run, Pallas kernels for 7% -> 7%
where the time goes in v12:
time: 49.3 us; the launch traced here: 49.2 us
  waiting for transfers between devices  20.7 us (42%)
  starting transfers between devices  20.1 us (41%)
  Pallas kernels  7.61 us (15%)
  between operations  0.72 us (1%)
    ppermute x11, starting transfers between devices, swap(): lax.ppermute(value, axis, [(i, i ^ bit) for i in range(lax.axis_size(axis...  11.5 us
    ppermute x4, waiting for transfers between devices, rotate(): lax.ppermute(value, axis, [(i, (i + step) % count) for i in range(count)])  9.92 us
    ppermute x11, waiting for transfers between devices, swap(): lax.ppermute(value, axis, [(i, i ^ bit) for i in range(lax.axis_size(axis...  9.64 us
    pallas_call x10, Pallas kernels, call(): pl.pallas_call(body, out_shape=out_shape, in_specs=specs or [VMEM] * len(...  7.61 us
    ppermute x4, starting transfers between devices, rotate(): lax.ppermute(value, axis, [(i, (i + step) % count) for i in range(count)])  5.25 us
    ppermute x4, starting transfers between devices, cross(): return lax.ppermute(value, ('slab', 'chan'), pairs)  3.4 us
    ppermute x4, waiting for transfers between devices, cross(): return lax.ppermute(value, ('slab', 'chan'), pairs)  1.15 us
  transfers between devices with their start and end apart: 19, of which 12 were waited for; matrix products, arithmetic and copies ran while one was open for 0% of the time, Pallas kernels for 7%

profile of v12, /device:TPU:0, one launch (start us, length us, event | category | flops | bytes accessed | tf_op | source)
XLA Modules:
  0.0 49.2 jit_solution(6556994651637797869)
XLA Ops:
  0.6 4.1 %collective-permute-start = (bf16[32,2,8,128]{3,2,1,0:T(8,128)(2,1)}, bf16[32,2,8,128]{3,2,1,0:T(8,128)(2,1)S(1)}, u32[]{:S(2)}, u32[]{:S(2)}) collective-permute-start(bf16[32,2,8,128]{3,2,1,0:T(8,128)(2,1)} %x_hbm.1), channel_id=1, source_target_pairs={{0,4},{1,5},{2,6},{3,7},{4,0},{5,1},{6,2},{7,3},{8,12},{9,13},{10,... | collective-permute-start | bytes 393224 | tf_op jit(solution)/shard_map/ppermute | solution.py:381
  4.7 1.6 %collective-permute-start.3 = (bf16[32,2,8,128]{3,2,1,0:T(8,128)(2,1)}, bf16[32,2,8,128]{3,2,1,0:T(8,128)(2,1)S(1)}, u32[]{:S(2)}, u32[]{:S(2)}) collective-permute-start(bf16[32,2,8,128]{3,2,1,0:T(8,128)(2,1)} %x_hbm.1), channel_id=1, source_target_pairs={{0,2},{1,3},{2,0},{3,1},{4,6},{5,7},{6,4},{7,5},{8,10},{9,11},{10,... | collective-permute-start | bytes 393224 | tf_op jit(solution)/shard_map/ppermute | solution.py:381
  6.3 1.4 %prepare.1 = (bf16[32,2,8,128]{3,2,1,0:T(8,128)(2,1)S(1)}, bf16[16,32,128]{2,1,0:T(8,128)(2,1)S(1)}, bf16[8,32,128]{2,1,0:T(8,128)(2,1)S(1)}, bf16[8,32,128]{2,1...) custom-call(bf16[32,2,8,128]{3,2,1,0:T(8,128)(2,1)} %x_hbm.1, ...), custom_call_target="tpu_custom_call" | custom-call | bytes 1998912 | tf_op jit(solution)/shard_map/prepare/pallas_call | solution.py:110
  7.7 2.5 %collective-permute-start.6 = (bf16[8,32,128]{2,1,0:T(8,128)(2,1)S(1)}, bf16[8,32,128]{2,1,0:T(8,128)(2,1)S(1)}, u32[]{:S(2)}, u32[]{:S(2)}) collective-permute-start(bf16[8,32,128]{2,1,0:T(8,128)(2,1)S(1)} %get-tuple-element.38), channel_id=1, source_target_pairs={{0,24},{8,0},{16,8},{24,16},{1,25},{9,1},{17,9},{25,17},{2,26},{10... | collective-permute-start | bytes 196616 | tf_op jit(solution)/shard_map/ppermute | solution.py:377
  10.2 1.2 %collective-permute-done.refs_2_ = bf16[32,2,8,128]{3,2,1,0:T(8,128)(2,1)S(1)} collective-permute-done((bf16[32,2,8,128]{3,2,1,0:T(8,128)(2,1)}, bf16[32,2,8,128]{3,2,1,0:T(8,128)(2,1)S(1)}, u32[]{:S(2)}, u32[]{:S(2)}) %collective-permute-start) | collective-permute-done | bytes 131104 | tf_op jit(solution)/shard_map/ppermute | solution.py:381
  11.4 0.7 %collective-permute-start.1 = (bf16[32,2,8,128]{3,2,1,0:T(8,128)(2,1)S(1)}, bf16[32,2,8,128]{3,2,1,0:T(8,128)(2,1)S(1)}, u32[]{:S(2)}, u32[]{:S(2)}) collective-permute-start(bf16[32,2,8,128]{3,2,1,0:T(8,128)(2,1)S(1)} %collective-permute-done.refs_2_), channel_id=1, source_target_pairs={{0,2},{1,3},{2,0},{3,1},{4,6},{5,7},{6,4},{7,5},{8,10},{9,11},{10,... | collective-permute-start | bytes 393224 | tf_op jit(solution)/shard_map/ppermute | solution.py:381
  12.4 3.0 %collective-permute-done.7.go_below_ref = bf16[8,32,128]{2,1,0:T(8,128)(2,1)S(1)} collective-permute-done((bf16[8,32,128]{2,1,0:T(8,128)(2,1)S(1)}, bf16[8,32,128]{2,1,0:T(8,128)(2,1)S(1)}, u32[]{:S(2)}, u32[]{:S(2)}) %collective-permute-start.7) | collective-permute-done | bytes 65568 | tf_op jit(solution)/shard_map/ppermute | solution.py:377
  15.4 0.5 %collective-permute-start.8 = (bf16[32,2,8,128]{3,2,1,0:T(8,128)(2,1)S(1)}, bf16[32,2,8,128]{3,2,1,0:T(8,128)(2,1)S(1)}, u32[]{:S(2)}, u32[]{:S(2)}) collective-permute-start(bf16[32,2,8,128]{3,2,1,0:T(8,128)(2,1)S(1)} %collective-permute-done.refs_2_), channel_id=1, source_target_pairs={{0,1},{1,0},{2,3},{3,2},{4,5},{5,4},{6,7},{7,6},{8,9},{9,8},{10,11... | collective-permute-start | bytes 393224 | tf_op jit(solution)/shard_map/ppermute | solution.py:381
  15.9 0.5 collective-permute-done.1.refs_3_
  16.9 0.7 %assemble.1.refs_1_ = bf16[256,2048]{1,0:T(8,128)(2,1)S(1)} custom-call(s32[1]{0:T(128)} %bitcast.me_ref, bf16[32,2,8,128]{3,2,1,0:T(8,128)(2,1)S(1)} %get-tuple-element.37.refs_0_, bf16[32,2,8,128]{3,2,1,0:T(8,128)(2,1)S(1)} %collective-permute-done.3.refs_1_, bf16[32,2,8,128]{3,2,1,0:T(8,128)(2,1)S(1)} %collective-permute-done.refs_2_, ...), custom_call_target="tpu_custom_call" | custom-call | flops 4000000000 | bytes 1966084 | tf_op jit(solution)/shard_map/assemble/pallas_call | solution.py:110
  17.7 1.3 %forward.1 = (f32[16,32,128]{2,1,0:T(8,128)S(1)}, bf16[16,32,128]{2,1,0:T(8,128)(2,1)S(1)}, bf16[16,32,128]{2,1,0:T(8,128)(2,1)S(1)}, bf16[256,2048]{1,0:T(8,128)(2,1)S(1)}) custom-call(s32[1]{0:T(128)} %bitcast.me_ref, bf16[864,256]{1,0:T(8,128)(2,1)S(1)} %get-tuple-element.35.w_ref, ...), custom_call_target="tpu_custom_call", output_to_operand_aliasing={{3}: (3, {})} | custom-call | flops 900000000 | bytes 3194884 | tf_op jit(solution)/shard_map/forward/pallas_call | solution.py:110
  19.0 2.7 %collective-permute-start.10 = (bf16[16,32,128]{2,1,0:T(8,128)(2,1)S(1)}, bf16[16,32,128]{2,1,0:T(8,128)(2,1)S(1)}, u32[]{:S(2)}, u32[]{:S(2)}) collective-permute-start(bf16[16,32,128]{2,1,0:T(8,128)(2,1)S(1)} %get-tuple-element.42.low_ref), channel_id=1, source_target_pairs={{0,24},{8,0},{16,8},{24,16},{1,25},{9,1},{17,9},{25,17},{2,26},{10... | collective-permute-start | bytes 393224 | tf_op jit(solution)/shard_map/ppermute | solution.py:377
  21.7 3.9 %collective-permute-done.10.above_ref = bf16[16,32,128]{2,1,0:T(8,128)(2,1)S(1)} collective-permute-done((bf16[16,32,128]{2,1,0:T(8,128)(2,1)S(1)}, bf16[16,32,128]{2,1,0:T(8,128)(2,1)S(1)}, u32[]{:S(2)}, u32[]{:S(2)}) %collective-permute-start.10) | collective-permute-done | bytes 131104 | tf_op jit(solution)/shard_map/ppermute | solution.py:377
  25.6 2.8 %collective-permute-done.9.below_ref = bf16[16,32,128]{2,1,0:T(8,128)(2,1)S(1)} collective-permute-done((bf16[16,32,128]{2,1,0:T(8,128)(2,1)S(1)}, bf16[16,32,128]{2,1,0:T(8,128)(2,1)S(1)}, u32[]{:S(2)}, u32[]{:S(2)}) %collective-permute-start.9) | collective-permute-done | bytes 131104 | tf_op jit(solution)/shard_map/ppermute | solution.py:377
  28.4 1.7 %gradient.1 = (bf16[32,2,8,128]{3,2,1,0:T(8,128)(2,1)}, f32[32,128]{1,0:T(8,128)S(1)}, bf16[864,2048]{1,0:T(8,128)(2,1)S(1)}, bf16[4,16,32,128]{3,2,1,0:T(8,128)(2,1)S(1)}, bf16[4,16,32,128]{3,2,1,0:T(8,128)(2,1)S(1)}) custom-call(s32[1]{0:T(128)} %bitcast.me_ref, f32[16,32,128]{2,1,0:T(8,128)S(1)} %get-tuple-element.41.own_ref, ...), custom_call_target="tpu_custom_call" | custom-call | flops 905969664 | bytes 6242308 | tf_op jit(solution)/shard_map/gradient/pallas_call | solution.py:110
  30.2 1.1 %filter_grad.1 = (bf16[448,256]{1,0:T(8,128)(2,1)S(1)}, bf16[448,256]{1,0:T(8,128)(2,1)S(1)}) custom-call(bf16[864,2048]{1,0:T(8,128)(2,1)S(1)} %get-tuple-element.50.s_ref, bf16[256,2048]{1,0:T(8,128)(2,1)S(1)} %get-tuple-element.51.x_ref, f32[32,128]{1,0:T(8,128)S(1)} %get-tuple-element.52.total_ref), custom_call_target="tpu_custom_call" | custom-call | flops 905969664 | bytes 5062656 | tf_op jit(solution)/shard_map/filter_grad/pallas_call | solution.py:110
  31.3 1.8 %collective-permute-start.11 = (bf16[448,256]{1,0:T(8,128)(2,1)S(1)}, bf16[448,256]{1,0:T(8,128)(2,1)S(1)}, u32[]{:S(2)}, u32[]{:S(2)}) collective-permute-start(bf16[448,256]{1,0:T(8,128)(2,1)S(1)} %get-tuple-element.53.a_ref), channel_id=1, source_target_pairs={{0,8},{1,17},{2,10},{3,19},{4,12},{5,21},{6,14},{7,23},{8,0},{9,25... | collective-permute-start | bytes 688136 | tf_op jit(solution)/shard_map/ppermute | solution.py:391
  33.5 1.2 %collective-permute-start.16 = (bf16[16,32,128]{2,1,0:T(8,128)(2,1)S(1)}, bf16[16,32,128]{2,1,0:T(8,128)(2,1)S(1)}, u32[]{:S(2)}, u32[]{:S(2)}) collective-permute-start(bf16[16,32,128]{2,1,0:T(8,128)(2,1)S(1)} %get-tuple-element.58), channel_id=1, source_target_pairs={{0,2},{1,3},{2,0},{3,1},{4,6},{5,7},{6,4},{7,5},{8,10},{9,11},{10,... | collective-permute-start | bytes 393224 | tf_op jit(solution)/shard_map/ppermute | solution.py:381
  34.7 3.3 %collective-permute-start.17 = (bf16[16,32,128]{2,1,0:T(8,128)(2,1)S(1)}, bf16[16,32,128]{2,1,0:T(8,128)(2,1)S(1)}, u32[]{:S(2)}, u32[]{:S(2)}) collective-permute-start(bf16[16,32,128]{2,1,0:T(8,128)(2,1)S(1)} %get-tuple-element.59), channel_id=1, source_target_pairs={{0,4},{1,5},{2,6},{3,7},{4,0},{5,1},{6,2},{7,3},{8,12},{9,13},{10,... | collective-permute-start | bytes 393224 | tf_op jit(solution)/shard_map/ppermute | solution.py:381
  38.0 0.6 %collective-permute-start.13 = (bf16[448,256]{1,0:T(8,128)(2,1)S(1)}, bf16[448,256]{1,0:T(8,128)(2,1)S(1)}, u32[]{:S(2)}, u32[]{:S(2)}) collective-permute-start(bf16[448,256]{1,0:T(8,128)(2,1)S(1)} %pair_sum.2.a_ref), channel_id=1, source_target_pairs={{0,16},{1,9},{2,18},{3,11},{4,20},{5,13},{6,22},{7,15},{8,24},{9,1... | collective-permute-start | bytes 688136 | tf_op jit(solution)/shard_map/ppermute | solution.py:391
  38.7 1.1 %collective-permute-done.14.b_ref = bf16[448,256]{1,0:T(8,128)(2,1)S(1)} collective-permute-done((bf16[448,256]{1,0:T(8,128)(2,1)S(1)}, bf16[448,256]{1,0:T(8,128)(2,1)S(1)}, u32[]{:S(2)}, u32[]{:S(2)}) %collective-permute-start.14) | collective-permute-done | bytes 229408 | tf_op jit(solution)/shard_map/ppermute | solution.py:391
  39.9 0.7 %collective-permute-start.15 = (bf16[448,256]{1,0:T(8,128)(2,1)S(1)}, bf16[448,256]{1,0:T(8,128)(2,1)S(1)}, u32[]{:S(2)}, u32[]{:S(2)}) collective-permute-start(bf16[448,256]{1,0:T(8,128)(2,1)S(1)} %pair_sum.3.c_ref), channel_id=1, source_target_pairs={{0,16},{1,9},{2,18},{3,11},{4,20},{5,13},{6,22},{7,15},{8,24},{9,1... | collective-permute-start | bytes 688136 | tf_op jit(solution)/shard_map/ppermute | solution.py:391
  40.7 7.2 %collective-permute-done.17.c_ref = bf16[16,32,128]{2,1,0:T(8,128)(2,1)S(1)} collective-permute-done((bf16[16,32,128]{2,1,0:T(8,128)(2,1)S(1)}, bf16[16,32,128]{2,1,0:T(8,128)(2,1)S(1)}, u32[]{:S(2)}, u32[]{:S(2)}) %collective-permute-start.17) | collective-permute-done | bytes 131104 | tf_op jit(solution)/shard_map/ppermute | solution.py:381
  48.0 1.1 %last.1 = (f32[27,32,256]{2,1,0:T(8,128)}, f32[1,32]{1,0:T(1,128)}, bf16[32,2,8,128]{3,2,1,0:T(8,128)(2,1)}) custom-call(bf16[448,256]{1,0:T(8,128)(2,1)S(1)} %pair_sum.2.a_ref, bf16[448,256]{1,0:T(8,128)(2,1)S(1)} %collective-permute-done.13.b_ref, bf16[448,256]{1,0:T(8,128)(2,1)S(1)} %pair_sum.3.c_ref, bf16[448,256]{1,0:T(8,128)(2,1)S(1)} %collective-permute-done.15.d_ref, ...), custom_call_target="tpu_custom_call" | custom-call | bytes 2195584 | tf_op jit(solution)/shard_map/last/pallas_call | solution.py:110
  (24 shorter events, 1.8 us)
Async XLA Ops:
  0.6 10.7 %collective-permute-start = (bf16[32,2,8,128]{3,2,1,0:T(8,128)(2,1)}, bf16[32,2,8,128]{3,2,1,0:T(8,128)(2,1)S(1)}, u32[]{:S(2)}, u32[]{:S(2)}) collective-permute-start(bf16[32,2,8,128]{3,2,1,0:T(8,128)(2,1)} %x_hbm.1), channel_id=1, source_target_pairs={{0,4},{1,5},{2,6},{3,7},{4,0},{5,1},{6,2},{7,3},{8,12},{9,13},{10,... | collective-permute-start | bytes 393224 | tf_op jit(solution)/shard_map/ppermute | solution.py:381
  4.7 10.6 %collective-permute-start.3 = (bf16[32,2,8,128]{3,2,1,0:T(8,128)(2,1)}, bf16[32,2,8,128]{3,2,1,0:T(8,128)(2,1)S(1)}, u32[]{:S(2)}, u32[]{:S(2)}) collective-permute-start(bf16[32,2,8,128]{3,2,1,0:T(8,128)(2,1)} %x_hbm.1), channel_id=1, source_target_pairs={{0,2},{1,3},{2,0},{3,1},{4,6},{5,7},{6,4},{7,5},{8,10},{9,11},{10,... | collective-permute-start | bytes 393224 | tf_op jit(solution)/shard_map/ppermute | solution.py:381
  7.7 4.7 %collective-permute-start.6 = (bf16[8,32,128]{2,1,0:T(8,128)(2,1)S(1)}, bf16[8,32,128]{2,1,0:T(8,128)(2,1)S(1)}, u32[]{:S(2)}, u32[]{:S(2)}) collective-permute-start(bf16[8,32,128]{2,1,0:T(8,128)(2,1)S(1)} %get-tuple-element.38), channel_id=1, source_target_pairs={{0,24},{8,0},{16,8},{24,16},{1,25},{9,1},{17,9},{25,17},{2,26},{10... | collective-permute-start | bytes 196616 | tf_op jit(solution)/shard_map/ppermute | solution.py:377
  10.2 5.2 %collective-permute-start.7 = (bf16[8,32,128]{2,1,0:T(8,128)(2,1)S(1)}, bf16[8,32,128]{2,1,0:T(8,128)(2,1)S(1)}, u32[]{:S(2)}, u32[]{:S(2)}) collective-permute-start(bf16[8,32,128]{2,1,0:T(8,128)(2,1)S(1)} %get-tuple-element.39), channel_id=1, source_target_pairs={{0,8},{8,16},{16,24},{24,0},{1,9},{9,17},{17,25},{25,1},{2,10},{10... | collective-permute-start | bytes 196616 | tf_op jit(solution)/shard_map/ppermute | solution.py:377
  10.2 6.2 %collective-permute-start.4 = (bf16[32,2,8,128]{3,2,1,0:T(8,128)(2,1)}, bf16[32,2,8,128]{3,2,1,0:T(8,128)(2,1)S(1)}, u32[]{:S(2)}, u32[]{:S(2)}) collective-permute-start(bf16[32,2,8,128]{3,2,1,0:T(8,128)(2,1)} %x_hbm.1), channel_id=1, source_target_pairs={{0,1},{1,0},{2,3},{3,2},{4,5},{5,4},{6,7},{7,6},{8,9},{9,8},{10,11... | collective-permute-start | bytes 393224 | tf_op jit(solution)/shard_map/ppermute | solution.py:381
  11.4 5.0 %collective-permute-start.1 = (bf16[32,2,8,128]{3,2,1,0:T(8,128)(2,1)S(1)}, bf16[32,2,8,128]{3,2,1,0:T(8,128)(2,1)S(1)}, u32[]{:S(2)}, u32[]{:S(2)}) collective-permute-start(bf16[32,2,8,128]{3,2,1,0:T(8,128)(2,1)S(1)} %collective-permute-done.refs_2_), channel_id=1, source_target_pairs={{0,2},{1,3},{2,0},{3,1},{4,6},{5,7},{6,4},{7,5},{8,10},{9,11},{10,... | collective-permute-start | bytes 393224 | tf_op jit(solution)/shard_map/ppermute | solution.py:381
  15.3 1.3 %collective-permute-start.5 = (bf16[32,2,8,128]{3,2,1,0:T(8,128)(2,1)S(1)}, bf16[32,2,8,128]{3,2,1,0:T(8,128)(2,1)S(1)}, u32[]{:S(2)}, u32[]{:S(2)}) collective-permute-start(bf16[32,2,8,128]{3,2,1,0:T(8,128)(2,1)S(1)} %collective-permute-done.3.refs_1_), channel_id=1, source_target_pairs={{0,1},{1,0},{2,3},{3,2},{4,5},{5,4},{6,7},{7,6},{8,9},{9,8},{10,11... | collective-permute-start | bytes 393224 | tf_op jit(solution)/shard_map/ppermute | solution.py:381
  15.4 1.5 %collective-permute-start.8 = (bf16[32,2,8,128]{3,2,1,0:T(8,128)(2,1)S(1)}, bf16[32,2,8,128]{3,2,1,0:T(8,128)(2,1)S(1)}, u32[]{:S(2)}, u32[]{:S(2)}) collective-permute-start(bf16[32,2,8,128]{3,2,1,0:T(8,128)(2,1)S(1)} %collective-permute-done.refs_2_), channel_id=1, source_target_pairs={{0,1},{1,0},{2,3},{3,2},{4,5},{5,4},{6,7},{7,6},{8,9},{9,8},{10,11... | collective-permute-start | bytes 393224 | tf_op jit(solution)/shard_map/ppermute | solution.py:381
  16.3 1.3 %collective-permute-start.2 = (bf16[32,2,8,128]{3,2,1,0:T(8,128)(2,1)S(1)}, bf16[32,2,8,128]{3,2,1,0:T(8,128)(2,1)S(1)}, u32[]{:S(2)}, u32[]{:S(2)}) collective-permute-start(bf16[32,2,8,128]{3,2,1,0:T(8,128)(2,1)S(1)} %collective-permute-done.1.refs_3_), channel_id=1, source_target_pairs={{0,1},{1,0},{2,3},{3,2},{4,5},{5,4},{6,7},{7,6},{8,9},{9,8},{10,11... | collective-permute-start | bytes 393224 | tf_op jit(solution)/shard_map/ppermute | solution.py:381
  19.0 6.6 %collective-permute-start.10 = (bf16[16,32,128]{2,1,0:T(8,128)(2,1)S(1)}, bf16[16,32,128]{2,1,0:T(8,128)(2,1)S(1)}, u32[]{:S(2)}, u32[]{:S(2)}) collective-permute-start(bf16[16,32,128]{2,1,0:T(8,128)(2,1)S(1)} %get-tuple-element.42.low_ref), channel_id=1, source_target_pairs={{0,24},{8,0},{16,8},{24,16},{1,25},{9,1},{17,9},{25,17},{2,26},{10... | collective-permute-start | bytes 393224 | tf_op jit(solution)/shard_map/ppermute | solution.py:377
  21.7 6.7 %collective-permute-start.9 = (bf16[16,32,128]{2,1,0:T(8,128)(2,1)S(1)}, bf16[16,32,128]{2,1,0:T(8,128)(2,1)S(1)}, u32[]{:S(2)}, u32[]{:S(2)}) collective-permute-start(bf16[16,32,128]{2,1,0:T(8,128)(2,1)S(1)} %get-tuple-element.43.high_ref), channel_id=1, source_target_pairs={{0,8},{8,16},{16,24},{24,0},{1,9},{9,17},{17,25},{25,1},{2,10},{10... | collective-permute-start | bytes 393224 | tf_op jit(solution)/shard_map/ppermute | solution.py:377
  30.1 3.3 %collective-permute-start.12 = (bf16[4,16,32,128]{3,2,1,0:T(8,128)(2,1)S(1)}, bf16[4,16,32,128]{3,2,1,0:T(8,128)(2,1)S(1)}, u32[]{:S(2)}, u32[]{:S(2)}) collective-permute-start(bf16[4,16,32,128]{3,2,1,0:T(8,128)(2,1)S(1)} %get-tuple-element.55), channel_id=1, source_target_pairs={{0,1},{1,0},{2,3},{3,2},{4,5},{5,4},{6,7},{7,6},{8,9},{9,8},{10,11... | collective-permute-start | bytes 1572872 | tf_op jit(solution)/shard_map/ppermute | solution.py:381
  31.3 6.7 %collective-permute-start.11 = (bf16[448,256]{1,0:T(8,128)(2,1)S(1)}, bf16[448,256]{1,0:T(8,128)(2,1)S(1)}, u32[]{:S(2)}, u32[]{:S(2)}) collective-permute-start(bf16[448,256]{1,0:T(8,128)(2,1)S(1)} %get-tuple-element.53.a_ref), channel_id=1, source_target_pairs={{0,8},{1,17},{2,10},{3,19},{4,12},{5,21},{6,14},{7,23},{8,0},{9,25... | collective-permute-start | bytes 688136 | tf_op jit(solution)/shard_map/ppermute | solution.py:391
  33.1 6.8 %collective-permute-start.14 = (bf16[448,256]{1,0:T(8,128)(2,1)S(1)}, bf16[448,256]{1,0:T(8,128)(2,1)S(1)}, u32[]{:S(2)}, u32[]{:S(2)}) collective-permute-start(bf16[448,256]{1,0:T(8,128)(2,1)S(1)} %get-tuple-element.57.a_ref), channel_id=1, source_target_pairs={{0,8},{1,17},{2,10},{3,19},{4,12},{5,21},{6,14},{7,23},{8,0},{9,25... | collective-permute-start | bytes 688136 | tf_op jit(solution)/shard_map/ppermute | solution.py:391
  33.5 7.2 %collective-permute-start.16 = (bf16[16,32,128]{2,1,0:T(8,128)(2,1)S(1)}, bf16[16,32,128]{2,1,0:T(8,128)(2,1)S(1)}, u32[]{:S(2)}, u32[]{:S(2)}) collective-permute-start(bf16[16,32,128]{2,1,0:T(8,128)(2,1)S(1)} %get-tuple-element.58), channel_id=1, source_target_pairs={{0,2},{1,3},{2,0},{3,1},{4,6},{5,7},{6,4},{7,5},{8,10},{9,11},{10,... | collective-permute-start | bytes 393224 | tf_op jit(solution)/shard_map/ppermute | solution.py:381
  34.7 13.3 %collective-permute-start.17 = (bf16[16,32,128]{2,1,0:T(8,128)(2,1)S(1)}, bf16[16,32,128]{2,1,0:T(8,128)(2,1)S(1)}, u32[]{:S(2)}, u32[]{:S(2)}) collective-permute-start(bf16[16,32,128]{2,1,0:T(8,128)(2,1)S(1)} %get-tuple-element.59), channel_id=1, source_target_pairs={{0,4},{1,5},{2,6},{3,7},{4,0},{5,1},{6,2},{7,3},{8,12},{9,13},{10,... | collective-permute-start | bytes 393224 | tf_op jit(solution)/shard_map/ppermute | solution.py:381
  38.0 10.0 %collective-permute-start.18 = (bf16[16,32,128]{2,1,0:T(8,128)(2,1)S(1)}, bf16[16,32,128]{2,1,0:T(8,128)(2,1)S(1)}, u32[]{:S(2)}, u32[]{:S(2)}) collective-permute-start(bf16[16,32,128]{2,1,0:T(8,128)(2,1)S(1)} %get-tuple-element.60), channel_id=1, source_target_pairs={{0,6},{1,7},{2,4},{3,5},{4,2},{5,3},{6,0},{7,1},{8,14},{9,15},{10,... | collective-permute-start | bytes 393224 | tf_op jit(solution)/shard_map/ppermute | solution.py:381
  38.0 10.0 %collective-permute-start.13 = (bf16[448,256]{1,0:T(8,128)(2,1)S(1)}, bf16[448,256]{1,0:T(8,128)(2,1)S(1)}, u32[]{:S(2)}, u32[]{:S(2)}) collective-permute-start(bf16[448,256]{1,0:T(8,128)(2,1)S(1)} %pair_sum.2.a_ref), channel_id=1, source_target_pairs={{0,16},{1,9},{2,18},{3,11},{4,20},{5,13},{6,22},{7,15},{8,24},{9,1... | collective-permute-start | bytes 688136 | tf_op jit(solution)/shard_map/ppermute | solution.py:391
  39.9 8.1 %collective-permute-start.15 = (bf16[448,256]{1,0:T(8,128)(2,1)S(1)}, bf16[448,256]{1,0:T(8,128)(2,1)S(1)}, u32[]{:S(2)}, u32[]{:S(2)}) collective-permute-start(bf16[448,256]{1,0:T(8,128)(2,1)S(1)} %pair_sum.3.c_ref), channel_id=1, source_target_pairs={{0,16},{1,9},{2,18},{3,11},{4,20},{5,13},{6,22},{7,15},{8,24},{9,1... | collective-permute-start | bytes 688136 | tf_op jit(solution)/shard_map/ppermute | solution.py:391

commit v13 on v12

--- a/solution.py
+++ b/solution.py
@@ -512,7 +512,7 @@
     (g_own,) = call(
         sum_body,
         [shape_of((cells, o, depth), f32)],
-        [g_own, g_a, g_b, g_ab],
+        [g_own, g_b, g_ab, g_a],
         flops=SUM_FLOPS,
         name="sum",
     )

time: 49.3 us -> 48.4 us (0.982)
  waiting for transfers between devices: 20.7 us -> 19.7 us
    ppermute x11, waiting for transfers between devices: 9.64 us -> 8.57 us  [swap(): lax.ppermute(value, axis, [(i, i ^ bit) for i in range(lax.axis_size(axis...]
where the time goes in v13:
time: 48.4 us; the launch traced here: 48.1 us
  starting transfers between devices  20 us (41%)
  waiting for transfers between devices  19.7 us (41%)
  Pallas kernels  7.61 us (16%)
  between operations  0.72 us (1%)
    ppermute x11, starting transfers between devices, swap(): lax.ppermute(value, axis, [(i, i ^ bit) for i in range(lax.axis_size(axis...  11.5 us
    ppermute x4, waiting for transfers between devices, rotate(): lax.ppermute(value, axis, [(i, (i + step) % count) for i in range(count)])  9.92 us
    ppermute x11, waiting for transfers between devices, swap(): lax.ppermute(value, axis, [(i, i ^ bit) for i in range(lax.axis_size(axis...  8.57 us
    pallas_call x10, Pallas kernels, call(): pl.pallas_call(body, out_shape=out_shape, in_specs=specs or [VMEM] * len(...  7.61 us
    ppermute x4, starting transfers between devices, rotate(): lax.ppermute(value, axis, [(i, (i + step) % count) for i in range(count)])  5.25 us
    ppermute x4, starting transfers between devices, cross(): return lax.ppermute(value, ('slab', 'chan'), pairs)  3.32 us
    ppermute x4, waiting for transfers between devices, cross(): return lax.ppermute(value, ('slab', 'chan'), pairs)  1.23 us
  transfers between devices with their start and end apart: 19, of which 12 were waited for; matrix products, arithmetic and copies ran while one was open for 0% of the time, Pallas kernels for 7%

profile of v13, /device:TPU:0, one launch (start us, length us, event | category | flops | bytes accessed | tf_op | source)
XLA Modules:
  0.0 48.1 jit_solution(264905938955001183)
XLA Ops:
  0.6 4.1 %collective-permute-start = (bf16[32,2,8,128]{3,2,1,0:T(8,128)(2,1)}, bf16[32,2,8,128]{3,2,1,0:T(8,128)(2,1)S(1)}, u32[]{:S(2)}, u32[]{:S(2)}) collective-permute-start(bf16[32,2,8,128]{3,2,1,0:T(8,128)(2,1)} %x_hbm.1), channel_id=1, source_target_pairs={{0,4},{1,5},{2,6},{3,7},{4,0},{5,1},{6,2},{7,3},{8,12},{9,13},{10,... | collective-permute-start | bytes 393224 | tf_op jit(solution)/shard_map/ppermute | solution.py:381
  4.7 1.6 %collective-permute-start.3 = (bf16[32,2,8,128]{3,2,1,0:T(8,128)(2,1)}, bf16[32,2,8,128]{3,2,1,0:T(8,128)(2,1)S(1)}, u32[]{:S(2)}, u32[]{:S(2)}) collective-permute-start(bf16[32,2,8,128]{3,2,1,0:T(8,128)(2,1)} %x_hbm.1), channel_id=1, source_target_pairs={{0,2},{1,3},{2,0},{3,1},{4,6},{5,7},{6,4},{7,5},{8,10},{9,11},{10,... | collective-permute-start | bytes 393224 | tf_op jit(solution)/shard_map/ppermute | solution.py:381
  6.3 1.4 %prepare.1 = (bf16[32,2,8,128]{3,2,1,0:T(8,128)(2,1)S(1)}, bf16[16,32,128]{2,1,0:T(8,128)(2,1)S(1)}, bf16[8,32,128]{2,1,0:T(8,128)(2,1)S(1)}, bf16[8,32,128]{2,1...) custom-call(bf16[32,2,8,128]{3,2,1,0:T(8,128)(2,1)} %x_hbm.1, ...), custom_call_target="tpu_custom_call" | custom-call | bytes 1998912 | tf_op jit(solution)/shard_map/prepare/pallas_call | solution.py:110
  7.7 2.5 %collective-permute-start.6 = (bf16[8,32,128]{2,1,0:T(8,128)(2,1)S(1)}, bf16[8,32,128]{2,1,0:T(8,128)(2,1)S(1)}, u32[]{:S(2)}, u32[]{:S(2)}) collective-permute-start(bf16[8,32,128]{2,1,0:T(8,128)(2,1)S(1)} %get-tuple-element.38), channel_id=1, source_target_pairs={{0,24},{8,0},{16,8},{24,16},{1,25},{9,1},{17,9},{25,17},{2,26},{10... | collective-permute-start | bytes 196616 | tf_op jit(solution)/shard_map/ppermute | solution.py:377
  10.2 1.2 %collective-permute-done.refs_2_ = bf16[32,2,8,128]{3,2,1,0:T(8,128)(2,1)S(1)} collective-permute-done((bf16[32,2,8,128]{3,2,1,0:T(8,128)(2,1)}, bf16[32,2,8,128]{3,2,1,0:T(8,128)(2,1)S(1)}, u32[]{:S(2)}, u32[]{:S(2)}) %collective-permute-start) | collective-permute-done | bytes 131104 | tf_op jit(solution)/shard_map/ppermute | solution.py:381
  11.4 0.7 %collective-permute-start.1 = (bf16[32,2,8,128]{3,2,1,0:T(8,128)(2,1)S(1)}, bf16[32,2,8,128]{3,2,1,0:T(8,128)(2,1)S(1)}, u32[]{:S(2)}, u32[]{:S(2)}) collective-permute-start(bf16[32,2,8,128]{3,2,1,0:T(8,128)(2,1)S(1)} %collective-permute-done.refs_2_), channel_id=1, source_target_pairs={{0,2},{1,3},{2,0},{3,1},{4,6},{5,7},{6,4},{7,5},{8,10},{9,11},{10,... | collective-permute-start | bytes 393224 | tf_op jit(solution)/shard_map/ppermute | solution.py:381
  12.4 3.0 %collective-permute-done.7.go_below_ref = bf16[8,32,128]{2,1,0:T(8,128)(2,1)S(1)} collective-permute-done((bf16[8,32,128]{2,1,0:T(8,128)(2,1)S(1)}, bf16[8,32,128]{2,1,0:T(8,128)(2,1)S(1)}, u32[]{:S(2)}, u32[]{:S(2)}) %collective-permute-start.7) | collective-permute-done | bytes 65568 | tf_op jit(solution)/shard_map/ppermute | solution.py:377
  15.4 0.5 %collective-permute-start.8 = (bf16[32,2,8,128]{3,2,1,0:T(8,128)(2,1)S(1)}, bf16[32,2,8,128]{3,2,1,0:T(8,128)(2,1)S(1)}, u32[]{:S(2)}, u32[]{:S(2)}) collective-permute-start(bf16[32,2,8,128]{3,2,1,0:T(8,128)(2,1)S(1)} %collective-permute-done.refs_2_), channel_id=1, source_target_pairs={{0,1},{1,0},{2,3},{3,2},{4,5},{5,4},{6,7},{7,6},{8,9},{9,8},{10,11... | collective-permute-start | bytes 393224 | tf_op jit(solution)/shard_map/ppermute | solution.py:381
  16.9 0.7 %assemble.1.refs_1_ = bf16[256,2048]{1,0:T(8,128)(2,1)S(1)} custom-call(s32[1]{0:T(128)} %bitcast.me_ref, bf16[32,2,8,128]{3,2,1,0:T(8,128)(2,1)S(1)} %get-tuple-element.37.refs_0_, bf16[32,2,8,128]{3,2,1,0:T(8,128)(2,1)S(1)} %collective-permute-done.3.refs_1_, bf16[32,2,8,128]{3,2,1,0:T(8,128)(2,1)S(1)} %collective-permute-done.refs_2_, ...), custom_call_target="tpu_custom_call" | custom-call | flops 4000000000 | bytes 1966084 | tf_op jit(solution)/shard_map/assemble/pallas_call | solution.py:110
  17.7 1.3 %forward.1 = (f32[16,32,128]{2,1,0:T(8,128)S(1)}, bf16[16,32,128]{2,1,0:T(8,128)(2,1)S(1)}, bf16[16,32,128]{2,1,0:T(8,128)(2,1)S(1)}, bf16[256,2048]{1,0:T(8,128)(2,1)S(1)}) custom-call(s32[1]{0:T(128)} %bitcast.me_ref, bf16[864,256]{1,0:T(8,128)(2,1)S(1)} %get-tuple-element.35.w_ref, ...), custom_call_target="tpu_custom_call", output_to_operand_aliasing={{3}: (3, {})} | custom-call | flops 900000000 | bytes 3194884 | tf_op jit(solution)/shard_map/forward/pallas_call | solution.py:110
  19.0 2.7 %collective-permute-start.10 = (bf16[16,32,128]{2,1,0:T(8,128)(2,1)S(1)}, bf16[16,32,128]{2,1,0:T(8,128)(2,1)S(1)}, u32[]{:S(2)}, u32[]{:S(2)}) collective-permute-start(bf16[16,32,128]{2,1,0:T(8,128)(2,1)S(1)} %get-tuple-element.42.low_ref), channel_id=1, source_target_pairs={{0,24},{8,0},{16,8},{24,16},{1,25},{9,1},{17,9},{25,17},{2,26},{10... | collective-permute-start | bytes 393224 | tf_op jit(solution)/shard_map/ppermute | solution.py:377
  21.7 3.9 %collective-permute-done.10.above_ref = bf16[16,32,128]{2,1,0:T(8,128)(2,1)S(1)} collective-permute-done((bf16[16,32,128]{2,1,0:T(8,128)(2,1)S(1)}, bf16[16,32,128]{2,1,0:T(8,128)(2,1)S(1)}, u32[]{:S(2)}, u32[]{:S(2)}) %collective-permute-start.10) | collective-permute-done | bytes 131104 | tf_op jit(solution)/shard_map/ppermute | solution.py:377
  25.6 2.8 %collective-permute-done.9.below_ref = bf16[16,32,128]{2,1,0:T(8,128)(2,1)S(1)} collective-permute-done((bf16[16,32,128]{2,1,0:T(8,128)(2,1)S(1)}, bf16[16,32,128]{2,1,0:T(8,128)(2,1)S(1)}, u32[]{:S(2)}, u32[]{:S(2)}) %collective-permute-start.9) | collective-permute-done | bytes 131104 | tf_op jit(solution)/shard_map/ppermute | solution.py:377
  28.4 1.7 %gradient.1 = (bf16[32,2,8,128]{3,2,1,0:T(8,128)(2,1)}, f32[32,128]{1,0:T(8,128)S(1)}, bf16[864,2048]{1,0:T(8,128)(2,1)S(1)}, bf16[4,16,32,128]{3,2,1,0:T(8,128)(2,1)S(1)}, bf16[4,16,32,128]{3,2,1,0:T(8,128)(2,1)S(1)}) custom-call(s32[1]{0:T(128)} %bitcast.me_ref, f32[16,32,128]{2,1,0:T(8,128)S(1)} %get-tuple-element.41.own_ref, ...), custom_call_target="tpu_custom_call" | custom-call | flops 905969664 | bytes 6242308 | tf_op jit(solution)/shard_map/gradient/pallas_call | solution.py:110
  30.2 1.1 %filter_grad.1 = (bf16[448,256]{1,0:T(8,128)(2,1)S(1)}, bf16[448,256]{1,0:T(8,128)(2,1)S(1)}) custom-call(bf16[864,2048]{1,0:T(8,128)(2,1)S(1)} %get-tuple-element.50.s_ref, bf16[256,2048]{1,0:T(8,128)(2,1)S(1)} %get-tuple-element.51.x_ref, f32[32,128]{1,0:T(8,128)S(1)} %get-tuple-element.52.total_ref), custom_call_target="tpu_custom_call" | custom-call | flops 905969664 | bytes 5062656 | tf_op jit(solution)/shard_map/filter_grad/pallas_call | solution.py:110
  31.3 1.8 %collective-permute-start.11 = (bf16[448,256]{1,0:T(8,128)(2,1)S(1)}, bf16[448,256]{1,0:T(8,128)(2,1)S(1)}, u32[]{:S(2)}, u32[]{:S(2)}) collective-permute-start(bf16[448,256]{1,0:T(8,128)(2,1)S(1)} %get-tuple-element.53.a_ref), channel_id=1, source_target_pairs={{0,8},{1,17},{2,10},{3,19},{4,12},{5,21},{6,14},{7,23},{8,0},{9,25... | collective-permute-start | bytes 688136 | tf_op jit(solution)/shard_map/ppermute | solution.py:391
  33.5 2.7 %collective-permute-start.16 = (bf16[16,32,128]{2,1,0:T(8,128)(2,1)S(1)}, bf16[16,32,128]{2,1,0:T(8,128)(2,1)S(1)}, u32[]{:S(2)}, u32[]{:S(2)}) collective-permute-start(bf16[16,32,128]{2,1,0:T(8,128)(2,1)S(1)} %get-tuple-element.58), channel_id=1, source_target_pairs={{0,4},{1,5},{2,6},{3,7},{4,0},{5,1},{6,2},{7,3},{8,12},{9,13},{10,... | collective-permute-start | bytes 393224 | tf_op jit(solution)/shard_map/ppermute | solution.py:381
  36.2 1.3 %collective-permute-start.17 = (bf16[16,32,128]{2,1,0:T(8,128)(2,1)S(1)}, bf16[16,32,128]{2,1,0:T(8,128)(2,1)S(1)}, u32[]{:S(2)}, u32[]{:S(2)}) collective-permute-start(bf16[16,32,128]{2,1,0:T(8,128)(2,1)S(1)} %get-tuple-element.59), channel_id=1, source_target_pairs={{0,6},{1,7},{2,4},{3,5},{4,2},{5,3},{6,0},{7,1},{8,14},{9,15},{10,... | collective-permute-start | bytes 393224 | tf_op jit(solution)/shard_map/ppermute | solution.py:381
  37.5 0.5 %collective-permute-start.18 = (bf16[16,32,128]{2,1,0:T(8,128)(2,1)S(1)}, bf16[16,32,128]{2,1,0:T(8,128)(2,1)S(1)}, u32[]{:S(2)}, u32[]{:S(2)}) collective-permute-start(bf16[16,32,128]{2,1,0:T(8,128)(2,1)S(1)} %get-tuple-element.60), channel_id=1, source_target_pairs={{0,2},{1,3},{2,0},{3,1},{4,6},{5,7},{6,4},{7,5},{8,10},{9,11},{10,... | collective-permute-start | bytes 393224 | tf_op jit(solution)/shard_map/ppermute | solution.py:381
  38.0 0.6 %collective-permute-start.13 = (bf16[448,256]{1,0:T(8,128)(2,1)S(1)}, bf16[448,256]{1,0:T(8,128)(2,1)S(1)}, u32[]{:S(2)}, u32[]{:S(2)}) collective-permute-start(bf16[448,256]{1,0:T(8,128)(2,1)S(1)} %pair_sum.2.a_ref), channel_id=1, source_target_pairs={{0,16},{1,9},{2,18},{3,11},{4,20},{5,13},{6,22},{7,15},{8,24},{9,1... | collective-permute-start | bytes 688136 | tf_op jit(solution)/shard_map/ppermute | solution.py:391
  38.6 1.2 %collective-permute-done.14.b_ref = bf16[448,256]{1,0:T(8,128)(2,1)S(1)} collective-permute-done((bf16[448,256]{1,0:T(8,128)(2,1)S(1)}, bf16[448,256]{1,0:T(8,128)(2,1)S(1)}, u32[]{:S(2)}, u32[]{:S(2)}) %collective-permute-start.14) | collective-permute-done | bytes 229408 | tf_op jit(solution)/shard_map/ppermute | solution.py:391
  39.9 0.7 %collective-permute-start.15 = (bf16[448,256]{1,0:T(8,128)(2,1)S(1)}, bf16[448,256]{1,0:T(8,128)(2,1)S(1)}, u32[]{:S(2)}, u32[]{:S(2)}) collective-permute-start(bf16[448,256]{1,0:T(8,128)(2,1)S(1)} %pair_sum.3.c_ref), channel_id=1, source_target_pairs={{0,16},{1,9},{2,18},{3,11},{4,20},{5,13},{6,22},{7,15},{8,24},{9,1... | collective-permute-start | bytes 688136 | tf_op jit(solution)/shard_map/ppermute | solution.py:391
  40.6 5.9 %collective-permute-done.16.b_ref = bf16[16,32,128]{2,1,0:T(8,128)(2,1)S(1)} collective-permute-done((bf16[16,32,128]{2,1,0:T(8,128)(2,1)S(1)}, bf16[16,32,128]{2,1,0:T(8,128)(2,1)S(1)}, u32[]{:S(2)}, u32[]{:S(2)}) %collective-permute-start.16) | collective-permute-done | bytes 131104 | tf_op jit(solution)/shard_map/ppermute | solution.py:381
  47.0 1.1 %last.1 = (f32[27,32,256]{2,1,0:T(8,128)}, f32[1,32]{1,0:T(1,128)}, bf16[32,2,8,128]{3,2,1,0:T(8,128)(2,1)}) custom-call(bf16[448,256]{1,0:T(8,128)(2,1)S(1)} %pair_sum.2.a_ref, bf16[448,256]{1,0:T(8,128)(2,1)S(1)} %collective-permute-done.13.b_ref, bf16[448,256]{1,0:T(8,128)(2,1)S(1)} %pair_sum.3.c_ref, bf16[448,256]{1,0:T(8,128)(2,1)S(1)} %collective-permute-done.15.d_ref, ...), custom_call_target="tpu_custom_call" | custom-call | bytes 2195584 | tf_op jit(solution)/shard_map/last/pallas_call | solution.py:110
  (24 shorter events, 2.4 us)
Async XLA Ops:
  0.6 10.7 %collective-permute-start = (bf16[32,2,8,128]{3,2,1,0:T(8,128)(2,1)}, bf16[32,2,8,128]{3,2,1,0:T(8,128)(2,1)S(1)}, u32[]{:S(2)}, u32[]{:S(2)}) collective-permute-start(bf16[32,2,8,128]{3,2,1,0:T(8,128)(2,1)} %x_hbm.1), channel_id=1, source_target_pairs={{0,4},{1,5},{2,6},{3,7},{4,0},{5,1},{6,2},{7,3},{8,12},{9,13},{10,... | collective-permute-start | bytes 393224 | tf_op jit(solution)/shard_map/ppermute | solution.py:381
  4.7 10.6 %collective-permute-start.3 = (bf16[32,2,8,128]{3,2,1,0:T(8,128)(2,1)}, bf16[32,2,8,128]{3,2,1,0:T(8,128)(2,1)S(1)}, u32[]{:S(2)}, u32[]{:S(2)}) collective-permute-start(bf16[32,2,8,128]{3,2,1,0:T(8,128)(2,1)} %x_hbm.1), channel_id=1, source_target_pairs={{0,2},{1,3},{2,0},{3,1},{4,6},{5,7},{6,4},{7,5},{8,10},{9,11},{10,... | collective-permute-start | bytes 393224 | tf_op jit(solution)/shard_map/ppermute | solution.py:381
  7.7 4.7 %collective-permute-start.6 = (bf16[8,32,128]{2,1,0:T(8,128)(2,1)S(1)}, bf16[8,32,128]{2,1,0:T(8,128)(2,1)S(1)}, u32[]{:S(2)}, u32[]{:S(2)}) collective-permute-start(bf16[8,32,128]{2,1,0:T(8,128)(2,1)S(1)} %get-tuple-element.38), channel_id=1, source_target_pairs={{0,24},{8,0},{16,8},{24,16},{1,25},{9,1},{17,9},{25,17},{2,26},{10... | collective-permute-start | bytes 196616 | tf_op jit(solution)/shard_map/ppermute | solution.py:377
  10.2 5.2 %collective-permute-start.7 = (bf16[8,32,128]{2,1,0:T(8,128)(2,1)S(1)}, bf16[8,32,128]{2,1,0:T(8,128)(2,1)S(1)}, u32[]{:S(2)}, u32[]{:S(2)}) collective-permute-start(bf16[8,32,128]{2,1,0:T(8,128)(2,1)S(1)} %get-tuple-element.39), channel_id=1, source_target_pairs={{0,8},{8,16},{16,24},{24,0},{1,9},{9,17},{17,25},{25,1},{2,10},{10... | collective-permute-start | bytes 196616 | tf_op jit(solution)/shard_map/ppermute | solution.py:377
  10.2 6.2 %collective-permute-start.4 = (bf16[32,2,8,128]{3,2,1,0:T(8,128)(2,1)}, bf16[32,2,8,128]{3,2,1,0:T(8,128)(2,1)S(1)}, u32[]{:S(2)}, u32[]{:S(2)}) collective-permute-start(bf16[32,2,8,128]{3,2,1,0:T(8,128)(2,1)} %x_hbm.1), channel_id=1, source_target_pairs={{0,1},{1,0},{2,3},{3,2},{4,5},{5,4},{6,7},{7,6},{8,9},{9,8},{10,11... | collective-permute-start | bytes 393224 | tf_op jit(solution)/shard_map/ppermute | solution.py:381
  11.4 5.0 %collective-permute-start.1 = (bf16[32,2,8,128]{3,2,1,0:T(8,128)(2,1)S(1)}, bf16[32,2,8,128]{3,2,1,0:T(8,128)(2,1)S(1)}, u32[]{:S(2)}, u32[]{:S(2)}) collective-permute-start(bf16[32,2,8,128]{3,2,1,0:T(8,128)(2,1)S(1)} %collective-permute-done.refs_2_), channel_id=1, source_target_pairs={{0,2},{1,3},{2,0},{3,1},{4,6},{5,7},{6,4},{7,5},{8,10},{9,11},{10,... | collective-permute-start | bytes 393224 | tf_op jit(solution)/shard_map/ppermute | solution.py:381
  15.3 1.3 %collective-permute-start.5 = (bf16[32,2,8,128]{3,2,1,0:T(8,128)(2,1)S(1)}, bf16[32,2,8,128]{3,2,1,0:T(8,128)(2,1)S(1)}, u32[]{:S(2)}, u32[]{:S(2)}) collective-permute-start(bf16[32,2,8,128]{3,2,1,0:T(8,128)(2,1)S(1)} %collective-permute-done.3.refs_1_), channel_id=1, source_target_pairs={{0,1},{1,0},{2,3},{3,2},{4,5},{5,4},{6,7},{7,6},{8,9},{9,8},{10,11... | collective-permute-start | bytes 393224 | tf_op jit(solution)/shard_map/ppermute | solution.py:381
  15.4 1.5 %collective-permute-start.8 = (bf16[32,2,8,128]{3,2,1,0:T(8,128)(2,1)S(1)}, bf16[32,2,8,128]{3,2,1,0:T(8,128)(2,1)S(1)}, u32[]{:S(2)}, u32[]{:S(2)}) collective-permute-start(bf16[32,2,8,128]{3,2,1,0:T(8,128)(2,1)S(1)} %collective-permute-done.refs_2_), channel_id=1, source_target_pairs={{0,1},{1,0},{2,3},{3,2},{4,5},{5,4},{6,7},{7,6},{8,9},{9,8},{10,11... | collective-permute-start | bytes 393224 | tf_op jit(solution)/shard_map/ppermute | solution.py:381
  16.3 1.3 %collective-permute-start.2 = (bf16[32,2,8,128]{3,2,1,0:T(8,128)(2,1)S(1)}, bf16[32,2,8,128]{3,2,1,0:T(8,128)(2,1)S(1)}, u32[]{:S(2)}, u32[]{:S(2)}) collective-permute-start(bf16[32,2,8,128]{3,2,1,0:T(8,128)(2,1)S(1)} %collective-permute-done.1.refs_3_), channel_id=1, source_target_pairs={{0,1},{1,0},{2,3},{3,2},{4,5},{5,4},{6,7},{7,6},{8,9},{9,8},{10,11... | collective-permute-start | bytes 393224 | tf_op jit(solution)/shard_map/ppermute | solution.py:381
  19.0 6.6 %collective-permute-start.10 = (bf16[16,32,128]{2,1,0:T(8,128)(2,1)S(1)}, bf16[16,32,128]{2,1,0:T(8,128)(2,1)S(1)}, u32[]{:S(2)}, u32[]{:S(2)}) collective-permute-start(bf16[16,32,128]{2,1,0:T(8,128)(2,1)S(1)} %get-tuple-element.42.low_ref), channel_id=1, source_target_pairs={{0,24},{8,0},{16,8},{24,16},{1,25},{9,1},{17,9},{25,17},{2,26},{10... | collective-permute-start | bytes 393224 | tf_op jit(solution)/shard_map/ppermute | solution.py:377
  21.7 6.7 %collective-permute-start.9 = (bf16[16,32,128]{2,1,0:T(8,128)(2,1)S(1)}, bf16[16,32,128]{2,1,0:T(8,128)(2,1)S(1)}, u32[]{:S(2)}, u32[]{:S(2)}) collective-permute-start(bf16[16,32,128]{2,1,0:T(8,128)(2,1)S(1)} %get-tuple-element.43.high_ref), channel_id=1, source_target_pairs={{0,8},{8,16},{16,24},{24,0},{1,9},{9,17},{17,25},{25,1},{2,10},{10... | collective-permute-start | bytes 393224 | tf_op jit(solution)/shard_map/ppermute | solution.py:377
  30.1 3.3 %collective-permute-start.12 = (bf16[4,16,32,128]{3,2,1,0:T(8,128)(2,1)S(1)}, bf16[4,16,32,128]{3,2,1,0:T(8,128)(2,1)S(1)}, u32[]{:S(2)}, u32[]{:S(2)}) collective-permute-start(bf16[4,16,32,128]{3,2,1,0:T(8,128)(2,1)S(1)} %get-tuple-element.55), channel_id=1, source_target_pairs={{0,1},{1,0},{2,3},{3,2},{4,5},{5,4},{6,7},{7,6},{8,9},{9,8},{10,11... | collective-permute-start | bytes 1572872 | tf_op jit(solution)/shard_map/ppermute | solution.py:381
  31.3 6.7 %collective-permute-start.11 = (bf16[448,256]{1,0:T(8,128)(2,1)S(1)}, bf16[448,256]{1,0:T(8,128)(2,1)S(1)}, u32[]{:S(2)}, u32[]{:S(2)}) collective-permute-start(bf16[448,256]{1,0:T(8,128)(2,1)S(1)} %get-tuple-element.53.a_ref), channel_id=1, source_target_pairs={{0,8},{1,17},{2,10},{3,19},{4,12},{5,21},{6,14},{7,23},{8,0},{9,25... | collective-permute-start | bytes 688136 | tf_op jit(solution)/shard_map/ppermute | solution.py:391
  33.1 6.8 %collective-permute-start.14 = (bf16[448,256]{1,0:T(8,128)(2,1)S(1)}, bf16[448,256]{1,0:T(8,128)(2,1)S(1)}, u32[]{:S(2)}, u32[]{:S(2)}) collective-permute-start(bf16[448,256]{1,0:T(8,128)(2,1)S(1)} %get-tuple-element.57.a_ref), channel_id=1, source_target_pairs={{0,8},{1,17},{2,10},{3,19},{4,12},{5,21},{6,14},{7,23},{8,0},{9,25... | collective-permute-start | bytes 688136 | tf_op jit(solution)/shard_map/ppermute | solution.py:391
  33.5 13.0 %collective-permute-start.16 = (bf16[16,32,128]{2,1,0:T(8,128)(2,1)S(1)}, bf16[16,32,128]{2,1,0:T(8,128)(2,1)S(1)}, u32[]{:S(2)}, u32[]{:S(2)}) collective-permute-start(bf16[16,32,128]{2,1,0:T(8,128)(2,1)S(1)} %get-tuple-element.58), channel_id=1, source_target_pairs={{0,4},{1,5},{2,6},{3,7},{4,0},{5,1},{6,2},{7,3},{8,12},{9,13},{10,... | collective-permute-start | bytes 393224 | tf_op jit(solution)/shard_map/ppermute | solution.py:381
  36.2 10.3 %collective-permute-start.17 = (bf16[16,32,128]{2,1,0:T(8,128)(2,1)S(1)}, bf16[16,32,128]{2,1,0:T(8,128)(2,1)S(1)}, u32[]{:S(2)}, u32[]{:S(2)}) collective-permute-start(bf16[16,32,128]{2,1,0:T(8,128)(2,1)S(1)} %get-tuple-element.59), channel_id=1, source_target_pairs={{0,6},{1,7},{2,4},{3,5},{4,2},{5,3},{6,0},{7,1},{8,14},{9,15},{10,... | collective-permute-start | bytes 393224 | tf_op jit(solution)/shard_map/ppermute | solution.py:381
  37.5 9.4 %collective-permute-start.18 = (bf16[16,32,128]{2,1,0:T(8,128)(2,1)S(1)}, bf16[16,32,128]{2,1,0:T(8,128)(2,1)S(1)}, u32[]{:S(2)}, u32[]{:S(2)}) collective-permute-start(bf16[16,32,128]{2,1,0:T(8,128)(2,1)S(1)} %get-tuple-element.60), channel_id=1, source_target_pairs={{0,2},{1,3},{2,0},{3,1},{4,6},{5,7},{6,4},{7,5},{8,10},{9,11},{10,... | collective-permute-start | bytes 393224 | tf_op jit(solution)/shard_map/ppermute | solution.py:381
  38.0 8.9 %collective-permute-start.13 = (bf16[448,256]{1,0:T(8,128)(2,1)S(1)}, bf16[448,256]{1,0:T(8,128)(2,1)S(1)}, u32[]{:S(2)}, u32[]{:S(2)}) collective-permute-start(bf16[448,256]{1,0:T(8,128)(2,1)S(1)} %pair_sum.2.a_ref), channel_id=1, source_target_pairs={{0,16},{1,9},{2,18},{3,11},{4,20},{5,13},{6,22},{7,15},{8,24},{9,1... | collective-permute-start | bytes 688136 | tf_op jit(solution)/shard_map/ppermute | solution.py:391
  39.9 7.1 %collective-permute-start.15 = (bf16[448,256]{1,0:T(8,128)(2,1)S(1)}, bf16[448,256]{1,0:T(8,128)(2,1)S(1)}, u32[]{:S(2)}, u32[]{:S(2)}) collective-permute-start(bf16[448,256]{1,0:T(8,128)(2,1)S(1)} %pair_sum.3.c_ref), channel_id=1, source_target_pairs={{0,16},{1,9},{2,18},{3,11},{4,20},{5,13},{6,22},{7,15},{8,24},{9,1... | collective-permute-start | bytes 688136 | tf_op jit(solution)/shard_map/ppermute | solution.py:391

commit v14 on v13

--- a/solution.py
+++ b/solution.py
@@ -104,14 +104,14 @@
     return (activation, grad_in.astype(jnp.bfloat16), weight_grad, bias_grad)
 
 
-def call(body, out_shape, operands, specs=None, scratch=(), flops=0, name=None, aliases=None):
+def call(body, out_shape, operands, specs=None, scratch=(), flops=0, name=None, aliases=None, out_specs=None):
     read = sum(math.prod(a.shape) * a.dtype.itemsize for a in operands)
     written = sum(math.prod(a.shape) * a.dtype.itemsize for a in out_shape)
     return pl.pallas_call(
         body,
         out_shape=out_shape,
         in_specs=specs or [VMEM] * len(operands),
-        out_specs=[VMEM] * len(out_shape),
+        out_specs=out_specs or [VMEM] * len(out_shape),
         scratch_shapes=list(scratch),
         input_output_aliases=aliases or {},
         compiler_params=pltpu.CompilerParams(vmem_limit_bytes=24 * 2**20),
@@ -126,6 +126,16 @@
     return jax.ShapeDtypeStruct(shape, dtype)
 
 
+def by_parity(slab_ref, a, b):
+    even = lax.rem(slab_ref[0], 2) == 0
+    f32 = jnp.float32
+    wide = a.astype(f32), b.astype(f32)
+    return (
+        jnp.where(even, wide[0], wide[1]).astype(a.dtype),
+        jnp.where(even, wide[1], wide[0]).astype(a.dtype),
+    )
+
+
 def turned(value, wide_ref):
     o = value.shape[0]
     cells = wide_ref.shape[0] // o
@@ -138,14 +148,15 @@
 def prepare_body(
     n,
     rows,
+    slab_ref,
     x_hbm,
     go_hbm,
     w_hbm,
     bias_hbm,
     x_ref,
     go_ref,
-    go_low_ref,
-    go_high_ref,
+    go_first_ref,
+    go_second_ref,
     flat_ref,
     back_ref,
     bias_ref,
@@ -164,12 +175,12 @@
     for copy in copies:
         copy.start()
     copies[0].wait()
-    for k, value in enumerate(turned(go_in[...], wide_ref)):
+    values = turned(go_in[...], wide_ref)
+    for k, value in enumerate(values):
         go_ref[k] = value
-        if k < rows:
-            go_low_ref[k] = value
-        if k >= (n - 1) * rows:
-            go_high_ref[k - (n - 1) * rows] = value
+    for y in range(rows):
+        low, high = values[y], values[(n - 1) * rows + y]
+        go_first_ref[y], go_second_ref[y] = by_parity(slab_ref, high, low)
     copies[1].wait()
     copies[2].wait()
     copies[3].wait()
@@ -200,9 +211,9 @@
     return jnp.bitwise_xor(me_ref[0], 2 * (b % 4) + b // 4)
 
 
-def forward_body(n, rows, o, places, me_ref, w_ref, *refs):
+def forward_body(n, rows, o, places, me_ref, slab_ref, w_ref, *refs):
     blocks = refs[: len(places)]
-    own_ref, low_ref, high_ref, x_ref, acc, wide_ref = refs[len(places) + 1 :]
+    own_ref, first_ref, second_ref, x_ref, acc, wide_ref = refs[len(places) + 1 :]
     for b, block in zip(places, blocks):
         place_block(me_ref, b, block, x_ref, wide_ref)
     w = w_ref[...]
@@ -222,23 +233,17 @@
                     else:
                         acc[slot] = value
                         seen.add(slot)
-    for q in range(n + 2):
-        for y in range(rows):
-            total = (
-                pltpu.roll(acc[0, q, y], 1, 1)
-                + acc[1, q, y]
-                + pltpu.roll(acc[2, q, y], LANES - 1, 1)
-            )
-            if q == 0:
-                low_ref[y] = total.astype(low_ref.dtype)
-            elif q == n + 1:
-                high_ref[y] = total.astype(high_ref.dtype)
-            else:
-                own_ref[(q - 1) * rows + y] = total
-            if q == 1:
-                low_ref[rows + y] = total.astype(low_ref.dtype)
-            if q == n:
-                high_ref[rows + y] = total.astype(high_ref.dtype)
+    for y in range(rows):
+        totals = [
+            pltpu.roll(acc[0, q, y], 1, 1) + acc[1, q, y] + pltpu.roll(acc[2, q, y], LANES - 1, 1)
+            for q in range(n + 2)
+        ]
+        for p in range(n):
+            own_ref[p * rows + y] = totals[p + 1]
+        for at, low, high in ((y, 0, n + 1), (rows + y, 1, n)):
+            first, second = by_parity(slab_ref, totals[high], totals[low])
+            first_ref[at] = first.astype(first_ref.dtype)
+            second_ref[at] = second.astype(second_ref.dtype)
 
 
 def gradient_body(
@@ -247,15 +252,16 @@
     o,
     scale,
     me_ref,
+    slab_ref,
     own_ref,
-    low_ref,
-    high_ref,
-    below_ref,
-    above_ref,
+    first_ref,
+    second_ref,
+    first_in_ref,
+    second_in_ref,
     bias_ref,
     go_ref,
-    go_below_ref,
-    go_above_ref,
+    go_first_ref,
+    go_second_ref,
     back_ref,
     act_ref,
     total_ref,
@@ -270,21 +276,29 @@
         place = pl.ds(pl.multiple_of(owner(me_ref, b) * o, o), o)
         w_ref[b * o : (b + 1) * o] = back_ref[place]
     total = jnp.zeros((o, LANES), f32)
+    even = lax.rem(slab_ref[0], 2) == 0
+
+    def above(first, second, at):
+        return jnp.where(even, first[at].astype(f32), second[at].astype(f32))
+
+    def below(first, second, at):
+        return above(second, first, at)
+
     for q in range(n + 2):
         for y in range(rows):
             if q == 0:
-                pre = below_ref[rows + y].astype(f32) + low_ref[y].astype(f32)
-                go = go_below_ref[y]
+                pre = below(first_in_ref, second_in_ref, rows + y) + below(first_ref, second_ref, y)
+                go = below(go_first_ref, go_second_ref, y)
             elif q == n + 1:
-                pre = above_ref[rows + y].astype(f32) + high_ref[y].astype(f32)
-                go = go_above_ref[y]
+                pre = above(first_in_ref, second_in_ref, rows + y) + above(first_ref, second_ref, y)
+                go = above(go_first_ref, go_second_ref, y)
             else:
                 pre = own_ref[(q - 1) * rows + y]
                 go = go_ref[(q - 1) * rows + y]
                 if q == 1:
-                    pre = pre + below_ref[y].astype(f32)
+                    pre = pre + below(first_in_ref, second_in_ref, y)
                 if q == n:
-                    pre = pre + above_ref[y].astype(f32)
+                    pre = pre + above(first_in_ref, second_in_ref, y)
             pre = pre + bias_ref[...]
             s = jax.nn.sigmoid(pre)
             slope = s * (1.0 + pre * (1.0 - s))
@@ -350,31 +364,37 @@
 
 
 def last_body(
-    taps, a_ref, b_ref, c_ref, d_ref, g_ref, out_ref, bias_ref, grad_ref, wide_ref
+    taps, a_ref, b_ref, c_ref, d_ref, g_ref, out_hbm, bias_ref, grad_hbm, wide_ref, grad_ref, out_ref, sems
 ):
     o = out_ref.shape[1]
     f32 = jnp.float32
     cells = g_ref.shape[0]
+    copies = []
+
+    def send(source, target):
+        copies.append(pltpu.make_async_copy(source, target, sems.at[len(copies)]))
+        copies[-1].start()
+
     for k in range(cells):
         wide_ref[pl.ds(k, o, stride=cells), :] = g_ref[k]
     grad_ref[...] = wide_ref[...].reshape(grad_ref.shape).astype(grad_ref.dtype)
+    send(grad_ref, grad_hbm)
     for k in range(27):
         left, right, at = (a_ref, b_ref, k) if k < taps else (c_ref, d_ref, k - taps)
         cut = slice(at * o, (at + 1) * o)
         out_ref[k] = left[cut].astype(f32) + right[cut].astype(f32)
+        if k % 9 == 8:
+            send(out_ref.at[pl.ds(k - 8, 9)], out_hbm.at[pl.ds(k - 8, 9)])
     cut = slice((27 - taps) * o, (28 - taps) * o)
     column = (c_ref[cut].astype(f32) + d_ref[cut].astype(f32))[:, :o]
     same = lax.broadcasted_iota(jnp.int32, (o, o), 0) == lax.broadcasted_iota(jnp.int32, (o, o), 1)
     bias_ref[...] = jnp.sum(jnp.where(same, column, 0.0), axis=0, keepdims=True)
+    for copy in copies:
+        copy.wait()
 
 
 def in_hbm(value):
     return pltpu.with_memory_space_constraint(value, pltpu.HBM)
-
-
-def rotate(value, axis, step):
-    count = lax.axis_size(axis)
-    return lax.ppermute(value, axis, [(i, (i + step) % count) for i in range(count)])
 
 
 def swap(value, axis, bit):
@@ -399,13 +419,14 @@
     flops = 2 * 27 * o * c_all * cells * depth
     scale = 1.0 / math.sqrt(lax.axis_size("slab") * cells * depth)
     me = lax.axis_index("chan").astype(jnp.int32).reshape(1)
+    slab = lax.axis_index("slab").astype(jnp.int32).reshape(1)
 
     block_wide = [pltpu.VMEM((o * cells, depth), f32)]
 
     x_b = swap(x_in, "chan", 4)
     x_a = swap(x_in, "chan", 2)
     x_side = swap(x_in, "chan", 1)
-    x_own, go, go_low, go_high, w_flat, w_back, bias = call(
+    x_own, go, go_first, go_second, w_flat, w_back, bias = call(
         functools.partial(prepare_body, n, rows),
         [
             shape_of((o, n, rows, depth), bf16),
@@ -416,8 +437,8 @@
             shape_of((c_all, 27 * o), bf16),
             shape_of((o, LANES), f32),
         ],
-        [in_hbm(a) for a in (x_in, grad_out, jnp.transpose(weight, (1, 0, 2)), bias_vec[None, :])],
-        [HBM] * 4,
+        [slab] + [in_hbm(a) for a in (x_in, grad_out, jnp.transpose(weight, (1, 0, 2)), bias_vec[None, :])],
+        [SMEM] + [HBM] * 4,
         [
             pltpu.VMEM((o, n, rows, depth), bf16),
             pltpu.VMEM((27, o, c_all), bf16),
@@ -427,11 +448,11 @@
         ],
         name="prepare",
     )
-    go_above = rotate(go_low, "slab", -1)
-    go_below = rotate(go_high, "slab", 1)
+    go_first = swap(go_first, "slab", 1)
+    go_second = swap(go_second, "slab", 3)
     x_b, w_flat = lax.optimization_barrier((x_b, w_flat))
     x_ab = swap(x_b, "chan", 2)
-    late_b, go_above, go_below = lax.optimization_barrier((x_b, go_above, go_below))
+    late_b, go_first, go_second = lax.optimization_barrier((x_b, go_first, go_second))
     x_a_side = swap(x_a, "chan", 1)
     x_b_side = swap(late_b, "chan", 1)
     early, late = (0, 1, 2, 3, 4, 5, 6), (7,)
@@ -445,7 +466,7 @@
         name="assemble",
     )
     x_ab_side = swap(x_ab, "chan", 1)
-    own, low, high, x_all = call(
+    own, first, second, x_all = call(
         functools.partial(forward_body, n, rows, o, late),
         [
             shape_of((cells, o, depth), f32),
@@ -453,15 +474,15 @@
             shape_of((2 * rows, o, depth), bf16),
             shape_of((c_all, cells * depth), bf16),
         ],
-        [me, w_flat, x_ab_side, x_all],
-        [SMEM] + [VMEM] * 3,
+        [me, slab, w_flat, x_ab_side, x_all],
+        [SMEM] * 2 + [VMEM] * 3,
         [pltpu.VMEM((3, n + 2, rows, o, depth), f32), *block_wide],
         flops=FORWARD_FLOPS,
         name="forward",
-        aliases={3: 3},
-    )
-    above = rotate(low, "slab", -1)
-    below = rotate(high, "slab", 1)
+        aliases={4: 3},
+    )
+    first_in = swap(first, "slab", 1)
+    second_in = swap(second, "slab", 3)
     act, total, stacked, other, mine = call(
         functools.partial(gradient_body, n, rows, o, scale),
         [
@@ -471,8 +492,8 @@
             shape_of((4, cells, o, depth), bf16),
             shape_of((4, cells, o, depth), bf16),
         ],
-        [me, own, low, high, below, above, bias, go, go_below, go_above, w_back],
-        [SMEM] + [VMEM] * 10,
+        [me, slab, own, first, second, first_in, second_in, bias, go, go_first, go_second, w_back],
+        [SMEM] * 2 + [VMEM] * 10,
         [pltpu.VMEM((c_all, 27 * o), bf16), *block_wide],
         flops=flops,
         name="gradient",
@@ -524,8 +545,14 @@
             shape_of((o, n, rows, depth), bf16),
         ],
         [first, first_far, second, second_far, g_own],
-        scratch=block_wide,
+        scratch=[
+            *block_wide,
+            pltpu.VMEM((o, n, rows, depth), bf16),
+            pltpu.VMEM((27, o, c_all), f32),
+            pltpu.SemaphoreType.DMA((4,)),
+        ],
         name="last",
+        out_specs=[HBM, VMEM, HBM],
     )
     return act, grad_in, jnp.transpose(weight_grad, (1, 0, 2)), bias_grad[0]
 

time: 48.4 us -> 49 us (1.012)
  starting transfers between devices: 20 us -> 20.8 us
  waiting for transfers between devices: 19.7 us -> 19 us
  Pallas kernels: 7.61 us -> 8.17 us
    ppermute x4 -> x0, waiting for transfers between devices: 9.92 us -> none  [rotate(): lax.ppermute(value, axis, [(i, (i + step) % count) for i in range(count)])]
    ppermute x11 -> x15, waiting for transfers between devices: 8.57 us -> 17.8 us  [swap(): lax.ppermute(value, axis, [(i, i ^ bit) for i in range(lax.axis_size(axis...]
    ppermute x11 -> x15, starting transfers between devices: 11.5 us -> 17.3 us  [swap(): lax.ppermute(value, axis, [(i, i ^ bit) for i in range(lax.axis_size(axis...]
    ppermute x4 -> x0, starting transfers between devices: 5.25 us -> none  [rotate(): lax.ppermute(value, axis, [(i, (i + step) % count) for i in range(count)])]
    pallas_call x10, Pallas kernels: 7.61 us -> 8.17 us  [call(): pl.pallas_call(body, out_shape=out_shape, in_specs=specs or [VMEM] * len(...]
  transfers between devices with their start and end apart: 19 -> 19, of which waited for: 12 -> 10; matrix products, arithmetic and copies ran while one was open for 0% -> 0% of each run, Pallas kernels for 7% -> 7%
where the time goes in v14:
time: 49 us; the launch traced here: 48.7 us
  starting transfers between devices  20.8 us (42%)
  waiting for transfers between devices  19 us (39%)
  Pallas kernels  8.17 us (17%)
  between operations  0.73 us (1%)
    ppermute x15, waiting for transfers between devices, swap(): lax.ppermute(value, axis, [(i, i ^ bit) for i in range(lax.axis_size(axis...  17.8 us
    ppermute x15, starting transfers between devices, swap(): lax.ppermute(value, axis, [(i, i ^ bit) for i in range(lax.axis_size(axis...  17.3 us
    pallas_call x10, Pallas kernels, call(): pl.pallas_call(body, out_shape=out_shape, in_specs=specs or [VMEM] * len(...  8.17 us
    ppermute x4, starting transfers between devices, cross(): return lax.ppermute(value, ('slab', 'chan'), pairs)  3.5 us
    ppermute x4, waiting for transfers between devices, cross(): return lax.ppermute(value, ('slab', 'chan'), pairs)  1.24 us
  transfers between devices with their start and end apart: 19, of which 10 were waited for; matrix products, arithmetic and copies ran while one was open for 0% of the time, Pallas kernels for 7%

profile of v14, /device:TPU:0, one launch (start us, length us, event | category | flops | bytes accessed | tf_op | source)
XLA Modules:
  0.0 48.7 jit_solution(5528717818449033255)
XLA Ops:
  0.6 4.1 %collective-permute-start = (bf16[32,2,8,128]{3,2,1,0:T(8,128)(2,1)}, bf16[32,2,8,128]{3,2,1,0:T(8,128)(2,1)S(1)}, u32[]{:S(2)}, u32[]{:S(2)}) collective-permute-start(bf16[32,2,8,128]{3,2,1,0:T(8,128)(2,1)} %x_hbm.1), channel_id=1, source_target_pairs={{0,4},{1,5},{2,6},{3,7},{4,0},{5,1},{6,2},{7,3},{8,12},{9,13},{10,... | collective-permute-start | bytes 393224 | tf_op jit(solution)/shard_map/ppermute | solution.py:401
  4.7 1.6 %collective-permute-start.3 = (bf16[32,2,8,128]{3,2,1,0:T(8,128)(2,1)}, bf16[32,2,8,128]{3,2,1,0:T(8,128)(2,1)S(1)}, u32[]{:S(2)}, u32[]{:S(2)}) collective-permute-start(bf16[32,2,8,128]{3,2,1,0:T(8,128)(2,1)} %x_hbm.1), channel_id=1, source_target_pairs={{0,2},{1,3},{2,0},{3,1},{4,6},{5,7},{6,4},{7,5},{8,10},{9,11},{10,... | collective-permute-start | bytes 393224 | tf_op jit(solution)/shard_map/ppermute | solution.py:401
  6.3 1.4 %prepare.1 = (bf16[32,2,8,128]{3,2,1,0:T(8,128)(2,1)S(1)}, bf16[16,32,128]{2,1,0:T(8,128)(2,1)S(1)}, bf16[8,32,128]{2,1,0:T(8,128)(2,1)S(1)}, bf16[8,32,128]{2,1...) custom-call(s32[1]{0:T(128)} %bitcast.1.slab_ref, ...), custom_call_target="tpu_custom_call" | custom-call | bytes 1998916 | tf_op jit(solution)/shard_map/prepare/pallas_call | solution.py:110
  7.7 1.6 %collective-permute-start.6 = (bf16[8,32,128]{2,1,0:T(8,128)(2,1)S(1)}, bf16[8,32,128]{2,1,0:T(8,128)(2,1)S(1)}, u32[]{:S(2)}, u32[]{:S(2)}) collective-permute-start(bf16[8,32,128]{2,1,0:T(8,128)(2,1)S(1)} %get-tuple-element.38), channel_id=1, source_target_pairs={{0,8},{8,0},{16,24},{24,16},{1,9},{9,1},{17,25},{25,17},{2,10},{10... | collective-permute-start | bytes 196616 | tf_op jit(solution)/shard_map/ppermute | solution.py:401
  9.2 1.5 %collective-permute-start.7 = (bf16[8,32,128]{2,1,0:T(8,128)(2,1)S(1)}, bf16[8,32,128]{2,1,0:T(8,128)(2,1)S(1)}, u32[]{:S(2)}, u32[]{:S(2)}) collective-permute-start(bf16[8,32,128]{2,1,0:T(8,128)(2,1)S(1)} %get-tuple-element.39), channel_id=1, source_target_pairs={{0,24},{8,16},{16,8},{24,0},{1,25},{9,17},{17,9},{25,1},{2,26},{10... | collective-permute-start | bytes 196616 | tf_op jit(solution)/shard_map/ppermute | solution.py:401
  10.7 0.6 %collective-permute-done.refs_2_ = bf16[32,2,8,128]{3,2,1,0:T(8,128)(2,1)S(1)} collective-permute-done((bf16[32,2,8,128]{3,2,1,0:T(8,128)(2,1)}, bf16[32,2,8,128]{3,2,1,0:T(8,128)(2,1)S(1)}, u32[]{:S(2)}, u32[]{:S(2)}) %collective-permute-start) | collective-permute-done | bytes 131104 | tf_op jit(solution)/shard_map/ppermute | solution.py:401
  11.4 0.7 %collective-permute-start.1 = (bf16[32,2,8,128]{3,2,1,0:T(8,128)(2,1)S(1)}, bf16[32,2,8,128]{3,2,1,0:T(8,128)(2,1)S(1)}, u32[]{:S(2)}, u32[]{:S(2)}) collective-permute-start(bf16[32,2,8,128]{3,2,1,0:T(8,128)(2,1)S(1)} %collective-permute-done.refs_2_), channel_id=1, source_target_pairs={{0,2},{1,3},{2,0},{3,1},{4,6},{5,7},{6,4},{7,5},{8,10},{9,11},{10,... | collective-permute-start | bytes 393224 | tf_op jit(solution)/shard_map/ppermute | solution.py:401
  12.3 2.1 %collective-permute-done.7.go_second_ref = bf16[8,32,128]{2,1,0:T(8,128)(2,1)S(1)} collective-permute-done((bf16[8,32,128]{2,1,0:T(8,128)(2,1)S(1)}, bf16[8,32,128]{2,1,0:T(8,128)(2,1)S(1)}, u32[]{:S(2)}, u32[]{:S(2)}) %collective-permute-start.7) | collective-permute-done | bytes 65568 | tf_op jit(solution)/shard_map/ppermute | solution.py:401
  14.9 1.7 %collective-permute-done.1.refs_3_ = bf16[32,2,8,128]{3,2,1,0:T(8,128)(2,1)S(1)} collective-permute-done((bf16[32,2,8,128]{3,2,1,0:T(8,128)(2,1)S(1)}, bf16[32,2,8,128]{3,2,1,0:T(8,128)(2,1)S(1)}, u32[]{:S(2)}, u32[]{:S(2)}) %collective-permute-start.1) | collective-permute-done | bytes 131104 | tf_op jit(solution)/shard_map/ppermute | solution.py:401
  16.7 0.7 %assemble.1.refs_1_ = bf16[256,2048]{1,0:T(8,128)(2,1)S(1)} custom-call(s32[1]{0:T(128)} %bitcast.me_ref, bf16[32,2,8,128]{3,2,1,0:T(8,128)(2,1)S(1)} %get-tuple-element.37.refs_0_, bf16[32,2,8,128]{3,2,1,0:T(8,128)(2,1)S(1)} %collective-permute-done.3.refs_1_, bf16[32,2,8,128]{3,2,1,0:T(8,128)(2,1)S(1)} %collective-permute-done.refs_2_, ...), custom_call_target="tpu_custom_call" | custom-call | flops 4000000000 | bytes 1966084 | tf_op jit(solution)/shard_map/assemble/pallas_call | solution.py:110
  18.0 1.3 %forward.1 = (f32[16,32,128]{2,1,0:T(8,128)S(1)}, bf16[16,32,128]{2,1,0:T(8,128)(2,1)S(1)}, bf16[16,32,128]{2,1,0:T(8,128)(2,1)S(1)}, bf16[256,2048]{1,0:T(8,128)(2,1)S(1)}) custom-call(s32[1]{0:T(128)} %bitcast.me_ref, s32[1]{0:T(128)} %bitcast.1.slab_ref, bf16[864,256]{1,0:T(8,128)(2,1)S(1)} %get-tuple-element.35.w_ref, ...), custom_call_target="tpu_custom_call", output_to_operand_aliasing={{3}: (4, {})} | custom-call | flops 900000000 | bytes 3194888 | tf_op jit(solution)/shard_map/forward/pallas_call | solution.py:110
  19.3 1.6 %collective-permute-start.9 = (bf16[16,32,128]{2,1,0:T(8,128)(2,1)S(1)}, bf16[16,32,128]{2,1,0:T(8,128)(2,1)S(1)}, u32[]{:S(2)}, u32[]{:S(2)}) collective-permute-start(bf16[16,32,128]{2,1,0:T(8,128)(2,1)S(1)} %get-tuple-element.42.first_ref), channel_id=1, source_target_pairs={{0,8},{8,0},{16,24},{24,16},{1,9},{9,1},{17,25},{25,17},{2,10},{10... | collective-permute-start | bytes 393224 | tf_op jit(solution)/shard_map/ppermute | solution.py:401
  20.8 1.2 %collective-permute-start.10 = (bf16[16,32,128]{2,1,0:T(8,128)(2,1)S(1)}, bf16[16,32,128]{2,1,0:T(8,128)(2,1)S(1)}, u32[]{:S(2)}, u32[]{:S(2)}) collective-permute-start(bf16[16,32,128]{2,1,0:T(8,128)(2,1)S(1)} %get-tuple-element.43.second_ref), channel_id=1, source_target_pairs={{0,24},{8,16},{16,8},{24,0},{1,25},{9,17},{17,9},{25,1},{2,26},{10... | collective-permute-start | bytes 393224 | tf_op jit(solution)/shard_map/ppermute | solution.py:401
  22.1 3.6 %collective-permute-done.9.first_in_ref = bf16[16,32,128]{2,1,0:T(8,128)(2,1)S(1)} collective-permute-done((bf16[16,32,128]{2,1,0:T(8,128)(2,1)S(1)}, bf16[16,32,128]{2,1,0:T(8,128)(2,1)S(1)}, u32[]{:S(2)}, u32[]{:S(2)}) %collective-permute-start.9) | collective-permute-done | bytes 131104 | tf_op jit(solution)/shard_map/ppermute | solution.py:401
  25.7 2.7 %collective-permute-done.10.second_in_ref = bf16[16,32,128]{2,1,0:T(8,128)(2,1)S(1)} collective-permute-done((bf16[16,32,128]{2,1,0:T(8,128)(2,1)S(1)}, bf16[16,32,128]{2,1,0:T(8,128)(2,1)S(1)}, u32[]{:S(2)}, u32[]{:S(2)}) %collective-permute-start.10) | collective-permute-done | bytes 131104 | tf_op jit(solution)/shard_map/ppermute | solution.py:401
  28.4 1.8 %gradient.1 = (bf16[32,2,8,128]{3,2,1,0:T(8,128)(2,1)}, f32[32,128]{1,0:T(8,128)S(1)}, bf16[864,2048]{1,0:T(8,128)(2,1)S(1)}, bf16[4,16,32,128]{3,2,1,0:T(8,128)(2,1)S(1)}, bf16[4,16,32,128]{3,2,1,0:T(8,128)(2,1)S(1)}) custom-call(s32[1]{0:T(128)} %bitcast.me_ref, s32[1]{0:T(128)} %bitcast.1.slab_ref, f32[16,32,128]{2,1,0:T(8,128)S(1)} %get-tuple-element.41.own_ref, ...), custom_call_target="tpu_custom_call" | custom-call | flops 905969664 | bytes 6242312 | tf_op jit(solution)/shard_map/gradient/pallas_call | solution.py:110
  30.2 1.1 %filter_grad.1 = (bf16[448,256]{1,0:T(8,128)(2,1)S(1)}, bf16[448,256]{1,0:T(8,128)(2,1)S(1)}) custom-call(bf16[864,2048]{1,0:T(8,128)(2,1)S(1)} %get-tuple-element.50.s_ref, bf16[256,2048]{1,0:T(8,128)(2,1)S(1)} %get-tuple-element.51.x_ref, f32[32,128]{1,0:T(8,128)S(1)} %get-tuple-element.52.total_ref), custom_call_target="tpu_custom_call" | custom-call | flops 905969664 | bytes 5062656 | tf_op jit(solution)/shard_map/filter_grad/pallas_call | solution.py:110
  31.4 1.6 %collective-permute-start.11 = (bf16[448,256]{1,0:T(8,128)(2,1)S(1)}, bf16[448,256]{1,0:T(8,128)(2,1)S(1)}, u32[]{:S(2)}, u32[]{:S(2)}) collective-permute-start(bf16[448,256]{1,0:T(8,128)(2,1)S(1)} %get-tuple-element.53.a_ref), channel_id=1, source_target_pairs={{0,8},{1,17},{2,10},{3,19},{4,12},{5,21},{6,14},{7,23},{8,0},{9,25... | collective-permute-start | bytes 688136 | tf_op jit(solution)/shard_map/ppermute | solution.py:411
  33.6 2.7 %collective-permute-start.16 = (bf16[16,32,128]{2,1,0:T(8,128)(2,1)S(1)}, bf16[16,32,128]{2,1,0:T(8,128)(2,1)S(1)}, u32[]{:S(2)}, u32[]{:S(2)}) collective-permute-start(bf16[16,32,128]{2,1,0:T(8,128)(2,1)S(1)} %get-tuple-element.58), channel_id=1, source_target_pairs={{0,4},{1,5},{2,6},{3,7},{4,0},{5,1},{6,2},{7,3},{8,12},{9,13},{10,... | collective-permute-start | bytes 393224 | tf_op jit(solution)/shard_map/ppermute | solution.py:401
  36.3 1.3 %collective-permute-start.17 = (bf16[16,32,128]{2,1,0:T(8,128)(2,1)S(1)}, bf16[16,32,128]{2,1,0:T(8,128)(2,1)S(1)}, u32[]{:S(2)}, u32[]{:S(2)}) collective-permute-start(bf16[16,32,128]{2,1,0:T(8,128)(2,1)S(1)} %get-tuple-element.59), channel_id=1, source_target_pairs={{0,6},{1,7},{2,4},{3,5},{4,2},{5,3},{6,0},{7,1},{8,14},{9,15},{10,... | collective-permute-start | bytes 393224 | tf_op jit(solution)/shard_map/ppermute | solution.py:401
  38.7 1.2 %collective-permute-done.14.b_ref = bf16[448,256]{1,0:T(8,128)(2,1)S(1)} collective-permute-done((bf16[448,256]{1,0:T(8,128)(2,1)S(1)}, bf16[448,256]{1,0:T(8,128)(2,1)S(1)}, u32[]{:S(2)}, u32[]{:S(2)}) %collective-permute-start.14) | collective-permute-done | bytes 229408 | tf_op jit(solution)/shard_map/ppermute | solution.py:411
  40.0 0.8 %collective-permute-start.15 = (bf16[448,256]{1,0:T(8,128)(2,1)S(1)}, bf16[448,256]{1,0:T(8,128)(2,1)S(1)}, u32[]{:S(2)}, u32[]{:S(2)}) collective-permute-start(bf16[448,256]{1,0:T(8,128)(2,1)S(1)} %pair_sum.3.c_ref), channel_id=1, source_target_pairs={{0,16},{1,9},{2,18},{3,11},{4,20},{5,13},{6,22},{7,15},{8,24},{9,1... | collective-permute-start | bytes 688136 | tf_op jit(solution)/shard_map/ppermute | solution.py:411
  40.8 5.8 %collective-permute-done.16.b_ref = bf16[16,32,128]{2,1,0:T(8,128)(2,1)S(1)} collective-permute-done((bf16[16,32,128]{2,1,0:T(8,128)(2,1)S(1)}, bf16[16,32,128]{2,1,0:T(8,128)(2,1)S(1)}, u32[]{:S(2)}, u32[]{:S(2)}) %collective-permute-start.16) | collective-permute-done | bytes 131104 | tf_op jit(solution)/shard_map/ppermute | solution.py:401
  47.0 1.6 %last.1 = (f32[27,32,256]{2,1,0:T(8,128)}, f32[1,32]{1,0:T(1,128)}, bf16[32,2,8,128]{3,2,1,0:T(8,128)(2,1)}) custom-call(bf16[448,256]{1,0:T(8,128)(2,1)S(1)} %pair_sum.2.a_ref, bf16[448,256]{1,0:T(8,128)(2,1)S(1)} %collective-permute-done.13.b_ref, bf16[448,256]{1,0:T(8,128)(2,1)S(1)} %pair_sum.3.c_ref, bf16[448,256]{1,0:T(8,128)(2,1)S(1)} %collective-permute-done.15.d_ref, ...), custom_call_target="tpu_custom_call" | custom-call | bytes 2195584 | tf_op jit(solution)/shard_map/last/pallas_call | solution.py:110
  (24 shorter events, 3.7 us)
Async XLA Ops:
  0.6 10.7 %collective-permute-start = (bf16[32,2,8,128]{3,2,1,0:T(8,128)(2,1)}, bf16[32,2,8,128]{3,2,1,0:T(8,128)(2,1)S(1)}, u32[]{:S(2)}, u32[]{:S(2)}) collective-permute-start(bf16[32,2,8,128]{3,2,1,0:T(8,128)(2,1)} %x_hbm.1), channel_id=1, source_target_pairs={{0,4},{1,5},{2,6},{3,7},{4,0},{5,1},{6,2},{7,3},{8,12},{9,13},{10,... | collective-permute-start | bytes 393224 | tf_op jit(solution)/shard_map/ppermute | solution.py:401
  4.7 9.7 %collective-permute-start.3 = (bf16[32,2,8,128]{3,2,1,0:T(8,128)(2,1)}, bf16[32,2,8,128]{3,2,1,0:T(8,128)(2,1)S(1)}, u32[]{:S(2)}, u32[]{:S(2)}) collective-permute-start(bf16[32,2,8,128]{3,2,1,0:T(8,128)(2,1)} %x_hbm.1), channel_id=1, source_target_pairs={{0,2},{1,3},{2,0},{3,1},{4,6},{5,7},{6,4},{7,5},{8,10},{9,11},{10,... | collective-permute-start | bytes 393224 | tf_op jit(solution)/shard_map/ppermute | solution.py:401
  7.7 4.6 %collective-permute-start.6 = (bf16[8,32,128]{2,1,0:T(8,128)(2,1)S(1)}, bf16[8,32,128]{2,1,0:T(8,128)(2,1)S(1)}, u32[]{:S(2)}, u32[]{:S(2)}) collective-permute-start(bf16[8,32,128]{2,1,0:T(8,128)(2,1)S(1)} %get-tuple-element.38), channel_id=1, source_target_pairs={{0,8},{8,0},{16,24},{24,16},{1,9},{9,1},{17,25},{25,17},{2,10},{10... | collective-permute-start | bytes 196616 | tf_op jit(solution)/shard_map/ppermute | solution.py:401
  9.2 5.2 %collective-permute-start.7 = (bf16[8,32,128]{2,1,0:T(8,128)(2,1)S(1)}, bf16[8,32,128]{2,1,0:T(8,128)(2,1)S(1)}, u32[]{:S(2)}, u32[]{:S(2)}) collective-permute-start(bf16[8,32,128]{2,1,0:T(8,128)(2,1)S(1)} %get-tuple-element.39), channel_id=1, source_target_pairs={{0,24},{8,16},{16,8},{24,0},{1,25},{9,17},{17,9},{25,1},{2,26},{10... | collective-permute-start | bytes 196616 | tf_op jit(solution)/shard_map/ppermute | solution.py:401
  10.7 5.9 %collective-permute-start.4 = (bf16[32,2,8,128]{3,2,1,0:T(8,128)(2,1)}, bf16[32,2,8,128]{3,2,1,0:T(8,128)(2,1)S(1)}, u32[]{:S(2)}, u32[]{:S(2)}) collective-permute-start(bf16[32,2,8,128]{3,2,1,0:T(8,128)(2,1)} %x_hbm.1), channel_id=1, source_target_pairs={{0,1},{1,0},{2,3},{3,2},{4,5},{5,4},{6,7},{7,6},{8,9},{9,8},{10,11... | collective-permute-start | bytes 393224 | tf_op jit(solution)/shard_map/ppermute | solution.py:401
  11.4 5.3 %collective-permute-start.1 = (bf16[32,2,8,128]{3,2,1,0:T(8,128)(2,1)S(1)}, bf16[32,2,8,128]{3,2,1,0:T(8,128)(2,1)S(1)}, u32[]{:S(2)}, u32[]{:S(2)}) collective-permute-start(bf16[32,2,8,128]{3,2,1,0:T(8,128)(2,1)S(1)} %collective-permute-done.refs_2_), channel_id=1, source_target_pairs={{0,2},{1,3},{2,0},{3,1},{4,6},{5,7},{6,4},{7,5},{8,10},{9,11},{10,... | collective-permute-start | bytes 393224 | tf_op jit(solution)/shard_map/ppermute | solution.py:401
  14.4 2.2 %collective-permute-start.5 = (bf16[32,2,8,128]{3,2,1,0:T(8,128)(2,1)S(1)}, bf16[32,2,8,128]{3,2,1,0:T(8,128)(2,1)S(1)}, u32[]{:S(2)}, u32[]{:S(2)}) collective-permute-start(bf16[32,2,8,128]{3,2,1,0:T(8,128)(2,1)S(1)} %collective-permute-done.3.refs_1_), channel_id=1, source_target_pairs={{0,1},{1,0},{2,3},{3,2},{4,5},{5,4},{6,7},{7,6},{8,9},{9,8},{10,11... | collective-permute-start | bytes 393224 | tf_op jit(solution)/shard_map/ppermute | solution.py:401
  14.4 2.3 %collective-permute-start.8 = (bf16[32,2,8,128]{3,2,1,0:T(8,128)(2,1)S(1)}, bf16[32,2,8,128]{3,2,1,0:T(8,128)(2,1)S(1)}, u32[]{:S(2)}, u32[]{:S(2)}) collective-permute-start(bf16[32,2,8,128]{3,2,1,0:T(8,128)(2,1)S(1)} %collective-permute-done.refs_2_), channel_id=1, source_target_pairs={{0,1},{1,0},{2,3},{3,2},{4,5},{5,4},{6,7},{7,6},{8,9},{9,8},{10,11... | collective-permute-start | bytes 393224 | tf_op jit(solution)/shard_map/ppermute | solution.py:401
  16.6 1.3 %collective-permute-start.2 = (bf16[32,2,8,128]{3,2,1,0:T(8,128)(2,1)S(1)}, bf16[32,2,8,128]{3,2,1,0:T(8,128)(2,1)S(1)}, u32[]{:S(2)}, u32[]{:S(2)}) collective-permute-start(bf16[32,2,8,128]{3,2,1,0:T(8,128)(2,1)S(1)} %collective-permute-done.1.refs_3_), channel_id=1, source_target_pairs={{0,1},{1,0},{2,3},{3,2},{4,5},{5,4},{6,7},{7,6},{8,9},{9,8},{10,11... | collective-permute-start | bytes 393224 | tf_op jit(solution)/shard_map/ppermute | solution.py:401
  19.3 6.4 %collective-permute-start.9 = (bf16[16,32,128]{2,1,0:T(8,128)(2,1)S(1)}, bf16[16,32,128]{2,1,0:T(8,128)(2,1)S(1)}, u32[]{:S(2)}, u32[]{:S(2)}) collective-permute-start(bf16[16,32,128]{2,1,0:T(8,128)(2,1)S(1)} %get-tuple-element.42.first_ref), channel_id=1, source_target_pairs={{0,8},{8,0},{16,24},{24,16},{1,9},{9,1},{17,25},{25,17},{2,10},{10... | collective-permute-start | bytes 393224 | tf_op jit(solution)/shard_map/ppermute | solution.py:401
  20.8 7.6 %collective-permute-start.10 = (bf16[16,32,128]{2,1,0:T(8,128)(2,1)S(1)}, bf16[16,32,128]{2,1,0:T(8,128)(2,1)S(1)}, u32[]{:S(2)}, u32[]{:S(2)}) collective-permute-start(bf16[16,32,128]{2,1,0:T(8,128)(2,1)S(1)} %get-tuple-element.43.second_ref), channel_id=1, source_target_pairs={{0,24},{8,16},{16,8},{24,0},{1,25},{9,17},{17,9},{25,1},{2,26},{10... | collective-permute-start | bytes 393224 | tf_op jit(solution)/shard_map/ppermute | solution.py:401
  30.2 3.3 %collective-permute-start.12 = (bf16[4,16,32,128]{3,2,1,0:T(8,128)(2,1)S(1)}, bf16[4,16,32,128]{3,2,1,0:T(8,128)(2,1)S(1)}, u32[]{:S(2)}, u32[]{:S(2)}) collective-permute-start(bf16[4,16,32,128]{3,2,1,0:T(8,128)(2,1)S(1)} %get-tuple-element.55), channel_id=1, source_target_pairs={{0,1},{1,0},{2,3},{3,2},{4,5},{5,4},{6,7},{7,6},{8,9},{9,8},{10,11... | collective-permute-start | bytes 1572872 | tf_op jit(solution)/shard_map/ppermute | solution.py:401
  31.4 6.7 %collective-permute-start.11 = (bf16[448,256]{1,0:T(8,128)(2,1)S(1)}, bf16[448,256]{1,0:T(8,128)(2,1)S(1)}, u32[]{:S(2)}, u32[]{:S(2)}) collective-permute-start(bf16[448,256]{1,0:T(8,128)(2,1)S(1)} %get-tuple-element.53.a_ref), channel_id=1, source_target_pairs={{0,8},{1,17},{2,10},{3,19},{4,12},{5,21},{6,14},{7,23},{8,0},{9,25... | collective-permute-start | bytes 688136 | tf_op jit(solution)/shard_map/ppermute | solution.py:411
  32.9 7.0 %collective-permute-start.14 = (bf16[448,256]{1,0:T(8,128)(2,1)S(1)}, bf16[448,256]{1,0:T(8,128)(2,1)S(1)}, u32[]{:S(2)}, u32[]{:S(2)}) collective-permute-start(bf16[448,256]{1,0:T(8,128)(2,1)S(1)} %get-tuple-element.57.a_ref), channel_id=1, source_target_pairs={{0,8},{1,17},{2,10},{3,19},{4,12},{5,21},{6,14},{7,23},{8,0},{9,25... | collective-permute-start | bytes 688136 | tf_op jit(solution)/shard_map/ppermute | solution.py:411
  33.6 13.0 %collective-permute-start.16 = (bf16[16,32,128]{2,1,0:T(8,128)(2,1)S(1)}, bf16[16,32,128]{2,1,0:T(8,128)(2,1)S(1)}, u32[]{:S(2)}, u32[]{:S(2)}) collective-permute-start(bf16[16,32,128]{2,1,0:T(8,128)(2,1)S(1)} %get-tuple-element.58), channel_id=1, source_target_pairs={{0,4},{1,5},{2,6},{3,7},{4,0},{5,1},{6,2},{7,3},{8,12},{9,13},{10,... | collective-permute-start | bytes 393224 | tf_op jit(solution)/shard_map/ppermute | solution.py:401
  36.3 10.3 %collective-permute-start.17 = (bf16[16,32,128]{2,1,0:T(8,128)(2,1)S(1)}, bf16[16,32,128]{2,1,0:T(8,128)(2,1)S(1)}, u32[]{:S(2)}, u32[]{:S(2)}) collective-permute-start(bf16[16,32,128]{2,1,0:T(8,128)(2,1)S(1)} %get-tuple-element.59), channel_id=1, source_target_pairs={{0,6},{1,7},{2,4},{3,5},{4,2},{5,3},{6,0},{7,1},{8,14},{9,15},{10,... | collective-permute-start | bytes 393224 | tf_op jit(solution)/shard_map/ppermute | solution.py:401
  37.6 9.4 %collective-permute-start.18 = (bf16[16,32,128]{2,1,0:T(8,128)(2,1)S(1)}, bf16[16,32,128]{2,1,0:T(8,128)(2,1)S(1)}, u32[]{:S(2)}, u32[]{:S(2)}) collective-permute-start(bf16[16,32,128]{2,1,0:T(8,128)(2,1)S(1)} %get-tuple-element.60), channel_id=1, source_target_pairs={{0,2},{1,3},{2,0},{3,1},{4,6},{5,7},{6,4},{7,5},{8,10},{9,11},{10,... | collective-permute-start | bytes 393224 | tf_op jit(solution)/shard_map/ppermute | solution.py:401
  38.1 8.9 %collective-permute-start.13 = (bf16[448,256]{1,0:T(8,128)(2,1)S(1)}, bf16[448,256]{1,0:T(8,128)(2,1)S(1)}, u32[]{:S(2)}, u32[]{:S(2)}) collective-permute-start(bf16[448,256]{1,0:T(8,128)(2,1)S(1)} %pair_sum.2.a_ref), channel_id=1, source_target_pairs={{0,16},{1,9},{2,18},{3,11},{4,20},{5,13},{6,22},{7,15},{8,24},{9,1... | collective-permute-start | bytes 688136 | tf_op jit(solution)/shard_map/ppermute | solution.py:411
  40.0 7.1 %collective-permute-start.15 = (bf16[448,256]{1,0:T(8,128)(2,1)S(1)}, bf16[448,256]{1,0:T(8,128)(2,1)S(1)}, u32[]{:S(2)}, u32[]{:S(2)}) collective-permute-start(bf16[448,256]{1,0:T(8,128)(2,1)S(1)} %pair_sum.3.c_ref), channel_id=1, source_target_pairs={{0,16},{1,9},{2,18},{3,11},{4,20},{5,13},{6,22},{7,15},{8,24},{9,1... | collective-permute-start | bytes 688136 | tf_op jit(solution)/shard_map/ppermute | solution.py:411

commit v15 on v13

--- a/solution.py
+++ b/solution.py
@@ -147,7 +147,10 @@
     go_low_ref,
     go_high_ref,
     flat_ref,
-    back_ref,
+    own_0_ref,
+    own_1_ref,
+    rim_0_ref,
+    rim_1_ref,
     bias_ref,
     go_in,
     w_in,
@@ -175,7 +178,11 @@
     copies[3].wait()
     flat = w_in[...].reshape(flat_ref.shape)
     flat_ref[...] = flat
-    back_ref[...] = jnp.transpose(flat)
+    third = flat.shape[0] // 3
+    own_0_ref[...] = jnp.transpose(flat[: 2 * third])
+    own_1_ref[...] = jnp.transpose(flat[third:])
+    rim_0_ref[...] = jnp.transpose(flat[2 * third :])
+    rim_1_ref[...] = jnp.transpose(flat[:third])
     o = bias_ref.shape[0]
     row = jnp.broadcast_to(bias_in[...].astype(jnp.float32), (o, o))
     same = lax.broadcasted_iota(jnp.int32, (o, o), 0) == lax.broadcasted_iota(jnp.int32, (o, o), 1)
@@ -202,7 +209,7 @@
 
 def forward_body(n, rows, o, places, me_ref, w_ref, *refs):
     blocks = refs[: len(places)]
-    own_ref, low_ref, high_ref, x_ref, acc, wide_ref = refs[len(places) + 1 :]
+    own_ref, low_ref, high_ref, first_ref, last_ref, x_ref, acc, wide_ref = refs[len(places) + 1 :]
     for b, block in zip(places, blocks):
         place_block(me_ref, b, block, x_ref, wide_ref)
     w = w_ref[...]
@@ -236,100 +243,151 @@
             else:
                 own_ref[(q - 1) * rows + y] = total
             if q == 1:
-                low_ref[rows + y] = total.astype(low_ref.dtype)
+                first_ref[y] = total.astype(first_ref.dtype)
             if q == n:
-                high_ref[rows + y] = total.astype(high_ref.dtype)
-
-
-def gradient_body(
-    n,
+                last_ref[y] = total.astype(last_ref.dtype)
+
+
+def ordered(me_ref, o, in_refs, out_refs):
+    for in_ref, out_ref in zip(in_refs, out_refs):
+        for b in range(8):
+            place = pl.ds(pl.multiple_of(owner(me_ref, b) * o, o), o)
+            out_ref[b * o : (b + 1) * o] = in_ref[place]
+
+
+def three_shifts(wide, dtype):
+    return [
+        pltpu.roll(wide, LANES - 1, 1).astype(dtype),
+        wide.astype(dtype),
+        pltpu.roll(wide, 1, 1).astype(dtype),
+    ]
+
+
+def own_gradient_body(
     rows,
     o,
     scale,
     me_ref,
     own_ref,
+    below_ref,
+    above_ref,
+    bias_ref,
+    go_ref,
+    w_0_ref,
+    w_1_ref,
+    act_ref,
+    total_ref,
+    s_ref,
+    partial_ref,
+    w_0,
+    w_1,
+    wide_ref,
+):
+    f32, bf16 = jnp.float32, jnp.bfloat16
+    ordered(me_ref, o, (w_0_ref, w_1_ref), (w_0, w_1))
+    total = jnp.zeros((o, LANES), f32)
+    for q in range(2):
+        for y in range(rows):
+            beside = below_ref if q == 0 else above_ref
+            pre = own_ref[q * rows + y] + beside[y].astype(f32) + bias_ref[...]
+            s = jax.nn.sigmoid(pre)
+            slope = s * (1.0 + pre * (1.0 - s))
+            wide = (go_ref[q * rows + y].astype(f32) * slope).astype(bf16).astype(f32)
+            wide_ref[pl.ds(q * rows + y, o, stride=2 * rows), :] = pre * s
+            total = total + wide
+            shifts = three_shifts(wide, bf16)
+            for k, i, j, l in tap_list():
+                p = q - 1 + i
+                if 0 <= p < 2:
+                    at = (p * rows + (y + j - 1) % rows) * LANES
+                    row = (k - 9 * p) * o
+                    s_ref[row : row + o, at : at + LANES] = shifts[l]
+    for t in range(0, 2 * rows, 2):
+        at = slice(t * LANES, (t + 2) * LANES)
+        w = w_0 if t < rows else w_1
+        partial_ref[:, at] = jnp.dot(w[...], s_ref[:, at], preferred_element_type=f32)
+    act_ref[...] = wide_ref[...].reshape(act_ref.shape).astype(bf16)
+    total_ref[...] = jnp.broadcast_to(
+        jnp.sum(total, axis=1, keepdims=True) * scale, total_ref.shape
+    )
+
+
+def rim_gradient_body(
+    rows,
+    o,
+    me_ref,
     low_ref,
     high_ref,
     below_ref,
     above_ref,
     bias_ref,
-    go_ref,
     go_below_ref,
     go_above_ref,
-    back_ref,
-    act_ref,
-    total_ref,
+    partial_ref,
+    w_0_ref,
+    w_1_ref,
+    _,
     s_ref,
     other_ref,
     mine_ref,
-    w_ref,
-    wide_ref,
+    w_0,
+    w_1,
 ):
     f32, bf16 = jnp.float32, jnp.bfloat16
-    for b in range(8):
-        place = pl.ds(pl.multiple_of(owner(me_ref, b) * o, o), o)
-        w_ref[b * o : (b + 1) * o] = back_ref[place]
-    total = jnp.zeros((o, LANES), f32)
-    for q in range(n + 2):
+    ordered(me_ref, o, (w_0_ref, w_1_ref), (w_0, w_1))
+    sides = ((below_ref, low_ref, go_below_ref), (above_ref, high_ref, go_above_ref))
+    for p, (theirs, ours, go) in enumerate(sides):
         for y in range(rows):
-            if q == 0:
-                pre = below_ref[rows + y].astype(f32) + low_ref[y].astype(f32)
-                go = go_below_ref[y]
-            elif q == n + 1:
-                pre = above_ref[rows + y].astype(f32) + high_ref[y].astype(f32)
-                go = go_above_ref[y]
-            else:
-                pre = own_ref[(q - 1) * rows + y]
-                go = go_ref[(q - 1) * rows + y]
-                if q == 1:
-                    pre = pre + below_ref[y].astype(f32)
-                if q == n:
-                    pre = pre + above_ref[y].astype(f32)
-            pre = pre + bias_ref[...]
+            pre = theirs[y].astype(f32) + ours[y].astype(f32) + bias_ref[...]
             s = jax.nn.sigmoid(pre)
             slope = s * (1.0 + pre * (1.0 - s))
-            value = (go.astype(f32) * slope).astype(bf16)
-            wide = value.astype(f32)
-            if 1 <= q <= n:
-                wide_ref[pl.ds((q - 1) * rows + y, o, stride=n * rows), :] = pre * s
-                total = total + wide
-            shifts = [
-                pltpu.roll(wide, LANES - 1, 1).astype(bf16),
-                value,
-                pltpu.roll(wide, 1, 1).astype(bf16),
-            ]
-            for k, i, j, l in tap_list():
-                p = q - 2 + i
-                if 0 <= p < n:
+            wide = (go[y].astype(f32) * slope).astype(bf16).astype(f32)
+            shifts = three_shifts(wide, bf16)
+            for j in range(3):
+                for l in range(3):
                     at = (p * rows + (y + j - 1) % rows) * LANES
-                    s_ref[k * o : (k + 1) * o, at : at + LANES] = shifts[l]
-    act_ref[...] = wide_ref[...].reshape(act_ref.shape).astype(bf16)
-    total_ref[...] = jnp.broadcast_to(
-        jnp.sum(total, axis=1, keepdims=True) * scale, total_ref.shape
-    )
-    input_grad(n * rows, o, w_ref[...], s_ref, [(ref, r) for ref in (mine_ref, other_ref) for r in range(4)])
-
-
-def input_grad(cells, o, w, s_ref, outs):
-    for t in range(0, cells, 2):
-        part = jnp.dot(
-            w, s_ref[:, t * LANES : (t + 2) * LANES], preferred_element_type=jnp.float32
-        ).astype(outs[0][0].dtype)
+                    row = (3 * j + l) * o
+                    s_ref[row : row + o, at : at + LANES] = shifts[l]
+    for t in range(0, 2 * rows, 2):
+        at = slice(t * LANES, (t + 2) * LANES)
+        w = w_0 if t < rows else w_1
+        part = jnp.dot(w[...], s_ref[:, at], preferred_element_type=f32)
+        part = (part + partial_ref[:, at]).astype(bf16)
         for h in range(2):
-            for r, (out_ref, at) in enumerate(outs):
-                cut = part[r * o : (r + 1) * o, h * LANES : (h + 1) * LANES]
-                out_ref[at, t + h] = cut
-
-
-def filter_grad_body(scale, taps, o, s_ref, x_ref, total_ref, first_ref, second_ref):
-    full = lax.dot_general(
-        s_ref[...], x_ref[...], (((1,), (1,)), ((), ())), preferred_element_type=jnp.float32
-    )
-    full = (full * scale).astype(first_ref.dtype)
-    first_ref[...] = full[: taps * o]
-    second_ref[: (27 - taps) * o] = full[taps * o :]
+            for b in range(8):
+                cut = part[b * o : (b + 1) * o, h * LANES : (h + 1) * LANES]
+                (mine_ref if b < 4 else other_ref)[b % 4, t + h] = cut
+
+
+def filter_product(s_ref, x_ref, plane):
+    half = x_ref.shape[1] // 2
+    at = slice(plane * half, (plane + 1) * half)
+    return lax.dot_general(
+        s_ref[:, at], x_ref[:, at], (((1,), (1,)), ((), ())), preferred_element_type=jnp.float32
+    )
+
+
+def own_filter_body(s_ref, x_ref, out_ref, token_ref):
+    token_ref[...] = jnp.zeros_like(token_ref)
+    third = out_ref.shape[0] // 3
+    low, high = (filter_product(s_ref, x_ref, p) for p in range(2))
+    out_ref[:third] = low[:third]
+    out_ref[third : 2 * third] = low[third:] + high[:third]
+    out_ref[2 * third :] = high[third:]
+
+
+def rim_filter_body(scale, taps, o, s_ref, x_ref, own_ref, total_ref, first_ref, second_ref):
+    third = own_ref.shape[0] // 3
+    cut = taps * o
+    high = own_ref[:third] + filter_product(s_ref, x_ref, 1)
+    low = own_ref[2 * third :] + filter_product(s_ref, x_ref, 0)
+    dtype = first_ref.dtype
+    first_ref[:third] = (high * scale).astype(dtype)
+    first_ref[third:] = (own_ref[third:cut] * scale).astype(dtype)
+    second_ref[: 2 * third - cut] = (own_ref[cut : 2 * third] * scale).astype(dtype)
+    second_ref[2 * third - cut : 27 * o - cut] = (low * scale).astype(dtype)
     row = jnp.concatenate([total_ref[...]] * (second_ref.shape[1] // LANES), axis=1)
-    second_ref[(27 - taps) * o :] = row.astype(second_ref.dtype)
+    second_ref[27 * o - cut :] = row.astype(dtype)
 
 
 def pair_body(a_ref, b_ref, _, out_ref):
@@ -405,7 +463,7 @@
     x_b = swap(x_in, "chan", 4)
     x_a = swap(x_in, "chan", 2)
     x_side = swap(x_in, "chan", 1)
-    x_own, go, go_low, go_high, w_flat, w_back, bias = call(
+    x_own, go, go_low, go_high, w_flat, *w_back, bias = call(
         functools.partial(prepare_body, n, rows),
         [
             shape_of((o, n, rows, depth), bf16),
@@ -413,7 +471,7 @@
             shape_of((rows, o, depth), bf16),
             shape_of((rows, o, depth), bf16),
             shape_of((27 * o, c_all), bf16),
-            shape_of((c_all, 27 * o), bf16),
+            *[shape_of((c_all, taps * o), bf16) for taps in (18, 18, 9, 9)],
             shape_of((o, LANES), f32),
         ],
         [in_hbm(a) for a in (x_in, grad_out, jnp.transpose(weight, (1, 0, 2)), bias_vec[None, :])],
@@ -445,12 +503,11 @@
         name="assemble",
     )
     x_ab_side = swap(x_ab, "chan", 1)
-    own, low, high, x_all = call(
+    own, low, high, first, last, x_all = call(
         functools.partial(forward_body, n, rows, o, late),
         [
             shape_of((cells, o, depth), f32),
-            shape_of((2 * rows, o, depth), bf16),
-            shape_of((2 * rows, o, depth), bf16),
+            *[shape_of((rows, o, depth), bf16)] * 4,
             shape_of((c_all, cells * depth), bf16),
         ],
         [me, w_flat, x_ab_side, x_all],
@@ -458,33 +515,54 @@
         [pltpu.VMEM((3, n + 2, rows, o, depth), f32), *block_wide],
         flops=FORWARD_FLOPS,
         name="forward",
-        aliases={3: 3},
+        aliases={3: 5},
     )
     above = rotate(low, "slab", -1)
     below = rotate(high, "slab", 1)
-    act, total, stacked, other, mine = call(
-        functools.partial(gradient_body, n, rows, o, scale),
+    above_own = rotate(first, "slab", -1)
+    below_own = rotate(last, "slab", 1)
+    act, total, own_shifts, partial = call(
+        functools.partial(own_gradient_body, rows, o, scale),
         [
             shape_of((o, n, rows, depth), bf16),
             shape_of((o, LANES), f32),
-            shape_of((27 * o, cells * depth), bf16),
+            shape_of((18 * o, cells * depth), bf16),
+            shape_of((c_all, cells * depth), f32),
+        ],
+        [me, own, below, above, bias, go, *w_back[:2]],
+        [SMEM] + [VMEM] * 7,
+        [*[pltpu.VMEM((c_all, 18 * o), bf16)] * 2, *block_wide],
+        flops=flops * 2 // 3,
+        name="own_gradient",
+    )
+    filters, token = call(
+        own_filter_body,
+        [shape_of((27 * o, c_all), f32), shape_of((8, LANES), f32)],
+        [own_shifts, x_all],
+        flops=flops * 2 // 3,
+        name="own_filter",
+    )
+    rim_shifts, other, mine = call(
+        functools.partial(rim_gradient_body, rows, o),
+        [
+            shape_of((9 * o, cells * depth), bf16),
             shape_of((4, cells, o, depth), bf16),
             shape_of((4, cells, o, depth), bf16),
         ],
-        [me, own, low, high, below, above, bias, go, go_below, go_above, w_back],
-        [SMEM] + [VMEM] * 10,
-        [pltpu.VMEM((c_all, 27 * o), bf16), *block_wide],
-        flops=flops,
-        name="gradient",
+        [me, low, high, below_own, above_own, bias, go_below, go_above, partial, *w_back[2:], token],
+        [SMEM] + [VMEM] * 10 + [ANY],
+        [pltpu.VMEM((c_all, 9 * o), bf16)] * 2,
+        flops=flops // 3,
+        name="rim_gradient",
     )
     other = swap(other, "chan", 1)
     taps = 14
     first, second = call(
-        functools.partial(filter_grad_body, scale, taps, o),
+        functools.partial(rim_filter_body, scale, taps, o),
         [shape_of((taps * o, c_all), bf16), shape_of(((28 - taps) * o, c_all), bf16)],
-        [stacked, x_all, total],
-        flops=flops,
-        name="filter_grad",
+        [rim_shifts, x_all, filters, total],
+        flops=flops // 3,
+        name="rim_filter",
     )
     first_far = cross(first, 0)
     second_far = cross(second, 0)
@@ -544,7 +622,7 @@
             and x_in.shape[3] == LANES
             and lax.axis_size("slab") == 4
             and lax.axis_size("chan") == 8
-            and x_in.shape[1] >= 2
+            and x_in.shape[1] == 2
         )
         return (on_device if tiled else plain)(x_in, weight, bias_vec, grad_out)
 

time: 48.4 us -> 47.5 us (0.981); the launches traced: 48.1 us -> 46.7 us
  waiting for transfers between devices: 19.7 us -> 12.8 us
  starting transfers between devices: 20 us -> 24.4 us
  Pallas kernels: 7.61 us -> 8.71 us
    ppermute x4 -> x6, waiting for transfers between devices: 9.92 us -> 4.38 us  [rotate(): lax.ppermute(value, axis, [(i, (i + step) % count) for i in range(count)])]
    ppermute x4 -> x6, starting transfers between devices: 5.25 us -> 8.4 us  [rotate(): lax.ppermute(value, axis, [(i, (i + step) % count) for i in range(count)])]
    ppermute x4, starting transfers between devices: 3.32 us -> 4.81 us  [cross(): return lax.ppermute(value, ('slab', 'chan'), pairs)]
    pallas_call x10 -> x12, Pallas kernels: 7.61 us -> 8.71 us  [call(): pl.pallas_call(body, out_shape=out_shape, in_specs=specs or [VMEM] * len(...]
    ppermute x11, waiting for transfers between devices: 8.57 us -> 7.56 us  [swap(): lax.ppermute(value, axis, [(i, i ^ bit) for i in range(lax.axis_size(axis...]
  transfers between devices with their start and end apart: 19 -> 21, of which waited for: 12 -> 10; matrix products, arithmetic and copies ran while one was open for 0% -> 0% of each run, Pallas kernels for 7% -> 12%
where the time goes in v15:
time: 47.5 us; the launch traced here: 46.7 us
  starting transfers between devices  24.4 us (51%)
  waiting for transfers between devices  12.8 us (27%)
  Pallas kernels  8.71 us (18%)
  between operations  0.75 us (2%)
    ppermute x11, starting transfers between devices, swap(): lax.ppermute(value, axis, [(i, i ^ bit) for i in range(lax.axis_size(axis...  11.2 us
    pallas_call x12, Pallas kernels, call(): pl.pallas_call(body, out_shape=out_shape, in_specs=specs or [VMEM] * len(...  8.71 us
    ppermute x6, starting transfers between devices, rotate(): lax.ppermute(value, axis, [(i, (i + step) % count) for i in range(count)])  8.4 us
    ppermute x11, waiting for transfers between devices, swap(): lax.ppermute(value, axis, [(i, i ^ bit) for i in range(lax.axis_size(axis...  7.56 us
    ppermute x4, starting transfers between devices, cross(): return lax.ppermute(value, ('slab', 'chan'), pairs)  4.81 us
    ppermute x6, waiting for transfers between devices, rotate(): lax.ppermute(value, axis, [(i, (i + step) % count) for i in range(count)])  4.38 us
  transfers between devices with their start and end apart: 21, of which 10 were waited for; matrix products, arithmetic and copies ran while one was open for 0% of the time, Pallas kernels for 12%

profile of v15, /device:TPU:0, one launch (start us, length us, event | category | flops | bytes accessed | tf_op | source)
XLA Modules:
  0.0 46.7 jit_solution(4349637009042433021)
XLA Ops:
  0.6 4.1 %collective-permute-start = (bf16[32,2,8,128]{3,2,1,0:T(8,128)(2,1)}, bf16[32,2,8,128]{3,2,1,0:T(8,128)(2,1)S(1)}, u32[]{:S(2)}, u32[]{:S(2)}) collective-permute-start(bf16[32,2,8,128]{3,2,1,0:T(8,128)(2,1)} %x_hbm.1), channel_id=1, source_target_pairs={{0,4},{1,5},{2,6},{3,7},{4,0},{5,1},{6,2},{7,3},{8,12},{9,13},{10,... | collective-permute-start | bytes 393224 | tf_op jit(solution)/shard_map/ppermute | solution.py:439
  4.7 1.6 %collective-permute-start.3 = (bf16[32,2,8,128]{3,2,1,0:T(8,128)(2,1)}, bf16[32,2,8,128]{3,2,1,0:T(8,128)(2,1)S(1)}, u32[]{:S(2)}, u32[]{:S(2)}) collective-permute-start(bf16[32,2,8,128]{3,2,1,0:T(8,128)(2,1)} %x_hbm.1), channel_id=1, source_target_pairs={{0,2},{1,3},{2,0},{3,1},{4,6},{5,7},{6,4},{7,5},{8,10},{9,11},{10,... | collective-permute-start | bytes 393224 | tf_op jit(solution)/shard_map/ppermute | solution.py:439
  6.3 1.5 %prepare.1 = (bf16[32,2,8,128]{3,2,1,0:T(8,128)(2,1)S(1)}, bf16[16,32,128]{2,1,0:T(8,128)(2,1)S(1)}, bf16[8,32,128]{2,1,0:T(8,128)(2,1)S(1)}, bf16[8,32,128]{2,1...) custom-call(bf16[32,2,8,128]{3,2,1,0:T(8,128)(2,1)} %x_hbm.1, ...), custom_call_target="tpu_custom_call" | custom-call | bytes 2441280 | tf_op jit(solution)/shard_map/prepare/pallas_call | solution.py:110
  7.8 2.5 %collective-permute-start.6 = (bf16[8,32,128]{2,1,0:T(8,128)(2,1)S(1)}, bf16[8,32,128]{2,1,0:T(8,128)(2,1)S(1)}, u32[]{:S(2)}, u32[]{:S(2)}) collective-permute-start(bf16[8,32,128]{2,1,0:T(8,128)(2,1)S(1)} %get-tuple-element.47), channel_id=1, source_target_pairs={{0,24},{8,0},{16,8},{24,16},{1,25},{9,1},{17,9},{25,17},{2,26},{10... | collective-permute-start | bytes 196616 | tf_op jit(solution)/shard_map/ppermute | solution.py:435
  10.3 1.1 %collective-permute-done.refs_2_ = bf16[32,2,8,128]{3,2,1,0:T(8,128)(2,1)S(1)} collective-permute-done((bf16[32,2,8,128]{3,2,1,0:T(8,128)(2,1)}, bf16[32,2,8,128]{3,2,1,0:T(8,128)(2,1)S(1)}, u32[]{:S(2)}, u32[]{:S(2)}) %collective-permute-start) | collective-permute-done | bytes 131104 | tf_op jit(solution)/shard_map/ppermute | solution.py:439
  12.5 3.0 %collective-permute-done.7.go_below_ref = bf16[8,32,128]{2,1,0:T(8,128)(2,1)S(1)} collective-permute-done((bf16[8,32,128]{2,1,0:T(8,128)(2,1)S(1)}, bf16[8,32,128]{2,1,0:T(8,128)(2,1)S(1)}, u32[]{:S(2)}, u32[]{:S(2)}) %collective-permute-start.7) | collective-permute-done | bytes 65568 | tf_op jit(solution)/shard_map/ppermute | solution.py:435
  17.0 0.7 %assemble.1.refs_1_ = bf16[256,2048]{1,0:T(8,128)(2,1)S(1)} custom-call(s32[1]{0:T(128)} %bitcast.me_ref, bf16[32,2,8,128]{3,2,1,0:T(8,128)(2,1)S(1)} %get-tuple-element.46.refs_0_, bf16[32,2,8,128]{3,2,1,0:T(8,128)(2,1)S(1)} %collective-permute-done.3.refs_1_, bf16[32,2,8,128]{3,2,1,0:T(8,128)(2,1)S(1)} %collective-permute-done.refs_2_, ...), custom_call_target="tpu_custom_call" | custom-call | flops 4000000000 | bytes 1966084 | tf_op jit(solution)/shard_map/assemble/pallas_call | solution.py:110
  17.8 1.3 %forward.1 = (f32[16,32,128]{2,1,0:T(8,128)S(1)}, bf16[8,32,128]{2,1,0:T(8,128)(2,1)S(1)}, bf16[8,32,128]{2,1,0:T(8,128)(2,1)S(1)}, bf16[8,32,128]{2,1,0:T(8,128...) custom-call(s32[1]{0:T(128)} %bitcast.me_ref, ...), custom_call_target="tpu_custom_call", output_to_operand_aliasing={{5}: (3, {})} | custom-call | flops 900000000 | bytes 3194884 | tf_op jit(solution)/shard_map/forward/pallas_call | solution.py:110
  19.0 1.8 %collective-permute-start.9 = (bf16[8,32,128]{2,1,0:T(8,128)(2,1)S(1)}, bf16[8,32,128]{2,1,0:T(8,128)(2,1)S(1)}, u32[]{:S(2)}, u32[]{:S(2)}) collective-permute-start(bf16[8,32,128]{2,1,0:T(8,128)(2,1)S(1)} %get-tuple-element.51.high_ref), channel_id=1, source_target_pairs={{0,8},{8,16},{16,24},{24,0},{1,9},{9,17},{17,25},{25,1},{2,10},{10... | collective-permute-start | bytes 196616 | tf_op jit(solution)/shard_map/ppermute | solution.py:435
  20.9 1.1 %collective-permute-start.10 = (bf16[8,32,128]{2,1,0:T(8,128)(2,1)S(1)}, bf16[8,32,128]{2,1,0:T(8,128)(2,1)S(1)}, u32[]{:S(2)}, u32[]{:S(2)}) collective-permute-start(bf16[8,32,128]{2,1,0:T(8,128)(2,1)S(1)} %get-tuple-element.52.low_ref), channel_id=1, source_target_pairs={{0,24},{8,0},{16,8},{24,16},{1,25},{9,1},{17,9},{25,17},{2,26},{10... | collective-permute-start | bytes 196616 | tf_op jit(solution)/shard_map/ppermute | solution.py:435
  22.0 0.9 %collective-permute-start.11 = (bf16[8,32,128]{2,1,0:T(8,128)(2,1)S(1)}, bf16[8,32,128]{2,1,0:T(8,128)(2,1)S(1)}, u32[]{:S(2)}, u32[]{:S(2)}) collective-permute-start(bf16[8,32,128]{2,1,0:T(8,128)(2,1)S(1)} %get-tuple-element.58), channel_id=1, source_target_pairs={{0,8},{8,16},{16,24},{24,0},{1,9},{9,17},{17,25},{25,1},{2,10},{10... | collective-permute-start | bytes 196616 | tf_op jit(solution)/shard_map/ppermute | solution.py:435
  22.9 2.0 %collective-permute-start.12 = (bf16[8,32,128]{2,1,0:T(8,128)(2,1)S(1)}, bf16[8,32,128]{2,1,0:T(8,128)(2,1)S(1)}, u32[]{:S(2)}, u32[]{:S(2)}) collective-permute-start(bf16[8,32,128]{2,1,0:T(8,128)(2,1)S(1)} %get-tuple-element.59), channel_id=1, source_target_pairs={{0,24},{8,0},{16,8},{24,16},{1,25},{9,1},{17,9},{25,17},{2,26},{10... | collective-permute-start | bytes 196616 | tf_op jit(solution)/shard_map/ppermute | solution.py:435
  24.9 1.0 %collective-permute-done.10.above_ref = bf16[8,32,128]{2,1,0:T(8,128)(2,1)S(1)} collective-permute-done((bf16[8,32,128]{2,1,0:T(8,128)(2,1)S(1)}, bf16[8,32,128]{2,1,0:T(8,128)(2,1)S(1)}, u32[]{:S(2)}, u32[]{:S(2)}) %collective-permute-start.10) | collective-permute-done | bytes 65568 | tf_op jit(solution)/shard_map/ppermute | solution.py:435
  25.9 1.6 %own_gradient.1 = (bf16[32,2,8,128]{3,2,1,0:T(8,128)(2,1)}, f32[32,128]{1,0:T(8,128)S(1)}, bf16[576,2048]{1,0:T(8,128)(2,1)S(1)}, f32[256,2048]{1,0:T(8,128)S(1)}) custom-call(s32[1]{0:T(128)} %bitcast.me_ref, f32[16,32,128]{2,1,0:T(8,128)S(1)} %get-tuple-element.50.own_ref, bf16[8,32,128]{2,1,0:T(8,128)(2,1)S(1)} %collective-permute-done.9.below_ref, ...), custom_call_target="tpu_custom_call" | custom-call | flops 603979776 | bytes 5734404 | tf_op jit(solution)/shard_map/own_gradient/pallas_call | solution.py:110
  27.6 0.8 %own_filter.1 = (f32[864,256]{1,0:T(8,128)S(1)}, f32[8,128]{1,0:T(8,128)S(1)}) custom-call(bf16[576,2048]{1,0:T(8,128)(2,1)S(1)} %get-tuple-element.65.s_ref, bf16[256,2048]{1,0:T(8,128)(2,1)S(1)} %get-tuple-element.66.x_ref), custom_call_target="tpu_custom_call" | custom-call | flops 603979776 | bytes 4296704 | tf_op jit(solution)/shard_map/own_filter/pallas_call | solution.py:110
  28.4 0.9 %rim_gradient.1 = (bf16[288,2048]{1,0:T(8,128)(2,1)S(1)}, bf16[4,16,32,128]{3,2,1,0:T(8,128)(2,1)S(1)}, bf16[4,16,32,128]{3,2,1,0:T(8,128)(2,1)S(1)}) custom-call(s32[1]{0:T(128)} %bitcast.me_ref, bf16[8,32,128]{2,1,0:T(8,128)(2,1)S(1)} %get-tuple-element.52.low_ref, bf16[8,32,128]{2,1,0:T(8,128)(2,1)S(1)} %get-tuple-element.51.high_ref, ...), custom_call_target="tpu_custom_call" | custom-call | flops 301989888 | bytes 5033988 | tf_op jit(solution)/shard_map/rim_gradient/pallas_call | solution.py:110
  29.9 2.3 %collective-permute-start.13 = (bf16[448,256]{1,0:T(8,128)(2,1)S(1)}, bf16[448,256]{1,0:T(8,128)(2,1)S(1)}, u32[]{:S(2)}, u32[]{:S(2)}) collective-permute-start(bf16[448,256]{1,0:T(8,128)(2,1)S(1)} %get-tuple-element.71.a_ref), channel_id=1, source_target_pairs={{0,8},{1,17},{2,10},{3,19},{4,12},{5,21},{6,14},{7,23},{8,0},{9,25... | collective-permute-start | bytes 688136 | tf_op jit(solution)/shard_map/ppermute | solution.py:449
  32.4 2.4 %collective-permute-start.18 = (bf16[16,32,128]{2,1,0:T(8,128)(2,1)S(1)}, bf16[16,32,128]{2,1,0:T(8,128)(2,1)S(1)}, u32[]{:S(2)}, u32[]{:S(2)}) collective-permute-start(bf16[16,32,128]{2,1,0:T(8,128)(2,1)S(1)} %get-tuple-element.76), channel_id=1, source_target_pairs={{0,4},{1,5},{2,6},{3,7},{4,0},{5,1},{6,2},{7,3},{8,12},{9,13},{10,... | collective-permute-start | bytes 393224 | tf_op jit(solution)/shard_map/ppermute | solution.py:439
  34.8 1.3 %collective-permute-start.19 = (bf16[16,32,128]{2,1,0:T(8,128)(2,1)S(1)}, bf16[16,32,128]{2,1,0:T(8,128)(2,1)S(1)}, u32[]{:S(2)}, u32[]{:S(2)}) collective-permute-start(bf16[16,32,128]{2,1,0:T(8,128)(2,1)S(1)} %get-tuple-element.77), channel_id=1, source_target_pairs={{0,6},{1,7},{2,4},{3,5},{4,2},{5,3},{6,0},{7,1},{8,14},{9,15},{10,... | collective-permute-start | bytes 393224 | tf_op jit(solution)/shard_map/ppermute | solution.py:439
  36.6 1.1 %collective-permute-start.15 = (bf16[448,256]{1,0:T(8,128)(2,1)S(1)}, bf16[448,256]{1,0:T(8,128)(2,1)S(1)}, u32[]{:S(2)}, u32[]{:S(2)}) collective-permute-start(bf16[448,256]{1,0:T(8,128)(2,1)S(1)} %pair_sum.2.a_ref), channel_id=1, source_target_pairs={{0,16},{1,9},{2,18},{3,11},{4,20},{5,13},{6,22},{7,15},{8,24},{9,1... | collective-permute-start | bytes 688136 | tf_op jit(solution)/shard_map/ppermute | solution.py:449
  37.8 0.9 %collective-permute-done.16.b_ref = bf16[448,256]{1,0:T(8,128)(2,1)S(1)} collective-permute-done((bf16[448,256]{1,0:T(8,128)(2,1)S(1)}, bf16[448,256]{1,0:T(8,128)(2,1)S(1)}, u32[]{:S(2)}, u32[]{:S(2)}) %collective-permute-start.16) | collective-permute-done | bytes 229408 | tf_op jit(solution)/shard_map/ppermute | solution.py:449
  38.7 1.3 %collective-permute-start.17 = (bf16[448,256]{1,0:T(8,128)(2,1)S(1)}, bf16[448,256]{1,0:T(8,128)(2,1)S(1)}, u32[]{:S(2)}, u32[]{:S(2)}) collective-permute-start(bf16[448,256]{1,0:T(8,128)(2,1)S(1)} %pair_sum.3.c_ref), channel_id=1, source_target_pairs={{0,16},{1,9},{2,18},{3,11},{4,20},{5,13},{6,22},{7,15},{8,24},{9,1... | collective-permute-start | bytes 688136 | tf_op jit(solution)/shard_map/ppermute | solution.py:449
  40.0 5.4 %collective-permute-done.18.b_ref = bf16[16,32,128]{2,1,0:T(8,128)(2,1)S(1)} collective-permute-done((bf16[16,32,128]{2,1,0:T(8,128)(2,1)S(1)}, bf16[16,32,128]{2,1,0:T(8,128)(2,1)S(1)}, u32[]{:S(2)}, u32[]{:S(2)}) %collective-permute-start.18) | collective-permute-done | bytes 131104 | tf_op jit(solution)/shard_map/ppermute | solution.py:439
  45.5 1.1 %last.1 = (f32[27,32,256]{2,1,0:T(8,128)}, f32[1,32]{1,0:T(1,128)}, bf16[32,2,8,128]{3,2,1,0:T(8,128)(2,1)}) custom-call(bf16[448,256]{1,0:T(8,128)(2,1)S(1)} %pair_sum.2.a_ref, bf16[448,256]{1,0:T(8,128)(2,1)S(1)} %collective-permute-done.15.b_ref, bf16[448,256]{1,0:T(8,128)(2,1)S(1)} %pair_sum.3.c_ref, bf16[448,256]{1,0:T(8,128)(2,1)S(1)} %collective-permute-done.17.d_ref, ...), custom_call_target="tpu_custom_call" | custom-call | bytes 2195584 | tf_op jit(solution)/shard_map/last/pallas_call | solution.py:110
  (30 shorter events, 4.2 us)
Async XLA Ops:
  0.6 10.7 %collective-permute-start = (bf16[32,2,8,128]{3,2,1,0:T(8,128)(2,1)}, bf16[32,2,8,128]{3,2,1,0:T(8,128)(2,1)S(1)}, u32[]{:S(2)}, u32[]{:S(2)}) collective-permute-start(bf16[32,2,8,128]{3,2,1,0:T(8,128)(2,1)} %x_hbm.1), channel_id=1, source_target_pairs={{0,4},{1,5},{2,6},{3,7},{4,0},{5,1},{6,2},{7,3},{8,12},{9,13},{10,... | collective-permute-start | bytes 393224 | tf_op jit(solution)/shard_map/ppermute | solution.py:439
  4.7 10.7 %collective-permute-start.3 = (bf16[32,2,8,128]{3,2,1,0:T(8,128)(2,1)}, bf16[32,2,8,128]{3,2,1,0:T(8,128)(2,1)S(1)}, u32[]{:S(2)}, u32[]{:S(2)}) collective-permute-start(bf16[32,2,8,128]{3,2,1,0:T(8,128)(2,1)} %x_hbm.1), channel_id=1, source_target_pairs={{0,2},{1,3},{2,0},{3,1},{4,6},{5,7},{6,4},{7,5},{8,10},{9,11},{10,... | collective-permute-start | bytes 393224 | tf_op jit(solution)/shard_map/ppermute | solution.py:439
  7.8 4.7 %collective-permute-start.6 = (bf16[8,32,128]{2,1,0:T(8,128)(2,1)S(1)}, bf16[8,32,128]{2,1,0:T(8,128)(2,1)S(1)}, u32[]{:S(2)}, u32[]{:S(2)}) collective-permute-start(bf16[8,32,128]{2,1,0:T(8,128)(2,1)S(1)} %get-tuple-element.47), channel_id=1, source_target_pairs={{0,24},{8,0},{16,8},{24,16},{1,25},{9,1},{17,9},{25,17},{2,26},{10... | collective-permute-start | bytes 196616 | tf_op jit(solution)/shard_map/ppermute | solution.py:435
  10.3 5.2 %collective-permute-start.7 = (bf16[8,32,128]{2,1,0:T(8,128)(2,1)S(1)}, bf16[8,32,128]{2,1,0:T(8,128)(2,1)S(1)}, u32[]{:S(2)}, u32[]{:S(2)}) collective-permute-start(bf16[8,32,128]{2,1,0:T(8,128)(2,1)S(1)} %get-tuple-element.48), channel_id=1, source_target_pairs={{0,8},{8,16},{16,24},{24,0},{1,9},{9,17},{17,25},{25,1},{2,10},{10... | collective-permute-start | bytes 196616 | tf_op jit(solution)/shard_map/ppermute | solution.py:435
  10.3 6.0 %collective-permute-start.4 = (bf16[32,2,8,128]{3,2,1,0:T(8,128)(2,1)}, bf16[32,2,8,128]{3,2,1,0:T(8,128)(2,1)S(1)}, u32[]{:S(2)}, u32[]{:S(2)}) collective-permute-start(bf16[32,2,8,128]{3,2,1,0:T(8,128)(2,1)} %x_hbm.1), channel_id=1, source_target_pairs={{0,1},{1,0},{2,3},{3,2},{4,5},{5,4},{6,7},{7,6},{8,9},{9,8},{10,11... | collective-permute-start | bytes 393224 | tf_op jit(solution)/shard_map/ppermute | solution.py:439
  11.4 5.0 %collective-permute-start.1 = (bf16[32,2,8,128]{3,2,1,0:T(8,128)(2,1)S(1)}, bf16[32,2,8,128]{3,2,1,0:T(8,128)(2,1)S(1)}, u32[]{:S(2)}, u32[]{:S(2)}) collective-permute-start(bf16[32,2,8,128]{3,2,1,0:T(8,128)(2,1)S(1)} %collective-permute-done.refs_2_), channel_id=1, source_target_pairs={{0,2},{1,3},{2,0},{3,1},{4,6},{5,7},{6,4},{7,5},{8,10},{9,11},{10,... | collective-permute-start | bytes 393224 | tf_op jit(solution)/shard_map/ppermute | solution.py:439
  15.5 1.3 %collective-permute-start.5 = (bf16[32,2,8,128]{3,2,1,0:T(8,128)(2,1)S(1)}, bf16[32,2,8,128]{3,2,1,0:T(8,128)(2,1)S(1)}, u32[]{:S(2)}, u32[]{:S(2)}) collective-permute-start(bf16[32,2,8,128]{3,2,1,0:T(8,128)(2,1)S(1)} %collective-permute-done.3.refs_1_), channel_id=1, source_target_pairs={{0,1},{1,0},{2,3},{3,2},{4,5},{5,4},{6,7},{7,6},{8,9},{9,8},{10,11... | collective-permute-start | bytes 393224 | tf_op jit(solution)/shard_map/ppermute | solution.py:439
  15.5 1.5 %collective-permute-start.8 = (bf16[32,2,8,128]{3,2,1,0:T(8,128)(2,1)S(1)}, bf16[32,2,8,128]{3,2,1,0:T(8,128)(2,1)S(1)}, u32[]{:S(2)}, u32[]{:S(2)}) collective-permute-start(bf16[32,2,8,128]{3,2,1,0:T(8,128)(2,1)S(1)} %collective-permute-done.refs_2_), channel_id=1, source_target_pairs={{0,1},{1,0},{2,3},{3,2},{4,5},{5,4},{6,7},{7,6},{8,9},{9,8},{10,11... | collective-permute-start | bytes 393224 | tf_op jit(solution)/shard_map/ppermute | solution.py:439
  16.3 1.4 %collective-permute-start.2 = (bf16[32,2,8,128]{3,2,1,0:T(8,128)(2,1)S(1)}, bf16[32,2,8,128]{3,2,1,0:T(8,128)(2,1)S(1)}, u32[]{:S(2)}, u32[]{:S(2)}) collective-permute-start(bf16[32,2,8,128]{3,2,1,0:T(8,128)(2,1)S(1)} %collective-permute-done.1.refs_3_), channel_id=1, source_target_pairs={{0,1},{1,0},{2,3},{3,2},{4,5},{5,4},{6,7},{7,6},{8,9},{9,8},{10,11... | collective-permute-start | bytes 393224 | tf_op jit(solution)/shard_map/ppermute | solution.py:439
  19.0 5.9 %collective-permute-start.9 = (bf16[8,32,128]{2,1,0:T(8,128)(2,1)S(1)}, bf16[8,32,128]{2,1,0:T(8,128)(2,1)S(1)}, u32[]{:S(2)}, u32[]{:S(2)}) collective-permute-start(bf16[8,32,128]{2,1,0:T(8,128)(2,1)S(1)} %get-tuple-element.51.high_ref), channel_id=1, source_target_pairs={{0,8},{8,16},{16,24},{24,0},{1,9},{9,17},{17,25},{25,1},{2,10},{10... | collective-permute-start | bytes 196616 | tf_op jit(solution)/shard_map/ppermute | solution.py:435
  20.9 5.1 %collective-permute-start.10 = (bf16[8,32,128]{2,1,0:T(8,128)(2,1)S(1)}, bf16[8,32,128]{2,1,0:T(8,128)(2,1)S(1)}, u32[]{:S(2)}, u32[]{:S(2)}) collective-permute-start(bf16[8,32,128]{2,1,0:T(8,128)(2,1)S(1)} %get-tuple-element.52.low_ref), channel_id=1, source_target_pairs={{0,24},{8,0},{16,8},{24,16},{1,25},{9,1},{17,9},{25,17},{2,26},{10... | collective-permute-start | bytes 196616 | tf_op jit(solution)/shard_map/ppermute | solution.py:435
  22.0 6.4 %collective-permute-start.11 = (bf16[8,32,128]{2,1,0:T(8,128)(2,1)S(1)}, bf16[8,32,128]{2,1,0:T(8,128)(2,1)S(1)}, u32[]{:S(2)}, u32[]{:S(2)}) collective-permute-start(bf16[8,32,128]{2,1,0:T(8,128)(2,1)S(1)} %get-tuple-element.58), channel_id=1, source_target_pairs={{0,8},{8,16},{16,24},{24,0},{1,9},{9,17},{17,25},{25,1},{2,10},{10... | collective-permute-start | bytes 196616 | tf_op jit(solution)/shard_map/ppermute | solution.py:435
  22.9 5.5 %collective-permute-start.12 = (bf16[8,32,128]{2,1,0:T(8,128)(2,1)S(1)}, bf16[8,32,128]{2,1,0:T(8,128)(2,1)S(1)}, u32[]{:S(2)}, u32[]{:S(2)}) collective-permute-start(bf16[8,32,128]{2,1,0:T(8,128)(2,1)S(1)} %get-tuple-element.59), channel_id=1, source_target_pairs={{0,24},{8,0},{16,8},{24,16},{1,25},{9,1},{17,9},{25,17},{2,26},{10... | collective-permute-start | bytes 196616 | tf_op jit(solution)/shard_map/ppermute | solution.py:435
  29.3 3.0 %collective-permute-start.14 = (bf16[4,16,32,128]{3,2,1,0:T(8,128)(2,1)S(1)}, bf16[4,16,32,128]{3,2,1,0:T(8,128)(2,1)S(1)}, u32[]{:S(2)}, u32[]{:S(2)}) collective-permute-start(bf16[4,16,32,128]{3,2,1,0:T(8,128)(2,1)S(1)} %get-tuple-element.73), channel_id=1, source_target_pairs={{0,1},{1,0},{2,3},{3,2},{4,5},{5,4},{6,7},{7,6},{8,9},{9,8},{10,11... | collective-permute-start | bytes 1572872 | tf_op jit(solution)/shard_map/ppermute | solution.py:439
  29.9 6.7 %collective-permute-start.13 = (bf16[448,256]{1,0:T(8,128)(2,1)S(1)}, bf16[448,256]{1,0:T(8,128)(2,1)S(1)}, u32[]{:S(2)}, u32[]{:S(2)}) collective-permute-start(bf16[448,256]{1,0:T(8,128)(2,1)S(1)} %get-tuple-element.71.a_ref), channel_id=1, source_target_pairs={{0,8},{1,17},{2,10},{3,19},{4,12},{5,21},{6,14},{7,23},{8,0},{9,25... | collective-permute-start | bytes 688136 | tf_op jit(solution)/shard_map/ppermute | solution.py:449
  32.2 6.5 %collective-permute-start.16 = (bf16[448,256]{1,0:T(8,128)(2,1)S(1)}, bf16[448,256]{1,0:T(8,128)(2,1)S(1)}, u32[]{:S(2)}, u32[]{:S(2)}) collective-permute-start(bf16[448,256]{1,0:T(8,128)(2,1)S(1)} %get-tuple-element.75.a_ref), channel_id=1, source_target_pairs={{0,8},{1,17},{2,10},{3,19},{4,12},{5,21},{6,14},{7,23},{8,0},{9,25... | collective-permute-start | bytes 688136 | tf_op jit(solution)/shard_map/ppermute | solution.py:449
  32.4 13.0 %collective-permute-start.18 = (bf16[16,32,128]{2,1,0:T(8,128)(2,1)S(1)}, bf16[16,32,128]{2,1,0:T(8,128)(2,1)S(1)}, u32[]{:S(2)}, u32[]{:S(2)}) collective-permute-start(bf16[16,32,128]{2,1,0:T(8,128)(2,1)S(1)} %get-tuple-element.76), channel_id=1, source_target_pairs={{0,4},{1,5},{2,6},{3,7},{4,0},{5,1},{6,2},{7,3},{8,12},{9,13},{10,... | collective-permute-start | bytes 393224 | tf_op jit(solution)/shard_map/ppermute | solution.py:439
  34.8 10.6 %collective-permute-start.19 = (bf16[16,32,128]{2,1,0:T(8,128)(2,1)S(1)}, bf16[16,32,128]{2,1,0:T(8,128)(2,1)S(1)}, u32[]{:S(2)}, u32[]{:S(2)}) collective-permute-start(bf16[16,32,128]{2,1,0:T(8,128)(2,1)S(1)} %get-tuple-element.77), channel_id=1, source_target_pairs={{0,6},{1,7},{2,4},{3,5},{4,2},{5,3},{6,0},{7,1},{8,14},{9,15},{10,... | collective-permute-start | bytes 393224 | tf_op jit(solution)/shard_map/ppermute | solution.py:439
  36.1 9.4 %collective-permute-start.20 = (bf16[16,32,128]{2,1,0:T(8,128)(2,1)S(1)}, bf16[16,32,128]{2,1,0:T(8,128)(2,1)S(1)}, u32[]{:S(2)}, u32[]{:S(2)}) collective-permute-start(bf16[16,32,128]{2,1,0:T(8,128)(2,1)S(1)} %get-tuple-element.78), channel_id=1, source_target_pairs={{0,2},{1,3},{2,0},{3,1},{4,6},{5,7},{6,4},{7,5},{8,10},{9,11},{10,... | collective-permute-start | bytes 393224 | tf_op jit(solution)/shard_map/ppermute | solution.py:439
  36.6 8.9 %collective-permute-start.15 = (bf16[448,256]{1,0:T(8,128)(2,1)S(1)}, bf16[448,256]{1,0:T(8,128)(2,1)S(1)}, u32[]{:S(2)}, u32[]{:S(2)}) collective-permute-start(bf16[448,256]{1,0:T(8,128)(2,1)S(1)} %pair_sum.2.a_ref), channel_id=1, source_target_pairs={{0,16},{1,9},{2,18},{3,11},{4,20},{5,13},{6,22},{7,15},{8,24},{9,1... | collective-permute-start | bytes 688136 | tf_op jit(solution)/shard_map/ppermute | solution.py:449
  38.7 6.8 %collective-permute-start.17 = (bf16[448,256]{1,0:T(8,128)(2,1)S(1)}, bf16[448,256]{1,0:T(8,128)(2,1)S(1)}, u32[]{:S(2)}, u32[]{:S(2)}) collective-permute-start(bf16[448,256]{1,0:T(8,128)(2,1)S(1)} %pair_sum.3.c_ref), channel_id=1, source_target_pairs={{0,16},{1,9},{2,18},{3,11},{4,20},{5,13},{6,22},{7,15},{8,24},{9,1... | collective-permute-start | bytes 688136 | tf_op jit(solution)/shard_map/ppermute | solution.py:449

commit v16 on v15

--- a/solution.py
+++ b/solution.py
@@ -9,7 +9,6 @@
 from jax.sharding import PartitionSpec as P
 
 LANES = 128
-FORWARD_FLOPS = 9 * 10**8
 SUM_FLOPS = 24 * 10**8
 ASSEMBLE_FLOPS = 40 * 10**8
 VMEM = pl.BlockSpec(memory_space=pltpu.VMEM)
@@ -207,45 +206,54 @@
     return jnp.bitwise_xor(me_ref[0], 2 * (b % 4) + b // 4)
 
 
-def forward_body(n, rows, o, places, me_ref, w_ref, *refs):
-    blocks = refs[: len(places)]
-    own_ref, low_ref, high_ref, first_ref, last_ref, x_ref, acc, wide_ref = refs[len(places) + 1 :]
-    for b, block in zip(places, blocks):
-        place_block(me_ref, b, block, x_ref, wide_ref)
-    w = w_ref[...]
+def plane_sums(rows, o, w_ref, x_ref, acc, chosen):
     seen = set()
-    for p in range(n):
+    for p in range(2):
+        near = [i for i in range(3) if (p, i) in chosen]
+        base = 9 * near[0]
+        w = w_ref[base * o : 9 * (near[-1] + 1) * o]
         for t in range(0, rows, 2):
             at = (p * rows + t) * LANES
             part = jnp.dot(
                 w, x_ref[:, at : at + 2 * LANES], preferred_element_type=jnp.float32
             )
             for k, i, j, l in tap_list():
+                if i not in near:
+                    continue
                 for h in range(2):
-                    slot = (l, p + 2 - i, (t + h + 1 - j) % rows)
-                    value = part[k * o : (k + 1) * o, h * LANES : (h + 1) * LANES]
+                    slot = (l, chosen[p, i], (t + h + 1 - j) % rows)
+                    value = part[(k - base) * o : (k - base + 1) * o, h * LANES : (h + 1) * LANES]
                     if slot in seen:
                         acc[slot] += value
                     else:
                         acc[slot] = value
                         seen.add(slot)
-    for q in range(n + 2):
-        for y in range(rows):
-            total = (
-                pltpu.roll(acc[0, q, y], 1, 1)
-                + acc[1, q, y]
-                + pltpu.roll(acc[2, q, y], LANES - 1, 1)
-            )
-            if q == 0:
-                low_ref[y] = total.astype(low_ref.dtype)
-            elif q == n + 1:
-                high_ref[y] = total.astype(high_ref.dtype)
-            else:
-                own_ref[(q - 1) * rows + y] = total
-            if q == 1:
-                first_ref[y] = total.astype(first_ref.dtype)
-            if q == n:
-                last_ref[y] = total.astype(last_ref.dtype)
+    return [
+        [
+            pltpu.roll(acc[0, q, y], 1, 1) + acc[1, q, y] + pltpu.roll(acc[2, q, y], LANES - 1, 1)
+            for y in range(rows)
+        ]
+        for q in range(2)
+    ]
+
+
+def rim_forward_body(rows, o, place, me_ref, w_ref, block_ref, _, low_ref, high_ref, x_ref, acc, wide_ref):
+    place_block(me_ref, place, block_ref, x_ref, wide_ref)
+    sums = plane_sums(rows, o, w_ref, x_ref, acc, {(0, 2): 0, (1, 0): 1})
+    for y in range(rows):
+        low_ref[y] = sums[0][y].astype(low_ref.dtype)
+        high_ref[y] = sums[1][y].astype(high_ref.dtype)
+
+
+def own_forward_body(rows, o, w_ref, x_ref, own_ref, first_ref, last_ref, acc):
+    sums = plane_sums(
+        rows, o, w_ref, x_ref, acc, {(0, 0): 1, (0, 1): 0, (1, 1): 1, (1, 2): 0}
+    )
+    for y in range(rows):
+        own_ref[y] = sums[0][y]
+        own_ref[rows + y] = sums[1][y]
+        first_ref[y] = sums[0][y].astype(first_ref.dtype)
+        last_ref[y] = sums[1][y].astype(last_ref.dtype)
 
 
 def ordered(me_ref, o, in_refs, out_refs):
@@ -492,7 +500,7 @@
     late_b, go_above, go_below = lax.optimization_barrier((x_b, go_above, go_below))
     x_a_side = swap(x_a, "chan", 1)
     x_b_side = swap(late_b, "chan", 1)
-    early, late = (0, 1, 2, 3, 4, 5, 6), (7,)
+    early = (0, 1, 2, 3, 4, 5, 6)
     (x_all,) = call(
         functools.partial(assemble_body, early),
         [shape_of((c_all, cells * depth), bf16)],
@@ -503,19 +511,24 @@
         name="assemble",
     )
     x_ab_side = swap(x_ab, "chan", 1)
-    own, low, high, first, last, x_all = call(
-        functools.partial(forward_body, n, rows, o, late),
-        [
-            shape_of((cells, o, depth), f32),
-            *[shape_of((rows, o, depth), bf16)] * 4,
-            shape_of((c_all, cells * depth), bf16),
-        ],
+    sums = [pltpu.VMEM((3, 2, rows, o, depth), f32)]
+    low, high, x_all = call(
+        functools.partial(rim_forward_body, rows, o, 7),
+        [shape_of((rows, o, depth), bf16)] * 2 + [shape_of((c_all, cells * depth), bf16)],
         [me, w_flat, x_ab_side, x_all],
         [SMEM] + [VMEM] * 3,
-        [pltpu.VMEM((3, n + 2, rows, o, depth), f32), *block_wide],
-        flops=FORWARD_FLOPS,
-        name="forward",
-        aliases={3: 5},
+        sums + block_wide,
+        flops=flops // 3,
+        name="rim_forward",
+        aliases={3: 2},
+    )
+    own, first, last = call(
+        functools.partial(own_forward_body, rows, o),
+        [shape_of((cells, o, depth), f32)] + [shape_of((rows, o, depth), bf16)] * 2,
+        [w_flat, x_all],
+        scratch=sums,
+        flops=flops * 2 // 3,
+        name="own_forward",
     )
     above = rotate(low, "slab", -1)
     below = rotate(high, "slab", 1)

time: 47.5 us -> 47.6 us (level)
  the two profiles are of different devices: /device:TPU:0 before, /device:TPU:19 now
where the time goes in v16:
time: 47.6 us; the launch traced here: 47.4 us
  starting transfers between devices  22.4 us (47%)
  waiting for transfers between devices  15.3 us (32%)
  Pallas kernels  8.96 us (19%)
  between operations  0.77 us (2%)
    ppermute x11, starting transfers between devices, swap(): lax.ppermute(value, axis, [(i, i ^ bit) for i in range(lax.axis_size(axis...  14.6 us
    ppermute x11, waiting for transfers between devices, swap(): lax.ppermute(value, axis, [(i, i ^ bit) for i in range(lax.axis_size(axis...  11.4 us
    pallas_call x13, Pallas kernels, call(): pl.pallas_call(body, out_shape=out_shape, in_specs=specs or [VMEM] * len(...  8.96 us
    ppermute x6, starting transfers between devices, rotate(): lax.ppermute(value, axis, [(i, (i + step) % count) for i in range(count)])  6.1 us
    ppermute x4, waiting for transfers between devices, cross(): return lax.ppermute(value, ('slab', 'chan'), pairs)  2.29 us
    ppermute x4, starting transfers between devices, cross(): return lax.ppermute(value, ('slab', 'chan'), pairs)  1.67 us
    ppermute x6, waiting for transfers between devices, rotate(): lax.ppermute(value, axis, [(i, (i + step) % count) for i in range(count)])  1.61 us
  transfers between devices with their start and end apart: 21, of which 7 were waited for; matrix products, arithmetic and copies ran while one was open for 0% of the time, Pallas kernels for 13%

profile of v16, /device:TPU:19, one launch (start us, length us, event | category | flops | bytes accessed | tf_op | source)
XLA Modules:
  0.0 47.4 jit_solution(7989162735449699792)
XLA Ops:
  0.8 1.3 %collective-permute-start.3 = (bf16[32,2,8,128]{3,2,1,0:T(8,128)(2,1)}, bf16[32,2,8,128]{3,2,1,0:T(8,128)(2,1)S(1)}, u32[]{:S(2)}, u32[]{:S(2)}) collective-permute-start(bf16[32,2,8,128]{3,2,1,0:T(8,128)(2,1)} %x_hbm.1), channel_id=1, source_target_pairs={{0,2},{1,3},{2,0},{3,1},{4,6},{5,7},{6,4},{7,5},{8,10},{9,11},{10,... | collective-permute-start | bytes 393224 | tf_op jit(solution)/shard_map/ppermute | solution.py:447
  2.1 1.5 %prepare.1 = (bf16[32,2,8,128]{3,2,1,0:T(8,128)(2,1)S(1)}, bf16[16,32,128]{2,1,0:T(8,128)(2,1)S(1)}, bf16[8,32,128]{2,1,0:T(8,128)(2,1)S(1)}, bf16[8,32,128]{2,1...) custom-call(bf16[32,2,8,128]{3,2,1,0:T(8,128)(2,1)} %x_hbm.1, ...), custom_call_target="tpu_custom_call" | custom-call | bytes 2441280 | tf_op jit(solution)/shard_map/prepare/pallas_call | solution.py:109
  3.9 2.1 %collective-permute-start.7 = (bf16[8,32,128]{2,1,0:T(8,128)(2,1)S(1)}, bf16[8,32,128]{2,1,0:T(8,128)(2,1)S(1)}, u32[]{:S(2)}, u32[]{:S(2)}) collective-permute-start(bf16[8,32,128]{2,1,0:T(8,128)(2,1)S(1)} %get-tuple-element.48), channel_id=1, source_target_pairs={{0,8},{8,16},{16,24},{24,0},{1,9},{9,17},{17,25},{25,1},{2,10},{10... | collective-permute-start | bytes 196616 | tf_op jit(solution)/shard_map/ppermute | solution.py:443
  6.0 1.8 %collective-permute-start.4 = (bf16[32,2,8,128]{3,2,1,0:T(8,128)(2,1)}, bf16[32,2,8,128]{3,2,1,0:T(8,128)(2,1)S(1)}, u32[]{:S(2)}, u32[]{:S(2)}) collective-permute-start(bf16[32,2,8,128]{3,2,1,0:T(8,128)(2,1)} %x_hbm.1), channel_id=1, source_target_pairs={{0,1},{1,0},{2,3},{3,2},{4,5},{5,4},{6,7},{7,6},{8,9},{9,8},{10,11... | collective-permute-start | bytes 393224 | tf_op jit(solution)/shard_map/ppermute | solution.py:447
  7.8 3.5 %collective-permute-start.1 = (bf16[32,2,8,128]{3,2,1,0:T(8,128)(2,1)S(1)}, bf16[32,2,8,128]{3,2,1,0:T(8,128)(2,1)S(1)}, u32[]{:S(2)}, u32[]{:S(2)}) collective-permute-start(bf16[32,2,8,128]{3,2,1,0:T(8,128)(2,1)S(1)} %collective-permute-done.refs_2_), channel_id=1, source_target_pairs={{0,2},{1,3},{2,0},{3,1},{4,6},{5,7},{6,4},{7,5},{8,10},{9,11},{10,... | collective-permute-start | bytes 393224 | tf_op jit(solution)/shard_map/ppermute | solution.py:447
  11.2 0.8 %collective-permute-start.5 = (bf16[32,2,8,128]{3,2,1,0:T(8,128)(2,1)S(1)}, bf16[32,2,8,128]{3,2,1,0:T(8,128)(2,1)S(1)}, u32[]{:S(2)}, u32[]{:S(2)}) collective-permute-start(bf16[32,2,8,128]{3,2,1,0:T(8,128)(2,1)S(1)} %collective-permute-done.3.refs_1_), channel_id=1, source_target_pairs={{0,1},{1,0},{2,3},{3,2},{4,5},{5,4},{6,7},{7,6},{8,9},{9,8},{10,11... | collective-permute-start | bytes 393224 | tf_op jit(solution)/shard_map/ppermute | solution.py:447
  12.1 2.5 %collective-permute-done.1.refs_3_ = bf16[32,2,8,128]{3,2,1,0:T(8,128)(2,1)S(1)} collective-permute-done((bf16[32,2,8,128]{3,2,1,0:T(8,128)(2,1)S(1)}, bf16[32,2,8,128]{3,2,1,0:T(8,128)(2,1)S(1)}, u32[]{:S(2)}, u32[]{:S(2)}) %collective-permute-start.1) | collective-permute-done | bytes 131104 | tf_op jit(solution)/shard_map/ppermute | solution.py:447
  14.6 1.0 %collective-permute-start.2 = (bf16[32,2,8,128]{3,2,1,0:T(8,128)(2,1)S(1)}, bf16[32,2,8,128]{3,2,1,0:T(8,128)(2,1)S(1)}, u32[]{:S(2)}, u32[]{:S(2)}) collective-permute-start(bf16[32,2,8,128]{3,2,1,0:T(8,128)(2,1)S(1)} %collective-permute-done.1.refs_3_), channel_id=1, source_target_pairs={{0,1},{1,0},{2,3},{3,2},{4,5},{5,4},{6,7},{7,6},{8,9},{9,8},{10,11... | collective-permute-start | bytes 393224 | tf_op jit(solution)/shard_map/ppermute | solution.py:447
  15.7 0.7 %assemble.1._ = bf16[256,2048]{1,0:T(8,128)(2,1)S(1)} custom-call(s32[1]{0:T(128)} %bitcast.me_ref, bf16[32,2,8,128]{3,2,1,0:T(8,128)(2,1)S(1)} %get-tuple-element.46.refs_0_, bf16[32,2,8,128]{3,2,1,0:T(8,128)(2,1)S(1)} %collective-permute-done.3.refs_1_, bf16[32,2,8,128]{3,2,1,0:T(8,128)(2,1)S(1)} %collective-permute-done.refs_2_, ...), custom_call_target="tpu_custom_call" | custom-call | flops 4000000000 | bytes 1966084 | tf_op jit(solution)/shard_map/assemble/pallas_call | solution.py:109
  17.3 1.3 %collective-permute-start.9 = (bf16[8,32,128]{2,1,0:T(8,128)(2,1)S(1)}, bf16[8,32,128]{2,1,0:T(8,128)(2,1)S(1)}, u32[]{:S(2)}, u32[]{:S(2)}) collective-permute-start(bf16[8,32,128]{2,1,0:T(8,128)(2,1)S(1)} %get-tuple-element.52.high_ref), channel_id=1, source_target_pairs={{0,8},{8,16},{16,24},{24,0},{1,9},{9,17},{17,25},{25,1},{2,10},{10... | collective-permute-start | bytes 196616 | tf_op jit(solution)/shard_map/ppermute | solution.py:443
  18.8 0.9 %own_forward.1 = (f32[16,32,128]{2,1,0:T(8,128)S(1)}, bf16[8,32,128]{2,1,0:T(8,128)(2,1)S(1)}, bf16[8,32,128]{2,1,0:T(8,128)(2,1)S(1)}) custom-call(bf16[864,256]{1,0:T(8,128)(2,1)S(1)} %get-tuple-element.44.w_ref, bf16[256,2048]{1,0:T(8,128)(2,1)S(1)} %get-tuple-element.50.x_ref), custom_call_target="tpu_custom_call" | custom-call | flops 603979776 | bytes 1884160 | tf_op jit(solution)/shard_map/own_forward/pallas_call | solution.py:109
  19.7 2.2 %collective-permute-start.11 = (bf16[8,32,128]{2,1,0:T(8,128)(2,1)S(1)}, bf16[8,32,128]{2,1,0:T(8,128)(2,1)S(1)}, u32[]{:S(2)}, u32[]{:S(2)}) collective-permute-start(bf16[8,32,128]{2,1,0:T(8,128)(2,1)S(1)} %get-tuple-element.59), channel_id=1, source_target_pairs={{0,8},{8,16},{16,24},{24,0},{1,9},{9,17},{17,25},{25,1},{2,10},{10... | collective-permute-start | bytes 196616 | tf_op jit(solution)/shard_map/ppermute | solution.py:443
  21.9 1.1 %collective-permute-done.10.above_ref = bf16[8,32,128]{2,1,0:T(8,128)(2,1)S(1)} collective-permute-done((bf16[8,32,128]{2,1,0:T(8,128)(2,1)S(1)}, bf16[8,32,128]{2,1,0:T(8,128)(2,1)S(1)}, u32[]{:S(2)}, u32[]{:S(2)}) %collective-permute-start.10) | collective-permute-done | bytes 65568 | tf_op jit(solution)/shard_map/ppermute | solution.py:443
  23.0 1.6 %own_gradient.1 = (bf16[32,2,8,128]{3,2,1,0:T(8,128)(2,1)}, f32[32,128]{1,0:T(8,128)S(1)}, bf16[576,2048]{1,0:T(8,128)(2,1)S(1)}, f32[256,2048]{1,0:T(8,128)S(1)}) custom-call(s32[1]{0:T(128)} %bitcast.me_ref, f32[16,32,128]{2,1,0:T(8,128)S(1)} %get-tuple-element.51.own_ref, bf16[8,32,128]{2,1,0:T(8,128)(2,1)S(1)} %collective-permute-done.9.below_ref, ...), custom_call_target="tpu_custom_call" | custom-call | flops 603979776 | bytes 5734404 | tf_op jit(solution)/shard_map/own_gradient/pallas_call | solution.py:109
  24.6 0.8 %own_filter.1 = (f32[864,256]{1,0:T(8,128)S(1)}, f32[8,128]{1,0:T(8,128)S(1)}) custom-call(bf16[576,2048]{1,0:T(8,128)(2,1)S(1)} %get-tuple-element.66.s_ref, bf16[256,2048]{1,0:T(8,128)(2,1)S(1)} %get-tuple-element.50.x_ref), custom_call_target="tpu_custom_call" | custom-call | flops 603979776 | bytes 4296704 | tf_op jit(solution)/shard_map/own_filter/pallas_call | solution.py:109
  25.9 0.9 %rim_gradient.1 = (bf16[288,2048]{1,0:T(8,128)(2,1)S(1)}, bf16[4,16,32,128]{3,2,1,0:T(8,128)(2,1)S(1)}, bf16[4,16,32,128]{3,2,1,0:T(8,128)(2,1)S(1)}) custom-call(s32[1]{0:T(128)} %bitcast.me_ref, bf16[8,32,128]{2,1,0:T(8,128)(2,1)S(1)} %get-tuple-element.53.low_ref, bf16[8,32,128]{2,1,0:T(8,128)(2,1)S(1)} %get-tuple-element.52.high_ref, ...), custom_call_target="tpu_custom_call" | custom-call | flops 301989888 | bytes 5033988 | tf_op jit(solution)/shard_map/rim_gradient/pallas_call | solution.py:109
  26.8 2.4 %collective-permute-start.14 = (bf16[4,16,32,128]{3,2,1,0:T(8,128)(2,1)S(1)}, bf16[4,16,32,128]{3,2,1,0:T(8,128)(2,1)S(1)}, u32[]{:S(2)}, u32[]{:S(2)}) collective-permute-start(bf16[4,16,32,128]{3,2,1,0:T(8,128)(2,1)S(1)} %get-tuple-element.73), channel_id=1, source_target_pairs={{0,1},{1,0},{2,3},{3,2},{4,5},{5,4},{6,7},{7,6},{8,9},{9,8},{10,11... | collective-permute-start | bytes 1572872 | tf_op jit(solution)/shard_map/ppermute | solution.py:447
  30.0 1.2 %collective-permute-start.16 = (bf16[448,256]{1,0:T(8,128)(2,1)S(1)}, bf16[448,256]{1,0:T(8,128)(2,1)S(1)}, u32[]{:S(2)}, u32[]{:S(2)}) collective-permute-start(bf16[448,256]{1,0:T(8,128)(2,1)S(1)} %get-tuple-element.75.a_ref), channel_id=1, source_target_pairs={{0,8},{1,17},{2,10},{3,19},{4,12},{5,21},{6,14},{7,23},{8,0},{9,25... | collective-permute-start | bytes 688136 | tf_op jit(solution)/shard_map/ppermute | solution.py:457
  31.4 2.6 %collective-permute-start.19 = (bf16[16,32,128]{2,1,0:T(8,128)(2,1)S(1)}, bf16[16,32,128]{2,1,0:T(8,128)(2,1)S(1)}, u32[]{:S(2)}, u32[]{:S(2)}) collective-permute-start(bf16[16,32,128]{2,1,0:T(8,128)(2,1)S(1)} %get-tuple-element.77), channel_id=1, source_target_pairs={{0,6},{1,7},{2,4},{3,5},{4,2},{5,3},{6,0},{7,1},{8,14},{9,15},{10,... | collective-permute-start | bytes 393224 | tf_op jit(solution)/shard_map/ppermute | solution.py:447
  34.1 0.9 %collective-permute-start.20 = (bf16[16,32,128]{2,1,0:T(8,128)(2,1)S(1)}, bf16[16,32,128]{2,1,0:T(8,128)(2,1)S(1)}, u32[]{:S(2)}, u32[]{:S(2)}) collective-permute-start(bf16[16,32,128]{2,1,0:T(8,128)(2,1)S(1)} %get-tuple-element.78), channel_id=1, source_target_pairs={{0,2},{1,3},{2,0},{3,1},{4,6},{5,7},{6,4},{7,5},{8,10},{9,11},{10,... | collective-permute-start | bytes 393224 | tf_op jit(solution)/shard_map/ppermute | solution.py:447
  35.1 2.3 %collective-permute-done.16.b_ref = bf16[448,256]{1,0:T(8,128)(2,1)S(1)} collective-permute-done((bf16[448,256]{1,0:T(8,128)(2,1)S(1)}, bf16[448,256]{1,0:T(8,128)(2,1)S(1)}, u32[]{:S(2)}, u32[]{:S(2)}) %collective-permute-start.16) | collective-permute-done | bytes 229408 | tf_op jit(solution)/shard_map/ppermute | solution.py:457
  37.5 1.2 %collective-permute-done.18.b_ref = bf16[16,32,128]{2,1,0:T(8,128)(2,1)S(1)} collective-permute-done((bf16[16,32,128]{2,1,0:T(8,128)(2,1)S(1)}, bf16[16,32,128]{2,1,0:T(8,128)(2,1)S(1)}, u32[]{:S(2)}, u32[]{:S(2)}) %collective-permute-start.18) | collective-permute-done | bytes 131104 | tf_op jit(solution)/shard_map/ppermute | solution.py:447
  38.8 7.4 %collective-permute-done.19.c_ref = bf16[16,32,128]{2,1,0:T(8,128)(2,1)S(1)} collective-permute-done((bf16[16,32,128]{2,1,0:T(8,128)(2,1)S(1)}, bf16[16,32,128]{2,1,0:T(8,128)(2,1)S(1)}, u32[]{:S(2)}, u32[]{:S(2)}) %collective-permute-start.19) | collective-permute-done | bytes 131104 | tf_op jit(solution)/shard_map/ppermute | solution.py:447
  46.3 1.1 %last.1 = (f32[27,32,256]{2,1,0:T(8,128)}, f32[1,32]{1,0:T(1,128)}, bf16[32,2,8,128]{3,2,1,0:T(8,128)(2,1)}) custom-call(bf16[448,256]{1,0:T(8,128)(2,1)S(1)} %pair_sum.2.a_ref, bf16[448,256]{1,0:T(8,128)(2,1)S(1)} %collective-permute-done.15.b_ref, bf16[448,256]{1,0:T(8,128)(2,1)S(1)} %pair_sum.3.c_ref, bf16[448,256]{1,0:T(8,128)(2,1)S(1)} %collective-permute-done.17.d_ref, ...), custom_call_target="tpu_custom_call" | custom-call | bytes 2195584 | tf_op jit(solution)/shard_map/last/pallas_call | solution.py:109
  (31 shorter events, 3.5 us)
Async XLA Ops:
  0.6 7.1 %collective-permute-start = (bf16[32,2,8,128]{3,2,1,0:T(8,128)(2,1)}, bf16[32,2,8,128]{3,2,1,0:T(8,128)(2,1)S(1)}, u32[]{:S(2)}, u32[]{:S(2)}) collective-permute-start(bf16[32,2,8,128]{3,2,1,0:T(8,128)(2,1)} %x_hbm.1), channel_id=1, source_target_pairs={{0,4},{1,5},{2,6},{3,7},{4,0},{5,1},{6,2},{7,3},{8,12},{9,13},{10,... | collective-permute-start | bytes 393224 | tf_op jit(solution)/shard_map/ppermute | solution.py:447
  0.8 10.5 %collective-permute-start.3 = (bf16[32,2,8,128]{3,2,1,0:T(8,128)(2,1)}, bf16[32,2,8,128]{3,2,1,0:T(8,128)(2,1)S(1)}, u32[]{:S(2)}, u32[]{:S(2)}) collective-permute-start(bf16[32,2,8,128]{3,2,1,0:T(8,128)(2,1)} %x_hbm.1), channel_id=1, source_target_pairs={{0,2},{1,3},{2,0},{3,1},{4,6},{5,7},{6,4},{7,5},{8,10},{9,11},{10,... | collective-permute-start | bytes 393224 | tf_op jit(solution)/shard_map/ppermute | solution.py:447
  3.6 7.7 %collective-permute-start.6 = (bf16[8,32,128]{2,1,0:T(8,128)(2,1)S(1)}, bf16[8,32,128]{2,1,0:T(8,128)(2,1)S(1)}, u32[]{:S(2)}, u32[]{:S(2)}) collective-permute-start(bf16[8,32,128]{2,1,0:T(8,128)(2,1)S(1)} %get-tuple-element.47), channel_id=1, source_target_pairs={{0,24},{8,0},{16,8},{24,16},{1,25},{9,1},{17,9},{25,17},{2,26},{10... | collective-permute-start | bytes 196616 | tf_op jit(solution)/shard_map/ppermute | solution.py:443
  3.9 7.4 %collective-permute-start.7 = (bf16[8,32,128]{2,1,0:T(8,128)(2,1)S(1)}, bf16[8,32,128]{2,1,0:T(8,128)(2,1)S(1)}, u32[]{:S(2)}, u32[]{:S(2)}) collective-permute-start(bf16[8,32,128]{2,1,0:T(8,128)(2,1)S(1)} %get-tuple-element.48), channel_id=1, source_target_pairs={{0,8},{8,16},{16,24},{24,0},{1,9},{9,17},{17,25},{25,1},{2,10},{10... | collective-permute-start | bytes 196616 | tf_op jit(solution)/shard_map/ppermute | solution.py:443
  6.0 9.7 %collective-permute-start.4 = (bf16[32,2,8,128]{3,2,1,0:T(8,128)(2,1)}, bf16[32,2,8,128]{3,2,1,0:T(8,128)(2,1)S(1)}, u32[]{:S(2)}, u32[]{:S(2)}) collective-permute-start(bf16[32,2,8,128]{3,2,1,0:T(8,128)(2,1)} %x_hbm.1), channel_id=1, source_target_pairs={{0,1},{1,0},{2,3},{3,2},{4,5},{5,4},{6,7},{7,6},{8,9},{9,8},{10,11... | collective-permute-start | bytes 393224 | tf_op jit(solution)/shard_map/ppermute | solution.py:447
  7.8 6.9 %collective-permute-start.1 = (bf16[32,2,8,128]{3,2,1,0:T(8,128)(2,1)S(1)}, bf16[32,2,8,128]{3,2,1,0:T(8,128)(2,1)S(1)}, u32[]{:S(2)}, u32[]{:S(2)}) collective-permute-start(bf16[32,2,8,128]{3,2,1,0:T(8,128)(2,1)S(1)} %collective-permute-done.refs_2_), channel_id=1, source_target_pairs={{0,2},{1,3},{2,0},{3,1},{4,6},{5,7},{6,4},{7,5},{8,10},{9,11},{10,... | collective-permute-start | bytes 393224 | tf_op jit(solution)/shard_map/ppermute | solution.py:447
  11.2 4.4 %collective-permute-start.5 = (bf16[32,2,8,128]{3,2,1,0:T(8,128)(2,1)S(1)}, bf16[32,2,8,128]{3,2,1,0:T(8,128)(2,1)S(1)}, u32[]{:S(2)}, u32[]{:S(2)}) collective-permute-start(bf16[32,2,8,128]{3,2,1,0:T(8,128)(2,1)S(1)} %collective-permute-done.3.refs_1_), channel_id=1, source_target_pairs={{0,1},{1,0},{2,3},{3,2},{4,5},{5,4},{6,7},{7,6},{8,9},{9,8},{10,11... | collective-permute-start | bytes 393224 | tf_op jit(solution)/shard_map/ppermute | solution.py:447
  12.1 3.6 %collective-permute-start.8 = (bf16[32,2,8,128]{3,2,1,0:T(8,128)(2,1)S(1)}, bf16[32,2,8,128]{3,2,1,0:T(8,128)(2,1)S(1)}, u32[]{:S(2)}, u32[]{:S(2)}) collective-permute-start(bf16[32,2,8,128]{3,2,1,0:T(8,128)(2,1)S(1)} %collective-permute-done.refs_2_), channel_id=1, source_target_pairs={{0,1},{1,0},{2,3},{3,2},{4,5},{5,4},{6,7},{7,6},{8,9},{9,8},{10,11... | collective-permute-start | bytes 393224 | tf_op jit(solution)/shard_map/ppermute | solution.py:447
  14.6 2.0 %collective-permute-start.2 = (bf16[32,2,8,128]{3,2,1,0:T(8,128)(2,1)S(1)}, bf16[32,2,8,128]{3,2,1,0:T(8,128)(2,1)S(1)}, u32[]{:S(2)}, u32[]{:S(2)}) collective-permute-start(bf16[32,2,8,128]{3,2,1,0:T(8,128)(2,1)S(1)} %collective-permute-done.1.refs_3_), channel_id=1, source_target_pairs={{0,1},{1,0},{2,3},{3,2},{4,5},{5,4},{6,7},{7,6},{8,9},{9,8},{10,11... | collective-permute-start | bytes 393224 | tf_op jit(solution)/shard_map/ppermute | solution.py:447
  17.3 4.6 %collective-permute-start.9 = (bf16[8,32,128]{2,1,0:T(8,128)(2,1)S(1)}, bf16[8,32,128]{2,1,0:T(8,128)(2,1)S(1)}, u32[]{:S(2)}, u32[]{:S(2)}) collective-permute-start(bf16[8,32,128]{2,1,0:T(8,128)(2,1)S(1)} %get-tuple-element.52.high_ref), channel_id=1, source_target_pairs={{0,8},{8,16},{16,24},{24,0},{1,9},{9,17},{17,25},{25,1},{2,10},{10... | collective-permute-start | bytes 196616 | tf_op jit(solution)/shard_map/ppermute | solution.py:443
  18.6 4.4 %collective-permute-start.10 = (bf16[8,32,128]{2,1,0:T(8,128)(2,1)S(1)}, bf16[8,32,128]{2,1,0:T(8,128)(2,1)S(1)}, u32[]{:S(2)}, u32[]{:S(2)}) collective-permute-start(bf16[8,32,128]{2,1,0:T(8,128)(2,1)S(1)} %get-tuple-element.53.low_ref), channel_id=1, source_target_pairs={{0,24},{8,0},{16,8},{24,16},{1,25},{9,1},{17,9},{25,17},{2,26},{10... | collective-permute-start | bytes 196616 | tf_op jit(solution)/shard_map/ppermute | solution.py:443
  19.7 5.7 %collective-permute-start.11 = (bf16[8,32,128]{2,1,0:T(8,128)(2,1)S(1)}, bf16[8,32,128]{2,1,0:T(8,128)(2,1)S(1)}, u32[]{:S(2)}, u32[]{:S(2)}) collective-permute-start(bf16[8,32,128]{2,1,0:T(8,128)(2,1)S(1)} %get-tuple-element.59), channel_id=1, source_target_pairs={{0,8},{8,16},{16,24},{24,0},{1,9},{9,17},{17,25},{25,1},{2,10},{10... | collective-permute-start | bytes 196616 | tf_op jit(solution)/shard_map/ppermute | solution.py:443
  21.9 4.0 %collective-permute-start.12 = (bf16[8,32,128]{2,1,0:T(8,128)(2,1)S(1)}, bf16[8,32,128]{2,1,0:T(8,128)(2,1)S(1)}, u32[]{:S(2)}, u32[]{:S(2)}) collective-permute-start(bf16[8,32,128]{2,1,0:T(8,128)(2,1)S(1)} %get-tuple-element.60), channel_id=1, source_target_pairs={{0,24},{8,0},{16,8},{24,16},{1,25},{9,1},{17,9},{25,17},{2,26},{10... | collective-permute-start | bytes 196616 | tf_op jit(solution)/shard_map/ppermute | solution.py:443
  26.8 4.4 %collective-permute-start.14 = (bf16[4,16,32,128]{3,2,1,0:T(8,128)(2,1)S(1)}, bf16[4,16,32,128]{3,2,1,0:T(8,128)(2,1)S(1)}, u32[]{:S(2)}, u32[]{:S(2)}) collective-permute-start(bf16[4,16,32,128]{3,2,1,0:T(8,128)(2,1)S(1)} %get-tuple-element.73), channel_id=1, source_target_pairs={{0,1},{1,0},{2,3},{3,2},{4,5},{5,4},{6,7},{7,6},{8,9},{9,8},{10,11... | collective-permute-start | bytes 1572872 | tf_op jit(solution)/shard_map/ppermute | solution.py:447
  29.7 5.3 %collective-permute-start.13 = (bf16[448,256]{1,0:T(8,128)(2,1)S(1)}, bf16[448,256]{1,0:T(8,128)(2,1)S(1)}, u32[]{:S(2)}, u32[]{:S(2)}) collective-permute-start(bf16[448,256]{1,0:T(8,128)(2,1)S(1)} %get-tuple-element.71.a_ref), channel_id=1, source_target_pairs={{0,8},{1,17},{2,10},{3,19},{4,12},{5,21},{6,14},{7,23},{8,0},{9,25... | collective-permute-start | bytes 688136 | tf_op jit(solution)/shard_map/ppermute | solution.py:457
  30.0 7.4 %collective-permute-start.16 = (bf16[448,256]{1,0:T(8,128)(2,1)S(1)}, bf16[448,256]{1,0:T(8,128)(2,1)S(1)}, u32[]{:S(2)}, u32[]{:S(2)}) collective-permute-start(bf16[448,256]{1,0:T(8,128)(2,1)S(1)} %get-tuple-element.75.a_ref), channel_id=1, source_target_pairs={{0,8},{1,17},{2,10},{3,19},{4,12},{5,21},{6,14},{7,23},{8,0},{9,25... | collective-permute-start | bytes 688136 | tf_op jit(solution)/shard_map/ppermute | solution.py:457
  31.4 7.4 %collective-permute-start.18 = (bf16[16,32,128]{2,1,0:T(8,128)(2,1)S(1)}, bf16[16,32,128]{2,1,0:T(8,128)(2,1)S(1)}, u32[]{:S(2)}, u32[]{:S(2)}) collective-permute-start(bf16[16,32,128]{2,1,0:T(8,128)(2,1)S(1)} %get-tuple-element.76), channel_id=1, source_target_pairs={{0,4},{1,5},{2,6},{3,7},{4,0},{5,1},{6,2},{7,3},{8,12},{9,13},{10,... | collective-permute-start | bytes 393224 | tf_op jit(solution)/shard_map/ppermute | solution.py:447
  31.4 14.8 %collective-permute-start.19 = (bf16[16,32,128]{2,1,0:T(8,128)(2,1)S(1)}, bf16[16,32,128]{2,1,0:T(8,128)(2,1)S(1)}, u32[]{:S(2)}, u32[]{:S(2)}) collective-permute-start(bf16[16,32,128]{2,1,0:T(8,128)(2,1)S(1)} %get-tuple-element.77), channel_id=1, source_target_pairs={{0,6},{1,7},{2,4},{3,5},{4,2},{5,3},{6,0},{7,1},{8,14},{9,15},{10,... | collective-permute-start | bytes 393224 | tf_op jit(solution)/shard_map/ppermute | solution.py:447
  34.1 12.1 %collective-permute-start.20 = (bf16[16,32,128]{2,1,0:T(8,128)(2,1)S(1)}, bf16[16,32,128]{2,1,0:T(8,128)(2,1)S(1)}, u32[]{:S(2)}, u32[]{:S(2)}) collective-permute-start(bf16[16,32,128]{2,1,0:T(8,128)(2,1)S(1)} %get-tuple-element.78), channel_id=1, source_target_pairs={{0,2},{1,3},{2,0},{3,1},{4,6},{5,7},{6,4},{7,5},{8,10},{9,11},{10,... | collective-permute-start | bytes 393224 | tf_op jit(solution)/shard_map/ppermute | solution.py:447
  35.0 11.2 %collective-permute-start.15 = (bf16[448,256]{1,0:T(8,128)(2,1)S(1)}, bf16[448,256]{1,0:T(8,128)(2,1)S(1)}, u32[]{:S(2)}, u32[]{:S(2)}) collective-permute-start(bf16[448,256]{1,0:T(8,128)(2,1)S(1)} %pair_sum.2.a_ref), channel_id=1, source_target_pairs={{0,16},{1,9},{2,18},{3,11},{4,20},{5,13},{6,22},{7,15},{8,24},{9,1... | collective-permute-start | bytes 688136 | tf_op jit(solution)/shard_map/ppermute | solution.py:457
  37.5 8.8 %collective-permute-start.17 = (bf16[448,256]{1,0:T(8,128)(2,1)S(1)}, bf16[448,256]{1,0:T(8,128)(2,1)S(1)}, u32[]{:S(2)}, u32[]{:S(2)}) collective-permute-start(bf16[448,256]{1,0:T(8,128)(2,1)S(1)} %pair_sum.3.c_ref), channel_id=1, source_target_pairs={{0,16},{1,9},{2,18},{3,11},{4,20},{5,13},{6,22},{7,15},{8,24},{9,1... | collective-permute-start | bytes 688136 | tf_op jit(solution)/shard_map/ppermute | solution.py:457

commit v17 on v15

--- a/solution.py
+++ b/solution.py
@@ -126,6 +126,16 @@
     return jax.ShapeDtypeStruct(shape, dtype)
 
 
+def by_parity(slab_ref, a, b):
+    even = lax.rem(slab_ref[0], 2) == 0
+    f32 = jnp.float32
+    wide = a.astype(f32), b.astype(f32)
+    return (
+        jnp.where(even, wide[0], wide[1]).astype(a.dtype),
+        jnp.where(even, wide[1], wide[0]).astype(a.dtype),
+    )
+
+
 def turned(value, wide_ref):
     o = value.shape[0]
     cells = wide_ref.shape[0] // o
@@ -138,14 +148,15 @@
 def prepare_body(
     n,
     rows,
+    slab_ref,
     x_hbm,
     go_hbm,
     w_hbm,
     bias_hbm,
     x_ref,
     go_ref,
-    go_low_ref,
-    go_high_ref,
+    go_first_ref,
+    go_second_ref,
     flat_ref,
     own_0_ref,
     own_1_ref,
@@ -167,12 +178,12 @@
     for copy in copies:
         copy.start()
     copies[0].wait()
-    for k, value in enumerate(turned(go_in[...], wide_ref)):
+    values = turned(go_in[...], wide_ref)
+    for k, value in enumerate(values):
         go_ref[k] = value
-        if k < rows:
-            go_low_ref[k] = value
-        if k >= (n - 1) * rows:
-            go_high_ref[k - (n - 1) * rows] = value
+    for y in range(rows):
+        low, high = values[y], values[(n - 1) * rows + y]
+        go_first_ref[y], go_second_ref[y] = by_parity(slab_ref, high, low)
     copies[1].wait()
     copies[2].wait()
     copies[3].wait()
@@ -207,9 +218,9 @@
     return jnp.bitwise_xor(me_ref[0], 2 * (b % 4) + b // 4)
 
 
-def forward_body(n, rows, o, places, me_ref, w_ref, *refs):
+def forward_body(n, rows, o, places, me_ref, slab_ref, w_ref, *refs):
     blocks = refs[: len(places)]
-    own_ref, low_ref, high_ref, first_ref, last_ref, x_ref, acc, wide_ref = refs[len(places) + 1 :]
+    own_ref, *sent, x_ref, acc, wide_ref = refs[len(places) + 1 :]
     for b, block in zip(places, blocks):
         place_block(me_ref, b, block, x_ref, wide_ref)
     w = w_ref[...]
@@ -229,23 +240,16 @@
                     else:
                         acc[slot] = value
                         seen.add(slot)
-    for q in range(n + 2):
-        for y in range(rows):
-            total = (
-                pltpu.roll(acc[0, q, y], 1, 1)
-                + acc[1, q, y]
-                + pltpu.roll(acc[2, q, y], LANES - 1, 1)
-            )
-            if q == 0:
-                low_ref[y] = total.astype(low_ref.dtype)
-            elif q == n + 1:
-                high_ref[y] = total.astype(high_ref.dtype)
-            else:
-                own_ref[(q - 1) * rows + y] = total
-            if q == 1:
-                first_ref[y] = total.astype(first_ref.dtype)
-            if q == n:
-                last_ref[y] = total.astype(last_ref.dtype)
+    for y in range(rows):
+        totals = [
+            pltpu.roll(acc[0, q, y], 1, 1) + acc[1, q, y] + pltpu.roll(acc[2, q, y], LANES - 1, 1)
+            for q in range(n + 2)
+        ]
+        for p in range(n):
+            own_ref[p * rows + y] = totals[p + 1]
+        for pair, low, high in ((sent[:2], 0, n + 1), (sent[2:], 1, n)):
+            for ref, value in zip(pair, by_parity(slab_ref, totals[high], totals[low])):
+                ref[y] = value.astype(ref.dtype)
 
 
 def ordered(me_ref, o, in_refs, out_refs):
@@ -268,9 +272,10 @@
     o,
     scale,
     me_ref,
+    slab_ref,
     own_ref,
-    below_ref,
-    above_ref,
+    first_ref,
+    second_ref,
     bias_ref,
     go_ref,
     w_0_ref,
@@ -288,8 +293,8 @@
     total = jnp.zeros((o, LANES), f32)
     for q in range(2):
         for y in range(rows):
-            beside = below_ref if q == 0 else above_ref
-            pre = own_ref[q * rows + y] + beside[y].astype(f32) + bias_ref[...]
+            beside = by_parity(slab_ref, first_ref[y], second_ref[y])[1 - q]
+            pre = own_ref[q * rows + y] + beside.astype(f32) + bias_ref[...]
             s = jax.nn.sigmoid(pre)
             slope = s * (1.0 + pre * (1.0 - s))
             wide = (go_ref[q * rows + y].astype(f32) * slope).astype(bf16).astype(f32)
@@ -316,13 +321,14 @@
     rows,
     o,
     me_ref,
-    low_ref,
-    high_ref,
-    below_ref,
-    above_ref,
+    slab_ref,
+    first_ref,
+    second_ref,
+    first_in_ref,
+    second_in_ref,
     bias_ref,
-    go_below_ref,
-    go_above_ref,
+    go_first_ref,
+    go_second_ref,
     partial_ref,
     w_0_ref,
     w_1_ref,
@@ -335,13 +341,21 @@
 ):
     f32, bf16 = jnp.float32, jnp.bfloat16
     ordered(me_ref, o, (w_0_ref, w_1_ref), (w_0, w_1))
-    sides = ((below_ref, low_ref, go_below_ref), (above_ref, high_ref, go_above_ref))
-    for p, (theirs, ours, go) in enumerate(sides):
+    pairs = (
+        (first_in_ref, second_in_ref),
+        (first_ref, second_ref),
+        (go_first_ref, go_second_ref),
+    )
+    for p in range(2):
         for y in range(rows):
-            pre = theirs[y].astype(f32) + ours[y].astype(f32) + bias_ref[...]
+            theirs, ours, go = (
+                by_parity(slab_ref, first[y], second[y])[1 - p].astype(f32)
+                for first, second in pairs
+            )
+            pre = theirs + ours + bias_ref[...]
             s = jax.nn.sigmoid(pre)
             slope = s * (1.0 + pre * (1.0 - s))
-            wide = (go[y].astype(f32) * slope).astype(bf16).astype(f32)
+            wide = (go * slope).astype(bf16).astype(f32)
             shifts = three_shifts(wide, bf16)
             for j in range(3):
                 for l in range(3):
@@ -430,11 +444,6 @@
     return pltpu.with_memory_space_constraint(value, pltpu.HBM)
 
 
-def rotate(value, axis, step):
-    count = lax.axis_size(axis)
-    return lax.ppermute(value, axis, [(i, (i + step) % count) for i in range(count)])
-
-
 def swap(value, axis, bit):
     return lax.ppermute(value, axis, [(i, i ^ bit) for i in range(lax.axis_size(axis))])
 
@@ -457,13 +466,14 @@
     flops = 2 * 27 * o * c_all * cells * depth
     scale = 1.0 / math.sqrt(lax.axis_size("slab") * cells * depth)
     me = lax.axis_index("chan").astype(jnp.int32).reshape(1)
+    slab = lax.axis_index("slab").astype(jnp.int32).reshape(1)
 
     block_wide = [pltpu.VMEM((o * cells, depth), f32)]
 
     x_b = swap(x_in, "chan", 4)
     x_a = swap(x_in, "chan", 2)
     x_side = swap(x_in, "chan", 1)
-    x_own, go, go_low, go_high, w_flat, *w_back, bias = call(
+    x_own, go, go_first, go_second, w_flat, *w_back, bias = call(
         functools.partial(prepare_body, n, rows),
         [
             shape_of((o, n, rows, depth), bf16),
@@ -474,8 +484,8 @@
             *[shape_of((c_all, taps * o), bf16) for taps in (18, 18, 9, 9)],
             shape_of((o, LANES), f32),
         ],
-        [in_hbm(a) for a in (x_in, grad_out, jnp.transpose(weight, (1, 0, 2)), bias_vec[None, :])],
-        [HBM] * 4,
+        [slab] + [in_hbm(a) for a in (x_in, grad_out, jnp.transpose(weight, (1, 0, 2)), bias_vec[None, :])],
+        [SMEM] + [HBM] * 4,
         [
             pltpu.VMEM((o, n, rows, depth), bf16),
             pltpu.VMEM((27, o, c_all), bf16),
@@ -485,11 +495,11 @@
         ],
         name="prepare",
     )
-    go_above = rotate(go_low, "slab", -1)
-    go_below = rotate(go_high, "slab", 1)
+    go_first = swap(go_first, "slab", 1)
+    go_second = swap(go_second, "slab", 3)
     x_b, w_flat = lax.optimization_barrier((x_b, w_flat))
     x_ab = swap(x_b, "chan", 2)
-    late_b, go_above, go_below = lax.optimization_barrier((x_b, go_above, go_below))
+    late_b, go_first, go_second = lax.optimization_barrier((x_b, go_first, go_second))
     x_a_side = swap(x_a, "chan", 1)
     x_b_side = swap(late_b, "chan", 1)
     early, late = (0, 1, 2, 3, 4, 5, 6), (7,)
@@ -503,24 +513,21 @@
         name="assemble",
     )
     x_ab_side = swap(x_ab, "chan", 1)
-    own, low, high, first, last, x_all = call(
+    own, *sent, x_all = call(
         functools.partial(forward_body, n, rows, o, late),
         [
             shape_of((cells, o, depth), f32),
             *[shape_of((rows, o, depth), bf16)] * 4,
             shape_of((c_all, cells * depth), bf16),
         ],
-        [me, w_flat, x_ab_side, x_all],
-        [SMEM] + [VMEM] * 3,
+        [me, slab, w_flat, x_ab_side, x_all],
+        [SMEM] * 2 + [VMEM] * 3,
         [pltpu.VMEM((3, n + 2, rows, o, depth), f32), *block_wide],
         flops=FORWARD_FLOPS,
         name="forward",
-        aliases={3: 5},
-    )
-    above = rotate(low, "slab", -1)
-    below = rotate(high, "slab", 1)
-    above_own = rotate(first, "slab", -1)
-    below_own = rotate(last, "slab", 1)
+        aliases={4: 5},
+    )
+    received = [swap(a, "slab", 1 + 2 * (at % 2)) for at, a in enumerate(sent)]
     act, total, own_shifts, partial = call(
         functools.partial(own_gradient_body, rows, o, scale),
         [
@@ -529,8 +536,8 @@
             shape_of((18 * o, cells * depth), bf16),
             shape_of((c_all, cells * depth), f32),
         ],
-        [me, own, below, above, bias, go, *w_back[:2]],
-        [SMEM] + [VMEM] * 7,
+        [me, slab, own, *received[:2], bias, go, *w_back[:2]],
+        [SMEM] * 2 + [VMEM] * 7,
         [*[pltpu.VMEM((c_all, 18 * o), bf16)] * 2, *block_wide],
         flops=flops * 2 // 3,
         name="own_gradient",
@@ -549,8 +556,8 @@
             shape_of((4, cells, o, depth), bf16),
             shape_of((4, cells, o, depth), bf16),
         ],
-        [me, low, high, below_own, above_own, bias, go_below, go_above, partial, *w_back[2:], token],
-        [SMEM] + [VMEM] * 10 + [ANY],
+        [me, slab, *sent[:2], *received[2:], bias, go_first, go_second, partial, *w_back[2:], token],
+        [SMEM] * 2 + [VMEM] * 10 + [ANY],
         [pltpu.VMEM((c_all, 9 * o), bf16)] * 2,
         flops=flops // 3,
         name="rim_gradient",

time: 47.5 us -> 47.5 us (level); the launches traced: 46.7 us -> 47.2 us
    ppermute x6 -> x0, starting transfers between devices: 8.4 us -> none  [rotate(): lax.ppermute(value, axis, [(i, (i + step) % count) for i in range(count)])]
    ppermute x11 -> x17, starting transfers between devices: 11.2 us -> 19.4 us  [swap(): lax.ppermute(value, axis, [(i, i ^ bit) for i in range(lax.axis_size(axis...]
    ppermute x11 -> x17, waiting for transfers between devices: 7.56 us -> 12.9 us  [swap(): lax.ppermute(value, axis, [(i, i ^ bit) for i in range(lax.axis_size(axis...]
    ppermute x6 -> x0, waiting for transfers between devices: 4.38 us -> none  [rotate(): lax.ppermute(value, axis, [(i, (i + step) % count) for i in range(count)])]
    ppermute x4, waiting for transfers between devices: 0.88 us -> 0.29 us  [cross(): return lax.ppermute(value, ('slab', 'chan'), pairs)]
  transfers between devices with their start and end apart: 21 -> 21, of which waited for: 10 -> 9; matrix products, arithmetic and copies ran while one was open for 0% -> 0% of each run, Pallas kernels for 12% -> 11%
where the time goes in v17:
time: 47.5 us; the launch traced here: 47.2 us
  starting transfers between devices  24.6 us (52%)
  waiting for transfers between devices  13.2 us (28%)
  Pallas kernels  8.74 us (18%)
  between operations  0.76 us (2%)
    ppermute x17, starting transfers between devices, swap(): lax.ppermute(value, axis, [(i, i ^ bit) for i in range(lax.axis_size(axis...  19.4 us
    ppermute x17, waiting for transfers between devices, swap(): lax.ppermute(value, axis, [(i, i ^ bit) for i in range(lax.axis_size(axis...  12.9 us
    pallas_call x12, Pallas kernels, call(): pl.pallas_call(body, out_shape=out_shape, in_specs=specs or [VMEM] * len(...  8.74 us
    ppermute x4, starting transfers between devices, cross(): return lax.ppermute(value, ('slab', 'chan'), pairs)  5.14 us
  transfers between devices with their start and end apart: 21, of which 9 were waited for; matrix products, arithmetic and copies ran while one was open for 0% of the time, Pallas kernels for 11%

profile of v17, /device:TPU:0, one launch (start us, length us, event | category | flops | bytes accessed | tf_op | source)
XLA Modules:
  0.0 47.2 jit_solution(2206871789526965490)
XLA Ops:
  0.6 4.1 %collective-permute-start = (bf16[32,2,8,128]{3,2,1,0:T(8,128)(2,1)}, bf16[32,2,8,128]{3,2,1,0:T(8,128)(2,1)S(1)}, u32[]{:S(2)}, u32[]{:S(2)}) collective-permute-start(bf16[32,2,8,128]{3,2,1,0:T(8,128)(2,1)} %x_hbm.1), channel_id=1, source_target_pairs={{0,4},{1,5},{2,6},{3,7},{4,0},{5,1},{6,2},{7,3},{8,12},{9,13},{10,... | collective-permute-start | bytes 393224 | tf_op jit(solution)/shard_map/ppermute | solution.py:448
  4.7 1.6 %collective-permute-start.3 = (bf16[32,2,8,128]{3,2,1,0:T(8,128)(2,1)}, bf16[32,2,8,128]{3,2,1,0:T(8,128)(2,1)S(1)}, u32[]{:S(2)}, u32[]{:S(2)}) collective-permute-start(bf16[32,2,8,128]{3,2,1,0:T(8,128)(2,1)} %x_hbm.1), channel_id=1, source_target_pairs={{0,2},{1,3},{2,0},{3,1},{4,6},{5,7},{6,4},{7,5},{8,10},{9,11},{10,... | collective-permute-start | bytes 393224 | tf_op jit(solution)/shard_map/ppermute | solution.py:448
  6.3 1.5 %prepare.1 = (bf16[32,2,8,128]{3,2,1,0:T(8,128)(2,1)S(1)}, bf16[16,32,128]{2,1,0:T(8,128)(2,1)S(1)}, bf16[8,32,128]{2,1,0:T(8,128)(2,1)S(1)}, bf16[8,32,128]{2,1...) custom-call(s32[1]{0:T(128)} %bitcast.1.slab_ref, ...), custom_call_target="tpu_custom_call" | custom-call | bytes 2441284 | tf_op jit(solution)/shard_map/prepare/pallas_call | solution.py:110
  7.8 1.6 %collective-permute-start.6 = (bf16[8,32,128]{2,1,0:T(8,128)(2,1)S(1)}, bf16[8,32,128]{2,1,0:T(8,128)(2,1)S(1)}, u32[]{:S(2)}, u32[]{:S(2)}) collective-permute-start(bf16[8,32,128]{2,1,0:T(8,128)(2,1)S(1)} %get-tuple-element.47), channel_id=1, source_target_pairs={{0,8},{8,0},{16,24},{24,16},{1,9},{9,1},{17,25},{25,17},{2,10},{10... | collective-permute-start | bytes 196616 | tf_op jit(solution)/shard_map/ppermute | solution.py:448
  9.4 1.5 %collective-permute-start.7 = (bf16[8,32,128]{2,1,0:T(8,128)(2,1)S(1)}, bf16[8,32,128]{2,1,0:T(8,128)(2,1)S(1)}, u32[]{:S(2)}, u32[]{:S(2)}) collective-permute-start(bf16[8,32,128]{2,1,0:T(8,128)(2,1)S(1)} %get-tuple-element.48), channel_id=1, source_target_pairs={{0,24},{8,16},{16,8},{24,0},{1,25},{9,17},{17,9},{25,1},{2,26},{10... | collective-permute-start | bytes 196616 | tf_op jit(solution)/shard_map/ppermute | solution.py:448
  12.4 2.1 %collective-permute-done.7.go_second_ref = bf16[8,32,128]{2,1,0:T(8,128)(2,1)S(1)} collective-permute-done((bf16[8,32,128]{2,1,0:T(8,128)(2,1)S(1)}, bf16[8,32,128]{2,1,0:T(8,128)(2,1)S(1)}, u32[]{:S(2)}, u32[]{:S(2)}) %collective-permute-start.7) | collective-permute-done | bytes 65568 | tf_op jit(solution)/shard_map/ppermute | solution.py:448
  15.0 1.7 %collective-permute-done.1.refs_3_ = bf16[32,2,8,128]{3,2,1,0:T(8,128)(2,1)S(1)} collective-permute-done((bf16[32,2,8,128]{3,2,1,0:T(8,128)(2,1)S(1)}, bf16[32,2,8,128]{3,2,1,0:T(8,128)(2,1)S(1)}, u32[]{:S(2)}, u32[]{:S(2)}) %collective-permute-start.1) | collective-permute-done | bytes 131104 | tf_op jit(solution)/shard_map/ppermute | solution.py:448
  16.8 0.7 %assemble.1.refs_1_ = bf16[256,2048]{1,0:T(8,128)(2,1)S(1)} custom-call(s32[1]{0:T(128)} %bitcast.me_ref, bf16[32,2,8,128]{3,2,1,0:T(8,128)(2,1)S(1)} %get-tuple-element.46.refs_0_, bf16[32,2,8,128]{3,2,1,0:T(8,128)(2,1)S(1)} %collective-permute-done.3.refs_1_, bf16[32,2,8,128]{3,2,1,0:T(8,128)(2,1)S(1)} %collective-permute-done.refs_2_, ...), custom_call_target="tpu_custom_call" | custom-call | flops 4000000000 | bytes 1966084 | tf_op jit(solution)/shard_map/assemble/pallas_call | solution.py:110
  18.1 1.3 %forward.1 = (f32[16,32,128]{2,1,0:T(8,128)S(1)}, bf16[8,32,128]{2,1,0:T(8,128)(2,1)S(1)}, bf16[8,32,128]{2,1,0:T(8,128)(2,1)S(1)}, bf16[8,32,128]{2,1,0:T(8,128...) custom-call(s32[1]{0:T(128)} %bitcast.me_ref, ...), custom_call_target="tpu_custom_call", output_to_operand_aliasing={{5}: (4, {})} | custom-call | flops 900000000 | bytes 3194888 | tf_op jit(solution)/shard_map/forward/pallas_call | solution.py:110
  19.4 1.6 %collective-permute-start.9 = (bf16[8,32,128]{2,1,0:T(8,128)(2,1)S(1)}, bf16[8,32,128]{2,1,0:T(8,128)(2,1)S(1)}, u32[]{:S(2)}, u32[]{:S(2)}) collective-permute-start(bf16[8,32,128]{2,1,0:T(8,128)(2,1)S(1)} %get-tuple-element.51.first_ref), channel_id=1, source_target_pairs={{0,8},{8,0},{16,24},{24,16},{1,9},{9,1},{17,25},{25,17},{2,10},{10... | collective-permute-start | bytes 196616 | tf_op jit(solution)/shard_map/ppermute | solution.py:448
  21.0 1.1 %collective-permute-start.10 = (bf16[8,32,128]{2,1,0:T(8,128)(2,1)S(1)}, bf16[8,32,128]{2,1,0:T(8,128)(2,1)S(1)}, u32[]{:S(2)}, u32[]{:S(2)}) collective-permute-start(bf16[8,32,128]{2,1,0:T(8,128)(2,1)S(1)} %get-tuple-element.52.second_ref), channel_id=1, source_target_pairs={{0,24},{8,16},{16,8},{24,0},{1,25},{9,17},{17,9},{25,1},{2,26},{10... | collective-permute-start | bytes 196616 | tf_op jit(solution)/shard_map/ppermute | solution.py:448
  22.1 1.5 %collective-permute-start.11 = (bf16[8,32,128]{2,1,0:T(8,128)(2,1)S(1)}, bf16[8,32,128]{2,1,0:T(8,128)(2,1)S(1)}, u32[]{:S(2)}, u32[]{:S(2)}) collective-permute-start(bf16[8,32,128]{2,1,0:T(8,128)(2,1)S(1)} %get-tuple-element.58), channel_id=1, source_target_pairs={{0,8},{8,0},{16,24},{24,16},{1,9},{9,1},{17,25},{25,17},{2,10},{10... | collective-permute-start | bytes 196616 | tf_op jit(solution)/shard_map/ppermute | solution.py:448
  23.5 0.9 %collective-permute-start.12 = (bf16[8,32,128]{2,1,0:T(8,128)(2,1)S(1)}, bf16[8,32,128]{2,1,0:T(8,128)(2,1)S(1)}, u32[]{:S(2)}, u32[]{:S(2)}) collective-permute-start(bf16[8,32,128]{2,1,0:T(8,128)(2,1)S(1)} %get-tuple-element.59), channel_id=1, source_target_pairs={{0,24},{8,16},{16,8},{24,0},{1,25},{9,17},{17,9},{25,1},{2,26},{10... | collective-permute-start | bytes 196616 | tf_op jit(solution)/shard_map/ppermute | solution.py:448
  24.4 2.1 %collective-permute-done.10.second_ref = bf16[8,32,128]{2,1,0:T(8,128)(2,1)S(1)} collective-permute-done((bf16[8,32,128]{2,1,0:T(8,128)(2,1)S(1)}, bf16[8,32,128]{2,1,0:T(8,128)(2,1)S(1)}, u32[]{:S(2)}, u32[]{:S(2)}) %collective-permute-start.10) | collective-permute-done | bytes 65568 | tf_op jit(solution)/shard_map/ppermute | solution.py:448
  26.5 1.6 %own_gradient.1 = (bf16[32,2,8,128]{3,2,1,0:T(8,128)(2,1)}, f32[32,128]{1,0:T(8,128)S(1)}, bf16[576,2048]{1,0:T(8,128)(2,1)S(1)}, f32[256,2048]{1,0:T(8,128)S(1)}) custom-call(s32[1]{0:T(128)} %bitcast.me_ref, s32[1]{0:T(128)} %bitcast.1.slab_ref, f32[16,32,128]{2,1,0:T(8,128)S(1)} %get-tuple-element.50.own_ref, ...), custom_call_target="tpu_custom_call" | custom-call | flops 603979776 | bytes 5734408 | tf_op jit(solution)/shard_map/own_gradient/pallas_call | solution.py:110
  28.1 0.8 %own_filter.1 = (f32[864,256]{1,0:T(8,128)S(1)}, f32[8,128]{1,0:T(8,128)S(1)}) custom-call(bf16[576,2048]{1,0:T(8,128)(2,1)S(1)} %get-tuple-element.65.s_ref, bf16[256,2048]{1,0:T(8,128)(2,1)S(1)} %get-tuple-element.66.x_ref), custom_call_target="tpu_custom_call" | custom-call | flops 603979776 | bytes 4296704 | tf_op jit(solution)/shard_map/own_filter/pallas_call | solution.py:110
  29.0 0.9 %rim_gradient.1 = (bf16[288,2048]{1,0:T(8,128)(2,1)S(1)}, bf16[4,16,32,128]{3,2,1,0:T(8,128)(2,1)S(1)}, bf16[4,16,32,128]{3,2,1,0:T(8,128)(2,1)S(1)}) custom-call(s32[1]{0:T(128)} %bitcast.me_ref, s32[1]{0:T(128)} %bitcast.1.slab_ref, bf16[8,32,128]{2,1,0:T(8,128)(2,1)S(1)} %get-tuple-element.51.first_ref, ...), custom_call_target="tpu_custom_call" | custom-call | flops 301989888 | bytes 5033992 | tf_op jit(solution)/shard_map/rim_gradient/pallas_call | solution.py:110
  30.5 1.4 %collective-permute-start.13 = (bf16[448,256]{1,0:T(8,128)(2,1)S(1)}, bf16[448,256]{1,0:T(8,128)(2,1)S(1)}, u32[]{:S(2)}, u32[]{:S(2)}) collective-permute-start(bf16[448,256]{1,0:T(8,128)(2,1)S(1)} %get-tuple-element.71.a_ref), channel_id=1, source_target_pairs={{0,8},{1,17},{2,10},{3,19},{4,12},{5,21},{6,14},{7,23},{8,0},{9,25... | collective-permute-start | bytes 688136 | tf_op jit(solution)/shard_map/ppermute | solution.py:458
  32.7 2.7 %collective-permute-start.18 = (bf16[16,32,128]{2,1,0:T(8,128)(2,1)S(1)}, bf16[16,32,128]{2,1,0:T(8,128)(2,1)S(1)}, u32[]{:S(2)}, u32[]{:S(2)}) collective-permute-start(bf16[16,32,128]{2,1,0:T(8,128)(2,1)S(1)} %get-tuple-element.76), channel_id=1, source_target_pairs={{0,4},{1,5},{2,6},{3,7},{4,0},{5,1},{6,2},{7,3},{8,12},{9,13},{10,... | collective-permute-start | bytes 393224 | tf_op jit(solution)/shard_map/ppermute | solution.py:448
  35.3 1.3 %collective-permute-start.19 = (bf16[16,32,128]{2,1,0:T(8,128)(2,1)S(1)}, bf16[16,32,128]{2,1,0:T(8,128)(2,1)S(1)}, u32[]{:S(2)}, u32[]{:S(2)}) collective-permute-start(bf16[16,32,128]{2,1,0:T(8,128)(2,1)S(1)} %get-tuple-element.77), channel_id=1, source_target_pairs={{0,6},{1,7},{2,4},{3,5},{4,2},{5,3},{6,0},{7,1},{8,14},{9,15},{10,... | collective-permute-start | bytes 393224 | tf_op jit(solution)/shard_map/ppermute | solution.py:448
  37.1 1.6 %collective-permute-start.15 = (bf16[448,256]{1,0:T(8,128)(2,1)S(1)}, bf16[448,256]{1,0:T(8,128)(2,1)S(1)}, u32[]{:S(2)}, u32[]{:S(2)}) collective-permute-start(bf16[448,256]{1,0:T(8,128)(2,1)S(1)} %pair_sum.2.a_ref), channel_id=1, source_target_pairs={{0,16},{1,9},{2,18},{3,11},{4,20},{5,13},{6,22},{7,15},{8,24},{9,1... | collective-permute-start | bytes 688136 | tf_op jit(solution)/shard_map/ppermute | solution.py:458
  39.1 1.5 %collective-permute-start.17 = (bf16[448,256]{1,0:T(8,128)(2,1)S(1)}, bf16[448,256]{1,0:T(8,128)(2,1)S(1)}, u32[]{:S(2)}, u32[]{:S(2)}) collective-permute-start(bf16[448,256]{1,0:T(8,128)(2,1)S(1)} %pair_sum.3.c_ref), channel_id=1, source_target_pairs={{0,16},{1,9},{2,18},{3,11},{4,20},{5,13},{6,22},{7,15},{8,24},{9,1... | collective-permute-start | bytes 688136 | tf_op jit(solution)/shard_map/ppermute | solution.py:458
  40.5 5.2 %collective-permute-done.18.b_ref = bf16[16,32,128]{2,1,0:T(8,128)(2,1)S(1)} collective-permute-done((bf16[16,32,128]{2,1,0:T(8,128)(2,1)S(1)}, bf16[16,32,128]{2,1,0:T(8,128)(2,1)S(1)}, u32[]{:S(2)}, u32[]{:S(2)}) %collective-permute-start.18) | collective-permute-done | bytes 131104 | tf_op jit(solution)/shard_map/ppermute | solution.py:448
  46.1 1.1 %last.1 = (f32[27,32,256]{2,1,0:T(8,128)}, f32[1,32]{1,0:T(1,128)}, bf16[32,2,8,128]{3,2,1,0:T(8,128)(2,1)}) custom-call(bf16[448,256]{1,0:T(8,128)(2,1)S(1)} %pair_sum.2.a_ref, bf16[448,256]{1,0:T(8,128)(2,1)S(1)} %collective-permute-done.15.b_ref, bf16[448,256]{1,0:T(8,128)(2,1)S(1)} %pair_sum.3.c_ref, bf16[448,256]{1,0:T(8,128)(2,1)S(1)} %collective-permute-done.17.d_ref, ...), custom_call_target="tpu_custom_call" | custom-call | bytes 2195584 | tf_op jit(solution)/shard_map/last/pallas_call | solution.py:110
  (30 shorter events, 5.4 us)
Async XLA Ops:
  0.6 10.7 %collective-permute-start = (bf16[32,2,8,128]{3,2,1,0:T(8,128)(2,1)}, bf16[32,2,8,128]{3,2,1,0:T(8,128)(2,1)S(1)}, u32[]{:S(2)}, u32[]{:S(2)}) collective-permute-start(bf16[32,2,8,128]{3,2,1,0:T(8,128)(2,1)} %x_hbm.1), channel_id=1, source_target_pairs={{0,4},{1,5},{2,6},{3,7},{4,0},{5,1},{6,2},{7,3},{8,12},{9,13},{10,... | collective-permute-start | bytes 393224 | tf_op jit(solution)/shard_map/ppermute | solution.py:448
  4.7 9.8 %collective-permute-start.3 = (bf16[32,2,8,128]{3,2,1,0:T(8,128)(2,1)}, bf16[32,2,8,128]{3,2,1,0:T(8,128)(2,1)S(1)}, u32[]{:S(2)}, u32[]{:S(2)}) collective-permute-start(bf16[32,2,8,128]{3,2,1,0:T(8,128)(2,1)} %x_hbm.1), channel_id=1, source_target_pairs={{0,2},{1,3},{2,0},{3,1},{4,6},{5,7},{6,4},{7,5},{8,10},{9,11},{10,... | collective-permute-start | bytes 393224 | tf_op jit(solution)/shard_map/ppermute | solution.py:448
  7.8 4.6 %collective-permute-start.6 = (bf16[8,32,128]{2,1,0:T(8,128)(2,1)S(1)}, bf16[8,32,128]{2,1,0:T(8,128)(2,1)S(1)}, u32[]{:S(2)}, u32[]{:S(2)}) collective-permute-start(bf16[8,32,128]{2,1,0:T(8,128)(2,1)S(1)} %get-tuple-element.47), channel_id=1, source_target_pairs={{0,8},{8,0},{16,24},{24,16},{1,9},{9,1},{17,25},{25,17},{2,10},{10... | collective-permute-start | bytes 196616 | tf_op jit(solution)/shard_map/ppermute | solution.py:448
  9.4 5.2 %collective-permute-start.7 = (bf16[8,32,128]{2,1,0:T(8,128)(2,1)S(1)}, bf16[8,32,128]{2,1,0:T(8,128)(2,1)S(1)}, u32[]{:S(2)}, u32[]{:S(2)}) collective-permute-start(bf16[8,32,128]{2,1,0:T(8,128)(2,1)S(1)} %get-tuple-element.48), channel_id=1, source_target_pairs={{0,24},{8,16},{16,8},{24,0},{1,25},{9,17},{17,9},{25,1},{2,26},{10... | collective-permute-start | bytes 196616 | tf_op jit(solution)/shard_map/ppermute | solution.py:448
  10.8 5.9 %collective-permute-start.4 = (bf16[32,2,8,128]{3,2,1,0:T(8,128)(2,1)}, bf16[32,2,8,128]{3,2,1,0:T(8,128)(2,1)S(1)}, u32[]{:S(2)}, u32[]{:S(2)}) collective-permute-start(bf16[32,2,8,128]{3,2,1,0:T(8,128)(2,1)} %x_hbm.1), channel_id=1, source_target_pairs={{0,1},{1,0},{2,3},{3,2},{4,5},{5,4},{6,7},{7,6},{8,9},{9,8},{10,11... | collective-permute-start | bytes 393224 | tf_op jit(solution)/shard_map/ppermute | solution.py:448
  11.4 5.4 %collective-permute-start.1 = (bf16[32,2,8,128]{3,2,1,0:T(8,128)(2,1)S(1)}, bf16[32,2,8,128]{3,2,1,0:T(8,128)(2,1)S(1)}, u32[]{:S(2)}, u32[]{:S(2)}) collective-permute-start(bf16[32,2,8,128]{3,2,1,0:T(8,128)(2,1)S(1)} %collective-permute-done.refs_2_), channel_id=1, source_target_pairs={{0,2},{1,3},{2,0},{3,1},{4,6},{5,7},{6,4},{7,5},{8,10},{9,11},{10,... | collective-permute-start | bytes 393224 | tf_op jit(solution)/shard_map/ppermute | solution.py:448
  14.5 2.2 %collective-permute-start.5 = (bf16[32,2,8,128]{3,2,1,0:T(8,128)(2,1)S(1)}, bf16[32,2,8,128]{3,2,1,0:T(8,128)(2,1)S(1)}, u32[]{:S(2)}, u32[]{:S(2)}) collective-permute-start(bf16[32,2,8,128]{3,2,1,0:T(8,128)(2,1)S(1)} %collective-permute-done.3.refs_1_), channel_id=1, source_target_pairs={{0,1},{1,0},{2,3},{3,2},{4,5},{5,4},{6,7},{7,6},{8,9},{9,8},{10,11... | collective-permute-start | bytes 393224 | tf_op jit(solution)/shard_map/ppermute | solution.py:448
  14.5 2.3 %collective-permute-start.8 = (bf16[32,2,8,128]{3,2,1,0:T(8,128)(2,1)S(1)}, bf16[32,2,8,128]{3,2,1,0:T(8,128)(2,1)S(1)}, u32[]{:S(2)}, u32[]{:S(2)}) collective-permute-start(bf16[32,2,8,128]{3,2,1,0:T(8,128)(2,1)S(1)} %collective-permute-done.refs_2_), channel_id=1, source_target_pairs={{0,1},{1,0},{2,3},{3,2},{4,5},{5,4},{6,7},{7,6},{8,9},{9,8},{10,11... | collective-permute-start | bytes 393224 | tf_op jit(solution)/shard_map/ppermute | solution.py:448
  16.8 1.3 %collective-permute-start.2 = (bf16[32,2,8,128]{3,2,1,0:T(8,128)(2,1)S(1)}, bf16[32,2,8,128]{3,2,1,0:T(8,128)(2,1)S(1)}, u32[]{:S(2)}, u32[]{:S(2)}) collective-permute-start(bf16[32,2,8,128]{3,2,1,0:T(8,128)(2,1)S(1)} %collective-permute-done.1.refs_3_), channel_id=1, source_target_pairs={{0,1},{1,0},{2,3},{3,2},{4,5},{5,4},{6,7},{7,6},{8,9},{9,8},{10,11... | collective-permute-start | bytes 393224 | tf_op jit(solution)/shard_map/ppermute | solution.py:448
  19.4 5.0 %collective-permute-start.9 = (bf16[8,32,128]{2,1,0:T(8,128)(2,1)S(1)}, bf16[8,32,128]{2,1,0:T(8,128)(2,1)S(1)}, u32[]{:S(2)}, u32[]{:S(2)}) collective-permute-start(bf16[8,32,128]{2,1,0:T(8,128)(2,1)S(1)} %get-tuple-element.51.first_ref), channel_id=1, source_target_pairs={{0,8},{8,0},{16,24},{24,16},{1,9},{9,1},{17,25},{25,17},{2,10},{10... | collective-permute-start | bytes 196616 | tf_op jit(solution)/shard_map/ppermute | solution.py:448
  21.0 5.5 %collective-permute-start.10 = (bf16[8,32,128]{2,1,0:T(8,128)(2,1)S(1)}, bf16[8,32,128]{2,1,0:T(8,128)(2,1)S(1)}, u32[]{:S(2)}, u32[]{:S(2)}) collective-permute-start(bf16[8,32,128]{2,1,0:T(8,128)(2,1)S(1)} %get-tuple-element.52.second_ref), channel_id=1, source_target_pairs={{0,24},{8,16},{16,8},{24,0},{1,25},{9,17},{17,9},{25,1},{2,26},{10... | collective-permute-start | bytes 196616 | tf_op jit(solution)/shard_map/ppermute | solution.py:448
  22.1 6.9 %collective-permute-start.11 = (bf16[8,32,128]{2,1,0:T(8,128)(2,1)S(1)}, bf16[8,32,128]{2,1,0:T(8,128)(2,1)S(1)}, u32[]{:S(2)}, u32[]{:S(2)}) collective-permute-start(bf16[8,32,128]{2,1,0:T(8,128)(2,1)S(1)} %get-tuple-element.58), channel_id=1, source_target_pairs={{0,8},{8,0},{16,24},{24,16},{1,9},{9,1},{17,25},{25,17},{2,10},{10... | collective-permute-start | bytes 196616 | tf_op jit(solution)/shard_map/ppermute | solution.py:448
  23.5 5.4 %collective-permute-start.12 = (bf16[8,32,128]{2,1,0:T(8,128)(2,1)S(1)}, bf16[8,32,128]{2,1,0:T(8,128)(2,1)S(1)}, u32[]{:S(2)}, u32[]{:S(2)}) collective-permute-start(bf16[8,32,128]{2,1,0:T(8,128)(2,1)S(1)} %get-tuple-element.59), channel_id=1, source_target_pairs={{0,24},{8,16},{16,8},{24,0},{1,25},{9,17},{17,9},{25,1},{2,26},{10... | collective-permute-start | bytes 196616 | tf_op jit(solution)/shard_map/ppermute | solution.py:448
  29.9 2.7 %collective-permute-start.14 = (bf16[4,16,32,128]{3,2,1,0:T(8,128)(2,1)S(1)}, bf16[4,16,32,128]{3,2,1,0:T(8,128)(2,1)S(1)}, u32[]{:S(2)}, u32[]{:S(2)}) collective-permute-start(bf16[4,16,32,128]{3,2,1,0:T(8,128)(2,1)S(1)} %get-tuple-element.73), channel_id=1, source_target_pairs={{0,1},{1,0},{2,3},{3,2},{4,5},{5,4},{6,7},{7,6},{8,9},{9,8},{10,11... | collective-permute-start | bytes 1572872 | tf_op jit(solution)/shard_map/ppermute | solution.py:448
  30.5 6.6 %collective-permute-start.13 = (bf16[448,256]{1,0:T(8,128)(2,1)S(1)}, bf16[448,256]{1,0:T(8,128)(2,1)S(1)}, u32[]{:S(2)}, u32[]{:S(2)}) collective-permute-start(bf16[448,256]{1,0:T(8,128)(2,1)S(1)} %get-tuple-element.71.a_ref), channel_id=1, source_target_pairs={{0,8},{1,17},{2,10},{3,19},{4,12},{5,21},{6,14},{7,23},{8,0},{9,25... | collective-permute-start | bytes 688136 | tf_op jit(solution)/shard_map/ppermute | solution.py:458
  31.9 7.1 %collective-permute-start.16 = (bf16[448,256]{1,0:T(8,128)(2,1)S(1)}, bf16[448,256]{1,0:T(8,128)(2,1)S(1)}, u32[]{:S(2)}, u32[]{:S(2)}) collective-permute-start(bf16[448,256]{1,0:T(8,128)(2,1)S(1)} %get-tuple-element.75.a_ref), channel_id=1, source_target_pairs={{0,8},{1,17},{2,10},{3,19},{4,12},{5,21},{6,14},{7,23},{8,0},{9,25... | collective-permute-start | bytes 688136 | tf_op jit(solution)/shard_map/ppermute | solution.py:458
  32.7 13.0 %collective-permute-start.18 = (bf16[16,32,128]{2,1,0:T(8,128)(2,1)S(1)}, bf16[16,32,128]{2,1,0:T(8,128)(2,1)S(1)}, u32[]{:S(2)}, u32[]{:S(2)}) collective-permute-start(bf16[16,32,128]{2,1,0:T(8,128)(2,1)S(1)} %get-tuple-element.76), channel_id=1, source_target_pairs={{0,4},{1,5},{2,6},{3,7},{4,0},{5,1},{6,2},{7,3},{8,12},{9,13},{10,... | collective-permute-start | bytes 393224 | tf_op jit(solution)/shard_map/ppermute | solution.py:448
  35.3 10.4 %collective-permute-start.19 = (bf16[16,32,128]{2,1,0:T(8,128)(2,1)S(1)}, bf16[16,32,128]{2,1,0:T(8,128)(2,1)S(1)}, u32[]{:S(2)}, u32[]{:S(2)}) collective-permute-start(bf16[16,32,128]{2,1,0:T(8,128)(2,1)S(1)} %get-tuple-element.77), channel_id=1, source_target_pairs={{0,6},{1,7},{2,4},{3,5},{4,2},{5,3},{6,0},{7,1},{8,14},{9,15},{10,... | collective-permute-start | bytes 393224 | tf_op jit(solution)/shard_map/ppermute | solution.py:448
  36.6 9.4 %collective-permute-start.20 = (bf16[16,32,128]{2,1,0:T(8,128)(2,1)S(1)}, bf16[16,32,128]{2,1,0:T(8,128)(2,1)S(1)}, u32[]{:S(2)}, u32[]{:S(2)}) collective-permute-start(bf16[16,32,128]{2,1,0:T(8,128)(2,1)S(1)} %get-tuple-element.78), channel_id=1, source_target_pairs={{0,2},{1,3},{2,0},{3,1},{4,6},{5,7},{6,4},{7,5},{8,10},{9,11},{10,... | collective-permute-start | bytes 393224 | tf_op jit(solution)/shard_map/ppermute | solution.py:448
  37.1 9.0 %collective-permute-start.15 = (bf16[448,256]{1,0:T(8,128)(2,1)S(1)}, bf16[448,256]{1,0:T(8,128)(2,1)S(1)}, u32[]{:S(2)}, u32[]{:S(2)}) collective-permute-start(bf16[448,256]{1,0:T(8,128)(2,1)S(1)} %pair_sum.2.a_ref), channel_id=1, source_target_pairs={{0,16},{1,9},{2,18},{3,11},{4,20},{5,13},{6,22},{7,15},{8,24},{9,1... | collective-permute-start | bytes 688136 | tf_op jit(solution)/shard_map/ppermute | solution.py:458
  39.1 7.0 %collective-permute-start.17 = (bf16[448,256]{1,0:T(8,128)(2,1)S(1)}, bf16[448,256]{1,0:T(8,128)(2,1)S(1)}, u32[]{:S(2)}, u32[]{:S(2)}) collective-permute-start(bf16[448,256]{1,0:T(8,128)(2,1)S(1)} %pair_sum.3.c_ref), channel_id=1, source_target_pairs={{0,16},{1,9},{2,18},{3,11},{4,20},{5,13},{6,22},{7,15},{8,24},{9,1... | collective-permute-start | bytes 688136 | tf_op jit(solution)/shard_map/ppermute | solution.py:458

commit v18 on v17

--- a/solution.py
+++ b/solution.py
@@ -9,7 +9,6 @@
 from jax.sharding import PartitionSpec as P
 
 LANES = 128
-FORWARD_FLOPS = 9 * 10**8
 SUM_FLOPS = 24 * 10**8
 ASSEMBLE_FLOPS = 40 * 10**8
 VMEM = pl.BlockSpec(memory_space=pltpu.VMEM)
@@ -218,38 +217,59 @@
     return jnp.bitwise_xor(me_ref[0], 2 * (b % 4) + b // 4)
 
 
-def forward_body(n, rows, o, places, me_ref, slab_ref, w_ref, *refs):
-    blocks = refs[: len(places)]
-    own_ref, *sent, x_ref, acc, wide_ref = refs[len(places) + 1 :]
-    for b, block in zip(places, blocks):
-        place_block(me_ref, b, block, x_ref, wide_ref)
-    w = w_ref[...]
+def plane_sums(rows, o, w_ref, x_ref, acc, chosen):
     seen = set()
-    for p in range(n):
+    for p in range(2):
+        near = [i for i in range(3) if (p, i) in chosen]
+        base = 9 * near[0]
+        w = w_ref[base * o : 9 * (near[-1] + 1) * o]
         for t in range(0, rows, 2):
             at = (p * rows + t) * LANES
             part = jnp.dot(
                 w, x_ref[:, at : at + 2 * LANES], preferred_element_type=jnp.float32
             )
             for k, i, j, l in tap_list():
+                if i not in near:
+                    continue
                 for h in range(2):
-                    slot = (l, p + 2 - i, (t + h + 1 - j) % rows)
-                    value = part[k * o : (k + 1) * o, h * LANES : (h + 1) * LANES]
+                    slot = (l, chosen[p, i], (t + h + 1 - j) % rows)
+                    value = part[(k - base) * o : (k - base + 1) * o, h * LANES : (h + 1) * LANES]
                     if slot in seen:
                         acc[slot] += value
                     else:
                         acc[slot] = value
                         seen.add(slot)
+    return [
+        [
+            pltpu.roll(acc[0, q, y], 1, 1) + acc[1, q, y] + pltpu.roll(acc[2, q, y], LANES - 1, 1)
+            for y in range(rows)
+        ]
+        for q in range(2)
+    ]
+
+
+def send_sums(slab_ref, sums, refs):
+    for y, (low, high) in enumerate(zip(*sums)):
+        for ref, value in zip(refs, by_parity(slab_ref, high, low)):
+            ref[y] = value.astype(ref.dtype)
+
+
+def rim_forward_body(
+    rows, o, place, me_ref, slab_ref, w_ref, block_ref, _, first_ref, second_ref, x_ref, acc, wide_ref
+):
+    place_block(me_ref, place, block_ref, x_ref, wide_ref)
+    sums = plane_sums(rows, o, w_ref, x_ref, acc, {(0, 2): 0, (1, 0): 1})
+    send_sums(slab_ref, sums, (first_ref, second_ref))
+
+
+def own_forward_body(rows, o, slab_ref, w_ref, x_ref, own_ref, first_ref, second_ref, acc):
+    sums = plane_sums(
+        rows, o, w_ref, x_ref, acc, {(0, 0): 1, (0, 1): 0, (1, 1): 1, (1, 2): 0}
+    )
     for y in range(rows):
-        totals = [
-            pltpu.roll(acc[0, q, y], 1, 1) + acc[1, q, y] + pltpu.roll(acc[2, q, y], LANES - 1, 1)
-            for q in range(n + 2)
-        ]
-        for p in range(n):
-            own_ref[p * rows + y] = totals[p + 1]
-        for pair, low, high in ((sent[:2], 0, n + 1), (sent[2:], 1, n)):
-            for ref, value in zip(pair, by_parity(slab_ref, totals[high], totals[low])):
-                ref[y] = value.astype(ref.dtype)
+        own_ref[y] = sums[0][y]
+        own_ref[rows + y] = sums[1][y]
+    send_sums(slab_ref, sums, (first_ref, second_ref))
 
 
 def ordered(me_ref, o, in_refs, out_refs):
@@ -502,7 +522,7 @@
     late_b, go_first, go_second = lax.optimization_barrier((x_b, go_first, go_second))
     x_a_side = swap(x_a, "chan", 1)
     x_b_side = swap(late_b, "chan", 1)
-    early, late = (0, 1, 2, 3, 4, 5, 6), (7,)
+    early = (0, 1, 2, 3, 4, 5, 6)
     (x_all,) = call(
         functools.partial(assemble_body, early),
         [shape_of((c_all, cells * depth), bf16)],
@@ -513,20 +533,27 @@
         name="assemble",
     )
     x_ab_side = swap(x_ab, "chan", 1)
-    own, *sent, x_all = call(
-        functools.partial(forward_body, n, rows, o, late),
-        [
-            shape_of((cells, o, depth), f32),
-            *[shape_of((rows, o, depth), bf16)] * 4,
-            shape_of((c_all, cells * depth), bf16),
-        ],
+    sums = [pltpu.VMEM((3, 2, rows, o, depth), f32)]
+    *sent, x_all = call(
+        functools.partial(rim_forward_body, rows, o, 7),
+        [shape_of((rows, o, depth), bf16)] * 2 + [shape_of((c_all, cells * depth), bf16)],
         [me, slab, w_flat, x_ab_side, x_all],
         [SMEM] * 2 + [VMEM] * 3,
-        [pltpu.VMEM((3, n + 2, rows, o, depth), f32), *block_wide],
-        flops=FORWARD_FLOPS,
-        name="forward",
-        aliases={4: 5},
-    )
+        sums + block_wide,
+        flops=flops // 3,
+        name="rim_forward",
+        aliases={4: 2},
+    )
+    own, *sent_own = call(
+        functools.partial(own_forward_body, rows, o),
+        [shape_of((cells, o, depth), f32)] + [shape_of((rows, o, depth), bf16)] * 2,
+        [slab, w_flat, x_all],
+        [SMEM] + [VMEM] * 2,
+        sums,
+        flops=flops * 2 // 3,
+        name="own_forward",
+    )
+    sent += sent_own
     received = [swap(a, "slab", 1 + 2 * (at % 2)) for at, a in enumerate(sent)]
     act, total, own_shifts, partial = call(
         functools.partial(own_gradient_body, rows, o, scale),

time: 47.5 us -> 47.7 us (level)
  starting transfers between devices: 24.6 us -> 23.3 us
  waiting for transfers between devices: 13.2 us -> 14.3 us
    ppermute x4, starting transfers between devices: 5.14 us -> 3.77 us  [cross(): return lax.ppermute(value, ('slab', 'chan'), pairs)]
    ppermute x4, waiting for transfers between devices: 0.29 us -> 1.1 us  [cross(): return lax.ppermute(value, ('slab', 'chan'), pairs)]
    pallas_call x12 -> x13, Pallas kernels: 8.74 us -> 8.98 us  [call(): pl.pallas_call(body, out_shape=out_shape, in_specs=specs or [VMEM] * len(...]
  transfers between devices with their start and end apart: 21 -> 21, of which waited for: 9 -> 10; matrix products, arithmetic and copies ran while one was open for 0% -> 0% of each run, Pallas kernels for 11% -> 13%
where the time goes in v18:
time: 47.7 us; the launch traced here: 47.3 us
  starting transfers between devices  23.3 us (49%)
  waiting for transfers between devices  14.3 us (30%)
  Pallas kernels  8.98 us (19%)
  between operations  0.76 us (2%)
    ppermute x17, starting transfers between devices, swap(): lax.ppermute(value, axis, [(i, i ^ bit) for i in range(lax.axis_size(axis...  19.6 us
    ppermute x17, waiting for transfers between devices, swap(): lax.ppermute(value, axis, [(i, i ^ bit) for i in range(lax.axis_size(axis...  13.2 us
    pallas_call x13, Pallas kernels, call(): pl.pallas_call(body, out_shape=out_shape, in_specs=specs or [VMEM] * len(...  8.98 us
    ppermute x4, starting transfers between devices, cross(): return lax.ppermute(value, ('slab', 'chan'), pairs)  3.77 us
    ppermute x4, waiting for transfers between devices, cross(): return lax.ppermute(value, ('slab', 'chan'), pairs)  1.1 us
  transfers between devices with their start and end apart: 21, of which 10 were waited for; matrix products, arithmetic and copies ran while one was open for 0% of the time, Pallas kernels for 13%

profile of v18, /device:TPU:0, one launch (start us, length us, event | category | flops | bytes accessed | tf_op | source)
XLA Modules:
  0.0 47.3 jit_solution(6350211110282005427)
XLA Ops:
  0.6 4.1 %collective-permute-start = (bf16[32,2,8,128]{3,2,1,0:T(8,128)(2,1)}, bf16[32,2,8,128]{3,2,1,0:T(8,128)(2,1)S(1)}, u32[]{:S(2)}, u32[]{:S(2)}) collective-permute-start(bf16[32,2,8,128]{3,2,1,0:T(8,128)(2,1)} %x_hbm.1), channel_id=1, source_target_pairs={{0,4},{1,5},{2,6},{3,7},{4,0},{5,1},{6,2},{7,3},{8,12},{9,13},{10,... | collective-permute-start | bytes 393224 | tf_op jit(solution)/shard_map/ppermute | solution.py:468
  4.7 1.6 %collective-permute-start.3 = (bf16[32,2,8,128]{3,2,1,0:T(8,128)(2,1)}, bf16[32,2,8,128]{3,2,1,0:T(8,128)(2,1)S(1)}, u32[]{:S(2)}, u32[]{:S(2)}) collective-permute-start(bf16[32,2,8,128]{3,2,1,0:T(8,128)(2,1)} %x_hbm.1), channel_id=1, source_target_pairs={{0,2},{1,3},{2,0},{3,1},{4,6},{5,7},{6,4},{7,5},{8,10},{9,11},{10,... | collective-permute-start | bytes 393224 | tf_op jit(solution)/shard_map/ppermute | solution.py:468
  6.3 1.5 %prepare.1 = (bf16[32,2,8,128]{3,2,1,0:T(8,128)(2,1)S(1)}, bf16[16,32,128]{2,1,0:T(8,128)(2,1)S(1)}, bf16[8,32,128]{2,1,0:T(8,128)(2,1)S(1)}, bf16[8,32,128]{2,1...) custom-call(s32[1]{0:T(128)} %bitcast.1.slab_ref, ...), custom_call_target="tpu_custom_call" | custom-call | bytes 2441284 | tf_op jit(solution)/shard_map/prepare/pallas_call | solution.py:109
  7.8 1.6 %collective-permute-start.6 = (bf16[8,32,128]{2,1,0:T(8,128)(2,1)S(1)}, bf16[8,32,128]{2,1,0:T(8,128)(2,1)S(1)}, u32[]{:S(2)}, u32[]{:S(2)}) collective-permute-start(bf16[8,32,128]{2,1,0:T(8,128)(2,1)S(1)} %get-tuple-element.47), channel_id=1, source_target_pairs={{0,8},{8,0},{16,24},{24,16},{1,9},{9,1},{17,25},{25,17},{2,10},{10... | collective-permute-start | bytes 196616 | tf_op jit(solution)/shard_map/ppermute | solution.py:468
  9.4 1.5 %collective-permute-start.7 = (bf16[8,32,128]{2,1,0:T(8,128)(2,1)S(1)}, bf16[8,32,128]{2,1,0:T(8,128)(2,1)S(1)}, u32[]{:S(2)}, u32[]{:S(2)}) collective-permute-start(bf16[8,32,128]{2,1,0:T(8,128)(2,1)S(1)} %get-tuple-element.48), channel_id=1, source_target_pairs={{0,24},{8,16},{16,8},{24,0},{1,25},{9,17},{17,9},{25,1},{2,26},{10... | collective-permute-start | bytes 196616 | tf_op jit(solution)/shard_map/ppermute | solution.py:468
  12.4 2.1 %collective-permute-done.7.go_second_ref = bf16[8,32,128]{2,1,0:T(8,128)(2,1)S(1)} collective-permute-done((bf16[8,32,128]{2,1,0:T(8,128)(2,1)S(1)}, bf16[8,32,128]{2,1,0:T(8,128)(2,1)S(1)}, u32[]{:S(2)}, u32[]{:S(2)}) %collective-permute-start.7) | collective-permute-done | bytes 65568 | tf_op jit(solution)/shard_map/ppermute | solution.py:468
  15.0 1.7 %collective-permute-done.1.refs_3_ = bf16[32,2,8,128]{3,2,1,0:T(8,128)(2,1)S(1)} collective-permute-done((bf16[32,2,8,128]{3,2,1,0:T(8,128)(2,1)S(1)}, bf16[32,2,8,128]{3,2,1,0:T(8,128)(2,1)S(1)}, u32[]{:S(2)}, u32[]{:S(2)}) %collective-permute-start.1) | collective-permute-done | bytes 131104 | tf_op jit(solution)/shard_map/ppermute | solution.py:468
  16.8 0.7 %assemble.1._ = bf16[256,2048]{1,0:T(8,128)(2,1)S(1)} custom-call(s32[1]{0:T(128)} %bitcast.me_ref, bf16[32,2,8,128]{3,2,1,0:T(8,128)(2,1)S(1)} %get-tuple-element.46.refs_0_, bf16[32,2,8,128]{3,2,1,0:T(8,128)(2,1)S(1)} %collective-permute-done.3.refs_1_, bf16[32,2,8,128]{3,2,1,0:T(8,128)(2,1)S(1)} %collective-permute-done.refs_2_, ...), custom_call_target="tpu_custom_call" | custom-call | flops 4000000000 | bytes 1966084 | tf_op jit(solution)/shard_map/assemble/pallas_call | solution.py:109
  18.8 1.6 %collective-permute-start.9 = (bf16[8,32,128]{2,1,0:T(8,128)(2,1)S(1)}, bf16[8,32,128]{2,1,0:T(8,128)(2,1)S(1)}, u32[]{:S(2)}, u32[]{:S(2)}) collective-permute-start(bf16[8,32,128]{2,1,0:T(8,128)(2,1)S(1)} %get-tuple-element.52.first_ref), channel_id=1, source_target_pairs={{0,8},{8,0},{16,24},{24,16},{1,9},{9,1},{17,25},{25,17},{2,10},{10... | collective-permute-start | bytes 196616 | tf_op jit(solution)/shard_map/ppermute | solution.py:468
  20.3 1.1 %collective-permute-start.10 = (bf16[8,32,128]{2,1,0:T(8,128)(2,1)S(1)}, bf16[8,32,128]{2,1,0:T(8,128)(2,1)S(1)}, u32[]{:S(2)}, u32[]{:S(2)}) collective-permute-start(bf16[8,32,128]{2,1,0:T(8,128)(2,1)S(1)} %get-tuple-element.53.second_ref), channel_id=1, source_target_pairs={{0,24},{8,16},{16,8},{24,0},{1,25},{9,17},{17,9},{25,1},{2,26},{10... | collective-permute-start | bytes 196616 | tf_op jit(solution)/shard_map/ppermute | solution.py:468
  21.4 0.9 %own_forward.1 = (f32[16,32,128]{2,1,0:T(8,128)S(1)}, bf16[8,32,128]{2,1,0:T(8,128)(2,1)S(1)}, bf16[8,32,128]{2,1,0:T(8,128)(2,1)S(1)}) custom-call(s32[1]{0:T(128)} %bitcast.1.slab_ref, bf16[864,256]{1,0:T(8,128)(2,1)S(1)} %get-tuple-element.44.w_ref, bf16[256,2048]{1,0:T(8,128)(2,1)S(1)} %get-tuple-element.50.x_ref), custom_call_target="tpu_custom_call" | custom-call | flops 603979776 | bytes 1884164 | tf_op jit(solution)/shard_map/own_forward/pallas_call | solution.py:109
  22.3 1.6 %collective-permute-start.11 = (bf16[8,32,128]{2,1,0:T(8,128)(2,1)S(1)}, bf16[8,32,128]{2,1,0:T(8,128)(2,1)S(1)}, u32[]{:S(2)}, u32[]{:S(2)}) collective-permute-start(bf16[8,32,128]{2,1,0:T(8,128)(2,1)S(1)} %get-tuple-element.59), channel_id=1, source_target_pairs={{0,8},{8,0},{16,24},{24,16},{1,9},{9,1},{17,25},{25,17},{2,10},{10... | collective-permute-start | bytes 196616 | tf_op jit(solution)/shard_map/ppermute | solution.py:468
  23.9 0.9 %collective-permute-start.12 = (bf16[8,32,128]{2,1,0:T(8,128)(2,1)S(1)}, bf16[8,32,128]{2,1,0:T(8,128)(2,1)S(1)}, u32[]{:S(2)}, u32[]{:S(2)}) collective-permute-start(bf16[8,32,128]{2,1,0:T(8,128)(2,1)S(1)} %get-tuple-element.60), channel_id=1, source_target_pairs={{0,24},{8,16},{16,8},{24,0},{1,25},{9,17},{17,9},{25,1},{2,26},{10... | collective-permute-start | bytes 196616 | tf_op jit(solution)/shard_map/ppermute | solution.py:468
  24.8 1.4 %collective-permute-done.10.second_ref = bf16[8,32,128]{2,1,0:T(8,128)(2,1)S(1)} collective-permute-done((bf16[8,32,128]{2,1,0:T(8,128)(2,1)S(1)}, bf16[8,32,128]{2,1,0:T(8,128)(2,1)S(1)}, u32[]{:S(2)}, u32[]{:S(2)}) %collective-permute-start.10) | collective-permute-done | bytes 65568 | tf_op jit(solution)/shard_map/ppermute | solution.py:468
  26.1 1.6 %own_gradient.1 = (bf16[32,2,8,128]{3,2,1,0:T(8,128)(2,1)}, f32[32,128]{1,0:T(8,128)S(1)}, bf16[576,2048]{1,0:T(8,128)(2,1)S(1)}, f32[256,2048]{1,0:T(8,128)S(1)}) custom-call(s32[1]{0:T(128)} %bitcast.me_ref, s32[1]{0:T(128)} %bitcast.1.slab_ref, f32[16,32,128]{2,1,0:T(8,128)S(1)} %get-tuple-element.51.own_ref, ...), custom_call_target="tpu_custom_call" | custom-call | flops 603979776 | bytes 5734408 | tf_op jit(solution)/shard_map/own_gradient/pallas_call | solution.py:109
  27.7 0.8 %own_filter.1 = (f32[864,256]{1,0:T(8,128)S(1)}, f32[8,128]{1,0:T(8,128)S(1)}) custom-call(bf16[576,2048]{1,0:T(8,128)(2,1)S(1)} %get-tuple-element.66.s_ref, bf16[256,2048]{1,0:T(8,128)(2,1)S(1)} %get-tuple-element.50.x_ref), custom_call_target="tpu_custom_call" | custom-call | flops 603979776 | bytes 4296704 | tf_op jit(solution)/shard_map/own_filter/pallas_call | solution.py:109
  29.0 0.9 %rim_gradient.1 = (bf16[288,2048]{1,0:T(8,128)(2,1)S(1)}, bf16[4,16,32,128]{3,2,1,0:T(8,128)(2,1)S(1)}, bf16[4,16,32,128]{3,2,1,0:T(8,128)(2,1)S(1)}) custom-call(s32[1]{0:T(128)} %bitcast.me_ref, s32[1]{0:T(128)} %bitcast.1.slab_ref, bf16[8,32,128]{2,1,0:T(8,128)(2,1)S(1)} %get-tuple-element.52.first_ref, ...), custom_call_target="tpu_custom_call" | custom-call | flops 301989888 | bytes 5033992 | tf_op jit(solution)/shard_map/rim_gradient/pallas_call | solution.py:109
  31.1 1.5 %collective-permute-start.16 = (bf16[448,256]{1,0:T(8,128)(2,1)S(1)}, bf16[448,256]{1,0:T(8,128)(2,1)S(1)}, u32[]{:S(2)}, u32[]{:S(2)}) collective-permute-start(bf16[448,256]{1,0:T(8,128)(2,1)S(1)} %get-tuple-element.75.a_ref), channel_id=1, source_target_pairs={{0,8},{1,17},{2,10},{3,19},{4,12},{5,21},{6,14},{7,23},{8,0},{9,25... | collective-permute-start | bytes 688136 | tf_op jit(solution)/shard_map/ppermute | solution.py:478
  32.8 2.7 %collective-permute-start.18 = (bf16[16,32,128]{2,1,0:T(8,128)(2,1)S(1)}, bf16[16,32,128]{2,1,0:T(8,128)(2,1)S(1)}, u32[]{:S(2)}, u32[]{:S(2)}) collective-permute-start(bf16[16,32,128]{2,1,0:T(8,128)(2,1)S(1)} %get-tuple-element.76), channel_id=1, source_target_pairs={{0,4},{1,5},{2,6},{3,7},{4,0},{5,1},{6,2},{7,3},{8,12},{9,13},{10,... | collective-permute-start | bytes 393224 | tf_op jit(solution)/shard_map/ppermute | solution.py:468
  35.5 1.3 %collective-permute-start.19 = (bf16[16,32,128]{2,1,0:T(8,128)(2,1)S(1)}, bf16[16,32,128]{2,1,0:T(8,128)(2,1)S(1)}, u32[]{:S(2)}, u32[]{:S(2)}) collective-permute-start(bf16[16,32,128]{2,1,0:T(8,128)(2,1)S(1)} %get-tuple-element.77), channel_id=1, source_target_pairs={{0,6},{1,7},{2,4},{3,5},{4,2},{5,3},{6,0},{7,1},{8,14},{9,15},{10,... | collective-permute-start | bytes 393224 | tf_op jit(solution)/shard_map/ppermute | solution.py:468
  38.0 1.1 %collective-permute-done.16.b_ref = bf16[448,256]{1,0:T(8,128)(2,1)S(1)} collective-permute-done((bf16[448,256]{1,0:T(8,128)(2,1)S(1)}, bf16[448,256]{1,0:T(8,128)(2,1)S(1)}, u32[]{:S(2)}, u32[]{:S(2)}) %collective-permute-start.16) | collective-permute-done | bytes 229408 | tf_op jit(solution)/shard_map/ppermute | solution.py:478
  39.1 1.0 %collective-permute-start.17 = (bf16[448,256]{1,0:T(8,128)(2,1)S(1)}, bf16[448,256]{1,0:T(8,128)(2,1)S(1)}, u32[]{:S(2)}, u32[]{:S(2)}) collective-permute-start(bf16[448,256]{1,0:T(8,128)(2,1)S(1)} %pair_sum.3.c_ref), channel_id=1, source_target_pairs={{0,16},{1,9},{2,18},{3,11},{4,20},{5,13},{6,22},{7,15},{8,24},{9,1... | collective-permute-start | bytes 688136 | tf_op jit(solution)/shard_map/ppermute | solution.py:478
  40.1 5.6 %collective-permute-done.18.b_ref = bf16[16,32,128]{2,1,0:T(8,128)(2,1)S(1)} collective-permute-done((bf16[16,32,128]{2,1,0:T(8,128)(2,1)S(1)}, bf16[16,32,128]{2,1,0:T(8,128)(2,1)S(1)}, u32[]{:S(2)}, u32[]{:S(2)}) %collective-permute-start.18) | collective-permute-done | bytes 131104 | tf_op jit(solution)/shard_map/ppermute | solution.py:468
  46.2 1.1 %last.1 = (f32[27,32,256]{2,1,0:T(8,128)}, f32[1,32]{1,0:T(1,128)}, bf16[32,2,8,128]{3,2,1,0:T(8,128)(2,1)}) custom-call(bf16[448,256]{1,0:T(8,128)(2,1)S(1)} %pair_sum.2.a_ref, bf16[448,256]{1,0:T(8,128)(2,1)S(1)} %collective-permute-done.15.b_ref, bf16[448,256]{1,0:T(8,128)(2,1)S(1)} %pair_sum.3.c_ref, bf16[448,256]{1,0:T(8,128)(2,1)S(1)} %collective-permute-done.17.d_ref, ...), custom_call_target="tpu_custom_call" | custom-call | bytes 2195584 | tf_op jit(solution)/shard_map/last/pallas_call | solution.py:109
  (31 shorter events, 6.9 us)
Async XLA Ops:
  0.6 10.7 %collective-permute-start = (bf16[32,2,8,128]{3,2,1,0:T(8,128)(2,1)}, bf16[32,2,8,128]{3,2,1,0:T(8,128)(2,1)S(1)}, u32[]{:S(2)}, u32[]{:S(2)}) collective-permute-start(bf16[32,2,8,128]{3,2,1,0:T(8,128)(2,1)} %x_hbm.1), channel_id=1, source_target_pairs={{0,4},{1,5},{2,6},{3,7},{4,0},{5,1},{6,2},{7,3},{8,12},{9,13},{10,... | collective-permute-start | bytes 393224 | tf_op jit(solution)/shard_map/ppermute | solution.py:468
  4.7 9.8 %collective-permute-start.3 = (bf16[32,2,8,128]{3,2,1,0:T(8,128)(2,1)}, bf16[32,2,8,128]{3,2,1,0:T(8,128)(2,1)S(1)}, u32[]{:S(2)}, u32[]{:S(2)}) collective-permute-start(bf16[32,2,8,128]{3,2,1,0:T(8,128)(2,1)} %x_hbm.1), channel_id=1, source_target_pairs={{0,2},{1,3},{2,0},{3,1},{4,6},{5,7},{6,4},{7,5},{8,10},{9,11},{10,... | collective-permute-start | bytes 393224 | tf_op jit(solution)/shard_map/ppermute | solution.py:468
  7.8 4.6 %collective-permute-start.6 = (bf16[8,32,128]{2,1,0:T(8,128)(2,1)S(1)}, bf16[8,32,128]{2,1,0:T(8,128)(2,1)S(1)}, u32[]{:S(2)}, u32[]{:S(2)}) collective-permute-start(bf16[8,32,128]{2,1,0:T(8,128)(2,1)S(1)} %get-tuple-element.47), channel_id=1, source_target_pairs={{0,8},{8,0},{16,24},{24,16},{1,9},{9,1},{17,25},{25,17},{2,10},{10... | collective-permute-start | bytes 196616 | tf_op jit(solution)/shard_map/ppermute | solution.py:468
  9.4 5.2 %collective-permute-start.7 = (bf16[8,32,128]{2,1,0:T(8,128)(2,1)S(1)}, bf16[8,32,128]{2,1,0:T(8,128)(2,1)S(1)}, u32[]{:S(2)}, u32[]{:S(2)}) collective-permute-start(bf16[8,32,128]{2,1,0:T(8,128)(2,1)S(1)} %get-tuple-element.48), channel_id=1, source_target_pairs={{0,24},{8,16},{16,8},{24,0},{1,25},{9,17},{17,9},{25,1},{2,26},{10... | collective-permute-start | bytes 196616 | tf_op jit(solution)/shard_map/ppermute | solution.py:468
  10.8 5.9 %collective-permute-start.4 = (bf16[32,2,8,128]{3,2,1,0:T(8,128)(2,1)}, bf16[32,2,8,128]{3,2,1,0:T(8,128)(2,1)S(1)}, u32[]{:S(2)}, u32[]{:S(2)}) collective-permute-start(bf16[32,2,8,128]{3,2,1,0:T(8,128)(2,1)} %x_hbm.1), channel_id=1, source_target_pairs={{0,1},{1,0},{2,3},{3,2},{4,5},{5,4},{6,7},{7,6},{8,9},{9,8},{10,11... | collective-permute-start | bytes 393224 | tf_op jit(solution)/shard_map/ppermute | solution.py:468
  11.4 5.4 %collective-permute-start.1 = (bf16[32,2,8,128]{3,2,1,0:T(8,128)(2,1)S(1)}, bf16[32,2,8,128]{3,2,1,0:T(8,128)(2,1)S(1)}, u32[]{:S(2)}, u32[]{:S(2)}) collective-permute-start(bf16[32,2,8,128]{3,2,1,0:T(8,128)(2,1)S(1)} %collective-permute-done.refs_2_), channel_id=1, source_target_pairs={{0,2},{1,3},{2,0},{3,1},{4,6},{5,7},{6,4},{7,5},{8,10},{9,11},{10,... | collective-permute-start | bytes 393224 | tf_op jit(solution)/shard_map/ppermute | solution.py:468
  14.5 2.2 %collective-permute-start.5 = (bf16[32,2,8,128]{3,2,1,0:T(8,128)(2,1)S(1)}, bf16[32,2,8,128]{3,2,1,0:T(8,128)(2,1)S(1)}, u32[]{:S(2)}, u32[]{:S(2)}) collective-permute-start(bf16[32,2,8,128]{3,2,1,0:T(8,128)(2,1)S(1)} %collective-permute-done.3.refs_1_), channel_id=1, source_target_pairs={{0,1},{1,0},{2,3},{3,2},{4,5},{5,4},{6,7},{7,6},{8,9},{9,8},{10,11... | collective-permute-start | bytes 393224 | tf_op jit(solution)/shard_map/ppermute | solution.py:468
  14.5 2.3 %collective-permute-start.8 = (bf16[32,2,8,128]{3,2,1,0:T(8,128)(2,1)S(1)}, bf16[32,2,8,128]{3,2,1,0:T(8,128)(2,1)S(1)}, u32[]{:S(2)}, u32[]{:S(2)}) collective-permute-start(bf16[32,2,8,128]{3,2,1,0:T(8,128)(2,1)S(1)} %collective-permute-done.refs_2_), channel_id=1, source_target_pairs={{0,1},{1,0},{2,3},{3,2},{4,5},{5,4},{6,7},{7,6},{8,9},{9,8},{10,11... | collective-permute-start | bytes 393224 | tf_op jit(solution)/shard_map/ppermute | solution.py:468
  16.8 1.3 %collective-permute-start.2 = (bf16[32,2,8,128]{3,2,1,0:T(8,128)(2,1)S(1)}, bf16[32,2,8,128]{3,2,1,0:T(8,128)(2,1)S(1)}, u32[]{:S(2)}, u32[]{:S(2)}) collective-permute-start(bf16[32,2,8,128]{3,2,1,0:T(8,128)(2,1)S(1)} %collective-permute-done.1.refs_3_), channel_id=1, source_target_pairs={{0,1},{1,0},{2,3},{3,2},{4,5},{5,4},{6,7},{7,6},{8,9},{9,8},{10,11... | collective-permute-start | bytes 393224 | tf_op jit(solution)/shard_map/ppermute | solution.py:468
  18.8 6.0 %collective-permute-start.9 = (bf16[8,32,128]{2,1,0:T(8,128)(2,1)S(1)}, bf16[8,32,128]{2,1,0:T(8,128)(2,1)S(1)}, u32[]{:S(2)}, u32[]{:S(2)}) collective-permute-start(bf16[8,32,128]{2,1,0:T(8,128)(2,1)S(1)} %get-tuple-element.52.first_ref), channel_id=1, source_target_pairs={{0,8},{8,0},{16,24},{24,16},{1,9},{9,1},{17,25},{25,17},{2,10},{10... | collective-permute-start | bytes 196616 | tf_op jit(solution)/shard_map/ppermute | solution.py:468
  20.3 5.8 %collective-permute-start.10 = (bf16[8,32,128]{2,1,0:T(8,128)(2,1)S(1)}, bf16[8,32,128]{2,1,0:T(8,128)(2,1)S(1)}, u32[]{:S(2)}, u32[]{:S(2)}) collective-permute-start(bf16[8,32,128]{2,1,0:T(8,128)(2,1)S(1)} %get-tuple-element.53.second_ref), channel_id=1, source_target_pairs={{0,24},{8,16},{16,8},{24,0},{1,25},{9,17},{17,9},{25,1},{2,26},{10... | collective-permute-start | bytes 196616 | tf_op jit(solution)/shard_map/ppermute | solution.py:468
  22.3 6.2 %collective-permute-start.11 = (bf16[8,32,128]{2,1,0:T(8,128)(2,1)S(1)}, bf16[8,32,128]{2,1,0:T(8,128)(2,1)S(1)}, u32[]{:S(2)}, u32[]{:S(2)}) collective-permute-start(bf16[8,32,128]{2,1,0:T(8,128)(2,1)S(1)} %get-tuple-element.59), channel_id=1, source_target_pairs={{0,8},{8,0},{16,24},{24,16},{1,9},{9,1},{17,25},{25,17},{2,10},{10... | collective-permute-start | bytes 196616 | tf_op jit(solution)/shard_map/ppermute | solution.py:468
  23.9 5.2 %collective-permute-start.12 = (bf16[8,32,128]{2,1,0:T(8,128)(2,1)S(1)}, bf16[8,32,128]{2,1,0:T(8,128)(2,1)S(1)}, u32[]{:S(2)}, u32[]{:S(2)}) collective-permute-start(bf16[8,32,128]{2,1,0:T(8,128)(2,1)S(1)} %get-tuple-element.60), channel_id=1, source_target_pairs={{0,24},{8,16},{16,8},{24,0},{1,25},{9,17},{17,9},{25,1},{2,26},{10... | collective-permute-start | bytes 196616 | tf_op jit(solution)/shard_map/ppermute | solution.py:468
  29.9 2.7 %collective-permute-start.14 = (bf16[4,16,32,128]{3,2,1,0:T(8,128)(2,1)S(1)}, bf16[4,16,32,128]{3,2,1,0:T(8,128)(2,1)S(1)}, u32[]{:S(2)}, u32[]{:S(2)}) collective-permute-start(bf16[4,16,32,128]{3,2,1,0:T(8,128)(2,1)S(1)} %get-tuple-element.73), channel_id=1, source_target_pairs={{0,1},{1,0},{2,3},{3,2},{4,5},{5,4},{6,7},{7,6},{8,9},{9,8},{10,11... | collective-permute-start | bytes 1572872 | tf_op jit(solution)/shard_map/ppermute | solution.py:468
  30.5 6.7 %collective-permute-start.13 = (bf16[448,256]{1,0:T(8,128)(2,1)S(1)}, bf16[448,256]{1,0:T(8,128)(2,1)S(1)}, u32[]{:S(2)}, u32[]{:S(2)}) collective-permute-start(bf16[448,256]{1,0:T(8,128)(2,1)S(1)} %get-tuple-element.71.a_ref), channel_id=1, source_target_pairs={{0,8},{1,17},{2,10},{3,19},{4,12},{5,21},{6,14},{7,23},{8,0},{9,25... | collective-permute-start | bytes 688136 | tf_op jit(solution)/shard_map/ppermute | solution.py:478
  31.1 7.9 %collective-permute-start.16 = (bf16[448,256]{1,0:T(8,128)(2,1)S(1)}, bf16[448,256]{1,0:T(8,128)(2,1)S(1)}, u32[]{:S(2)}, u32[]{:S(2)}) collective-permute-start(bf16[448,256]{1,0:T(8,128)(2,1)S(1)} %get-tuple-element.75.a_ref), channel_id=1, source_target_pairs={{0,8},{1,17},{2,10},{3,19},{4,12},{5,21},{6,14},{7,23},{8,0},{9,25... | collective-permute-start | bytes 688136 | tf_op jit(solution)/shard_map/ppermute | solution.py:478
  32.8 13.0 %collective-permute-start.18 = (bf16[16,32,128]{2,1,0:T(8,128)(2,1)S(1)}, bf16[16,32,128]{2,1,0:T(8,128)(2,1)S(1)}, u32[]{:S(2)}, u32[]{:S(2)}) collective-permute-start(bf16[16,32,128]{2,1,0:T(8,128)(2,1)S(1)} %get-tuple-element.76), channel_id=1, source_target_pairs={{0,4},{1,5},{2,6},{3,7},{4,0},{5,1},{6,2},{7,3},{8,12},{9,13},{10,... | collective-permute-start | bytes 393224 | tf_op jit(solution)/shard_map/ppermute | solution.py:468
  35.5 10.3 %collective-permute-start.19 = (bf16[16,32,128]{2,1,0:T(8,128)(2,1)S(1)}, bf16[16,32,128]{2,1,0:T(8,128)(2,1)S(1)}, u32[]{:S(2)}, u32[]{:S(2)}) collective-permute-start(bf16[16,32,128]{2,1,0:T(8,128)(2,1)S(1)} %get-tuple-element.77), channel_id=1, source_target_pairs={{0,6},{1,7},{2,4},{3,5},{4,2},{5,3},{6,0},{7,1},{8,14},{9,15},{10,... | collective-permute-start | bytes 393224 | tf_op jit(solution)/shard_map/ppermute | solution.py:468
  36.7 9.4 %collective-permute-start.20 = (bf16[16,32,128]{2,1,0:T(8,128)(2,1)S(1)}, bf16[16,32,128]{2,1,0:T(8,128)(2,1)S(1)}, u32[]{:S(2)}, u32[]{:S(2)}) collective-permute-start(bf16[16,32,128]{2,1,0:T(8,128)(2,1)S(1)} %get-tuple-element.78), channel_id=1, source_target_pairs={{0,2},{1,3},{2,0},{3,1},{4,6},{5,7},{6,4},{7,5},{8,10},{9,11},{10,... | collective-permute-start | bytes 393224 | tf_op jit(solution)/shard_map/ppermute | solution.py:468
  37.3 8.9 %collective-permute-start.15 = (bf16[448,256]{1,0:T(8,128)(2,1)S(1)}, bf16[448,256]{1,0:T(8,128)(2,1)S(1)}, u32[]{:S(2)}, u32[]{:S(2)}) collective-permute-start(bf16[448,256]{1,0:T(8,128)(2,1)S(1)} %pair_sum.2.a_ref), channel_id=1, source_target_pairs={{0,16},{1,9},{2,18},{3,11},{4,20},{5,13},{6,22},{7,15},{8,24},{9,1... | collective-permute-start | bytes 688136 | tf_op jit(solution)/shard_map/ppermute | solution.py:478
  39.1 7.1 %collective-permute-start.17 = (bf16[448,256]{1,0:T(8,128)(2,1)S(1)}, bf16[448,256]{1,0:T(8,128)(2,1)S(1)}, u32[]{:S(2)}, u32[]{:S(2)}) collective-permute-start(bf16[448,256]{1,0:T(8,128)(2,1)S(1)} %pair_sum.3.c_ref), channel_id=1, source_target_pairs={{0,16},{1,9},{2,18},{3,11},{4,20},{5,13},{6,22},{7,15},{8,24},{9,1... | collective-permute-start | bytes 688136 | tf_op jit(solution)/shard_map/ppermute | solution.py:478

commit v19 on v18

--- a/solution.py
+++ b/solution.py
@@ -352,7 +352,6 @@
     partial_ref,
     w_0_ref,
     w_1_ref,
-    _,
     s_ref,
     other_ref,
     mine_ref,
@@ -401,8 +400,7 @@
     )
 
 
-def own_filter_body(s_ref, x_ref, out_ref, token_ref):
-    token_ref[...] = jnp.zeros_like(token_ref)
+def own_filter_body(s_ref, x_ref, out_ref):
     third = out_ref.shape[0] // 3
     low, high = (filter_product(s_ref, x_ref, p) for p in range(2))
     out_ref[:third] = low[:third]
@@ -569,9 +567,9 @@
         flops=flops * 2 // 3,
         name="own_gradient",
     )
-    filters, token = call(
+    (filters,) = call(
         own_filter_body,
-        [shape_of((27 * o, c_all), f32), shape_of((8, LANES), f32)],
+        [shape_of((27 * o, c_all), f32)],
         [own_shifts, x_all],
         flops=flops * 2 // 3,
         name="own_filter",
@@ -583,8 +581,8 @@
             shape_of((4, cells, o, depth), bf16),
             shape_of((4, cells, o, depth), bf16),
         ],
-        [me, slab, *sent[:2], *received[2:], bias, go_first, go_second, partial, *w_back[2:], token],
-        [SMEM] * 2 + [VMEM] * 10 + [ANY],
+        [me, slab, *sent[:2], *received[2:], bias, go_first, go_second, partial, *w_back[2:]],
+        [SMEM] * 2 + [VMEM] * 10,
         [pltpu.VMEM((c_all, 9 * o), bf16)] * 2,
         flops=flops // 3,
         name="rim_gradient",

time: 47.7 us -> 48.5 us (1.017)
  waiting for transfers between devices: 14.3 us -> 15.2 us
    ppermute x17, waiting for transfers between devices: 13.2 us -> 14 us  [swap(): lax.ppermute(value, axis, [(i, i ^ bit) for i in range(lax.axis_size(axis...]
where the time goes in v19:
time: 48.5 us; the launch traced here: 48.2 us
  starting transfers between devices  23.2 us (48%)
  waiting for transfers between devices  15.2 us (31%)
  Pallas kernels  8.99 us (19%)
  between operations  0.75 us (2%)
    ppermute x17, starting transfers between devices, swap(): lax.ppermute(value, axis, [(i, i ^ bit) for i in range(lax.axis_size(axis...  19.6 us
    ppermute x17, waiting for transfers between devices, swap(): lax.ppermute(value, axis, [(i, i ^ bit) for i in range(lax.axis_size(axis...  14 us
    pallas_call x13, Pallas kernels, call(): pl.pallas_call(body, out_shape=out_shape, in_specs=specs or [VMEM] * len(...  8.99 us
    ppermute x4, starting transfers between devices, cross(): return lax.ppermute(value, ('slab', 'chan'), pairs)  3.67 us
    ppermute x4, waiting for transfers between devices, cross(): return lax.ppermute(value, ('slab', 'chan'), pairs)  1.24 us
  transfers between devices with their start and end apart: 21, of which 10 were waited for; matrix products, arithmetic and copies ran while one was open for 0% of the time, Pallas kernels for 13%

profile of v19, /device:TPU:0, one launch (start us, length us, event | category | flops | bytes accessed | tf_op | source)
XLA Modules:
  0.0 48.2 jit_solution(13375594705710024793)
XLA Ops:
  0.6 4.1 %collective-permute-start = (bf16[32,2,8,128]{3,2,1,0:T(8,128)(2,1)}, bf16[32,2,8,128]{3,2,1,0:T(8,128)(2,1)S(1)}, u32[]{:S(2)}, u32[]{:S(2)}) collective-permute-start(bf16[32,2,8,128]{3,2,1,0:T(8,128)(2,1)} %x_hbm.1), channel_id=1, source_target_pairs={{0,4},{1,5},{2,6},{3,7},{4,0},{5,1},{6,2},{7,3},{8,12},{9,13},{10,... | collective-permute-start | bytes 393224 | tf_op jit(solution)/shard_map/ppermute | solution.py:466
  4.7 1.6 %collective-permute-start.3 = (bf16[32,2,8,128]{3,2,1,0:T(8,128)(2,1)}, bf16[32,2,8,128]{3,2,1,0:T(8,128)(2,1)S(1)}, u32[]{:S(2)}, u32[]{:S(2)}) collective-permute-start(bf16[32,2,8,128]{3,2,1,0:T(8,128)(2,1)} %x_hbm.1), channel_id=1, source_target_pairs={{0,2},{1,3},{2,0},{3,1},{4,6},{5,7},{6,4},{7,5},{8,10},{9,11},{10,... | collective-permute-start | bytes 393224 | tf_op jit(solution)/shard_map/ppermute | solution.py:466
  6.3 1.5 %prepare.1 = (bf16[32,2,8,128]{3,2,1,0:T(8,128)(2,1)S(1)}, bf16[16,32,128]{2,1,0:T(8,128)(2,1)S(1)}, bf16[8,32,128]{2,1,0:T(8,128)(2,1)S(1)}, bf16[8,32,128]{2,1...) custom-call(s32[1]{0:T(128)} %bitcast.1.slab_ref, ...), custom_call_target="tpu_custom_call" | custom-call | bytes 2441284 | tf_op jit(solution)/shard_map/prepare/pallas_call | solution.py:109
  7.8 1.6 %collective-permute-start.6 = (bf16[8,32,128]{2,1,0:T(8,128)(2,1)S(1)}, bf16[8,32,128]{2,1,0:T(8,128)(2,1)S(1)}, u32[]{:S(2)}, u32[]{:S(2)}) collective-permute-start(bf16[8,32,128]{2,1,0:T(8,128)(2,1)S(1)} %get-tuple-element.45), channel_id=1, source_target_pairs={{0,8},{8,0},{16,24},{24,16},{1,9},{9,1},{17,25},{25,17},{2,10},{10... | collective-permute-start | bytes 196616 | tf_op jit(solution)/shard_map/ppermute | solution.py:466
  9.4 1.5 %collective-permute-start.7 = (bf16[8,32,128]{2,1,0:T(8,128)(2,1)S(1)}, bf16[8,32,128]{2,1,0:T(8,128)(2,1)S(1)}, u32[]{:S(2)}, u32[]{:S(2)}) collective-permute-start(bf16[8,32,128]{2,1,0:T(8,128)(2,1)S(1)} %get-tuple-element.46), channel_id=1, source_target_pairs={{0,24},{8,16},{16,8},{24,0},{1,25},{9,17},{17,9},{25,1},{2,26},{10... | collective-permute-start | bytes 196616 | tf_op jit(solution)/shard_map/ppermute | solution.py:466
  12.4 2.1 %collective-permute-done.7.go_second_ref = bf16[8,32,128]{2,1,0:T(8,128)(2,1)S(1)} collective-permute-done((bf16[8,32,128]{2,1,0:T(8,128)(2,1)S(1)}, bf16[8,32,128]{2,1,0:T(8,128)(2,1)S(1)}, u32[]{:S(2)}, u32[]{:S(2)}) %collective-permute-start.7) | collective-permute-done | bytes 65568 | tf_op jit(solution)/shard_map/ppermute | solution.py:466
  15.0 1.7 %collective-permute-done.1.refs_3_ = bf16[32,2,8,128]{3,2,1,0:T(8,128)(2,1)S(1)} collective-permute-done((bf16[32,2,8,128]{3,2,1,0:T(8,128)(2,1)S(1)}, bf16[32,2,8,128]{3,2,1,0:T(8,128)(2,1)S(1)}, u32[]{:S(2)}, u32[]{:S(2)}) %collective-permute-start.1) | collective-permute-done | bytes 131104 | tf_op jit(solution)/shard_map/ppermute | solution.py:466
  18.8 1.6 %collective-permute-start.9 = (bf16[8,32,128]{2,1,0:T(8,128)(2,1)S(1)}, bf16[8,32,128]{2,1,0:T(8,128)(2,1)S(1)}, u32[]{:S(2)}, u32[]{:S(2)}) collective-permute-start(bf16[8,32,128]{2,1,0:T(8,128)(2,1)S(1)} %get-tuple-element.50.first_ref), channel_id=1, source_target_pairs={{0,8},{8,0},{16,24},{24,16},{1,9},{9,1},{17,25},{25,17},{2,10},{10... | collective-permute-start | bytes 196616 | tf_op jit(solution)/shard_map/ppermute | solution.py:466
  20.3 1.1 %collective-permute-start.10 = (bf16[8,32,128]{2,1,0:T(8,128)(2,1)S(1)}, bf16[8,32,128]{2,1,0:T(8,128)(2,1)S(1)}, u32[]{:S(2)}, u32[]{:S(2)}) collective-permute-start(bf16[8,32,128]{2,1,0:T(8,128)(2,1)S(1)} %get-tuple-element.51.second_ref), channel_id=1, source_target_pairs={{0,24},{8,16},{16,8},{24,0},{1,25},{9,17},{17,9},{25,1},{2,26},{10... | collective-permute-start | bytes 196616 | tf_op jit(solution)/shard_map/ppermute | solution.py:466
  21.4 0.9 %own_forward.1 = (f32[16,32,128]{2,1,0:T(8,128)S(1)}, bf16[8,32,128]{2,1,0:T(8,128)(2,1)S(1)}, bf16[8,32,128]{2,1,0:T(8,128)(2,1)S(1)}) custom-call(s32[1]{0:T(128)} %bitcast.1.slab_ref, bf16[864,256]{1,0:T(8,128)(2,1)S(1)} %get-tuple-element.42.w_ref, bf16[256,2048]{1,0:T(8,128)(2,1)S(1)} %get-tuple-element.48.x_ref), custom_call_target="tpu_custom_call" | custom-call | flops 603979776 | bytes 1884164 | tf_op jit(solution)/shard_map/own_forward/pallas_call | solution.py:109
  22.3 1.6 %collective-permute-start.11 = (bf16[8,32,128]{2,1,0:T(8,128)(2,1)S(1)}, bf16[8,32,128]{2,1,0:T(8,128)(2,1)S(1)}, u32[]{:S(2)}, u32[]{:S(2)}) collective-permute-start(bf16[8,32,128]{2,1,0:T(8,128)(2,1)S(1)} %get-tuple-element.57), channel_id=1, source_target_pairs={{0,8},{8,0},{16,24},{24,16},{1,9},{9,1},{17,25},{25,17},{2,10},{10... | collective-permute-start | bytes 196616 | tf_op jit(solution)/shard_map/ppermute | solution.py:466
  23.9 0.9 %collective-permute-start.12 = (bf16[8,32,128]{2,1,0:T(8,128)(2,1)S(1)}, bf16[8,32,128]{2,1,0:T(8,128)(2,1)S(1)}, u32[]{:S(2)}, u32[]{:S(2)}) collective-permute-start(bf16[8,32,128]{2,1,0:T(8,128)(2,1)S(1)} %get-tuple-element.58), channel_id=1, source_target_pairs={{0,24},{8,16},{16,8},{24,0},{1,25},{9,17},{17,9},{25,1},{2,26},{10... | collective-permute-start | bytes 196616 | tf_op jit(solution)/shard_map/ppermute | solution.py:466
  24.8 1.4 %collective-permute-done.10.second_ref = bf16[8,32,128]{2,1,0:T(8,128)(2,1)S(1)} collective-permute-done((bf16[8,32,128]{2,1,0:T(8,128)(2,1)S(1)}, bf16[8,32,128]{2,1,0:T(8,128)(2,1)S(1)}, u32[]{:S(2)}, u32[]{:S(2)}) %collective-permute-start.10) | collective-permute-done | bytes 65568 | tf_op jit(solution)/shard_map/ppermute | solution.py:466
  26.1 1.6 %own_gradient.1 = (bf16[32,2,8,128]{3,2,1,0:T(8,128)(2,1)}, f32[32,128]{1,0:T(8,128)S(1)}, bf16[576,2048]{1,0:T(8,128)(2,1)S(1)}, f32[256,2048]{1,0:T(8,128)S(1)}) custom-call(s32[1]{0:T(128)} %bitcast.me_ref, s32[1]{0:T(128)} %bitcast.1.slab_ref, f32[16,32,128]{2,1,0:T(8,128)S(1)} %get-tuple-element.49.own_ref, ...), custom_call_target="tpu_custom_call" | custom-call | flops 603979776 | bytes 5734408 | tf_op jit(solution)/shard_map/own_gradient/pallas_call | solution.py:109
  27.7 1.3 %collective-permute-done.12.second_in_ref = bf16[8,32,128]{2,1,0:T(8,128)(2,1)S(1)} collective-permute-done((bf16[8,32,128]{2,1,0:T(8,128)(2,1)S(1)}, bf16[8,32,128]{2,1,0:T(8,128)(2,1)S(1)}, u32[]{:S(2)}, u32[]{:S(2)}) %collective-permute-start.12) | collective-permute-done | bytes 65568 | tf_op jit(solution)/shard_map/ppermute | solution.py:466
  29.0 0.9 %rim_gradient.1 = (bf16[288,2048]{1,0:T(8,128)(2,1)S(1)}, bf16[4,16,32,128]{3,2,1,0:T(8,128)(2,1)S(1)}, bf16[4,16,32,128]{3,2,1,0:T(8,128)(2,1)S(1)}) custom-call(s32[1]{0:T(128)} %bitcast.me_ref, s32[1]{0:T(128)} %bitcast.1.slab_ref, bf16[8,32,128]{2,1,0:T(8,128)(2,1)S(1)} %get-tuple-element.50.first_ref, ...), custom_call_target="tpu_custom_call" | custom-call | flops 301989888 | bytes 5029896 | tf_op jit(solution)/shard_map/rim_gradient/pallas_call | solution.py:109
  30.0 0.8 %own_filter.1.own_ref = f32[864,256]{1,0:T(8,128)S(1)} custom-call(bf16[576,2048]{1,0:T(8,128)(2,1)S(1)} %get-tuple-element.65.s_ref, bf16[256,2048]{1,0:T(8,128)(2,1)S(1)} %get-tuple-element.48.x_ref), custom_call_target="tpu_custom_call" | custom-call | flops 603979776 | bytes 4292608 | tf_op jit(solution)/shard_map/own_filter/pallas_call | solution.py:109
  32.0 1.5 %collective-permute-start.16 = (bf16[448,256]{1,0:T(8,128)(2,1)S(1)}, bf16[448,256]{1,0:T(8,128)(2,1)S(1)}, u32[]{:S(2)}, u32[]{:S(2)}) collective-permute-start(bf16[448,256]{1,0:T(8,128)(2,1)S(1)} %get-tuple-element.71.a_ref), channel_id=1, source_target_pairs={{0,8},{1,17},{2,10},{3,19},{4,12},{5,21},{6,14},{7,23},{8,0},{9,25... | collective-permute-start | bytes 688136 | tf_op jit(solution)/shard_map/ppermute | solution.py:476
  33.6 2.7 %collective-permute-start.18 = (bf16[16,32,128]{2,1,0:T(8,128)(2,1)S(1)}, bf16[16,32,128]{2,1,0:T(8,128)(2,1)S(1)}, u32[]{:S(2)}, u32[]{:S(2)}) collective-permute-start(bf16[16,32,128]{2,1,0:T(8,128)(2,1)S(1)} %get-tuple-element.72), channel_id=1, source_target_pairs={{0,4},{1,5},{2,6},{3,7},{4,0},{5,1},{6,2},{7,3},{8,12},{9,13},{10,... | collective-permute-start | bytes 393224 | tf_op jit(solution)/shard_map/ppermute | solution.py:466
  36.3 1.2 %collective-permute-start.19 = (bf16[16,32,128]{2,1,0:T(8,128)(2,1)S(1)}, bf16[16,32,128]{2,1,0:T(8,128)(2,1)S(1)}, u32[]{:S(2)}, u32[]{:S(2)}) collective-permute-start(bf16[16,32,128]{2,1,0:T(8,128)(2,1)S(1)} %get-tuple-element.73), channel_id=1, source_target_pairs={{0,6},{1,7},{2,4},{3,5},{4,2},{5,3},{6,0},{7,1},{8,14},{9,15},{10,... | collective-permute-start | bytes 393224 | tf_op jit(solution)/shard_map/ppermute | solution.py:466
  38.7 1.2 %collective-permute-done.16.b_ref = bf16[448,256]{1,0:T(8,128)(2,1)S(1)} collective-permute-done((bf16[448,256]{1,0:T(8,128)(2,1)S(1)}, bf16[448,256]{1,0:T(8,128)(2,1)S(1)}, u32[]{:S(2)}, u32[]{:S(2)}) %collective-permute-start.16) | collective-permute-done | bytes 229408 | tf_op jit(solution)/shard_map/ppermute | solution.py:476
  40.0 1.0 %collective-permute-start.17 = (bf16[448,256]{1,0:T(8,128)(2,1)S(1)}, bf16[448,256]{1,0:T(8,128)(2,1)S(1)}, u32[]{:S(2)}, u32[]{:S(2)}) collective-permute-start(bf16[448,256]{1,0:T(8,128)(2,1)S(1)} %pair_sum.3.c_ref), channel_id=1, source_target_pairs={{0,16},{1,9},{2,18},{3,11},{4,20},{5,13},{6,22},{7,15},{8,24},{9,1... | collective-permute-start | bytes 688136 | tf_op jit(solution)/shard_map/ppermute | solution.py:476
  41.0 5.6 %collective-permute-done.18.b_ref = bf16[16,32,128]{2,1,0:T(8,128)(2,1)S(1)} collective-permute-done((bf16[16,32,128]{2,1,0:T(8,128)(2,1)S(1)}, bf16[16,32,128]{2,1,0:T(8,128)(2,1)S(1)}, u32[]{:S(2)}, u32[]{:S(2)}) %collective-permute-start.18) | collective-permute-done | bytes 131104 | tf_op jit(solution)/shard_map/ppermute | solution.py:466
  47.0 1.1 %last.1 = (f32[27,32,256]{2,1,0:T(8,128)}, f32[1,32]{1,0:T(1,128)}, bf16[32,2,8,128]{3,2,1,0:T(8,128)(2,1)}) custom-call(bf16[448,256]{1,0:T(8,128)(2,1)S(1)} %pair_sum.2.a_ref, bf16[448,256]{1,0:T(8,128)(2,1)S(1)} %collective-permute-done.15.b_ref, bf16[448,256]{1,0:T(8,128)(2,1)S(1)} %pair_sum.3.c_ref, bf16[448,256]{1,0:T(8,128)(2,1)S(1)} %collective-permute-done.17.d_ref, ...), custom_call_target="tpu_custom_call" | custom-call | bytes 2195584 | tf_op jit(solution)/shard_map/last/pallas_call | solution.py:109
  (31 shorter events, 7.0 us)
Async XLA Ops:
  0.6 10.7 %collective-permute-start = (bf16[32,2,8,128]{3,2,1,0:T(8,128)(2,1)}, bf16[32,2,8,128]{3,2,1,0:T(8,128)(2,1)S(1)}, u32[]{:S(2)}, u32[]{:S(2)}) collective-permute-start(bf16[32,2,8,128]{3,2,1,0:T(8,128)(2,1)} %x_hbm.1), channel_id=1, source_target_pairs={{0,4},{1,5},{2,6},{3,7},{4,0},{5,1},{6,2},{7,3},{8,12},{9,13},{10,... | collective-permute-start | bytes 393224 | tf_op jit(solution)/shard_map/ppermute | solution.py:466
  4.7 9.8 %collective-permute-start.3 = (bf16[32,2,8,128]{3,2,1,0:T(8,128)(2,1)}, bf16[32,2,8,128]{3,2,1,0:T(8,128)(2,1)S(1)}, u32[]{:S(2)}, u32[]{:S(2)}) collective-permute-start(bf16[32,2,8,128]{3,2,1,0:T(8,128)(2,1)} %x_hbm.1), channel_id=1, source_target_pairs={{0,2},{1,3},{2,0},{3,1},{4,6},{5,7},{6,4},{7,5},{8,10},{9,11},{10,... | collective-permute-start | bytes 393224 | tf_op jit(solution)/shard_map/ppermute | solution.py:466
  7.8 4.6 %collective-permute-start.6 = (bf16[8,32,128]{2,1,0:T(8,128)(2,1)S(1)}, bf16[8,32,128]{2,1,0:T(8,128)(2,1)S(1)}, u32[]{:S(2)}, u32[]{:S(2)}) collective-permute-start(bf16[8,32,128]{2,1,0:T(8,128)(2,1)S(1)} %get-tuple-element.45), channel_id=1, source_target_pairs={{0,8},{8,0},{16,24},{24,16},{1,9},{9,1},{17,25},{25,17},{2,10},{10... | collective-permute-start | bytes 196616 | tf_op jit(solution)/shard_map/ppermute | solution.py:466
  9.4 5.2 %collective-permute-start.7 = (bf16[8,32,128]{2,1,0:T(8,128)(2,1)S(1)}, bf16[8,32,128]{2,1,0:T(8,128)(2,1)S(1)}, u32[]{:S(2)}, u32[]{:S(2)}) collective-permute-start(bf16[8,32,128]{2,1,0:T(8,128)(2,1)S(1)} %get-tuple-element.46), channel_id=1, source_target_pairs={{0,24},{8,16},{16,8},{24,0},{1,25},{9,17},{17,9},{25,1},{2,26},{10... | collective-permute-start | bytes 196616 | tf_op jit(solution)/shard_map/ppermute | solution.py:466
  10.8 5.9 %collective-permute-start.4 = (bf16[32,2,8,128]{3,2,1,0:T(8,128)(2,1)}, bf16[32,2,8,128]{3,2,1,0:T(8,128)(2,1)S(1)}, u32[]{:S(2)}, u32[]{:S(2)}) collective-permute-start(bf16[32,2,8,128]{3,2,1,0:T(8,128)(2,1)} %x_hbm.1), channel_id=1, source_target_pairs={{0,1},{1,0},{2,3},{3,2},{4,5},{5,4},{6,7},{7,6},{8,9},{9,8},{10,11... | collective-permute-start | bytes 393224 | tf_op jit(solution)/shard_map/ppermute | solution.py:466
  11.4 5.4 %collective-permute-start.1 = (bf16[32,2,8,128]{3,2,1,0:T(8,128)(2,1)S(1)}, bf16[32,2,8,128]{3,2,1,0:T(8,128)(2,1)S(1)}, u32[]{:S(2)}, u32[]{:S(2)}) collective-permute-start(bf16[32,2,8,128]{3,2,1,0:T(8,128)(2,1)S(1)} %collective-permute-done.refs_2_), channel_id=1, source_target_pairs={{0,2},{1,3},{2,0},{3,1},{4,6},{5,7},{6,4},{7,5},{8,10},{9,11},{10,... | collective-permute-start | bytes 393224 | tf_op jit(solution)/shard_map/ppermute | solution.py:466
  14.5 2.2 %collective-permute-start.5 = (bf16[32,2,8,128]{3,2,1,0:T(8,128)(2,1)S(1)}, bf16[32,2,8,128]{3,2,1,0:T(8,128)(2,1)S(1)}, u32[]{:S(2)}, u32[]{:S(2)}) collective-permute-start(bf16[32,2,8,128]{3,2,1,0:T(8,128)(2,1)S(1)} %collective-permute-done.3.refs_1_), channel_id=1, source_target_pairs={{0,1},{1,0},{2,3},{3,2},{4,5},{5,4},{6,7},{7,6},{8,9},{9,8},{10,11... | collective-permute-start | bytes 393224 | tf_op jit(solution)/shard_map/ppermute | solution.py:466
  14.5 2.3 %collective-permute-start.8 = (bf16[32,2,8,128]{3,2,1,0:T(8,128)(2,1)S(1)}, bf16[32,2,8,128]{3,2,1,0:T(8,128)(2,1)S(1)}, u32[]{:S(2)}, u32[]{:S(2)}) collective-permute-start(bf16[32,2,8,128]{3,2,1,0:T(8,128)(2,1)S(1)} %collective-permute-done.refs_2_), channel_id=1, source_target_pairs={{0,1},{1,0},{2,3},{3,2},{4,5},{5,4},{6,7},{7,6},{8,9},{9,8},{10,11... | collective-permute-start | bytes 393224 | tf_op jit(solution)/shard_map/ppermute | solution.py:466
  16.8 1.3 %collective-permute-start.2 = (bf16[32,2,8,128]{3,2,1,0:T(8,128)(2,1)S(1)}, bf16[32,2,8,128]{3,2,1,0:T(8,128)(2,1)S(1)}, u32[]{:S(2)}, u32[]{:S(2)}) collective-permute-start(bf16[32,2,8,128]{3,2,1,0:T(8,128)(2,1)S(1)} %collective-permute-done.1.refs_3_), channel_id=1, source_target_pairs={{0,1},{1,0},{2,3},{3,2},{4,5},{5,4},{6,7},{7,6},{8,9},{9,8},{10,11... | collective-permute-start | bytes 393224 | tf_op jit(solution)/shard_map/ppermute | solution.py:466
  18.8 6.0 %collective-permute-start.9 = (bf16[8,32,128]{2,1,0:T(8,128)(2,1)S(1)}, bf16[8,32,128]{2,1,0:T(8,128)(2,1)S(1)}, u32[]{:S(2)}, u32[]{:S(2)}) collective-permute-start(bf16[8,32,128]{2,1,0:T(8,128)(2,1)S(1)} %get-tuple-element.50.first_ref), channel_id=1, source_target_pairs={{0,8},{8,0},{16,24},{24,16},{1,9},{9,1},{17,25},{25,17},{2,10},{10... | collective-permute-start | bytes 196616 | tf_op jit(solution)/shard_map/ppermute | solution.py:466
  20.3 5.8 %collective-permute-start.10 = (bf16[8,32,128]{2,1,0:T(8,128)(2,1)S(1)}, bf16[8,32,128]{2,1,0:T(8,128)(2,1)S(1)}, u32[]{:S(2)}, u32[]{:S(2)}) collective-permute-start(bf16[8,32,128]{2,1,0:T(8,128)(2,1)S(1)} %get-tuple-element.51.second_ref), channel_id=1, source_target_pairs={{0,24},{8,16},{16,8},{24,0},{1,25},{9,17},{17,9},{25,1},{2,26},{10... | collective-permute-start | bytes 196616 | tf_op jit(solution)/shard_map/ppermute | solution.py:466
  22.3 5.4 %collective-permute-start.11 = (bf16[8,32,128]{2,1,0:T(8,128)(2,1)S(1)}, bf16[8,32,128]{2,1,0:T(8,128)(2,1)S(1)}, u32[]{:S(2)}, u32[]{:S(2)}) collective-permute-start(bf16[8,32,128]{2,1,0:T(8,128)(2,1)S(1)} %get-tuple-element.57), channel_id=1, source_target_pairs={{0,8},{8,0},{16,24},{24,16},{1,9},{9,1},{17,25},{25,17},{2,10},{10... | collective-permute-start | bytes 196616 | tf_op jit(solution)/shard_map/ppermute | solution.py:466
  23.9 5.2 %collective-permute-start.12 = (bf16[8,32,128]{2,1,0:T(8,128)(2,1)S(1)}, bf16[8,32,128]{2,1,0:T(8,128)(2,1)S(1)}, u32[]{:S(2)}, u32[]{:S(2)}) collective-permute-start(bf16[8,32,128]{2,1,0:T(8,128)(2,1)S(1)} %get-tuple-element.58), channel_id=1, source_target_pairs={{0,24},{8,16},{16,8},{24,0},{1,25},{9,17},{17,9},{25,1},{2,26},{10... | collective-permute-start | bytes 196616 | tf_op jit(solution)/shard_map/ppermute | solution.py:466
  30.0 3.5 %collective-permute-start.14 = (bf16[4,16,32,128]{3,2,1,0:T(8,128)(2,1)S(1)}, bf16[4,16,32,128]{3,2,1,0:T(8,128)(2,1)S(1)}, u32[]{:S(2)}, u32[]{:S(2)}) collective-permute-start(bf16[4,16,32,128]{3,2,1,0:T(8,128)(2,1)S(1)} %get-tuple-element.69), channel_id=1, source_target_pairs={{0,1},{1,0},{2,3},{3,2},{4,5},{5,4},{6,7},{7,6},{8,9},{9,8},{10,11... | collective-permute-start | bytes 1572872 | tf_op jit(solution)/shard_map/ppermute | solution.py:466
  31.4 6.7 %collective-permute-start.13 = (bf16[448,256]{1,0:T(8,128)(2,1)S(1)}, bf16[448,256]{1,0:T(8,128)(2,1)S(1)}, u32[]{:S(2)}, u32[]{:S(2)}) collective-permute-start(bf16[448,256]{1,0:T(8,128)(2,1)S(1)} %get-tuple-element.67.a_ref), channel_id=1, source_target_pairs={{0,8},{1,17},{2,10},{3,19},{4,12},{5,21},{6,14},{7,23},{8,0},{9,25... | collective-permute-start | bytes 688136 | tf_op jit(solution)/shard_map/ppermute | solution.py:476
  32.0 7.9 %collective-permute-start.16 = (bf16[448,256]{1,0:T(8,128)(2,1)S(1)}, bf16[448,256]{1,0:T(8,128)(2,1)S(1)}, u32[]{:S(2)}, u32[]{:S(2)}) collective-permute-start(bf16[448,256]{1,0:T(8,128)(2,1)S(1)} %get-tuple-element.71.a_ref), channel_id=1, source_target_pairs={{0,8},{1,17},{2,10},{3,19},{4,12},{5,21},{6,14},{7,23},{8,0},{9,25... | collective-permute-start | bytes 688136 | tf_op jit(solution)/shard_map/ppermute | solution.py:476
  33.6 13.0 %collective-permute-start.18 = (bf16[16,32,128]{2,1,0:T(8,128)(2,1)S(1)}, bf16[16,32,128]{2,1,0:T(8,128)(2,1)S(1)}, u32[]{:S(2)}, u32[]{:S(2)}) collective-permute-start(bf16[16,32,128]{2,1,0:T(8,128)(2,1)S(1)} %get-tuple-element.72), channel_id=1, source_target_pairs={{0,4},{1,5},{2,6},{3,7},{4,0},{5,1},{6,2},{7,3},{8,12},{9,13},{10,... | collective-permute-start | bytes 393224 | tf_op jit(solution)/shard_map/ppermute | solution.py:466
  36.3 10.3 %collective-permute-start.19 = (bf16[16,32,128]{2,1,0:T(8,128)(2,1)S(1)}, bf16[16,32,128]{2,1,0:T(8,128)(2,1)S(1)}, u32[]{:S(2)}, u32[]{:S(2)}) collective-permute-start(bf16[16,32,128]{2,1,0:T(8,128)(2,1)S(1)} %get-tuple-element.73), channel_id=1, source_target_pairs={{0,6},{1,7},{2,4},{3,5},{4,2},{5,3},{6,0},{7,1},{8,14},{9,15},{10,... | collective-permute-start | bytes 393224 | tf_op jit(solution)/shard_map/ppermute | solution.py:466
  37.6 9.4 %collective-permute-start.20 = (bf16[16,32,128]{2,1,0:T(8,128)(2,1)S(1)}, bf16[16,32,128]{2,1,0:T(8,128)(2,1)S(1)}, u32[]{:S(2)}, u32[]{:S(2)}) collective-permute-start(bf16[16,32,128]{2,1,0:T(8,128)(2,1)S(1)} %get-tuple-element.74), channel_id=1, source_target_pairs={{0,2},{1,3},{2,0},{3,1},{4,6},{5,7},{6,4},{7,5},{8,10},{9,11},{10,... | collective-permute-start | bytes 393224 | tf_op jit(solution)/shard_map/ppermute | solution.py:466
  38.1 8.9 %collective-permute-start.15 = (bf16[448,256]{1,0:T(8,128)(2,1)S(1)}, bf16[448,256]{1,0:T(8,128)(2,1)S(1)}, u32[]{:S(2)}, u32[]{:S(2)}) collective-permute-start(bf16[448,256]{1,0:T(8,128)(2,1)S(1)} %pair_sum.2.a_ref), channel_id=1, source_target_pairs={{0,16},{1,9},{2,18},{3,11},{4,20},{5,13},{6,22},{7,15},{8,24},{9,1... | collective-permute-start | bytes 688136 | tf_op jit(solution)/shard_map/ppermute | solution.py:476
  40.0 7.1 %collective-permute-start.17 = (bf16[448,256]{1,0:T(8,128)(2,1)S(1)}, bf16[448,256]{1,0:T(8,128)(2,1)S(1)}, u32[]{:S(2)}, u32[]{:S(2)}) collective-permute-start(bf16[448,256]{1,0:T(8,128)(2,1)S(1)} %pair_sum.3.c_ref), channel_id=1, source_target_pairs={{0,16},{1,9},{2,18},{3,11},{4,20},{5,13},{6,22},{7,15},{8,24},{9,1... | collective-permute-start | bytes 688136 | tf_op jit(solution)/shard_map/ppermute | solution.py:476
